TPU v7x, 32 devices: a whole 2x2x4 slice. The times are simulated.
32 devices in a mesh: wide: 8 (over z, x), narrow: 4 (over y, core).
Axes of the slice: x: 2, y: 2, z: 4, core: 2. Of those that a mesh axis runs over, the one named last changes fastest.
Arguments:
- tokens: bfloat16 [8192, 1024], P(('wide', 'narrow')), may hold values from -6 to 6
- memory: bfloat16 [128, 588, 1024], P(('wide', 'narrow')), may hold values from -6 to 6
- segment_ids: int32 [64, 128], P(('wide', 'narrow')), may hold values from 0 to 1, as said below
- page_map: int32 [64, 2], P(('wide', 'narrow')), may hold values from 0 to 127, as said below
- mem_lengths: int32 [128], P(('wide', 'narrow')), may hold values from 294 to 588
- gains: bfloat16 [3, 1024], P(None, ('wide', 'narrow')), may hold values from 0.099609375 to 1.8984375
- biases: bfloat16 [10, 1024], P(None, ('wide', 'narrow')), may hold values from -3 to 3
- fc1_bias: bfloat16 [4096], P(('wide', 'narrow')), may hold values from -3 to 3
- self_qkv: bfloat16 [3, 1024, 1024], P(None, 'wide', 'narrow'), may hold values from -0.25 to 0.25
- self_out: bfloat16 [1024, 1024], P('wide', 'narrow'), may hold values from -0.375 to 0.375
- cross_q: bfloat16 [1024, 1024], P('wide', 'narrow'), may hold values from -0.25 to 0.25
- cross_kv: bfloat16 [2, 1024, 1024], P(None, 'wide', 'narrow'), may hold values from -0.25 to 0.25
- cross_out: bfloat16 [1024, 1024], P('wide', 'narrow'), may hold values from -0.75 to 0.75
- fc1: bfloat16 [1024, 4096], P('wide', 'narrow'), may hold values from -0.1875 to 0.1875
- fc2: bfloat16 [4096, 1024], P('wide', 'narrow'), may hold values from -0.125 to 0.125
- cotangent: bfloat16 [8192, 1024], P(('wide', 'narrow')), may hold values from -6 to 6
Outputs:
- layer_out: bfloat16 [8192, 1024], P(('wide', 'narrow'))
- grad_tokens: bfloat16 [8192, 1024], P(('wide', 'narrow'))
- grad_memory: bfloat16 [128, 588, 1024], P(('wide', 'narrow'))
- grad_gains: float32 [3, 1024], P(None, ('wide', 'narrow'))
- grad_biases: float32 [10, 1024], P(None, ('wide', 'narrow'))
- grad_fc1_bias: float32 [4096], P(('wide', 'narrow'))
- grad_self_qkv: float32 [3, 1024, 1024], P(None, 'wide', 'narrow')
- grad_self_out: float32 [1024, 1024], P('wide', 'narrow')
- grad_cross_q: float32 [1024, 1024], P('wide', 'narrow')
- grad_cross_kv: float32 [2, 1024, 1024], P(None, 'wide', 'narrow')
- grad_cross_out: float32 [1024, 1024], P('wide', 'narrow')
- grad_fc1: float32 [1024, 4096], P('wide', 'narrow')
- grad_fc2: float32 [4096, 1024], P('wide', 'narrow')
Inputs may be any that keep to these rules, and one draw needn't show every extreme that they name: `segment_ids`: each row holds one or two pages: values never fall along a row, and each page present has at least 32 tokens. `page_map`: the entries of row r lie in [(r // 2) * 4, (r // 2 + 1) * 4); no memory is named twice; entry 1 is read only where the row has a page 1.
All inputs are finite; a program needn't handle non-finite values.
Results may differ from a plain program's by a relative error of at most 0.03.
The roundings to bfloat16 on the way count: a program that leaves them out, or rounds other values in their place, can miss the bound.
Values may be sent and summed in bfloat16 or wider, within the bound.
No kernel may reach another device: no remote copies, remote signals or barrier semaphores. Data moves between devices by JAX's collectives and lax.ppermute only.
A program may use at most 320 MiB of HBM per device.

v0:
```python
import math

import jax
import jax.numpy as jnp
from jax import lax
from jax.sharding import PartitionSpec as P

D = 1024
HEADS = 16
HEAD_DIM = 64


EPSILON = 1e-05
NEG_FILL = -1e30


def layer_norm(values, gain_row, bias_row):
    centre = values - jnp.mean(values, axis=-1, keepdims=True)
    spread = jnp.mean(centre * centre, axis=-1, keepdims=True)
    return centre * lax.rsqrt(spread + EPSILON) * gain_row + bias_row


def gelu_exact(values):
    return jax.nn.gelu(values, approximate=False)


def gather_weights(first, second):
    cols_first, cols_second = (
        lax.all_gather(first, "narrow", axis=2, tiled=True),
        lax.all_gather(second, "narrow", axis=2, tiled=True),
    )
    return (
        lax.all_gather(cols_first, "wide", axis=1, tiled=True),
        lax.all_gather(cols_second, "wide", axis=1, tiled=True),
    )


def settle(first, second):
    rows_first, rows_second = (
        lax.psum_scatter(
            first.astype(jnp.bfloat16), "wide", scatter_dimension=1, tiled=True
        ).astype(jnp.float32),
        lax.psum_scatter(
            second.astype(jnp.bfloat16), "wide", scatter_dimension=1, tiled=True
        ).astype(jnp.float32),
    )
    return (
        lax.psum_scatter(
            rows_first.astype(jnp.bfloat16), "narrow", scatter_dimension=2, tiled=True
        ).astype(jnp.float32),
        lax.psum_scatter(
            rows_second.astype(jnp.bfloat16), "narrow", scatter_dimension=2, tiled=True
        ).astype(jnp.float32),
    )


def masked_scores(queries, keys, allowed):
    head_scale = 1.0 / math.sqrt(queries.shape[-1])
    scores = (
        jnp.einsum("bthd,bshd->bhts", queries, keys, preferred_element_type=jnp.float32)
        * head_scale
    )
    return jnp.where(allowed[:, None], scores, NEG_FILL)


def attend(queries, keys, values, allowed):
    scores = masked_scores(queries, keys, allowed)
    row_top = jnp.max(scores, axis=-1, keepdims=True)
    expo_scores = jnp.exp(scores - row_top)
    row_total = jnp.sum(expo_scores, axis=-1, keepdims=True)
    soft_weights = (expo_scores / row_total).astype(jnp.bfloat16)
    mixed_heads = jnp.einsum(
        "bhts,bshd->bthd", soft_weights, values, preferred_element_type=jnp.float32
    )
    return (mixed_heads.astype(jnp.bfloat16), row_top + jnp.log(row_total))


def attend_back(queries, keys, values, allowed, log_total, grad_mixed):
    head_scale = 1.0 / math.sqrt(queries.shape[-1])
    soft_weights = jnp.exp(masked_scores(queries, keys, allowed) - log_total)
    grad_values = jnp.einsum(
        "bhts,bthd->bshd",
        soft_weights.astype(jnp.bfloat16),
        grad_mixed,
        preferred_element_type=jnp.float32,
    )
    grad_weights = jnp.einsum(
        "bthd,bshd->bhts", grad_mixed, values, preferred_element_type=jnp.float32
    )
    row_inner = jnp.sum(soft_weights * grad_weights, axis=-1, keepdims=True)
    grad_scores = (soft_weights * (grad_weights - row_inner)).astype(jnp.bfloat16)
    grad_queries = (
        jnp.einsum("bhts,bshd->bthd", grad_scores, keys, preferred_element_type=jnp.float32)
        * head_scale
    )
    grad_keys = (
        jnp.einsum("bhts,bthd->bshd", grad_scores, queries, preferred_element_type=jnp.float32)
        * head_scale
    )
    return (grad_queries, grad_keys, grad_values)


def attend_by_row(queries, keys, values, allowed):

    def one_row(items):
        return attend(items[0][None], items[1][None], items[2][None], items[3][None])

    mixed_rows, lse_rows = lax.map(one_row, (queries, keys, values, allowed))
    return (mixed_rows[:, 0], lse_rows[:, 0])


def attend_back_by_row(queries, keys, values, allowed, log_total, grad_mixed):

    def one_row(items):
        return attend_back(
            items[0][None],
            items[1][None],
            items[2][None],
            items[3][None],
            items[4][None],
            items[5][None],
        )

    grad_q, grad_k, grad_v = lax.map(
        one_row, (queries, keys, values, allowed, log_total, grad_mixed)
    )
    return (grad_q[:, 0], grad_k[:, 0], grad_v[:, 0])


def local(
    tokens,
    memory,
    segment_ids,
    page_map,
    mem_lengths,
    gains,
    biases,
    fc1_bias,
    self_qkv,
    self_out,
    cross_q,
    cross_kv,
    cross_out,
    fc1,
    fc2,
    cotangent,
):
    gain_all, bias_all, fc1_bias_all = (
        lax.all_gather(gains, ("wide", "narrow"), axis=1, tiled=True),
        lax.all_gather(biases, ("wide", "narrow"), axis=1, tiled=True),
        lax.all_gather(fc1_bias.reshape(1, -1), ("wide", "narrow"), axis=1, tiled=True),
    )
    gain_full = gain_all.astype(jnp.float32)
    bias_full = bias_all.astype(jnp.float32)
    fc1_bias_full = fc1_bias_all[0].astype(jnp.float32)
    cross_stack = jnp.concatenate((cross_q[None], cross_kv), axis=0)
    rows_here = segment_ids.shape[0]
    row_len = segment_ids.shape[1]
    token_count = tokens.shape[0]
    mem_count = memory.shape[0]
    mem_len = memory.shape[1]
    gathered_qkv, gathered_self_out = gather_weights(self_qkv, self_out[None])
    token_full = tokens.astype(jnp.float32)
    hidden_one, norm_one_back = jax.vjp(layer_norm, token_full, gain_full[0], bias_full[0])
    normed_one = hidden_one.astype(jnp.bfloat16)
    projected = jnp.einsum(
        "td,kde->kte", normed_one, gathered_qkv, preferred_element_type=jnp.float32
    )
    head_shape = (1, token_count, HEADS, HEAD_DIM)
    self_queries = (projected[0] + bias_full[1]).astype(jnp.bfloat16).reshape(head_shape)
    self_keys = projected[1].astype(jnp.bfloat16).reshape(head_shape)
    self_values = (projected[2] + bias_full[2]).astype(jnp.bfloat16).reshape(head_shape)
    seg_flat = segment_ids.reshape(-1)
    positions = jnp.arange(token_count, dtype=jnp.int32)
    row_of = positions // row_len
    self_allowed = (
        (row_of[:, None] == row_of[None, :])
        & (seg_flat[:, None] == seg_flat[None, :])
        & (positions[None, :] <= positions[:, None])
    )[None]
    self_mixed, self_lse = attend(self_queries, self_keys, self_values, self_allowed)
    self_mixed_flat = self_mixed.reshape(token_count, D)
    after_self = (
        token_full
        + jnp.dot(self_mixed_flat, gathered_self_out[0], preferred_element_type=jnp.float32)
        + bias_full[3]
    )
    gathered_cross, gathered_cross_out = gather_weights(cross_stack, cross_out[None])
    hidden_two, norm_two_back = jax.vjp(layer_norm, after_self, gain_full[1], bias_full[4])
    normed_two = hidden_two.astype(jnp.bfloat16)
    cross_shape = (rows_here, row_len, HEADS, HEAD_DIM)
    cross_queries = (
        (jnp.dot(normed_two, gathered_cross[0], preferred_element_type=jnp.float32) + bias_full[5])
        .astype(jnp.bfloat16)
        .reshape(cross_shape)
    )
    memory_proj = jnp.einsum(
        "mld,kde->kmle", memory, gathered_cross[1:], preferred_element_type=jnp.float32
    )
    mem_keys = memory_proj[0].astype(jnp.bfloat16)
    mem_values = (memory_proj[1] + bias_full[6]).astype(jnp.bfloat16)
    local_map = page_map - lax.axis_index(("wide", "narrow")) * mem_count
    page_picks = local_map[:, :, None] == jnp.arange(mem_count, dtype=jnp.int32)[None, None, :]
    picks_bf = page_picks.astype(jnp.bfloat16)
    key_shape = (rows_here, 2 * mem_len, HEADS, HEAD_DIM)
    row_keys = jnp.take(mem_keys, local_map.reshape(-1), axis=0).reshape(key_shape)
    row_values = jnp.take(mem_values, local_map.reshape(-1), axis=0).reshape(key_shape)
    row_lengths = jnp.sum(jnp.where(page_picks, mem_lengths[None, None, :], 0), axis=-1)
    key_positions = jnp.arange(2 * mem_len, dtype=jnp.int32)
    part_of = key_positions // mem_len
    index_of = key_positions % mem_len
    length_of = jnp.where(part_of[None, :] == 0, row_lengths[:, 0:1], row_lengths[:, 1:2])
    cross_allowed = (segment_ids[:, :, None] == part_of[None, None, :]) & (
        index_of[None, None, :] < length_of[:, None, :]
    )
    cross_mixed, cross_lse = attend_by_row(cross_queries, row_keys, row_values, cross_allowed)
    cross_mixed_flat = cross_mixed.reshape(token_count, D)
    after_cross = (
        after_self
        + jnp.dot(cross_mixed_flat, gathered_cross_out[0], preferred_element_type=jnp.float32)
        + bias_full[7]
    )
    gathered_fc1, gathered_fc2 = gather_weights(fc1[None], fc2[None])
    hidden_three, norm_three_back = jax.vjp(layer_norm, after_cross, gain_full[2], bias_full[8])
    normed_three = hidden_three.astype(jnp.bfloat16)
    pre_act = (
        jnp.dot(normed_three, gathered_fc1[0], preferred_element_type=jnp.float32) + fc1_bias_full
    )
    activated_full, gelu_back = jax.vjp(gelu_exact, pre_act)
    activated = activated_full.astype(jnp.bfloat16)
    layer_full = (
        after_cross
        + jnp.dot(activated, gathered_fc2[0], preferred_element_type=jnp.float32)
        + bias_full[9]
    )
    layer_out = layer_full.astype(jnp.bfloat16)
    tied_shards = lax.optimization_barrier(
        (layer_out, self_qkv, self_out, cross_stack, cross_out, fc1, fc2)
    )
    back_fc1, back_fc2 = gather_weights(tied_shards[5][None], tied_shards[6][None])
    back_cross, back_cross_out = gather_weights(tied_shards[3], tied_shards[4][None])
    back_qkv, back_self_out = gather_weights(tied_shards[1], tied_shards[2][None])
    grad_out = cotangent.astype(jnp.float32)
    grad_fc2_full = jnp.einsum(
        "tf,td->fd", activated, cotangent, preferred_element_type=jnp.float32
    )
    grad_bias_nine = jnp.sum(grad_out, axis=0)
    grad_act = jnp.einsum("td,fd->tf", cotangent, back_fc2[0], preferred_element_type=jnp.float32)
    grad_pre = gelu_back(grad_act)[0].astype(jnp.bfloat16)
    grad_fc1_full = jnp.einsum(
        "td,tf->df", normed_three, grad_pre, preferred_element_type=jnp.float32
    )
    grad_fc1_bias_full = jnp.sum(grad_pre, axis=0, dtype=jnp.float32)
    grad_normed_three = jnp.einsum(
        "tf,df->td", grad_pre, back_fc1[0], preferred_element_type=jnp.float32
    )
    grad_from_three, grad_gain_three, grad_bias_eight = norm_three_back(grad_normed_three)
    grad_after_cross = grad_out + grad_from_three
    grad_fc1_shard, grad_fc2_shard = settle(grad_fc1_full[None], grad_fc2_full[None])
    grad_branch_two = grad_after_cross.astype(jnp.bfloat16)
    grad_cross_out_full = jnp.einsum(
        "td,te->de", cross_mixed_flat, grad_branch_two, preferred_element_type=jnp.float32
    )
    grad_bias_seven = jnp.sum(grad_branch_two, axis=0, dtype=jnp.float32)
    grad_cross_mixed = (
        jnp.einsum(
            "te,de->td", grad_branch_two, back_cross_out[0], preferred_element_type=jnp.float32
        )
        .astype(jnp.bfloat16)
        .reshape(cross_shape)
    )
    grad_cq, grad_rk, grad_rv = attend_back_by_row(
        cross_queries, row_keys, row_values, cross_allowed, cross_lse, grad_cross_mixed
    )
    grad_cq_bf = grad_cq.reshape(token_count, D).astype(jnp.bfloat16)
    grad_rk_bf = grad_rk.astype(jnp.bfloat16).reshape(rows_here, 2, mem_len, D)
    grad_rv_bf = grad_rv.astype(jnp.bfloat16).reshape(rows_here, 2, mem_len, D)
    grad_mem_keys = jnp.einsum(
        "rpm,rpld->mld", picks_bf, grad_rk_bf, preferred_element_type=jnp.float32
    ).astype(jnp.bfloat16)
    grad_mem_values = jnp.einsum(
        "rpm,rpld->mld", picks_bf, grad_rv_bf, preferred_element_type=jnp.float32
    ).astype(jnp.bfloat16)
    grad_cross_stack = jnp.stack(
        (
            jnp.einsum("td,te->de", normed_two, grad_cq_bf, preferred_element_type=jnp.float32),
            jnp.einsum("mld,mle->de", memory, grad_mem_keys, preferred_element_type=jnp.float32),
            jnp.einsum("mld,mle->de", memory, grad_mem_values, preferred_element_type=jnp.float32),
        )
    )
    grad_bias_five = jnp.sum(grad_cq_bf, axis=0, dtype=jnp.float32)
    grad_bias_six = jnp.sum(grad_mem_values, axis=(0, 1), dtype=jnp.float32)
    grad_memory = (
        jnp.einsum("mle,de->mld", grad_mem_keys, back_cross[1], preferred_element_type=jnp.float32)
        + jnp.einsum(
            "mle,de->mld", grad_mem_values, back_cross[2], preferred_element_type=jnp.float32
        )
    ).astype(jnp.bfloat16)
    grad_normed_two = jnp.einsum(
        "te,de->td", grad_cq_bf, back_cross[0], preferred_element_type=jnp.float32
    )
    grad_from_two, grad_gain_two, grad_bias_four = norm_two_back(grad_normed_two)
    grad_after_self = grad_after_cross + grad_from_two
    grad_cross_shard, grad_cross_out_shard = settle(grad_cross_stack, grad_cross_out_full[None])
    grad_branch_one = grad_after_self.astype(jnp.bfloat16)
    grad_self_out_full = jnp.einsum(
        "td,te->de", self_mixed_flat, grad_branch_one, preferred_element_type=jnp.float32
    )
    grad_bias_three = jnp.sum(grad_branch_one, axis=0, dtype=jnp.float32)
    grad_self_mixed = (
        jnp.einsum(
            "te,de->td", grad_branch_one, back_self_out[0], preferred_element_type=jnp.float32
        )
        .astype(jnp.bfloat16)
        .reshape(head_shape)
    )
    grad_sq, grad_sk, grad_sv = attend_back(
        self_queries, self_keys, self_values, self_allowed, self_lse, grad_self_mixed
    )
    grad_proj = jnp.stack(
        (
            grad_sq.reshape(token_count, D),
            grad_sk.reshape(token_count, D),
            grad_sv.reshape(token_count, D),
        )
    ).astype(jnp.bfloat16)
    grad_qkv_full = jnp.einsum(
        "td,kte->kde", normed_one, grad_proj, preferred_element_type=jnp.float32
    )
    grad_bias_one = jnp.sum(grad_proj[0], axis=0, dtype=jnp.float32)
    grad_bias_two = jnp.sum(grad_proj[2], axis=0, dtype=jnp.float32)
    grad_normed_one = jnp.einsum(
        "kte,kde->td", grad_proj, back_qkv, preferred_element_type=jnp.float32
    )
    grad_from_one, grad_gain_one, grad_bias_zero = norm_one_back(grad_normed_one)
    grad_tokens = (grad_after_self + grad_from_one).astype(jnp.bfloat16)
    grad_qkv_shard, grad_self_out_shard = settle(grad_qkv_full, grad_self_out_full[None])
    gain_grads = jnp.stack((grad_gain_one, grad_gain_two, grad_gain_three))
    bias_grads = jnp.stack(
        (
            grad_bias_zero,
            grad_bias_one,
            grad_bias_two,
            grad_bias_three,
            grad_bias_four,
            grad_bias_five,
            grad_bias_six,
            grad_bias_seven,
            grad_bias_eight,
            grad_bias_nine,
        )
    )
    gain_shard, bias_shard, fc1_bias_shard = (
        lax.psum_scatter(gain_grads, ("wide", "narrow"), scatter_dimension=1, tiled=True),
        lax.psum_scatter(bias_grads, ("wide", "narrow"), scatter_dimension=1, tiled=True),
        lax.psum_scatter(
            grad_fc1_bias_full[None], ("wide", "narrow"), scatter_dimension=1, tiled=True
        ),
    )
    return (
        layer_out,
        grad_tokens,
        grad_memory,
        gain_shard,
        bias_shard,
        fc1_bias_shard[0],
        grad_qkv_shard,
        grad_self_out_shard[0],
        grad_cross_shard[0],
        grad_cross_shard[1:],
        grad_cross_out_shard[0],
        grad_fc1_shard[0],
        grad_fc2_shard[0],
    )


def solution(mesh):
    in_specs = (
        P(("wide", "narrow"), None),
        P(("wide", "narrow"), None, None),
        P(("wide", "narrow"), None),
        P(("wide", "narrow"), None),
        P(("wide", "narrow")),
        P(None, ("wide", "narrow")),
        P(None, ("wide", "narrow")),
        P(("wide", "narrow")),
        P(None, "wide", "narrow"),
        P("wide", "narrow"),
        P("wide", "narrow"),
        P(None, "wide", "narrow"),
        P("wide", "narrow"),
        P("wide", "narrow"),
        P("wide", "narrow"),
        P(("wide", "narrow"), None),
    )
    out_specs = (
        P(("wide", "narrow"), None),
        P(("wide", "narrow"), None),
        P(("wide", "narrow"), None, None),
        P(None, ("wide", "narrow")),
        P(None, ("wide", "narrow")),
        P(("wide", "narrow")),
        P(None, "wide", "narrow"),
        P("wide", "narrow"),
        P("wide", "narrow"),
        P(None, "wide", "narrow"),
        P("wide", "narrow"),
        P("wide", "narrow"),
        P("wide", "narrow"),
    )
    return jax.shard_map(local, mesh=mesh, in_specs=in_specs, out_specs=out_specs, check_vma=False)
```

profile of v0, /device:TPU:0, one launch (start us, length us, event | category | flops | bytes accessed | tf_op | source)
XLA Modules:
  0.0 2439.3 jit_solution(11099079106070786412)
XLA Ops:
  8.8 11.7 all_gather.83
  20.6 8.4 all-gather
  30.6 9.2 all_gather.87
  39.9 8.1 all-gather.2
  49.0 43.0 %all-gather.18 = bf16[32,32,10]{1,2,0:T(8,128)(2,1)S(1)} all-gather(bf16[1,32,10]{1,2,0:T(8,128)(2,1)S(1)} %bitcast.434), channel_id=1, replica_groups=mesh['wide'=8,'narrow'=4] {'wide','narrow'}, dimensions={0}, use_global_device_ids=true | all-gather | bytes 21120 | tf_op jit(solution)/shard_map/all_gather | solution.py:150
  92.2 37.0 %all-gather.17 = bf16[32,32,3]{1,2,0:T(4,128)(2,1)S(1)} all-gather(bf16[1,32,3]{1,2,0:T(4,128)(2,1)S(1)} %bitcast.445), channel_id=1, replica_groups=mesh['wide'=8,'narrow'=4] {'wide','narrow'}, dimensions={0}, use_global_device_ids=true | all-gather | bytes 6336 | tf_op jit(solution)/shard_map/all_gather | solution.py:149
  130.1 38.0 %all-gather.19 = bf16[32,1,128]{2,1,0:T(2,128)(2,1)S(1)} all-gather(bf16[1,1,128]{2,1,0:T(2,128)(2,1)S(1)} %bitcast.447), channel_id=8, replica_groups=mesh['wide'=8,'narrow'=4] {'wide','narrow'}, dimensions={0}, use_global_device_ids=true | all-gather | bytes 8448 | tf_op jit(solution)/shard_map/all_gather | solution.py:151
  186.0 15.9 all-gather.45.cloned.1.call-done
  204.6 96.9 %all-gather.39.cloned.1.call-done = bf16[3,1024,1024]{2,1,0:T(8,128)(2,1)} async-done(((bf16[3,128,1024]{2,1,0:T(8,128)(2,1)}), bf16[3,1024,1024]{2,1,0:T(8,128)(2,1)}) %all-gather.39.cloned.1.call-update) | async-done | bytes 6291472 | tf_op jit(solution)/shard_map/all_gather | solution.py:33
  305.4 19.7 convolution_bitcast_fusion
  325.1 7.6 fusion.58
  338.2 6.7 fusion.59
  350.6 8.6 broadcast_select_fusion
  359.2 9.8 reshape.678
  369.0 12.6 copy.157
  381.6 9.6 reshape.680
  391.2 12.5 copy.159
  403.7 19.8 while.26
  427.0 49.5 %all-gather.51.cloned.1.call-done = bf16[1024,4096]{1,0:T(8,128)(2,1)} async-done(((bf16[128,4096]{1,0:T(8,128)(2,1)}), bf16[1024,4096]{1,0:T(8,128)(2,1)}) %all-gather.51.cloned.1.call-update) | async-done | bytes 8388624 | tf_op jit(solution)/shard_map/all_gather | solution.py:33
  476.5 16.1 multiply_convert_fusion.2
  492.6 109.2 %all-gather.55.cloned.1.call-done = bf16[4096,1024]{1,0:T(8,128)(2,1)} async-done(((bf16[512,1024]{1,0:T(8,128)(2,1)}), bf16[4096,1024]{1,0:T(8,128)(2,1)}) %all-gather.55.cloned.1.call-update) | async-done | bytes 8388624 | tf_op jit(solution)/shard_map/all_gather | solution.py:34
  601.8 7.2 fusion.106
  609.7 14.6 all-gather.57.cloned.1.call-done
  624.3 18.1 all-gather.61.cloned.1.call-done
  648.8 9.2 all_gather.102
  664.5 9.2 all_gather.106
  674.1 7.3 convert_bitcast_fusion
  681.5 88.0 %all-gather.59.cloned.1.call-done = bf16[4096,1024]{1,0:T(8,128)(2,1)} async-done(((bf16[512,1024]{1,0:T(8,128)(2,1)}), bf16[4096,1024]{1,0:T(8,128)(2,1)}) %all-gather.59.cloned.1.call-update) | async-done | bytes 8388624 | tf_op jit(solution)/shard_map/all_gather | solution.py:34
  769.5 13.0 convert_reduce_fusion.1
  782.5 112.1 %all-gather.63.cloned.1.call-done = bf16[1024,4096]{1,0:T(8,128)(2,1)} async-done(((bf16[128,4096]{1,0:T(8,128)(2,1)}), bf16[1024,4096]{1,0:T(8,128)(2,1)}) %all-gather.63.cloned.1.call-update) | async-done | bytes 8388624 | tf_op jit(solution)/shard_map/all_gather | solution.py:33
  894.6 7.2 multiply_reduce_fusion.2
  903.1 41.1 %all-gather.65.cloned.1.call-done = bf16[1024,1024]{1,0:T(8,128)(2,1)} async-done(((bf16[128,1024]{1,0:T(8,128)(2,1)}), bf16[1024,1024]{1,0:T(8,128)(2,1)}) %all-gather.65.cloned.1.call-update) | async-done | bytes 2097168 | tf_op jit(solution)/shard_map/all_gather | solution.py:34
  954.2 69.1 %while.27 = (s32[]{:T(128)}, bf16[2,1,128,16,64]{2,4,3,1,0:T(8,128)(2,1)S(1)}, bf16[2,1,1176,16,64]{2,4,3,1,0:T(8,128)(2,1)}, bf16[2,1,1176,16,64]{2,4,3,1,0:T(8...) while((s32[]{:T(128)}, ...), condition=%wide.region_17.19_spmd, body=%wide.region_15.18_spmd.sunk | while | flops 1564416000 | bytes 178526480 | solution.py:124
  965.5 9.8 multiply_convert_fusion.4
  993.6 6.5 multiply_reduce_fusion.9
  1000.2 9.7 multiply_convert_fusion.4
  1023.9 12.7 convert_element_type.261
  1036.7 24.3 copy.176
  1060.9 12.9 convert_element_type.258
  1073.8 24.8 %copy.174 = bf16[2,2,588,1024]{3,0,1,2:T(2,128)(2,1)} copy(bf16[2,2,588,1024]{2,1,3,0:T(2,128)(2,1)} %convert_element_type.258) | data formatting | bytes 9633792 | tf_op jit(solution)/shard_map/convert_element_type | solution.py:276
  1108.0 9.1 bitcast_convert_fusion.1
  1117.1 10.9 convert_reduce_fusion
  1128.1 10.9 fusion.85
  1139.0 11.1 fusion.84
  1179.0 14.4 copy.207
  1193.4 10.2 copy.217
  1204.9 7.4 convert_bitcast_fusion.1
  1225.2 118.4 %reduce-scatter.42.cloned.1.call-done = bf16[1,512,1024]{2,1,0:T(8,128)(2,1)} async-done(((bf16[1,4096,1024]{2,1,0:T(8,128)(2,1)}), bf16[1,512,1024]{2,1,0:T(8,128)(2,1)}) %reduce-scatter.42.cloned.1.call-update) | async-done | bytes 1048592 | tf_op jit(solution)/shard_map/reduce_scatter | solution.py:43
  1343.7 70.5 %reduce-scatter.34.cloned.1.call-done = bf16[1,128,1024]{2,1,0:T(8,128)(2,1)} async-done(((bf16[1,1024,1024]{2,1,0:T(8,128)(2,1)}), bf16[1,128,1024]{2,1,0:T(8,128)(2,1)}) %reduce-scatter.34.cloned.1.call-update) | async-done | bytes 262160 | tf_op jit(solution)/shard_map/reduce_scatter | solution.py:43
  1414.2 70.6 %reduce-scatter.26.cloned.1.call-done = bf16[1,128,1024]{2,1,0:T(8,128)(2,1)} async-done(((bf16[1,1024,1024]{2,1,0:T(8,128)(2,1)}), bf16[1,128,1024]{2,1,0:T(8,128)(2,1)}) %reduce-scatter.26.cloned.1.call-update) | async-done | bytes 262160 | tf_op jit(solution)/shard_map/reduce_scatter | solution.py:43
  1484.9 121.2 %reduce-scatter.30.cloned.1.call-done = bf16[3,128,1024]{2,1,0:T(8,128)(2,1)} async-done(((bf16[3,1024,1024]{2,1,0:T(8,128)(2,1)}), bf16[3,128,1024]{2,1,0:T(8,128)(2,1)}) %reduce-scatter.30.cloned.1.call-update) | async-done | bytes 786448 | tf_op jit(solution)/shard_map/reduce_scatter | solution.py:40
  1606.1 121.1 %reduce-scatter.52.cloned.1.call-done = bf16[128,3072]{1,0:T(8,128)(2,1)} async-done(((bf16[1024,3072]{1,0:T(8,128)(2,1)}), bf16[128,3072]{1,0:T(8,128)(2,1)}) %reduce-scatter.52.cloned.1.call-update) | async-done | bytes 786448
  1731.9 12.0 fusion.63
  1743.9 135.4 %reduce-scatter.38.cloned.1.call-done = bf16[1,128,4096]{2,1,0:T(8,128)(2,1)} async-done(((bf16[1,1024,4096]{2,1,0:T(8,128)(2,1)}), bf16[1,128,4096]{2,1,0:T(8,128)(2,1)}) %reduce-scatter.38.cloned.1.call-update) | async-done | bytes 1048592 | tf_op jit(solution)/shard_map/reduce_scatter | solution.py:40
  1879.4 12.0 add_convert_fusion
  1898.6 116.5 %reduce-scatter.46.cloned.1.call-done = f32[32,3]{1,0:T(8,128)} async-done(((f32[1024,3]{1,0:T(8,128)}), f32[32,3]{1,0:T(8,128)}) %reduce-scatter.46.cloned.1.call-update) | async-done | bytes 400
  2016.5 133.7 %reduce-scatter.50.cloned.1.call-done = f32[128,1]{1,0:T(8,128)} async-done(((f32[4096,1]{1,0:T(8,128)}), f32[128,1]{1,0:T(8,128)}) %reduce-scatter.50.cloned.1.call-update) | async-done | bytes 528
  2151.6 131.2 %reduce-scatter.48.cloned.1.call-done = f32[32,10]{1,0:T(8,128)} async-done(((f32[1024,10]{1,0:T(8,128)}), f32[32,10]{1,0:T(8,128)}) %reduce-scatter.48.cloned.1.call-update) | async-done | bytes 1296
  2284.3 22.0 reduce-scatter.44.cloned.1.call-done
  2308.1 20.6 reduce-scatter.36.cloned.1.call-done
  2330.1 21.2 reduce-scatter.28.cloned.1.call-done
  2352.8 24.3 reduce-scatter.32.cloned.1.call-done
  2379.7 23.3 reduce-scatter.24.cloned.1.call-done
  2405.5 25.0 %reduce-scatter.40.cloned.1.call-done = bf16[1,128,1024]{2,1,0:T(8,128)(2,1)} async-done(((bf16[1,128,4096]{2,1,0:T(8,128)(2,1)}), bf16[1,128,1024]{2,1,0:T(8,128)(2,1)}) %reduce-scatter.40.cloned.1.call-update) | async-done | bytes 262160 | tf_op jit(solution)/shard_map/reduce_scatter | solution.py:48
  (439 shorter events, 212.1 us)
Async XLA Ops:
  7.2 41.8 %copy-start.83 = (bf16[10,32]{1,0:T(8,128)(2,1)S(1)}, bf16[10,32]{1,0:T(8,128)(2,1)}, u32[]{:S(2)}) copy-start(bf16[10,32]{1,0:T(8,128)(2,1)} %param.28) | copy-start | bytes 1924
  7.2 85.0 %copy-start.92 = (bf16[3,32]{1,0:T(4,128)(2,1)S(1)}, bf16[3,32]{1,0:T(4,128)(2,1)}, u32[]{:S(2)}) copy-start(bf16[3,32]{1,0:T(4,128)(2,1)} %param.27) | copy-start | bytes 580
  7.2 122.9 %copy-start.95 = (bf16[128]{0:T(256)(128)(2,1)S(1)}, bf16[128]{0:T(256)(128)(2,1)}, u32[]{:S(2)}) copy-start(bf16[128]{0:T(256)(128)(2,1)} %param.29) | copy-start | bytes 772
  7.2 162.1 %copy-start.96 = (s32[4]{0:T(128)S(1)}, s32[4]{0:T(128)}, u32[]{:S(2)}) copy-start(s32[4]{0:T(128)} %param.26) | copy-start | bytes 52
  7.2 162.3 %copy-start.9 = (bf16[256,1024]{1,0:T(8,128)(2,1)S(1)}, bf16[256,1024]{1,0:T(8,128)(2,1)}, u32[]{:S(2)}) copy-start(bf16[256,1024]{1,0:T(8,128)(2,1)} %param.22) | copy-start | bytes 1572868
  7.3 40.8 %all-gather.49.cloned.1.call-start = ((), (), s32[]{:S(2)}) async-start(), calls=%async_computation.32 | async-start | bytes 1310720 | tf_op jit(solution)/shard_map/all_gather | solution.py:29
  8.0 164.4 %all-gather.53.cloned.1.call-start = ((), (), s32[]{:S(2)}) async-start(), calls=%async_computation.34 | async-start | bytes 1310720 | tf_op jit(solution)/shard_map/all_gather | solution.py:30
  8.7 162.4 %copy-start.78 = (s32[2,128]{1,0:T(2,128)S(1)}, s32[2,128]{1,0:T(2,128)}, u32[]{:S(2)}) copy-start(s32[2,128]{1,0:T(2,128)} %param.24) | copy-start | bytes 3076
  8.7 164.1 %all-gather.37.cloned.1.call-start = ((), (), s32[]{:S(2)}) async-start(), calls=%async_computation.15 | async-start | bytes 7077888 | tf_op jit(solution)/shard_map/all_gather | solution.py:33
  20.6 181.3 %all-gather.45.cloned.1.call-start = ((), (), s32[]{:S(2)}) async-start(), calls=%async_computation.30 | async-start | bytes 2359296 | tf_op jit(solution)/shard_map/all_gather | solution.py:34
  29.0 272.5 %all-gather.39.cloned.1.call-start = ((), (), s32[]{:S(2)}) async-start(), calls=%async_computation.16 | async-start | bytes 7077888 | tf_op jit(solution)/shard_map/all_gather | solution.py:33
  39.8 384.3 %all-gather.47.cloned.1.call-start = ((), (), s32[]{:S(2)}) async-start(), calls=%async_computation.31 | async-start | bytes 2359296 | tf_op jit(solution)/shard_map/all_gather | solution.py:34
  48.0 428.5 %all-gather.51.cloned.1.call-start = ((), (), s32[]{:S(2)}) async-start(), calls=%async_computation.33 | async-start | bytes 9437184 | tf_op jit(solution)/shard_map/all_gather | solution.py:33
  48.7 553.0 %all-gather.55.cloned.1.call-start = ((), (), s32[]{:S(2)}) async-start(), calls=%async_computation.35 | async-start | bytes 9437184 | tf_op jit(solution)/shard_map/all_gather | solution.py:34
  49.0 128.5 %copy-start.89 = (s32[2,2]{0,1:T(2,128)}, s32[2,2]{0,1:T(2,128)S(1)}, u32[]{:S(2)}) copy-start(s32[2,2]{0,1:T(2,128)S(1)} %copy.154) | copy-start | bytes 52
  129.9 47.6 %copy-start.84 = (f32[1,1024]{1,0:T(1,128)}, f32[1,1024]{1,0:T(1,128)S(1)}, u32[]{:S(2)}) copy-start(f32[1,1024]{1,0:T(1,128)S(1)} %get-tuple-element.315) | copy-start | bytes 12292
  130.0 52.2 %copy-start.49 = (f32[16,64]{1,0:T(8,128)}, f32[16,64]{1,0:T(8,128)S(1)}, u32[]{:S(2)}) copy-start(f32[16,64]{1,0:T(8,128)S(1)} %add.270) | copy-start | bytes 12292
  130.1 53.7 %copy-start.58 = (f32[16,64]{1,0:T(8,128)}, f32[16,64]{1,0:T(8,128)S(1)}, u32[]{:S(2)}) copy-start(f32[16,64]{1,0:T(8,128)S(1)} %add.267) | copy-start | bytes 12292
  171.1 130.3 %copy-start.55 = (f32[1,1024]{1,0:T(1,128)}, f32[1,1024]{1,0:T(1,128)S(1)}, u32[]{:S(2)}) copy-start(f32[1,1024]{1,0:T(1,128)S(1)} %get-tuple-element.317) | copy-start | bytes 12292
  172.4 451.8 %all-gather.57.cloned.1.call-start = ((), (), s32[]{:S(2)}) async-start(), calls=%async_computation.36 | async-start | bytes 1310720 | tf_op jit(solution)/shard_map/all_gather | solution.py:30
  186.0 115.5 %copy-start.27 = (bf16[16,64,256]{2,1,0:T(8,128)(2,1)}, bf16[16,64,256]{2,1,0:T(8,128)(2,1)S(1)}, u32[]{:S(2)}) copy-start(bf16[16,64,256]{2,1,0:T(8,128)(2,1)S(1)} %fusion.113) | copy-start | bytes 1572868
  186.0 115.5 %copy-start.65 = (f32[1,1024]{1,0:T(1,128)S(1)}, f32[1,1024]{1,0:T(1,128)}, u32[]{:S(2)}) copy-start(f32[1,1024]{1,0:T(1,128)} %get-tuple-element.310) | copy-start | bytes 12292
  186.0 115.5 %copy-start.88 = (f32[1,1024]{1,0:T(1,128)S(1)}, f32[1,1024]{1,0:T(1,128)}, u32[]{:S(2)}) copy-start(f32[1,1024]{1,0:T(1,128)} %get-tuple-element.309) | copy-start | bytes 12292
  204.3 99.6 %copy-start.4 = (f32[256,1024]{1,0:T(8,128)}, f32[256,1024]{1,0:T(8,128)S(1)}, u32[]{:S(2)}) copy-start(f32[256,1024]{1,0:T(8,128)S(1)} %get-tuple-element.326) | copy-start | bytes 3145732
  204.3 101.1 %copy-start.69 = (f32[256]{0:T(256)}, f32[256]{0:T(256)S(1)}, u32[]{:S(2)}) copy-start(f32[256]{0:T(256)S(1)} %broadcast_multiply_fusion.1) | copy-start | bytes 3076
  204.6 96.9 %copy-start.81 = (f32[256]{0:T(256)}, f32[256]{0:T(256)S(1)}, u32[]{:S(2)}) copy-start(f32[256]{0:T(256)S(1)} %multiply_reduce_fusion.7) | copy-start | bytes 3076
  204.6 100.8 %copy-start.76 = (f32[256]{0:T(256)}, f32[256]{0:T(256)S(1)}, u32[]{:S(2)}) copy-start(f32[256]{0:T(256)S(1)} %fusion.147) | copy-start | bytes 3076
  423.5 53.0 %copy-start.43 = (f32[1,1024]{1,0:T(1,128)S(1)}, f32[1,1024]{1,0:T(1,128)}, u32[]{:S(2)}) copy-start(f32[1,1024]{1,0:T(1,128)} %get-tuple-element.316) | copy-start | bytes 12292
  423.5 53.0 %copy-start.47 = (f32[1,1024]{1,0:T(1,128)S(1)}, f32[1,1024]{1,0:T(1,128)}, u32[]{:S(2)}) copy-start(f32[1,1024]{1,0:T(1,128)} %get-tuple-element.307) | copy-start | bytes 12292
  423.5 53.0 %copy-start.68 = (f32[32,1,128]{2,1,0:T(1,128)S(1)}, f32[32,1,128]{2,1,0:T(1,128)}, u32[]{:S(2)}) copy-start(f32[32,1,128]{2,1,0:T(1,128)} %add.313) | copy-start | bytes 49156
  424.1 68.5 %copy-start.21 = (bf16[2,1,128,16,64]{2,0,4,3,1:T(2,128)(2,1)}, bf16[2,1,128,16,64]{2,0,4,3,1:T(2,128)(2,1)S(1)}, u32[]{:S(2)}) copy-start(bf16[2,1,128,16,64]{2,0,4,3,1:T(2,128)(2,1)S(1)} %copy.160) | copy-start | bytes 1572868
  426.7 475.1 %copy-start.7 = (f32[256,1024]{1,0:T(8,128)}, f32[256,1024]{1,0:T(8,128)S(1)}, u32[]{:S(2)}) copy-start(f32[256,1024]{1,0:T(8,128)S(1)} %get-tuple-element.328) | copy-start | bytes 3145732
  426.7 475.1 %copy-start.60 = (f32[256]{0:T(256)}, f32[256]{0:T(256)S(1)}, u32[]{:S(2)}) copy-start(f32[256]{0:T(256)S(1)} %broadcast_multiply_fusion) | copy-start | bytes 3076
  427.0 474.9 %copy-start.71 = (f32[256]{0:T(256)}, f32[256]{0:T(256)S(1)}, u32[]{:S(2)}) copy-start(f32[256]{0:T(256)S(1)} %fusion.148) | copy-start | bytes 3076
  476.5 125.3 %copy-start.87 = (f32[1,1024]{1,0:T(1,128)S(1)}, f32[1,1024]{1,0:T(1,128)}, u32[]{:S(2)}) copy-start(f32[1,1024]{1,0:T(1,128)} %get-tuple-element.306) | copy-start | bytes 12292
  601.8 47.0 %copy-start.34 = (bf16[3,128,256]{2,1,0:T(8,128)(2,1)S(1)}, bf16[3,128,256]{2,1,0:T(8,128)(2,1)}, u32[]{:S(2)}) copy-start(bf16[3,128,256]{2,1,0:T(8,128)(2,1)} %copy-done.33) | copy-start | bytes 589828
  609.0 49.1 %copy-start.42 = (bf16[128,256]{1,0:T(8,128)(2,1)S(1)}, bf16[128,256]{1,0:T(8,128)(2,1)}, u32[]{:S(2)}) copy-start(bf16[128,256]{1,0:T(8,128)(2,1)} %param.31) | copy-start | bytes 196612
  609.0 55.5 %copy-start.35 = (bf16[3,128,256]{2,1,0:T(8,128)(2,1)S(1)}, bf16[3,128,256]{2,1,0:T(8,128)(2,1)}, u32[]{:S(2)}) copy-start(bf16[3,128,256]{2,1,0:T(8,128)(2,1)} %param.30) | copy-start | bytes 589828
  609.0 65.1 %copy-start.16 = (bf16[256,1024]{1,0:T(8,128)(2,1)S(1)}, bf16[256,1024]{1,0:T(8,128)(2,1)}, u32[]{:S(2)}) copy-start(bf16[256,1024]{1,0:T(8,128)(2,1)} %param.37) | copy-start | bytes 1572868
  609.0 33.4 %all-gather.61.cloned.1.call-start = ((), (), s32[]{:S(2)}) async-start(), calls=%async_computation.38 | async-start | bytes 1310720 | tf_op jit(solution)/shard_map/all_gather | solution.py:29
  609.6 159.9 %all-gather.59.cloned.1.call-start = ((), (), s32[]{:S(2)}) async-start(), calls=%async_computation.37 | async-start | bytes 9437184 | tf_op jit(solution)/shard_map/all_gather | solution.py:34
  624.2 270.4 %all-gather.63.cloned.1.call-start = ((), (), s32[]{:S(2)}) async-start(), calls=%async_computation.39 | async-start | bytes 9437184 | tf_op jit(solution)/shard_map/all_gather | solution.py:33
  642.4 301.8 %all-gather.65.cloned.1.call-start = ((), (), s32[]{:S(2)}) async-start(), calls=%async_computation.40 | async-start | bytes 2359296 | tf_op jit(solution)/shard_map/all_gather | solution.py:34
  648.7 449.9 %all-gather.41.cloned.1.call-start = ((), (), s32[]{:S(2)}) async-start(), calls=%async_computation.17 | async-start | bytes 7077888 | tf_op jit(solution)/shard_map/all_gather | solution.py:33
  658.0 496.0 %all-gather.67.cloned.1.call-start = ((), (), s32[]{:S(2)}) async-start(), calls=%async_computation.41 | async-start | bytes 2359296 | tf_op jit(solution)/shard_map/all_gather | solution.py:34
  664.4 548.0 %all-gather.43.cloned.1.call-start = ((), (), s32[]{:S(2)}) async-start(), calls=%async_computation.18 | async-start | bytes 7077888 | tf_op jit(solution)/shard_map/all_gather | solution.py:33
  673.7 669.9 %reduce-scatter.42.cloned.1.call-start = ((), (), s32[]{:S(2)}) async-start(), calls=%async_computation.28 | async-start | bytes 9437184 | tf_op jit(solution)/shard_map/reduce_scatter | solution.py:43
  681.4 732.7 %reduce-scatter.34.cloned.1.call-start = ((), (), s32[]{:S(2)}) async-start(), calls=%async_computation.24 | async-start | bytes 2359296 | tf_op jit(solution)/shard_map/reduce_scatter | solution.py:43
  902.3 45.1 %copy-start.11 = (f32[256,1024]{1,0:T(8,128)}, f32[256,1024]{1,0:T(8,128)S(1)}, u32[]{:S(2)}) copy-start(f32[256,1024]{1,0:T(8,128)S(1)} %get-tuple-element.296) | copy-start | bytes 3145732
  902.3 49.6 %copy-start.22 = (bf16[2,1,128,16,64]{2,0,4,3,1:T(2,128)(2,1)S(1)}, bf16[2,1,128,16,64]{2,0,4,3,1:T(2,128)(2,1)}, u32[]{:S(2)}) copy-start(bf16[2,1,128,16,64]{2,0,4,3,1:T(2,128)(2,1)} %copy-done.21) | copy-start | bytes 1572868
  954.0 530.8 %reduce-scatter.26.cloned.1.call-start = ((), (), s32[]{:S(2)}) async-start(), calls=%async_computation.20 | async-start | bytes 2359296 | tf_op jit(solution)/shard_map/reduce_scatter | solution.py:43
  1023.9 74.7 %copy-start.29 = (bf16[2,1,128,16,64]{2,0,4,3,1:T(2,128)(2,1)}, bf16[2,1,128,16,64]{2,0,4,3,1:T(2,128)(2,1)S(1)}, u32[]{:S(2)}) copy-start(bf16[2,1,128,16,64]{2,0,4,3,1:T(2,128)(2,1)S(1)} %copy.166) | copy-start | bytes 1572868
  1107.9 498.1 %reduce-scatter.30.cloned.1.call-start = ((), (), s32[]{:S(2)}) async-start(), calls=%async_computation.22 | async-start | bytes 7077888 | tf_op jit(solution)/shard_map/reduce_scatter | solution.py:40
  1153.2 573.9 %reduce-scatter.52.cloned.1.call-start = ((), (), s32[]{:S(2)}) async-start(), calls=%async_computation.45 | async-start | bytes 7077888
  1203.7 675.7 %reduce-scatter.38.cloned.1.call-start = ((), (), s32[]{:S(2)}) async-start(), calls=%async_computation.26 | async-start | bytes 9437184 | tf_op jit(solution)/shard_map/reduce_scatter | solution.py:40
  1212.4 802.8 %reduce-scatter.46.cloned.1.call-start = ((), (), s32[]{:S(2)}) async-start(), calls=%async_computation.42 | async-start | bytes 540672
  1221.4 928.9 %reduce-scatter.50.cloned.1.call-start = ((), (), s32[]{:S(2)}) async-start(), calls=%async_computation.44 | async-start | bytes 2162688
  1223.6 1059.3 %reduce-scatter.48.cloned.1.call-start = ((), (), s32[]{:S(2)}) async-start(), calls=%async_computation.43 | async-start | bytes 540672
  1225.1 1081.2 %reduce-scatter.44.cloned.1.call-start = ((), (), s32[]{:S(2)}) async-start(), calls=%async_computation.29 | async-start | bytes 1310720 | tf_op jit(solution)/shard_map/reduce_scatter | solution.py:51
  1343.6 985.0 %reduce-scatter.36.cloned.1.call-start = ((), (), s32[]{:S(2)}) async-start(), calls=%async_computation.25 | async-start | bytes 327680 | tf_op jit(solution)/shard_map/reduce_scatter | solution.py:51
  1414.1 937.2 %reduce-scatter.28.cloned.1.call-start = ((), (), s32[]{:S(2)}) async-start(), calls=%async_computation.21 | async-start | bytes 327680 | tf_op jit(solution)/shard_map/reduce_scatter | solution.py:51
  1484.8 892.3 %reduce-scatter.32.cloned.1.call-start = ((), (), s32[]{:S(2)}) async-start(), calls=%async_computation.23 | async-start | bytes 983040 | tf_op jit(solution)/shard_map/reduce_scatter | solution.py:48
  1606.1 796.9 %reduce-scatter.24.cloned.1.call-start = ((), (), s32[]{:S(2)}) async-start(), calls=%async_computation.19 | async-start | bytes 983040 | tf_op jit(solution)/shard_map/reduce_scatter | solution.py:48
  1731.5 699.0 %reduce-scatter.40.cloned.1.call-start = ((), (), s32[]{:S(2)}) async-start(), calls=%async_computation.27 | async-start | bytes 1310720 | tf_op jit(solution)/shard_map/reduce_scatter | solution.py:48
  (80 other events, 671.2 us)
Sparse Core Ops, SparseCore 0:
  9.7 20.8 all-gather.48
  32.1 18.2 all-gather.52
  52.6 99.5 all-gather.36
  154.2 47.6 all-gather.44
  203.9 97.5 all-gather.38
  303.4 47.4 all-gather.46
  353.1 123.4 all-gather.50
  478.6 123.1 all-gather.54
  609.1 15.0 all-gather.56
  625.6 16.7 all-gather.60
  644.5 124.9 all-gather.58
  771.4 123.1 all-gather.62
  896.7 47.4 all-gather.64
  946.3 97.5 all-gather.40
  1045.8 47.4 all-gather.66
  1095.3 97.5 all-gather.42
  1196.4 147.1 reduce-scatter.41
  1347.4 66.6 reduce-scatter.33
  1418.1 66.6 reduce-scatter.25
  1488.7 117.3 reduce-scatter.29
  1610.0 117.0 reduce-scatter.51
  1731.2 148.1 reduce-scatter.37
  1882.2 132.8 reduce-scatter.45
  2017.4 132.8 reduce-scatter.49
  2153.0 129.8 reduce-scatter.47
  2285.4 20.8 reduce-scatter.43
  2308.6 19.9 reduce-scatter.35
  2331.2 20.0 reduce-scatter.27
  2353.9 23.2 reduce-scatter.31
  2379.7 23.2 reduce-scatter.23
  2405.5 24.8 reduce-scatter.39
where the time goes:
time: 2450 us; the launch traced here: 2440 us
  waiting for transfers between devices  1700 us (69%)
  matrix products  260 us (11%)
  local copies, waits for them, and re-layouts  209 us (9%)
  blocking collectives  186 us (8%)
  other arithmetic  61.4 us (3%)
    unnamed x35, waiting for transfers between devices  506 us
    reduce_scatter x3, waiting for transfers between devices, settle(): lax.psum_scatter(second.astype(jnp.bfloat16), 'wide', scatter_dimension=1...  259 us
    all_gather x6, waiting for transfers between devices, gather_weights(): lax.all_gather(cols_first, 'wide', axis=1, tiled=True)  259 us
    reduce_scatter x2, waiting for transfers between devices, settle(): lax.psum_scatter(first.astype(jnp.bfloat16), 'wide', scatter_dimension=1,...  257 us
    all_gather x6, waiting for transfers between devices, gather_weights(): lax.all_gather(cols_second, 'wide', axis=1, tiled=True)  254 us
    reduce_scatter x3, waiting for transfers between devices, settle(): lax.psum_scatter(rows_first.astype(jnp.bfloat16), 'narrow', scatter_dimen...  72.6 us
    reduce_scatter x3, waiting for transfers between devices, settle(): lax.psum_scatter(rows_second.astype(jnp.bfloat16), 'narrow', scatter_dime...  63.8 us
    unnamed x210, local copies, waits for them, and re-layouts  51 us
  transfers between devices with their start and end apart: 31, of which 24 were waited for; matrix products, arithmetic and copies ran while one was open for 21% of the time, Pallas kernels for 0%

commit v1 on v0

v1 whole, which is shorter than its diff:
```python
import functools
import math

import jax
import jax.numpy as jnp
from jax import lax
from jax.experimental import pallas as pl
from jax.experimental.pallas import tpu as pltpu
from jax.sharding import PartitionSpec as P

D = 1024
HEADS = 16
HEAD_DIM = 64
PAIRS = HEADS // 2

EPSILON = 1e-05
NEG_FILL = -1e30
LOG2E = math.log2(math.e)
SCALE = 1.0 / math.sqrt(HEAD_DIM)
AXES = ("wide", "narrow")

F32 = jnp.float32
BF16 = jnp.bfloat16


def layer_norm(values, gain_row, bias_row):
    centre = values - jnp.mean(values, axis=-1, keepdims=True)
    spread = jnp.mean(centre * centre, axis=-1, keepdims=True)
    return centre * lax.rsqrt(spread + EPSILON) * gain_row + bias_row


def gelu_exact(values):
    return jax.nn.gelu(values, approximate=False)


def dot_nt(a, b):
    return lax.dot_general(a, b, (((1,), (1,)), ((), ())), preferred_element_type=F32)


def dot_nn(a, b):
    return lax.dot_general(a, b, (((1,), (0,)), ((), ())), preferred_element_type=F32)


def dot_tn(a, b):
    return lax.dot_general(a, b, (((0,), (0,)), ((), ())), preferred_element_type=F32)


def two_heads(block):
    lane = lax.broadcasted_iota(jnp.int32, block.shape, 1)
    zero = jnp.zeros_like(block)
    return jnp.concatenate(
        (jnp.where(lane < HEAD_DIM, block, zero), jnp.where(lane < HEAD_DIM, zero, block)), axis=0
    )


def join_heads(both):
    half = both.shape[0] // 2
    lane = lax.broadcasted_iota(jnp.int32, (half, both.shape[1]), 1)
    return jnp.where(lane < HEAD_DIM, both[:half], both[half:])


def pair_forward(q2, k2, v2, valid):
    scores = dot_nt(k2, two_heads(q2)) * (SCALE * LOG2E)
    scores = jnp.where(valid, scores, NEG_FILL)
    top = jnp.max(scores, axis=0, keepdims=True)
    expo = jnp.exp2(scores - top)
    total = jnp.sum(expo, axis=0, keepdims=True)
    weights = (expo * (1.0 / total)).astype(BF16)
    mixed = join_heads(dot_tn(weights, v2)).astype(BF16)
    return mixed, top + jnp.log2(total)


def pair_backward(q2, k2, v2, do2, lse, valid):
    qq = two_heads(q2)
    dd = two_heads(do2)
    scores = dot_nt(k2, qq) * (SCALE * LOG2E)
    weights = jnp.where(valid, jnp.exp2(scores - lse), 0.0)
    grad_weights = dot_nt(v2, dd)
    inner = jnp.sum(weights * grad_weights, axis=0, keepdims=True)
    grad_scores = (weights * (grad_weights - inner)).astype(BF16)
    grad_v = dot_nn(weights.astype(BF16), dd).astype(BF16)
    grad_k = (dot_nn(grad_scores, qq) * SCALE).astype(BF16)
    grad_q = (join_heads(dot_tn(grad_scores, k2)) * SCALE).astype(BF16)
    return grad_q, grad_k, grad_v


def self_valid(seg_row, seg_col):
    length = seg_row.shape[-1]
    key = lax.broadcasted_iota(jnp.int32, (length, length), 0)
    tok = lax.broadcasted_iota(jnp.int32, (length, length), 1)
    one = (key <= tok) & (seg_row == seg_col)
    return jnp.concatenate((one, one), axis=1)


def self_fwd_kernel(seg_row, seg_col, q_ref, k_ref, v_ref, o_ref, lse_ref):
    valid = self_valid(seg_row[0], seg_col[0])
    for h in range(PAIRS):
        cut = slice(128 * h, 128 * h + 128)
        mixed, lse = pair_forward(q_ref[:, cut], k_ref[:, cut], v_ref[:, cut], valid)
        o_ref[:, cut] = mixed
        lse_ref[0, h : h + 1, :] = lse


def self_bwd_kernel(seg_row, seg_col, q_ref, k_ref, v_ref, do_ref, lse_ref, dq_ref, dk_ref, dv_ref):
    valid = self_valid(seg_row[0], seg_col[0])
    for h in range(PAIRS):
        cut = slice(128 * h, 128 * h + 128)
        gq, gk, gv = pair_backward(
            q_ref[:, cut], k_ref[:, cut], v_ref[:, cut], do_ref[:, cut],
            lse_ref[0, h : h + 1, :], valid,
        )
        dq_ref[:, cut] = gq
        dk_ref[:, cut] = gk
        dv_ref[:, cut] = gv


def self_specs(row_len):
    seg = [
        pl.BlockSpec((1, 1, row_len), lambda r: (r, 0, 0)),
        pl.BlockSpec((1, row_len, 1), lambda r: (r, 0, 0)),
    ]
    row = pl.BlockSpec((row_len, D), lambda r: (r, 0))
    lse = pl.BlockSpec((1, PAIRS, 2 * row_len), lambda r: (r, 0, 0))
    return seg, row, lse


def self_forward(seg, queries, keys, values):
    rows, row_len = seg.shape
    seg_specs, row, lse = self_specs(row_len)
    return pl.pallas_call(
        self_fwd_kernel,
        grid=(rows,),
        in_specs=seg_specs + [row] * 3,
        out_specs=[row, lse],
        out_shape=[
            jax.ShapeDtypeStruct(queries.shape, BF16),
            jax.ShapeDtypeStruct((rows, PAIRS, 2 * row_len), F32),
        ],
        cost_estimate=pl.CostEstimate(flops=rows * 2 * 10**8, bytes_accessed=2 * 10**6, transcendentals=rows * 3 * 10**5),
        name="self_forward",
    )(seg[:, None, :], seg[:, :, None], queries, keys, values)


def self_backward(seg, queries, keys, values, grad_mixed, lse_rows):
    rows, row_len = seg.shape
    seg_specs, row, lse = self_specs(row_len)
    return pl.pallas_call(
        self_bwd_kernel,
        grid=(rows,),
        in_specs=seg_specs + [row] * 4 + [lse],
        out_specs=[row] * 3,
        out_shape=[jax.ShapeDtypeStruct(queries.shape, BF16)] * 3,
        cost_estimate=pl.CostEstimate(flops=rows * 5 * 10**8, bytes_accessed=4 * 10**6, transcendentals=rows * 3 * 10**5),
        name="self_backward",
    )(seg[:, None, :], seg[:, :, None], queries, keys, values, grad_mixed, lse_rows)


def cross_fwd_kernel(map_ref, len_ref, seg_row, seg_col, q_ref, k_ref, v_ref, o_ref, lse_ref):
    r, page = pl.program_id(0), pl.program_id(1)
    keys, toks = k_ref.shape[1], q_ref.shape[0]
    valid = lax.broadcasted_iota(jnp.int32, (keys, 2 * toks), 0) < len_ref[r * 2 + page]
    mine_col = (seg_col[0] == page) | (page == 0)
    mine_row = (seg_row[0] == page) | (page == 0)
    mine_row = jnp.concatenate((mine_row, mine_row), axis=1)
    for h in range(PAIRS):
        cut = slice(128 * h, 128 * h + 128)
        mixed, lse = pair_forward(q_ref[:, cut], k_ref[0, :, cut], v_ref[0, :, cut], valid)
        o_ref[:, cut] = jnp.where(mine_col, mixed, o_ref[:, cut])
        lse_ref[0, h : h + 1, :] = jnp.where(mine_row, lse, lse_ref[0, h : h + 1, :])


def cross_bwd_kernel(
    map_ref, len_ref, seg_row, seg_col, q_ref, k_ref, v_ref, do_ref, lse_ref, dq_ref, dk_ref, dv_ref
):
    r, page = pl.program_id(0), pl.program_id(1)
    keys, toks = k_ref.shape[1], q_ref.shape[0]
    valid = lax.broadcasted_iota(jnp.int32, (keys, 2 * toks), 0) < len_ref[r * 2 + page]
    mine_col = (seg_col[0] == page) | (page == 0)
    mine_row = seg_row[0] == page
    mine_row = jnp.concatenate((mine_row, mine_row), axis=1)
    for h in range(PAIRS):
        cut = slice(128 * h, 128 * h + 128)
        lse = jnp.where(mine_row, lse_ref[0, h : h + 1, :], -NEG_FILL)
        gq, gk, gv = pair_backward(
            q_ref[:, cut], k_ref[0, :, cut], v_ref[0, :, cut], do_ref[:, cut], lse, valid
        )
        dq_ref[:, cut] = jnp.where(mine_col, gq, dq_ref[:, cut])
        dk_ref[0, :, cut] = gk
        dv_ref[0, :, cut] = gv


def cross_specs(row_len, mem_len):
    seg = [
        pl.BlockSpec((1, 1, row_len), lambda r, p, *_: (r, 0, 0)),
        pl.BlockSpec((1, row_len, 1), lambda r, p, *_: (r, 0, 0)),
    ]
    row = pl.BlockSpec((row_len, D), lambda r, p, *_: (r, 0))
    mem = pl.BlockSpec((1, mem_len, D), lambda r, p, mp, ln: (mp[r * 2 + p], 0, 0))
    lse = pl.BlockSpec((1, PAIRS, 2 * row_len), lambda r, p, *_: (r, 0, 0))
    return seg, row, mem, lse


CROSS_PARAMS = pltpu.CompilerParams(
    dimension_semantics=("arbitrary", "arbitrary"), vmem_limit_bytes=40 * 2**20
)


def cross_forward(local_map, lengths, seg, queries, keys, values):
    rows, row_len = seg.shape
    mem_len = keys.shape[1]
    seg_specs, row, mem, lse = cross_specs(row_len, mem_len)
    return pl.pallas_call(
        cross_fwd_kernel,
        grid_spec=pltpu.PrefetchScalarGridSpec(
            num_scalar_prefetch=2,
            grid=(rows, 2),
            in_specs=seg_specs + [row, mem, mem],
            out_specs=[row, lse],
        ),
        out_shape=[
            jax.ShapeDtypeStruct(queries.shape, BF16),
            jax.ShapeDtypeStruct((rows, PAIRS, 2 * row_len), F32),
        ],
        compiler_params=CROSS_PARAMS,
        cost_estimate=pl.CostEstimate(flops=5 * 10**9, bytes_accessed=11 * 10**6, transcendentals=5 * 10**6),
        name="cross_forward",
    )(local_map, lengths, seg[:, None, :], seg[:, :, None], queries, keys, values)


def cross_backward(local_map, lengths, seg, queries, keys, values, grad_mixed, lse_rows):
    rows, row_len = seg.shape
    mem_len = keys.shape[1]
    seg_specs, row, mem, lse = cross_specs(row_len, mem_len)
    return pl.pallas_call(
        cross_bwd_kernel,
        grid_spec=pltpu.PrefetchScalarGridSpec(
            num_scalar_prefetch=2,
            grid=(rows, 2),
            in_specs=seg_specs + [row, mem, mem, row, lse],
            out_specs=[row, mem, mem],
        ),
        out_shape=[
            jax.ShapeDtypeStruct(queries.shape, BF16),
            jax.ShapeDtypeStruct(keys.shape, BF16),
            jax.ShapeDtypeStruct(values.shape, BF16),
        ],
        compiler_params=CROSS_PARAMS,
        cost_estimate=pl.CostEstimate(flops=12 * 10**9, bytes_accessed=22 * 10**6, transcendentals=5 * 10**6),
        name="cross_backward",
    )(local_map, lengths, seg[:, None, :], seg[:, :, None], queries, keys, values, grad_mixed, lse_rows)


class Grid:
    def __init__(self, wide, narrow):
        self.wide, self.narrow, self.ring = wide, narrow, wide // 2
        moves = {
            "z": lambda w, n: ((w + 2) % wide, n),
            "x": lambda w, n: (w ^ 1, n),
            "y": lambda w, n: (w, n ^ 2),
            "c": lambda w, n: (w, n ^ 1),
        }
        self.perms = {}
        for name, move in moves.items():
            pairs = []
            for w in range(wide):
                for n in range(narrow):
                    w2, n2 = move(w, n)
                    pairs.append((w * narrow + n, w2 * narrow + n2))
            self.perms[name] = pairs

    def send(self, name, array):
        return lax.ppermute(array, AXES, self.perms[name])


def assemble_kernel(labels, ring, place, *refs):
    pieces, whole, sems = refs[:-2], refs[-2], refs[-1]
    z, x, y, c = place[0], place[1], place[2], place[3]
    cols = pieces[0].shape[-1]
    copies = []
    for piece, piece_labels in zip(pieces, labels):
        for i, (dz, dx, dy, dc) in enumerate(piece_labels):
            row = 2 * lax.rem(z + (ring - dz), ring) + (x + dx - 2 * x * dx)
            col = 2 * (y + dy - 2 * y * dy) + (c + dc - 2 * c * dc)
            copies.append(
                pltpu.make_async_copy(
                    piece.at[i],
                    whole.at[:, row, :, pl.ds(pl.multiple_of(col * cols, 128), cols)],
                    sems.at[len(copies)],
                )
            )
    for copy in copies:
        copy.start()
    for copy in copies:
        copy.wait()


def gather_whole(grid, place, shard, order):
    g, rows, cols = shard.shape
    parts = [([(0, 0, 0, 0)], shard[None])]
    for stage in order + "c":
        if stage == "z":
            if len(parts) > 1:
                labels = [label for ls, _ in parts for label in ls]
                parts = [(labels, jnp.concatenate([a for _, a in parts], axis=0))]
            (labels, array), = parts
            ring = [(labels, array)]
            for step in range(1, grid.ring):
                array = grid.send("z", array)
                ring.append(([(step, dx, dy, dc) for _, dx, dy, dc in labels], array))
            if order[0] == "z":
                ring = [([l for ls, _ in ring for l in ls], jnp.concatenate([a for _, a in ring], axis=0))]
            parts = ring
        else:
            axis = "zxyc".index(stage)
            new = []
            for labels, array in parts:
                far = [tuple(1 if i == axis else v for i, v in enumerate(l)) for l in labels]
                new.append((far, grid.send(stage, array)))
            parts = parts + new
    n_blocks = grid.wide * grid.narrow
    whole = pl.pallas_call(
        functools.partial(assemble_kernel, [labels for labels, _ in parts], grid.ring),
        in_specs=[pl.BlockSpec(memory_space=pltpu.SMEM)] + [pl.BlockSpec(memory_space=pl.ANY)] * len(parts),
        out_specs=pl.BlockSpec(memory_space=pltpu.VMEM),
        out_shape=jax.ShapeDtypeStruct((g, grid.wide, rows, grid.narrow * cols), shard.dtype),
        compiler_params=pltpu.CompilerParams(vmem_limit_bytes=32 * 2**20),
        scratch_shapes=[pltpu.SemaphoreType.DMA((n_blocks,))],
        cost_estimate=pl.CostEstimate(flops=0, bytes_accessed=2 * n_blocks * shard.size * 2, transcendentals=0),
        name="assemble",
    )(place, *[array for _, array in parts])
    return whole.reshape(g, grid.wide * rows, grid.narrow * cols)


def reduce_to_owner(grid, place, columns, rows, order):
    z, x, y, c = place[0], place[1], place[2], place[3]

    def split(term):
        g, _, cols = term.shape
        return term.reshape(g, grid.ring, 2, rows, cols)

    def row_half(term, index):
        return lax.dynamic_index_in_dim(term, index, 2, keepdims=False)

    here, there = 2 * y + c, 2 * (1 - y) + c
    far = [columns(2 * y + (1 - c)).astype(BF16), columns(2 * (1 - y) + (1 - c)).astype(BF16)]
    from_c = [grid.send("c", f) for f in far]
    keep = columns(here) + from_c[0].astype(F32)
    other = columns(there) + from_c[1].astype(F32)
    if order == "yx":
        keep = keep + grid.send("y", other.astype(BF16)).astype(F32)
        keep = split(keep)
        from_x = grid.send("x", row_half(keep, 1 - x).astype(BF16))
        mine = row_half(keep, x) + from_x.astype(F32)
    else:
        keep, other = split(keep), split(other)
        from_x = grid.send(
            "x", jnp.stack((row_half(keep, 1 - x), row_half(other, 1 - x))).astype(BF16)
        ).astype(F32)
        mine = row_half(keep, x) + from_x[0]
        other = row_half(other, x) + from_x[1]
        mine = mine + grid.send("y", other.astype(BF16)).astype(F32)

    def chunk(step):
        index = lax.rem(z + (grid.ring - step), grid.ring)
        return lax.dynamic_index_in_dim(mine, index, 1, keepdims=False)

    total = chunk(1)
    for step in range(2, grid.ring + 1):
        total = chunk(step % grid.ring) + grid.send("z", total.astype(BF16)).astype(F32)
    return total


def reduce_small(grid, place, terms):
    z, x, y, c = place[0], place[1], place[2], place[3]
    mine = terms.reshape(grid.ring, 2, 2, 2, -1)
    for name, axis, at in (("c", 3, c), ("y", 2, y), ("x", 1, x)):
        far = lax.dynamic_index_in_dim(mine, 1 - at, axis, keepdims=False)
        mine = lax.dynamic_index_in_dim(mine, at, axis, keepdims=False) + grid.send(name, far)

    def chunk(step):
        return lax.dynamic_index_in_dim(mine, lax.rem(z + (grid.ring - step), grid.ring), 0, keepdims=False)

    total = chunk(1)
    for step in range(2, grid.ring + 1):
        total = chunk(step % grid.ring) + grid.send("z", total)
    return total


def columns_of(a, d, spec, grid):
    cols = d.shape[-1] // grid.narrow

    def term(n):
        cut = lax.dynamic_slice_in_dim(d, n * cols, cols, axis=d.ndim - 1)
        out = jnp.einsum(spec, a, cut, preferred_element_type=F32)
        return out if out.ndim == 3 else out[None]

    return term


def local(
    grid,
    tokens,
    memory,
    segment_ids,
    page_map,
    mem_lengths,
    gains,
    biases,
    fc1_bias,
    self_qkv,
    self_out,
    cross_q,
    cross_kv,
    cross_out,
    fc1,
    fc2,
    cotangent,
):
    wide_at, narrow_at = lax.axis_index("wide"), lax.axis_index("narrow")
    place = jnp.stack((wide_at // 2, wide_at % 2, narrow_at // 2, narrow_at % 2)).astype(jnp.int32)
    devices = grid.wide * grid.narrow
    token_count = tokens.shape[0]
    mem_count = memory.shape[0]

    small = jnp.concatenate((gains.reshape(-1), biases.reshape(-1), fc1_bias))
    small_all = lax.all_gather(small[None, None], AXES, axis=1, tiled=True)[0].astype(F32)
    n_gain, n_bias = gains.size, biases.size
    gain_full = small_all[:, :n_gain].reshape(devices, 3, -1).transpose(1, 0, 2).reshape(3, D)
    bias_full = (
        small_all[:, n_gain : n_gain + n_bias].reshape(devices, 10, -1).transpose(1, 0, 2).reshape(10, D)
    )
    fc1_bias_full = small_all[:, n_gain + n_bias :].reshape(-1)

    gather = functools.partial(gather_whole, grid, place)
    w_qkv = gather(self_qkv, "zyx")
    w_ckv = gather(cross_kv, "xyz")
    w_so = gather(self_out[None], "yxz")[0]
    w_cq = gather(cross_q[None], "yxz")[0]
    w_co = gather(cross_out[None], "zxy")[0]
    w_fc1 = gather(fc1[None], "zxy")[0]
    w_fc2 = gather(fc2[None], "zyx")[0]

    token_full = tokens.astype(F32)
    hidden_one, norm_one_back = jax.vjp(layer_norm, token_full, gain_full[0], bias_full[0])
    normed_one = hidden_one.astype(BF16)
    projected = jnp.einsum("td,kde->kte", normed_one, w_qkv, preferred_element_type=F32)
    self_queries = (projected[0] + bias_full[1]).astype(BF16)
    self_keys = projected[1].astype(BF16)
    self_values = (projected[2] + bias_full[2]).astype(BF16)
    self_mixed, self_lse = self_forward(segment_ids, self_queries, self_keys, self_values)
    after_self = token_full + jnp.dot(self_mixed, w_so, preferred_element_type=F32) + bias_full[3]

    hidden_two, norm_two_back = jax.vjp(layer_norm, after_self, gain_full[1], bias_full[4])
    normed_two = hidden_two.astype(BF16)
    cross_queries = (
        jnp.dot(normed_two, w_cq, preferred_element_type=F32) + bias_full[5]
    ).astype(BF16)
    mem_keys = jnp.einsum("mld,de->mle", memory, w_ckv[0], preferred_element_type=F32).astype(BF16)
    mem_values = (
        jnp.einsum("mld,de->mle", memory, w_ckv[1], preferred_element_type=F32) + bias_full[6]
    ).astype(BF16)
    first_mem = lax.axis_index(AXES) * mem_count
    local_map = (page_map - first_mem).reshape(-1).astype(jnp.int32)
    picks = local_map[:, None] == jnp.arange(mem_count, dtype=jnp.int32)[None, :]
    row_lengths = jnp.sum(jnp.where(picks, mem_lengths[None, :], 0), axis=-1).astype(jnp.int32)
    cross_mixed, cross_lse = cross_forward(
        local_map, row_lengths, segment_ids, cross_queries, mem_keys, mem_values
    )
    after_cross = (
        after_self + jnp.dot(cross_mixed, w_co, preferred_element_type=F32) + bias_full[7]
    )

    hidden_three, norm_three_back = jax.vjp(layer_norm, after_cross, gain_full[2], bias_full[8])
    normed_three = hidden_three.astype(BF16)
    pre_act = jnp.dot(normed_three, w_fc1, preferred_element_type=F32) + fc1_bias_full
    activated_full, gelu_back = jax.vjp(gelu_exact, pre_act)
    activated = activated_full.astype(BF16)
    layer_out = (
        after_cross + jnp.dot(activated, w_fc2, preferred_element_type=F32) + bias_full[9]
    ).astype(BF16)

    settle = functools.partial(reduce_to_owner, grid, place)
    grad_out = cotangent.astype(F32)
    fc2_shard = settle(
        columns_of(activated, cotangent, "tf,td->fd", grid), fc2.shape[0], "yx"
    )
    grad_bias_nine = jnp.sum(grad_out, axis=0)
    grad_act = jnp.einsum("td,fd->tf", cotangent, w_fc2, preferred_element_type=F32)
    grad_pre = gelu_back(grad_act)[0].astype(BF16)
    fc1_shard = settle(
        columns_of(normed_three, grad_pre, "td,tf->df", grid), fc1.shape[0], "xy"
    )
    grad_fc1_bias = jnp.sum(grad_pre, axis=0, dtype=F32)
    grad_normed_three = jnp.einsum("tf,df->td", grad_pre, w_fc1, preferred_element_type=F32)
    grad_from_three, grad_gain_three, grad_bias_eight = norm_three_back(grad_normed_three)
    grad_after_cross = grad_out + grad_from_three

    grad_branch_two = grad_after_cross.astype(BF16)
    cross_out_shard = settle(
        columns_of(cross_mixed, grad_branch_two, "td,te->de", grid), cross_out.shape[0], "yx"
    )
    grad_bias_seven = jnp.sum(grad_branch_two, axis=0, dtype=F32)
    grad_cross_mixed = jnp.einsum(
        "te,de->td", grad_branch_two, w_co, preferred_element_type=F32
    ).astype(BF16)
    grad_cq, grad_ck, grad_cv = cross_backward(
        local_map, row_lengths, segment_ids, cross_queries, mem_keys, mem_values,
        grad_cross_mixed, cross_lse,
    )
    grad_bias_five = jnp.sum(grad_cq, axis=0, dtype=F32)
    grad_bias_six = jnp.sum(grad_cv, axis=(0, 1), dtype=F32)
    cross_q_shard = settle(
        columns_of(normed_two, grad_cq, "td,te->de", grid), cross_q.shape[0], "yx"
    )
    cross_k_shard = settle(
        columns_of(memory, grad_ck, "mld,mle->de", grid), cross_q.shape[0], "xy"
    )
    cross_v_shard = settle(
        columns_of(memory, grad_cv, "mld,mle->de", grid), cross_q.shape[0], "yx"
    )
    grad_normed_two = jnp.einsum("te,de->td", grad_cq, w_cq, preferred_element_type=F32)
    grad_from_two, grad_gain_two, grad_bias_four = norm_two_back(grad_normed_two)
    grad_after_self = grad_after_cross + grad_from_two

    grad_branch_one = grad_after_self.astype(BF16)
    self_out_shard = settle(
        columns_of(self_mixed, grad_branch_one, "td,te->de", grid), self_out.shape[0], "yx"
    )
    grad_bias_three = jnp.sum(grad_branch_one, axis=0, dtype=F32)
    grad_self_mixed = jnp.einsum(
        "te,de->td", grad_branch_one, w_so, preferred_element_type=F32
    ).astype(BF16)
    grad_proj = self_backward(
        segment_ids, self_queries, self_keys, self_values, grad_self_mixed, self_lse
    )
    grad_proj = jnp.stack(grad_proj)
    qkv_shard = settle(
        columns_of(normed_one, grad_proj, "td,kte->kde", grid), self_qkv.shape[1], "xy"
    )
    grad_bias_one = jnp.sum(grad_proj[0], axis=0, dtype=F32)
    grad_bias_two = jnp.sum(grad_proj[2], axis=0, dtype=F32)
    grad_normed_one = jnp.einsum("kte,kde->td", grad_proj, w_qkv, preferred_element_type=F32)
    grad_from_one, grad_gain_one, grad_bias_zero = norm_one_back(grad_normed_one)
    grad_tokens = (grad_after_self + grad_from_one).astype(BF16)

    grad_memory = (
        jnp.einsum("mle,de->mld", grad_ck, w_ckv[0], preferred_element_type=F32)
        + jnp.einsum("mle,de->mld", grad_cv, w_ckv[1], preferred_element_type=F32)
    ).astype(BF16)

    def by_device(rows):
        array = jnp.stack(rows)
        return array.reshape(len(rows), devices, -1).transpose(1, 0, 2).reshape(devices, -1)

    small_grads = jnp.concatenate(
        (
            by_device((grad_gain_one, grad_gain_two, grad_gain_three)),
            by_device(
                (
                    grad_bias_zero,
                    grad_bias_one,
                    grad_bias_two,
                    grad_bias_three,
                    grad_bias_four,
                    grad_bias_five,
                    grad_bias_six,
                    grad_bias_seven,
                    grad_bias_eight,
                    grad_bias_nine,
                )
            ),
            by_device((grad_fc1_bias,)),
        ),
        axis=1,
    )
    small_shard = reduce_small(grid, place, small_grads)
    return (
        layer_out,
        grad_tokens,
        grad_memory,
        small_shard[:n_gain].reshape(gains.shape),
        small_shard[n_gain : n_gain + n_bias].reshape(biases.shape),
        small_shard[n_gain + n_bias :],
        qkv_shard,
        self_out_shard[0],
        cross_q_shard[0],
        jnp.concatenate((cross_k_shard, cross_v_shard), axis=0),
        cross_out_shard[0],
        fc1_shard[0],
        fc2_shard[0],
    )


def solution(mesh):
    grid = Grid(mesh.shape["wide"], mesh.shape["narrow"])
    in_specs = (
        P(AXES, None),
        P(AXES, None, None),
        P(AXES, None),
        P(AXES, None),
        P(AXES),
        P(None, AXES),
        P(None, AXES),
        P(AXES),
        P(None, "wide", "narrow"),
        P("wide", "narrow"),
        P("wide", "narrow"),
        P(None, "wide", "narrow"),
        P("wide", "narrow"),
        P("wide", "narrow"),
        P("wide", "narrow"),
        P(AXES, None),
    )
    out_specs = (
        P(AXES, None),
        P(AXES, None),
        P(AXES, None, None),
        P(None, AXES),
        P(None, AXES),
        P(AXES),
        P(None, "wide", "narrow"),
        P("wide", "narrow"),
        P("wide", "narrow"),
        P(None, "wide", "narrow"),
        P("wide", "narrow"),
        P("wide", "narrow"),
        P("wide", "narrow"),
    )
    return jax.shard_map(
        functools.partial(local, grid), mesh=mesh, in_specs=in_specs, out_specs=out_specs, check_vma=False
    )
```

time: 2450 us -> 900 us (0.37)
  waiting for transfers between devices: 1700 us -> 320 us
  blocking collectives: 186 us -> 51.4 us
  matrix products: 260 us -> 173 us
  local copies, waits for them, and re-layouts: 209 us -> 134 us
  Pallas kernels: 0 us -> 67.1 us
  starting transfers between devices: 2.74 us -> 69.6 us
    reduce_scatter x11 -> x0, waiting for transfers between devices: 652 us -> none  [the longest x3 259 us: settle(): lax.psum_scatter(second.astype(jnp.bfloat16), 'wide', scatter_dimension=1...]
    all_gather x16 -> x0, waiting for transfers between devices: 545 us -> none  [the longest x6 259 us: gather_weights(): lax.all_gather(cols_first, 'wide', axis=1, tiled=True)]
    unnamed x35 -> x0, waiting for transfers between devices: 506 us -> none
    ppermute x0 -> x132, waiting for transfers between devices: none -> 320 us  [send(): return lax.ppermute(array, AXES, self.perms[name])]
    all_gather x11 -> x0, blocking collectives: 186 us -> none  [the longest x1 43 us: local(): lax.all_gather(biases, ('wide', 'narrow'), axis=1, tiled=True)]
    dot_general x45 -> x48, matrix products: 260 us -> 173 us  [the longest x32 95.7 us: term(): out = jnp.einsum(spec, a, cut, preferred_element_type=F32)]
    convert_element_type x9 -> x14, local copies, waits for them, and re-layouts: 82.4 us -> 6.9 us  [the longest x4 5.74 us: reduce_to_owner(): from_x = grid.send('x', row_half(keep, 1 - x).astype(BF16))]
    ppermute x0 -> x132, starting transfers between devices: none -> 69.6 us  [send(): return lax.ppermute(array, AXES, self.perms[name])]
  transfers between devices with their start and end apart: 31 -> 132, of which waited for: 24 -> 55; matrix products, arithmetic and copies ran while one was open for 21% -> 30% of each run, Pallas kernels for 0% -> 4%
where the time goes in v1:
time: 900 us; the launch traced here: 892 us
  waiting for transfers between devices  320 us (36%)
  matrix products  173 us (19%)
  local copies, waits for them, and re-layouts  134 us (15%)
  other arithmetic  73.6 us (8%)
  starting transfers between devices  69.6 us (8%)
  Pallas kernels  67.1 us (7%)
  blocking collectives  51.4 us (6%)
    ppermute x132, waiting for transfers between devices, send(): return lax.ppermute(array, AXES, self.perms[name])  320 us
    dot_general x32, matrix products, term(): out = jnp.einsum(spec, a, cut, preferred_element_type=F32)  95.7 us
    ppermute x132, starting transfers between devices, send(): return lax.ppermute(array, AXES, self.perms[name])  69.6 us
    unnamed x1, blocking collectives  51.4 us
    unnamed x327, local copies, waits for them, and re-layouts  45.7 us
    dynamic_slice x15, local copies, waits for them, and re-layouts, row_half(): return lax.dynamic_index_in_dim(term, index, 2, keepdims=False)  36.5 us
    pallas_call x1, Pallas kernels, cross_backward(): pl.pallas_call(cross_bwd_kernel, grid_spec=pltpu.PrefetchScalarGridSpec(n...  22.1 us
    reshape x5, local copies, waits for them, and re-layouts, split(): return term.reshape(g, grid.ring, 2, rows, cols)  20.5 us
  transfers between devices with their start and end apart: 132, of which 55 were waited for; matrix products, arithmetic and copies ran while one was open for 30% of the time, Pallas kernels for 4%

profile of v1, /device:TPU:0, one launch (start us, length us, event | category | flops | bytes accessed | tf_op | source)
XLA Modules:
  0.0 891.7 jit_solution(9883046312658197756)
XLA Ops:
  18.3 5.4 collective-permute-done.41
  26.3 7.6 collective-permute-done.42
  39.3 5.6 collective-permute-done.23.refs_1_
  57.3 4.1 collective-permute-done.51
  61.4 5.6 collective-permute-done.61
  67.7 14.7 %collective-permute-done.2 = bf16[1,3,128,256]{3,2,1,0:T(8,128)(2,1)S(1)} collective-permute-done((bf16[1,3,128,256]{3,2,1,0:T(8,128)(2,1)S(1)}, bf16[1,3,128,256]{3,2,1,0:T(8,128)(2,1)S(1)}, u32[]{:S(2)}, u32[]{:S(2)}) %collective-permute-start.2) | collective-permute-done | bytes 196640 | tf_op jit(solution)/shard_map/ppermute | solution.py:272
  83.2 4.8 collective-permute-done.24.refs_2_
  100.1 5.0 collective-permute-done.52
  105.4 14.0 %collective-permute-done.62 = bf16[1,1,512,256]{3,2,1,0:T(8,128)(2,1)} collective-permute-done((bf16[1,1,512,256]{3,2,1,0:T(8,128)(2,1)}, bf16[1,1,512,256]{3,2,1,0:T(8,128)(2,1)}, u32[]{:S(2)}, u32[]{:S(2)}) %collective-permute-start.62) | collective-permute-done | bytes 262176 | tf_op jit(solution)/shard_map/ppermute | solution.py:272
  123.4 4.3 collective-permute-done.25.refs_3_
  135.2 51.4 %all-reduce = bf16[17408]{0:T(1024)(128)(2,1)S(1)} all-reduce(bf16[17408]{0:T(1024)(128)(2,1)S(1)} %dynamic-update-slice), channel_id=2, replica_groups=mesh['wide'=8,'narrow'=4] {'wide','narrow'}, use_global_device_ids=true, to_apply=%add | all-reduce | flops 17408 | bytes 69632
  227.8 7.4 fusion.2.v_ref
  235.2 7.3 convert_bitcast_fusion.k_ref
  244.5 4.7 collective-permute-done.53.refs_1_
  272.6 17.6 %cross_forward.1 = (bf16[256,1024]{1,0:T(8,128)(2,1)S(1)}, f32[2,8,256]{2,1,0:T(8,128)S(1)}) custom-call(s32[4]{0:T(128)S(1)} %reshape.608.map_ref, s32[4]{0:T(128)S(1)} %select_reduce_fusion.len_ref, s32[2,1,128]{2,1,0:T(1,128)S(1)} %bitcast.518, s32[2,128,1]{2,1,0:T(8,128)S(1)} %copy-done.18, bf16[256,1024]{1,0:T(8,128)(2,1)S(1)} %fusion.31.q_ref, ...), custom_call_target="tpu_custom_call" | custom-call | flops 5000000000 | bytes 11000000 | tf_op jit(solution)/shard_map/cross_forward/pallas_call | solution.py:212
  291.5 6.6 collective-permute-done.54.refs_2_
  298.1 19.8 %collective-permute-done.55.refs_3_ = bf16[4,1,128,1024]{3,2,1,0:T(8,128)(2,1)} collective-permute-done((bf16[4,1,128,1024]{3,2,1,0:T(8,128)(2,1)}, bf16[4,1,128,1024]{3,2,1,0:T(8,128)(2,1)}, u32[]{:S(2)}, u32[]{:S(2)}) %collective-permute-start.55) | collective-permute-done | bytes 1048608 | tf_op jit(solution)/shard_map/ppermute | solution.py:272
  324.2 13.5 %multiply_convert_fusion = (bf16[256,4096]{1,0:T(8,128)(2,1)}, f32[256,4096]{1,0:T(8,128)}, f32[256,4096]{1,0:T(8,128)}) fusion(f32[4096]{0:T(1024)S(1)} %slice_bitcast_fusion.8, bf16[256,1024]{1,0:T(8,128)(2,1)S(1)} %add_convert_fusion.9, bf16[1024,4096]{1,0:T(8,128)(2,1)S(1)} %bitcast.503), kind=kOutput, calls=%fused_computation.21 | convolution fusion | flops 2216689664 | bytes 19415040 | tf_op jit(solution)/shard_map/dot_general | solution.py:475
  340.4 9.8 %convert_reduce_fusion.1 = (f32[4096]{0:T(1024)}, bf16[256,4096]{1,0:T(8,128)(2,1)S(1)}) fusion(f32[256,4096]{1,0:T(8,128)} %get-tuple-element.107, f32[256,4096]{1,0:T(8,128)} %get-tuple-element.124, bf16[4096,1024]{1,0:T(8,128)(2,1)S(1)} %bitcast.499, bf16[256,1024]{1,0:T(8,128)(2,1)S(1)} %copy-done.92), kind=kOutput, calls=%fused_computation.19 | convolution fusion | flops 2164256768 | bytes 19415040 | tf_op jit(solution)/shard_map/td,fd->tf/dot_general | solution.py:488
  354.3 22.1 %cross_backward.1 = (bf16[256,1024]{1,0:T(8,128)(2,1)S(1)}, bf16[4,588,1024]{2,1,0:T(8,128)(2,1)S(1)}, bf16[4,588,1024]{2,1,0:T(8,128)(2,1)S(1)}) custom-call(s32[4]{0:T(128)S(1)} %reshape.608.map_ref, s32[4]{0:T(128)S(1)} %select_reduce_fusion.len_ref, s32[2,1,128]{2,1,0:T(1,128)S(1)} %bitcast.519, s32[2,128,1]{2,1,0:T(8,128)S(1)} %copy-done.18, ...), custom_call_target="tpu_custom_call" | custom-call | flops 12000000000 | bytes 22000000 | tf_op jit(solution)/shard_map/cross_backward/pallas_call | solution.py:234
  379.7 4.2 fusion.40
  383.9 4.1 fusion.41
  389.9 4.2 fusion.38
  394.1 4.6 fusion.39
  402.8 6.5 self_backward.1
  411.8 6.2 fusion.56
  419.7 6.7 convolution_bitcast_fusion.9
  437.4 8.0 fusion.205
  486.7 9.6 %add_convert_fusion = bf16[4,588,1024]{2,1,0:T(8,128)(2,1)S(1)} fusion(f32[4,588,1024]{2,1,0:T(8,128)} %fusion.205, bf16[4,588,1024]{2,1,0:T(8,128)(2,1)} %copy-done.57, bf16[1024,1024,1]{1,0,2:T(8,128)(2,1)S(1)} %bitcast.539), kind=kOutput, calls=%fused_computation.1 | convolution fusion | flops 4937318400 | bytes 21364736 | tf_op jit(solution)/shard_map/mle,de->mld/dot_general | solution.py:547
  496.3 5.9 copy.135
  504.8 7.1 convert_add_fusion.6
  515.0 7.0 add_convert_fusion.5
  522.4 7.4 convert_add_fusion.5
  557.2 10.0 %collective-permute-done.85 = bf16[1,1024,256]{2,1,0:T(8,128)(2,1)S(1)} collective-permute-done((bf16[1,1024,256]{2,1,0:T(8,128)(2,1)S(1)}, bf16[1,1024,256]{2,1,0:T(8,128)(2,1)S(1)}, u32[]{:S(2)}, u32[]{:S(2)}) %collective-permute-start.85) | collective-permute-done | bytes 524320 | tf_op jit(solution)/shard_map/ppermute | solution.py:272
  570.6 7.9 collective-permute-done.113
  581.3 7.9 collective-permute-done.106
  626.6 5.6 collective-permute-done.107
  632.3 6.0 collective-permute-done.87
  638.3 6.0 collective-permute-done.115
  644.4 6.5 collective-permute-done.94
  650.9 6.0 collective-permute-done.101
  657.1 6.0 collective-permute-done.108
  663.2 6.0 collective-permute-done.88
  669.2 6.2 collective-permute-done.116
  675.4 6.0 collective-permute-done.95
  681.5 6.0 collective-permute-done.102
  692.1 5.6 reshape.610
  697.7 4.4 constant_dynamic-slice_fusion.7
  702.2 4.6 copy.149
  710.8 5.6 reshape.609
  716.4 4.5 constant_dynamic-slice_fusion.8
  720.9 4.6 copy.148
  756.3 5.1 collective-permute-done.110
  762.4 5.3 collective-permute-done.96
  778.1 34.6 %collective-permute-done.120 = bf16[2,1,4,128,1024]{4,3,2,1,0:T(8,128)(2,1)} collective-permute-done((bf16[2,1,4,128,1024]{4,3,2,1,0:T(8,128)(2,1)}, bf16[2,1,4,128,1024]{4,3,2,1,0:T(8,128)(2,1)}, u32[]{:S(2)}, u32[]{:S(2)}) %collective-permute-start.120) | collective-permute-done | bytes 2097184 | tf_op jit(solution)/shard_map/ppermute | solution.py:272
  828.9 4.8 copy.109
  836.1 6.6 collective-permute-done.121
  845.3 4.6 collective-permute-done.128
  856.0 6.4 collective-permute-done.129
  862.6 4.1 collective-permute-done.81
  866.8 5.5 collective-permute-done.123
  872.4 5.5 collective-permute-done.130
  878.0 4.1 collective-permute-done.82
  882.9 4.8 collective-permute-done.124
  (772 shorter events, 368.4 us)
Async XLA Ops:
  12.9 21.0 %collective-permute-start = (bf16[1,3,128,256]{3,2,1,0:T(8,128)(2,1)}, bf16[1,3,128,256]{3,2,1,0:T(8,128)(2,1)S(1)}, u32[]{:S(2)}, u32[]{:S(2)}) collective-permute-start(bf16[1,3,128,256]{3,2,1,0:T(8,128)(2,1)} %bitcast.554), channel_id=1, source_target_pairs={{0,8},{1,9},{2,10},{3,11},{4,12},{5,13},{6,14},{7,15},{8,16},{9,17... | collective-permute-start | bytes 589832 | tf_op jit(solution)/shard_map/ppermute | solution.py:272
  16.8 18.7 %collective-permute-start.50 = (bf16[1,1,128,1024]{3,2,1,0:T(8,128)(2,1)}, bf16[1,1,128,1024]{3,2,1,0:T(8,128)(2,1)S(1)}, u32[]{:S(2)}, u32[]{:S(2)}) collective-permute-start(bf16[1,1,128,1024]{3,2,1,0:T(8,128)(2,1)} %bitcast.549), channel_id=1, source_target_pairs={{0,8},{1,9},{2,10},{3,11},{4,12},{5,13},{6,14},{7,15},{8,16},{9,17... | collective-permute-start | bytes 786440 | tf_op jit(solution)/shard_map/ppermute | solution.py:272
  37.4 17.0 %collective-permute-start.46 = (bf16[4,1,128,256]{3,2,1,0:T(8,128)(2,1)S(1)}, bf16[4,1,128,256]{3,2,1,0:T(8,128)(2,1)S(1)}, u32[]{:S(2)}, u32[]{:S(2)}) collective-permute-start(bf16[4,1,128,256]{3,2,1,0:T(8,128)(2,1)S(1)} %pad_maximum_fusion.10.refs_0_), channel_id=1, source_target_pairs={{0,1},{1,0},{2,3},{3,2},{4,5},{5,4},{6,7},{7,6},{8,9},{9,8},{10,11... | collective-permute-start | bytes 786440 | tf_op jit(solution)/shard_map/ppermute | solution.py:272
  38.2 16.1 %collective-permute-start.1 = (bf16[1,3,128,256]{3,2,1,0:T(8,128)(2,1)S(1)}, bf16[1,3,128,256]{3,2,1,0:T(8,128)(2,1)S(1)}, u32[]{:S(2)}, u32[]{:S(2)}) collective-permute-start(bf16[1,3,128,256]{3,2,1,0:T(8,128)(2,1)S(1)} %collective-permute-done), channel_id=1, source_target_pairs={{0,8},{1,9},{2,10},{3,11},{4,12},{5,13},{6,14},{7,15},{8,16},{9,17... | collective-permute-start | bytes 589832 | tf_op jit(solution)/shard_map/ppermute | solution.py:272
  55.1 27.3 %collective-permute-start.27 = (bf16[4,1,128,256]{3,2,1,0:T(8,128)(2,1)S(1)}, bf16[4,1,128,256]{3,2,1,0:T(8,128)(2,1)S(1)}, u32[]{:S(2)}, u32[]{:S(2)}) collective-permute-start(bf16[4,1,128,256]{3,2,1,0:T(8,128)(2,1)S(1)} %collective-permute-done.23.refs_1_), channel_id=1, source_target_pairs={{0,1},{1,0},{2,3},{3,2},{4,5},{5,4},{6,7},{7,6},{8,9},{9,8},{10,11... | collective-permute-start | bytes 786440 | tf_op jit(solution)/shard_map/ppermute | solution.py:272
  56.1 37.9 %collective-permute-start.33 = (bf16[4,2,128,256]{3,2,1,0:T(8,128)(2,1)S(1)}, bf16[4,2,128,256]{3,2,1,0:T(8,128)(2,1)}, u32[]{:S(2)}, u32[]{:S(2)}) collective-permute-start(bf16[4,2,128,256]{3,2,1,0:T(8,128)(2,1)S(1)} %pad_maximum_fusion.6.refs_0_), channel_id=1, source_target_pairs={{0,8},{1,9},{2,10},{3,11},{4,12},{5,13},{6,14},{7,15},{8,16},{9,17... | collective-permute-start | bytes 1572872 | tf_op jit(solution)/shard_map/ppermute | solution.py:272
  56.2 26.2 %collective-permute-start.2 = (bf16[1,3,128,256]{3,2,1,0:T(8,128)(2,1)S(1)}, bf16[1,3,128,256]{3,2,1,0:T(8,128)(2,1)S(1)}, u32[]{:S(2)}, u32[]{:S(2)}) collective-permute-start(bf16[1,3,128,256]{3,2,1,0:T(8,128)(2,1)S(1)} %collective-permute-done.1), channel_id=1, source_target_pairs={{0,8},{1,9},{2,10},{3,11},{4,12},{5,13},{6,14},{7,15},{8,16},{9,17... | collective-permute-start | bytes 589832 | tf_op jit(solution)/shard_map/ppermute | solution.py:272
  61.4 26.7 %collective-permute-start.24 = (bf16[4,1,128,256]{3,2,1,0:T(8,128)(2,1)S(1)}, bf16[4,1,128,256]{3,2,1,0:T(8,128)(2,1)S(1)}, u32[]{:S(2)}, u32[]{:S(2)}) collective-permute-start(bf16[4,1,128,256]{3,2,1,0:T(8,128)(2,1)S(1)} %collective-permute-done.23.refs_1_), channel_id=1, source_target_pairs={{0,8},{1,9},{2,10},{3,11},{4,12},{5,13},{6,14},{7,15},{8,16},{9,17... | collective-permute-start | bytes 786440 | tf_op jit(solution)/shard_map/ppermute | solution.py:272
  67.0 22.3 %collective-permute-start.17 = (bf16[4,1,128,256]{3,2,1,0:T(8,128)(2,1)S(1)}, bf16[4,1,128,256]{3,2,1,0:T(8,128)(2,1)S(1)}, u32[]{:S(2)}, u32[]{:S(2)}) collective-permute-start(bf16[4,1,128,256]{3,2,1,0:T(8,128)(2,1)S(1)} %collective-permute-done.13.refs_1_), channel_id=1, source_target_pairs={{0,1},{1,0},{2,3},{3,2},{4,5},{5,4},{6,7},{7,6},{8,9},{9,8},{10,11... | collective-permute-start | bytes 786440 | tf_op jit(solution)/shard_map/ppermute | solution.py:272
  90.0 31.4 %collective-permute-start.36 = (bf16[4,2,128,256]{3,2,1,0:T(8,128)(2,1)S(1)}, bf16[4,2,128,256]{3,2,1,0:T(8,128)(2,1)S(1)}, u32[]{:S(2)}, u32[]{:S(2)}) collective-permute-start(bf16[4,2,128,256]{3,2,1,0:T(8,128)(2,1)S(1)} %pad_maximum_fusion.6.refs_0_), channel_id=1, source_target_pairs={{0,1},{1,0},{2,3},{3,2},{4,5},{5,4},{6,7},{7,6},{8,9},{9,8},{10,11... | collective-permute-start | bytes 1572872 | tf_op jit(solution)/shard_map/ppermute | solution.py:272
  94.1 28.3 %collective-permute-start.34 = (bf16[4,2,128,256]{3,2,1,0:T(8,128)(2,1)}, bf16[4,2,128,256]{3,2,1,0:T(8,128)(2,1)}, u32[]{:S(2)}, u32[]{:S(2)}) collective-permute-start(bf16[4,2,128,256]{3,2,1,0:T(8,128)(2,1)} %collective-permute-done.33.refs_1_), channel_id=1, source_target_pairs={{0,8},{1,9},{2,10},{3,11},{4,12},{5,13},{6,14},{7,15},{8,16},{9,17... | collective-permute-start | bytes 1572872 | tf_op jit(solution)/shard_map/ppermute | solution.py:272
  94.2 25.1 %collective-permute-start.62 = (bf16[1,1,512,256]{3,2,1,0:T(8,128)(2,1)}, bf16[1,1,512,256]{3,2,1,0:T(8,128)(2,1)}, u32[]{:S(2)}, u32[]{:S(2)}) collective-permute-start(bf16[1,1,512,256]{3,2,1,0:T(8,128)(2,1)} %copy-done.126), channel_id=1, source_target_pairs={{0,8},{1,9},{2,10},{3,11},{4,12},{5,13},{6,14},{7,15},{8,16},{9,17... | collective-permute-start | bytes 786440 | tf_op jit(solution)/shard_map/ppermute | solution.py:272
  99.0 87.6 %collective-permute-start.3 = (bf16[4,3,128,256]{3,2,1,0:T(8,128)(2,1)S(1)}, bf16[4,3,128,256]{3,2,1,0:T(8,128)(2,1)}, u32[]{:S(2)}, u32[]{:S(2)}) collective-permute-start(bf16[4,3,128,256]{3,2,1,0:T(8,128)(2,1)S(1)} %pad_maximum_fusion.5.refs_0_), channel_id=1, source_target_pairs={{0,2},{1,3},{2,0},{3,1},{4,6},{5,7},{6,4},{7,5},{8,10},{9,11},{10,... | collective-permute-start | bytes 2359304 | tf_op jit(solution)/shard_map/ppermute | solution.py:272
  105.2 16.3 %collective-permute-start.28 = (bf16[4,1,128,256]{3,2,1,0:T(8,128)(2,1)S(1)}, bf16[4,1,128,256]{3,2,1,0:T(8,128)(2,1)S(1)}, u32[]{:S(2)}, u32[]{:S(2)}) collective-permute-start(bf16[4,1,128,256]{3,2,1,0:T(8,128)(2,1)S(1)} %collective-permute-done.24.refs_2_), channel_id=1, source_target_pairs={{0,1},{1,0},{2,3},{3,2},{4,5},{5,4},{6,7},{7,6},{8,9},{9,8},{10,11... | collective-permute-start | bytes 786440 | tf_op jit(solution)/shard_map/ppermute | solution.py:272
  122.3 70.3 %collective-permute-start.35 = (bf16[4,2,128,256]{3,2,1,0:T(8,128)(2,1)}, bf16[4,2,128,256]{3,2,1,0:T(8,128)(2,1)}, u32[]{:S(2)}, u32[]{:S(2)}) collective-permute-start(bf16[4,2,128,256]{3,2,1,0:T(8,128)(2,1)} %collective-permute-done.34.refs_2_), channel_id=1, source_target_pairs={{0,8},{1,9},{2,10},{3,11},{4,12},{5,13},{6,14},{7,15},{8,16},{9,17... | collective-permute-start | bytes 1572872 | tf_op jit(solution)/shard_map/ppermute | solution.py:272
  129.0 63.2 %collective-permute-start.29 = (bf16[4,1,128,256]{3,2,1,0:T(8,128)(2,1)}, bf16[4,1,128,256]{3,2,1,0:T(8,128)(2,1)}, u32[]{:S(2)}, u32[]{:S(2)}) collective-permute-start(bf16[4,1,128,256]{3,2,1,0:T(8,128)(2,1)} %collective-permute-done.25.refs_3_), channel_id=1, source_target_pairs={{0,1},{1,0},{2,3},{3,2},{4,5},{5,4},{6,7},{7,6},{8,9},{9,8},{10,11... | collective-permute-start | bytes 786440 | tf_op jit(solution)/shard_map/ppermute | solution.py:272
  133.3 58.8 %collective-permute-start.19 = (bf16[4,1,128,256]{3,2,1,0:T(8,128)(2,1)S(1)}, bf16[4,1,128,256]{3,2,1,0:T(8,128)(2,1)S(1)}, u32[]{:S(2)}, u32[]{:S(2)}) collective-permute-start(bf16[4,1,128,256]{3,2,1,0:T(8,128)(2,1)S(1)} %collective-permute-done.15.refs_3_), channel_id=1, source_target_pairs={{0,1},{1,0},{2,3},{3,2},{4,5},{5,4},{6,7},{7,6},{8,9},{9,8},{10,11... | collective-permute-start | bytes 786440 | tf_op jit(solution)/shard_map/ppermute | solution.py:272
  134.2 88.7 %collective-permute-start.4 = (bf16[4,3,128,256]{3,2,1,0:T(8,128)(2,1)S(1)}, bf16[4,3,128,256]{3,2,1,0:T(8,128)(2,1)}, u32[]{:S(2)}, u32[]{:S(2)}) collective-permute-start(bf16[4,3,128,256]{3,2,1,0:T(8,128)(2,1)S(1)} %pad_maximum_fusion.5.refs_0_), channel_id=1, source_target_pairs={{0,4},{1,5},{2,6},{3,7},{4,0},{5,1},{6,2},{7,3},{8,12},{9,13},{10,... | collective-permute-start | bytes 2359304 | tf_op jit(solution)/shard_map/ppermute | solution.py:272
  186.7 36.4 %collective-permute-start.5 = (bf16[4,3,128,256]{3,2,1,0:T(8,128)(2,1)}, bf16[4,3,128,256]{3,2,1,0:T(8,128)(2,1)}, u32[]{:S(2)}, u32[]{:S(2)}) collective-permute-start(bf16[4,3,128,256]{3,2,1,0:T(8,128)(2,1)} %collective-permute-done.3.refs_1_), channel_id=1, source_target_pairs={{0,4},{1,5},{2,6},{3,7},{4,0},{5,1},{6,2},{7,3},{8,12},{9,13},{10,... | collective-permute-start | bytes 2359304 | tf_op jit(solution)/shard_map/ppermute | solution.py:272
  192.1 30.3 %collective-permute-start.37 = (bf16[4,2,128,256]{3,2,1,0:T(8,128)(2,1)}, bf16[4,2,128,256]{3,2,1,0:T(8,128)(2,1)}, u32[]{:S(2)}, u32[]{:S(2)}) collective-permute-start(bf16[4,2,128,256]{3,2,1,0:T(8,128)(2,1)} %collective-permute-done.33.refs_1_), channel_id=1, source_target_pairs={{0,1},{1,0},{2,3},{3,2},{4,5},{5,4},{6,7},{7,6},{8,9},{9,8},{10,11... | collective-permute-start | bytes 1572872 | tf_op jit(solution)/shard_map/ppermute | solution.py:272
  192.1 30.8 %collective-permute-start.38 = (bf16[4,2,128,256]{3,2,1,0:T(8,128)(2,1)}, bf16[4,2,128,256]{3,2,1,0:T(8,128)(2,1)}, u32[]{:S(2)}, u32[]{:S(2)}) collective-permute-start(bf16[4,2,128,256]{3,2,1,0:T(8,128)(2,1)} %collective-permute-done.34.refs_2_), channel_id=1, source_target_pairs={{0,1},{1,0},{2,3},{3,2},{4,5},{5,4},{6,7},{7,6},{8,9},{9,8},{10,11... | collective-permute-start | bytes 1572872 | tf_op jit(solution)/shard_map/ppermute | solution.py:272
  192.6 30.9 %collective-permute-start.39 = (bf16[4,2,128,256]{3,2,1,0:T(8,128)(2,1)}, bf16[4,2,128,256]{3,2,1,0:T(8,128)(2,1)}, u32[]{:S(2)}, u32[]{:S(2)}) collective-permute-start(bf16[4,2,128,256]{3,2,1,0:T(8,128)(2,1)} %collective-permute-done.35.refs_3_), channel_id=1, source_target_pairs={{0,1},{1,0},{2,3},{3,2},{4,5},{5,4},{6,7},{7,6},{8,9},{9,8},{10,11... | collective-permute-start | bytes 1572872 | tf_op jit(solution)/shard_map/ppermute | solution.py:272
  222.5 20.1 %collective-permute-start.6 = (bf16[4,3,128,256]{3,2,1,0:T(8,128)(2,1)S(1)}, bf16[4,3,128,256]{3,2,1,0:T(8,128)(2,1)S(1)}, u32[]{:S(2)}, u32[]{:S(2)}) collective-permute-start(bf16[4,3,128,256]{3,2,1,0:T(8,128)(2,1)S(1)} %pad_maximum_fusion.5.refs_0_), channel_id=1, source_target_pairs={{0,1},{1,0},{2,3},{3,2},{4,5},{5,4},{6,7},{7,6},{8,9},{9,8},{10,11... | collective-permute-start | bytes 2359304 | tf_op jit(solution)/shard_map/ppermute | solution.py:272
  222.9 26.3 %collective-permute-start.53 = (bf16[4,1,128,1024]{3,2,1,0:T(8,128)(2,1)}, bf16[4,1,128,1024]{3,2,1,0:T(8,128)(2,1)}, u32[]{:S(2)}, u32[]{:S(2)}) collective-permute-start(bf16[4,1,128,1024]{3,2,1,0:T(8,128)(2,1)} %pad_maximum_fusion.3.refs_0_), channel_id=1, source_target_pairs={{0,4},{1,5},{2,6},{3,7},{4,0},{5,1},{6,2},{7,3},{8,12},{9,13},{10,... | collective-permute-start | bytes 3145736 | tf_op jit(solution)/shard_map/ppermute | solution.py:272
  222.9 27.5 %collective-permute-start.7 = (bf16[4,3,128,256]{3,2,1,0:T(8,128)(2,1)}, bf16[4,3,128,256]{3,2,1,0:T(8,128)(2,1)S(1)}, u32[]{:S(2)}, u32[]{:S(2)}) collective-permute-start(bf16[4,3,128,256]{3,2,1,0:T(8,128)(2,1)} %collective-permute-done.3.refs_1_), channel_id=1, source_target_pairs={{0,1},{1,0},{2,3},{3,2},{4,5},{5,4},{6,7},{7,6},{8,9},{9,8},{10,11... | collective-permute-start | bytes 2359304 | tf_op jit(solution)/shard_map/ppermute | solution.py:272
  223.1 27.3 %collective-permute-start.8 = (bf16[4,3,128,256]{3,2,1,0:T(8,128)(2,1)}, bf16[4,3,128,256]{3,2,1,0:T(8,128)(2,1)S(1)}, u32[]{:S(2)}, u32[]{:S(2)}) collective-permute-start(bf16[4,3,128,256]{3,2,1,0:T(8,128)(2,1)} %collective-permute-done.4.refs_2_), channel_id=1, source_target_pairs={{0,1},{1,0},{2,3},{3,2},{4,5},{5,4},{6,7},{7,6},{8,9},{9,8},{10,11... | collective-permute-start | bytes 2359304 | tf_op jit(solution)/shard_map/ppermute | solution.py:272
  223.5 27.8 %collective-permute-start.9 = (bf16[4,3,128,256]{3,2,1,0:T(8,128)(2,1)}, bf16[4,3,128,256]{3,2,1,0:T(8,128)(2,1)S(1)}, u32[]{:S(2)}, u32[]{:S(2)}) collective-permute-start(bf16[4,3,128,256]{3,2,1,0:T(8,128)(2,1)} %collective-permute-done.5.refs_3_), channel_id=1, source_target_pairs={{0,1},{1,0},{2,3},{3,2},{4,5},{5,4},{6,7},{7,6},{8,9},{9,8},{10,11... | collective-permute-start | bytes 2359304 | tf_op jit(solution)/shard_map/ppermute | solution.py:272
  242.5 47.8 %collective-permute-start.64 = (bf16[4,1,512,256]{3,2,1,0:T(8,128)(2,1)}, bf16[4,1,512,256]{3,2,1,0:T(8,128)(2,1)}, u32[]{:S(2)}, u32[]{:S(2)}) collective-permute-start(bf16[4,1,512,256]{3,2,1,0:T(8,128)(2,1)} %pad_maximum_fusion.4.refs_0_), channel_id=1, source_target_pairs={{0,4},{1,5},{2,6},{3,7},{4,0},{5,1},{6,2},{7,3},{8,12},{9,13},{10,... | collective-permute-start | bytes 3145736 | tf_op jit(solution)/shard_map/ppermute | solution.py:272
  249.2 41.2 %collective-permute-start.63 = (bf16[4,1,512,256]{3,2,1,0:T(8,128)(2,1)}, bf16[4,1,512,256]{3,2,1,0:T(8,128)(2,1)}, u32[]{:S(2)}, u32[]{:S(2)}) collective-permute-start(bf16[4,1,512,256]{3,2,1,0:T(8,128)(2,1)} %pad_maximum_fusion.4.refs_0_), channel_id=1, source_target_pairs={{0,2},{1,3},{2,0},{3,1},{4,6},{5,7},{6,4},{7,5},{8,10},{9,11},{10,... | collective-permute-start | bytes 3145736 | tf_op jit(solution)/shard_map/ppermute | solution.py:272
  250.4 68.9 %collective-permute-start.56 = (bf16[4,1,128,1024]{3,2,1,0:T(8,128)(2,1)}, bf16[4,1,128,1024]{3,2,1,0:T(8,128)(2,1)}, u32[]{:S(2)}, u32[]{:S(2)}) collective-permute-start(bf16[4,1,128,1024]{3,2,1,0:T(8,128)(2,1)} %pad_maximum_fusion.3.refs_0_), channel_id=1, source_target_pairs={{0,1},{1,0},{2,3},{3,2},{4,5},{5,4},{6,7},{7,6},{8,9},{9,8},{10,11... | collective-permute-start | bytes 3145736 | tf_op jit(solution)/shard_map/ppermute | solution.py:272
  250.4 47.7 %collective-permute-start.54 = (bf16[4,1,128,1024]{3,2,1,0:T(8,128)(2,1)}, bf16[4,1,128,1024]{3,2,1,0:T(8,128)(2,1)}, u32[]{:S(2)}, u32[]{:S(2)}) collective-permute-start(bf16[4,1,128,1024]{3,2,1,0:T(8,128)(2,1)} %pad_maximum_fusion.3.refs_0_), channel_id=1, source_target_pairs={{0,2},{1,3},{2,0},{3,1},{4,6},{5,7},{6,4},{7,5},{8,10},{9,11},{10,... | collective-permute-start | bytes 3145736 | tf_op jit(solution)/shard_map/ppermute | solution.py:272
  251.3 66.6 %collective-permute-start.55 = (bf16[4,1,128,1024]{3,2,1,0:T(8,128)(2,1)}, bf16[4,1,128,1024]{3,2,1,0:T(8,128)(2,1)}, u32[]{:S(2)}, u32[]{:S(2)}) collective-permute-start(bf16[4,1,128,1024]{3,2,1,0:T(8,128)(2,1)} %collective-permute-done.53.refs_1_), channel_id=1, source_target_pairs={{0,2},{1,3},{2,0},{3,1},{4,6},{5,7},{6,4},{7,5},{8,10},{9,11},{10,... | collective-permute-start | bytes 3145736 | tf_op jit(solution)/shard_map/ppermute | solution.py:272
  290.3 30.1 %collective-permute-start.57 = (bf16[4,1,128,1024]{3,2,1,0:T(8,128)(2,1)}, bf16[4,1,128,1024]{3,2,1,0:T(8,128)(2,1)S(1)}, u32[]{:S(2)}, u32[]{:S(2)}) collective-permute-start(bf16[4,1,128,1024]{3,2,1,0:T(8,128)(2,1)} %collective-permute-done.53.refs_1_), channel_id=1, source_target_pairs={{0,1},{1,0},{2,3},{3,2},{4,5},{5,4},{6,7},{7,6},{8,9},{9,8},{10,11... | collective-permute-start | bytes 3145736 | tf_op jit(solution)/shard_map/ppermute | solution.py:272
  290.4 29.5 %collective-permute-start.65 = (bf16[4,1,512,256]{3,2,1,0:T(8,128)(2,1)}, bf16[4,1,512,256]{3,2,1,0:T(8,128)(2,1)S(1)}, u32[]{:S(2)}, u32[]{:S(2)}) collective-permute-start(bf16[4,1,512,256]{3,2,1,0:T(8,128)(2,1)} %collective-permute-done.63.refs_1_), channel_id=1, source_target_pairs={{0,4},{1,5},{2,6},{3,7},{4,0},{5,1},{6,2},{7,3},{8,12},{9,13},{10,... | collective-permute-start | bytes 3145736 | tf_op jit(solution)/shard_map/ppermute | solution.py:272
  298.1 21.9 %collective-permute-start.58 = (bf16[4,1,128,1024]{3,2,1,0:T(8,128)(2,1)}, bf16[4,1,128,1024]{3,2,1,0:T(8,128)(2,1)S(1)}, u32[]{:S(2)}, u32[]{:S(2)}) collective-permute-start(bf16[4,1,128,1024]{3,2,1,0:T(8,128)(2,1)} %collective-permute-done.54.refs_2_), channel_id=1, source_target_pairs={{0,1},{1,0},{2,3},{3,2},{4,5},{5,4},{6,7},{7,6},{8,9},{9,8},{10,11... | collective-permute-start | bytes 3145736 | tf_op jit(solution)/shard_map/ppermute | solution.py:272
  319.3 18.3 %collective-permute-start.66 = (bf16[4,1,512,256]{3,2,1,0:T(8,128)(2,1)}, bf16[4,1,512,256]{3,2,1,0:T(8,128)(2,1)S(1)}, u32[]{:S(2)}, u32[]{:S(2)}) collective-permute-start(bf16[4,1,512,256]{3,2,1,0:T(8,128)(2,1)} %pad_maximum_fusion.4.refs_0_), channel_id=1, source_target_pairs={{0,1},{1,0},{2,3},{3,2},{4,5},{5,4},{6,7},{7,6},{8,9},{9,8},{10,11... | collective-permute-start | bytes 3145736 | tf_op jit(solution)/shard_map/ppermute | solution.py:272
  319.9 17.7 %collective-permute-start.67 = (bf16[4,1,512,256]{3,2,1,0:T(8,128)(2,1)}, bf16[4,1,512,256]{3,2,1,0:T(8,128)(2,1)S(1)}, u32[]{:S(2)}, u32[]{:S(2)}) collective-permute-start(bf16[4,1,512,256]{3,2,1,0:T(8,128)(2,1)} %collective-permute-done.63.refs_1_), channel_id=1, source_target_pairs={{0,1},{1,0},{2,3},{3,2},{4,5},{5,4},{6,7},{7,6},{8,9},{9,8},{10,11... | collective-permute-start | bytes 3145736 | tf_op jit(solution)/shard_map/ppermute | solution.py:272
  320.0 17.6 %collective-permute-start.68 = (bf16[4,1,512,256]{3,2,1,0:T(8,128)(2,1)}, bf16[4,1,512,256]{3,2,1,0:T(8,128)(2,1)S(1)}, u32[]{:S(2)}, u32[]{:S(2)}) collective-permute-start(bf16[4,1,512,256]{3,2,1,0:T(8,128)(2,1)} %collective-permute-done.64.refs_2_), channel_id=1, source_target_pairs={{0,1},{1,0},{2,3},{3,2},{4,5},{5,4},{6,7},{7,6},{8,9},{9,8},{10,11... | collective-permute-start | bytes 3145736 | tf_op jit(solution)/shard_map/ppermute | solution.py:272
  320.4 17.2 %collective-permute-start.69 = (bf16[4,1,512,256]{3,2,1,0:T(8,128)(2,1)S(1)}, bf16[4,1,512,256]{3,2,1,0:T(8,128)(2,1)S(1)}, u32[]{:S(2)}, u32[]{:S(2)}) collective-permute-start(bf16[4,1,512,256]{3,2,1,0:T(8,128)(2,1)S(1)} %collective-permute-done.65.refs_3_), channel_id=1, source_target_pairs={{0,1},{1,0},{2,3},{3,2},{4,5},{5,4},{6,7},{7,6},{8,9},{9,8},{10,11... | collective-permute-start | bytes 3145736 | tf_op jit(solution)/shard_map/ppermute | solution.py:272
  459.8 92.6 %collective-permute-start.112 = (bf16[1,1024,256]{2,1,0:T(8,128)(2,1)}, bf16[1,1024,256]{2,1,0:T(8,128)(2,1)}, u32[]{:S(2)}, u32[]{:S(2)}) collective-permute-start(bf16[1,1024,256]{2,1,0:T(8,128)(2,1)} %fusion.37), channel_id=1, source_target_pairs={{0,1},{1,0},{2,3},{3,2},{4,5},{5,4},{6,7},{7,6},{8,9},{9,8},{10,11... | collective-permute-start | bytes 1572872 | tf_op jit(solution)/shard_map/ppermute | solution.py:272
  460.2 44.1 %collective-permute-start.97 = (bf16[1,1024,256]{1,2,0:T(8,128)(2,1)}, bf16[1,1024,256]{1,2,0:T(8,128)(2,1)}, u32[]{:S(2)}, u32[]{:S(2)}) collective-permute-start(bf16[1,1024,256]{1,2,0:T(8,128)(2,1)} %fusion.41), channel_id=1, source_target_pairs={{0,1},{1,0},{2,3},{3,2},{4,5},{5,4},{6,7},{7,6},{8,9},{9,8},{10,11... | collective-permute-start | bytes 1572872 | tf_op jit(solution)/shard_map/ppermute | solution.py:272
  482.7 67.9 %collective-permute-start.84 = (bf16[1,1024,256]{2,1,0:T(8,128)(2,1)}, bf16[1,1024,256]{2,1,0:T(8,128)(2,1)}, u32[]{:S(2)}, u32[]{:S(2)}) collective-permute-start(bf16[1,1024,256]{2,1,0:T(8,128)(2,1)} %fusion.33), channel_id=1, source_target_pairs={{0,1},{1,0},{2,3},{3,2},{4,5},{5,4},{6,7},{7,6},{8,9},{9,8},{10,11... | collective-permute-start | bytes 1572872 | tf_op jit(solution)/shard_map/ppermute | solution.py:272
  482.7 74.5 %collective-permute-start.83 = (bf16[1,1024,256]{2,1,0:T(8,128)(2,1)}, bf16[1,1024,256]{2,1,0:T(8,128)(2,1)}, u32[]{:S(2)}, u32[]{:S(2)}) collective-permute-start(bf16[1,1024,256]{2,1,0:T(8,128)(2,1)} %fusion.32), channel_id=1, source_target_pairs={{0,1},{1,0},{2,3},{3,2},{4,5},{5,4},{6,7},{7,6},{8,9},{9,8},{10,11... | collective-permute-start | bytes 1572872 | tf_op jit(solution)/shard_map/ppermute | solution.py:272
  502.2 68.4 %collective-permute-start.111 = (bf16[1,1024,256]{2,1,0:T(8,128)(2,1)}, bf16[1,1024,256]{2,1,0:T(8,128)(2,1)}, u32[]{:S(2)}, u32[]{:S(2)}) collective-permute-start(bf16[1,1024,256]{2,1,0:T(8,128)(2,1)} %fusion.36), channel_id=1, source_target_pairs={{0,1},{1,0},{2,3},{3,2},{4,5},{5,4},{6,7},{7,6},{8,9},{9,8},{10,11... | collective-permute-start | bytes 1572872 | tf_op jit(solution)/shard_map/ppermute | solution.py:272
  521.9 59.3 %collective-permute-start.104 = (bf16[1,1024,256]{1,2,0:T(8,128)(2,1)}, bf16[1,1024,256]{1,2,0:T(8,128)(2,1)}, u32[]{:S(2)}, u32[]{:S(2)}) collective-permute-start(bf16[1,1024,256]{1,2,0:T(8,128)(2,1)} %fusion.39), channel_id=1, source_target_pairs={{0,1},{1,0},{2,3},{3,2},{4,5},{5,4},{6,7},{7,6},{8,9},{9,8},{10,11... | collective-permute-start | bytes 1572872 | tf_op jit(solution)/shard_map/ppermute | solution.py:272
  555.2 23.3 %collective-permute-start.113 = (bf16[1,1024,256]{2,1,0:T(8,128)(2,1)S(1)}, bf16[1,1024,256]{2,1,0:T(8,128)(2,1)S(1)}, u32[]{:S(2)}, u32[]{:S(2)}) collective-permute-start(bf16[1,1024,256]{2,1,0:T(8,128)(2,1)S(1)} %add_convert_fusion.4), channel_id=1, source_target_pairs={{0,2},{1,3},{2,0},{3,1},{4,6},{5,7},{6,4},{7,5},{8,10},{9,11},{10,... | collective-permute-start | bytes 1572872 | tf_op jit(solution)/shard_map/ppermute | solution.py:272
  557.2 44.7 %collective-permute-start.90 = (bf16[1,1024,256]{2,1,0:T(8,128)(2,1)}, bf16[1,1024,256]{2,1,0:T(8,128)(2,1)}, u32[]{:S(2)}, u32[]{:S(2)}) collective-permute-start(bf16[1,1024,256]{2,1,0:T(8,128)(2,1)} %fusion.34), channel_id=1, source_target_pairs={{0,1},{1,0},{2,3},{3,2},{4,5},{5,4},{6,7},{7,6},{8,9},{9,8},{10,11... | collective-permute-start | bytes 1572872 | tf_op jit(solution)/shard_map/ppermute | solution.py:272
  567.2 21.9 %collective-permute-start.106 = (bf16[1,1024,256]{1,2,0:T(8,128)(2,1)S(1)}, bf16[1,1024,256]{1,2,0:T(8,128)(2,1)S(1)}, u32[]{:S(2)}, u32[]{:S(2)}) collective-permute-start(bf16[1,1024,256]{1,2,0:T(8,128)(2,1)S(1)} %copy-done.147), channel_id=1, source_target_pairs={{0,2},{1,3},{2,0},{3,1},{4,6},{5,7},{6,4},{7,5},{8,10},{9,11},{10,... | collective-permute-start | bytes 1572872 | tf_op jit(solution)/shard_map/ppermute | solution.py:272
  570.6 117.0 %collective-permute-start.77 = (bf16[3,1024,256]{1,2,0:T(8,128)(2,1)}, bf16[3,1024,256]{1,2,0:T(8,128)(2,1)}, u32[]{:S(2)}, u32[]{:S(2)}) collective-permute-start(bf16[3,1024,256]{1,2,0:T(8,128)(2,1)} %fusion.22), channel_id=1, source_target_pairs={{0,1},{1,0},{2,3},{3,2},{4,5},{5,4},{6,7},{7,6},{8,9},{9,8},{10,11... | collective-permute-start | bytes 4718600 | tf_op jit(solution)/shard_map/ppermute | solution.py:272
  578.5 17.2 %collective-permute-start.99 = (bf16[2,1,4,128,256]{4,3,2,1,0:T(8,128)(2,1)}, bf16[2,1,4,128,256]{4,3,2,1,0:T(8,128)(2,1)}, u32[]{:S(2)}, u32[]{:S(2)}) collective-permute-start(bf16[2,1,4,128,256]{4,3,2,1,0:T(8,128)(2,1)} %pad_maximum_fusion.7), channel_id=1, source_target_pairs={{0,4},{1,5},{2,6},{3,7},{4,0},{5,1},{6,2},{7,3},{8,12},{9,13},{10,... | collective-permute-start | bytes 1572872 | tf_op jit(solution)/shard_map/ppermute | solution.py:272
  581.3 125.5 %collective-permute-start.76 = (bf16[3,1024,256]{1,2,0:T(8,128)(2,1)}, bf16[3,1024,256]{1,2,0:T(8,128)(2,1)}, u32[]{:S(2)}, u32[]{:S(2)}) collective-permute-start(bf16[3,1024,256]{1,2,0:T(8,128)(2,1)} %fusion.21), channel_id=1, source_target_pairs={{0,1},{1,0},{2,3},{3,2},{4,5},{5,4},{6,7},{7,6},{8,9},{9,8},{10,11... | collective-permute-start | bytes 4718600 | tf_op jit(solution)/shard_map/ppermute | solution.py:272
  595.6 132.6 %collective-permute-start.119 = (bf16[1,1024,1024]{2,1,0:T(8,128)(2,1)}, bf16[1,1024,1024]{2,1,0:T(8,128)(2,1)}, u32[]{:S(2)}, u32[]{:S(2)}) collective-permute-start(bf16[1,1024,1024]{2,1,0:T(8,128)(2,1)} %convert_bitcast_fusion.1), channel_id=1, source_target_pairs={{0,1},{1,0},{2,3},{3,2},{4,5},{5,4},{6,7},{7,6},{8,9},{9,8},{10,11... | collective-permute-start | bytes 6291464 | tf_op jit(solution)/shard_map/ppermute | solution.py:272
  622.1 108.9 %collective-permute-start.118 = (bf16[1,1024,1024]{2,1,0:T(8,128)(2,1)}, bf16[1,1024,1024]{2,1,0:T(8,128)(2,1)}, u32[]{:S(2)}, u32[]{:S(2)}) collective-permute-start(bf16[1,1024,1024]{2,1,0:T(8,128)(2,1)} %convert_bitcast_fusion.2), channel_id=1, source_target_pairs={{0,1},{1,0},{2,3},{3,2},{4,5},{5,4},{6,7},{7,6},{8,9},{9,8},{10,11... | collective-permute-start | bytes 6291464 | tf_op jit(solution)/shard_map/ppermute | solution.py:272
  687.5 131.3 %collective-permute-start.125 = (bf16[1,4096,256]{2,1,0:T(8,128)(2,1)}, bf16[1,4096,256]{2,1,0:T(8,128)(2,1)}, u32[]{:S(2)}, u32[]{:S(2)}) collective-permute-start(bf16[1,4096,256]{2,1,0:T(8,128)(2,1)} %fusion), channel_id=1, source_target_pairs={{0,1},{1,0},{2,3},{3,2},{4,5},{5,4},{6,7},{7,6},{8,9},{9,8},{10,11... | collective-permute-start | bytes 6291464 | tf_op jit(solution)/shard_map/ppermute | solution.py:272
  687.6 49.1 %collective-permute-start.126 = (bf16[1,4096,256]{2,1,0:T(8,128)(2,1)}, bf16[1,4096,256]{2,1,0:T(8,128)(2,1)}, u32[]{:S(2)}, u32[]{:S(2)}) collective-permute-start(bf16[1,4096,256]{2,1,0:T(8,128)(2,1)} %fusion.1), channel_id=1, source_target_pairs={{0,1},{1,0},{2,3},{3,2},{4,5},{5,4},{6,7},{7,6},{8,9},{9,8},{10,11... | collective-permute-start | bytes 6291464 | tf_op jit(solution)/shard_map/ppermute | solution.py:272
  706.8 34.7 %collective-permute-start.109 = (bf16[1,128,256]{2,1,0:T(8,128)(2,1)S(1)}, bf16[1,128,256]{2,1,0:T(8,128)(2,1)}, u32[]{:S(2)}, u32[]{:S(2)}) collective-permute-start(bf16[1,128,256]{2,1,0:T(8,128)(2,1)S(1)} %fusion.96), channel_id=1, source_target_pairs={{0,8},{1,9},{2,10},{3,11},{4,12},{5,13},{6,14},{7,15},{8,16},{9,17... | collective-permute-start | bytes 196616 | tf_op jit(solution)/shard_map/ppermute | solution.py:272
  731.0 42.8 %collective-permute-start.78 = (bf16[2,3,4,128,256]{4,3,1,2,0:T(8,128)(2,1)}, bf16[2,3,4,128,256]{4,3,1,2,0:T(8,128)(2,1)}, u32[]{:S(2)}, u32[]{:S(2)}) collective-permute-start(bf16[2,3,4,128,256]{4,3,1,2,0:T(8,128)(2,1)} %pad_maximum_fusion.2), channel_id=1, source_target_pairs={{0,4},{1,5},{2,6},{3,7},{4,0},{5,1},{6,2},{7,3},{8,12},{9,13},{10,... | collective-permute-start | bytes 4718600 | tf_op jit(solution)/shard_map/ppermute | solution.py:272
  736.7 76.0 %collective-permute-start.120 = (bf16[2,1,4,128,1024]{4,3,2,1,0:T(8,128)(2,1)}, bf16[2,1,4,128,1024]{4,3,2,1,0:T(8,128)(2,1)}, u32[]{:S(2)}, u32[]{:S(2)}) collective-permute-start(bf16[2,1,4,128,1024]{4,3,2,1,0:T(8,128)(2,1)} %pad_maximum_fusion), channel_id=1, source_target_pairs={{0,4},{1,5},{2,6},{3,7},{4,0},{5,1},{6,2},{7,3},{8,12},{9,13},{10,... | collective-permute-start | bytes 6291464 | tf_op jit(solution)/shard_map/ppermute | solution.py:272
  741.5 77.4 %collective-permute-start.127 = (bf16[1,4096,256]{2,1,0:T(8,128)(2,1)}, bf16[1,4096,256]{2,1,0:T(8,128)(2,1)}, u32[]{:S(2)}, u32[]{:S(2)}) collective-permute-start(bf16[1,4096,256]{2,1,0:T(8,128)(2,1)} %add_convert_fusion.2), channel_id=1, source_target_pairs={{0,2},{1,3},{2,0},{3,1},{4,6},{5,7},{6,4},{7,5},{8,10},{9,11},{10,... | collective-permute-start | bytes 6291464 | tf_op jit(solution)/shard_map/ppermute | solution.py:272
  776.9 56.8 %collective-permute-start.79 = (bf16[3,4,128,256]{3,2,0,1:T(8,128)(2,1)}, bf16[3,4,128,256]{3,2,0,1:T(8,128)(2,1)}, u32[]{:S(2)}, u32[]{:S(2)}) collective-permute-start(bf16[3,4,128,256]{3,2,0,1:T(8,128)(2,1)} %fusion.14), channel_id=1, source_target_pairs={{0,2},{1,3},{2,0},{3,1},{4,6},{5,7},{6,4},{7,5},{8,10},{9,11},{10,... | collective-permute-start | bytes 2359304 | tf_op jit(solution)/shard_map/ppermute | solution.py:272
  818.1 24.6 %collective-permute-start.121 = (bf16[1,4,128,1024]{3,2,1,0:T(8,128)(2,1)}, bf16[1,4,128,1024]{3,2,1,0:T(8,128)(2,1)}, u32[]{:S(2)}, u32[]{:S(2)}) collective-permute-start(bf16[1,4,128,1024]{3,2,1,0:T(8,128)(2,1)} %fusion.10), channel_id=1, source_target_pairs={{0,2},{1,3},{2,0},{3,1},{4,6},{5,7},{6,4},{7,5},{8,10},{9,11},{10,... | collective-permute-start | bytes 3145736 | tf_op jit(solution)/shard_map/ppermute | solution.py:272
  825.3 24.6 %collective-permute-start.128 = (bf16[1,4,512,256]{3,2,1,0:T(8,128)(2,1)}, bf16[1,4,512,256]{3,2,1,0:T(8,128)(2,1)}, u32[]{:S(2)}, u32[]{:S(2)}) collective-permute-start(bf16[1,4,512,256]{3,2,1,0:T(8,128)(2,1)} %fusion.59), channel_id=1, source_target_pairs={{0,4},{1,5},{2,6},{3,7},{4,0},{5,1},{6,2},{7,3},{8,12},{9,13},{10,... | collective-permute-start | bytes 3145736 | tf_op jit(solution)/shard_map/ppermute | solution.py:272
  835.8 15.6 %collective-permute-start.80 = (bf16[3,128,256]{2,1,0:T(8,128)(2,1)S(1)}, bf16[3,128,256]{2,1,0:T(8,128)(2,1)S(1)}, u32[]{:S(2)}, u32[]{:S(2)}) collective-permute-start(bf16[3,128,256]{2,1,0:T(8,128)(2,1)S(1)} %fusion.92), channel_id=1, source_target_pairs={{0,8},{1,9},{2,10},{3,11},{4,12},{5,13},{6,14},{7,15},{8,16},{9,17... | collective-permute-start | bytes 589832 | tf_op jit(solution)/shard_map/ppermute | solution.py:272
  855.3 16.9 %collective-permute-start.123 = (bf16[1,128,1024]{2,1,0:T(8,128)(2,1)S(1)}, bf16[1,128,1024]{2,1,0:T(8,128)(2,1)S(1)}, u32[]{:S(2)}, u32[]{:S(2)}) collective-permute-start(bf16[1,128,1024]{2,1,0:T(8,128)(2,1)S(1)} %fusion.74), channel_id=1, source_target_pairs={{0,8},{1,9},{2,10},{3,11},{4,12},{5,13},{6,14},{7,15},{8,16},{9,17... | collective-permute-start | bytes 786440 | tf_op jit(solution)/shard_map/ppermute | solution.py:272
  (226 other events, 4102.7 us)

commit v2 on v1

v2 whole, which is shorter than its diff:
```python
import functools
import math

import jax
import jax.numpy as jnp
from jax import lax
from jax.experimental import pallas as pl
from jax.experimental.pallas import tpu as pltpu
from jax.sharding import PartitionSpec as P

D = 1024
HEADS = 16
HEAD_DIM = 64
PAIRS = HEADS // 2

EPSILON = 1e-05
NEG_FILL = -1e30
LOG2E = math.log2(math.e)
SCALE = 1.0 / math.sqrt(HEAD_DIM)
AXES = ("wide", "narrow")

F32 = jnp.float32
BF16 = jnp.bfloat16


def dot_nt(a, b):
    return lax.dot_general(a, b, (((1,), (1,)), ((), ())), preferred_element_type=F32)


def dot_nn(a, b):
    return lax.dot_general(a, b, (((1,), (0,)), ((), ())), preferred_element_type=F32)


def dot_tn(a, b):
    return lax.dot_general(a, b, (((0,), (0,)), ((), ())), preferred_element_type=F32)


def two_heads(block):
    lane = lax.broadcasted_iota(jnp.int32, block.shape, 1)
    zero = jnp.zeros_like(block)
    return jnp.concatenate(
        (jnp.where(lane < HEAD_DIM, block, zero), jnp.where(lane < HEAD_DIM, zero, block)), axis=0
    )


def join_heads(both):
    half = both.shape[0] // 2
    lane = lax.broadcasted_iota(jnp.int32, (half, both.shape[1]), 1)
    return jnp.where(lane < HEAD_DIM, both[:half], both[half:])


def pair_forward(q2, k2, v2, valid):
    scores = dot_nt(k2, two_heads(q2)) * (SCALE * LOG2E)
    scores = jnp.where(valid, scores, NEG_FILL)
    top = jnp.max(scores, axis=0, keepdims=True)
    expo = jnp.exp2(scores - top)
    total = jnp.sum(expo, axis=0, keepdims=True)
    weights = (expo * (1.0 / total)).astype(BF16)
    mixed = join_heads(dot_tn(weights, v2)).astype(BF16)
    return mixed, top + jnp.log2(total)


def pair_backward(q2, k2, v2, do2, lse, valid):
    qq = two_heads(q2)
    dd = two_heads(do2)
    scores = dot_nt(k2, qq) * (SCALE * LOG2E)
    weights = jnp.where(valid, jnp.exp2(scores - lse), 0.0)
    grad_weights = dot_nt(v2, dd)
    inner = jnp.sum(weights * grad_weights, axis=0, keepdims=True)
    grad_scores = (weights * (grad_weights - inner)).astype(BF16)
    grad_v = dot_nn(weights.astype(BF16), dd).astype(BF16)
    grad_k = (dot_nn(grad_scores, qq) * SCALE).astype(BF16)
    grad_q = (join_heads(dot_tn(grad_scores, k2)) * SCALE).astype(BF16)
    return grad_q, grad_k, grad_v


def self_valid(seg_row, seg_col):
    length = seg_row.shape[-1]
    key = lax.broadcasted_iota(jnp.int32, (length, length), 0)
    tok = lax.broadcasted_iota(jnp.int32, (length, length), 1)
    one = (key <= tok) & (seg_row == seg_col)
    return jnp.concatenate((one, one), axis=1)


def self_fwd_kernel(seg_row, seg_col, q_ref, k_ref, v_ref, o_ref, lse_ref):
    valid = self_valid(seg_row[0], seg_col[0])
    for h in range(PAIRS):
        cut = slice(128 * h, 128 * h + 128)
        mixed, lse = pair_forward(q_ref[:, cut], k_ref[:, cut], v_ref[:, cut], valid)
        o_ref[:, cut] = mixed
        lse_ref[0, h : h + 1, :] = lse


def self_bwd_kernel(seg_row, seg_col, q_ref, k_ref, v_ref, do_ref, lse_ref, dq_ref, dk_ref, dv_ref):
    valid = self_valid(seg_row[0], seg_col[0])
    for h in range(PAIRS):
        cut = slice(128 * h, 128 * h + 128)
        gq, gk, gv = pair_backward(
            q_ref[:, cut], k_ref[:, cut], v_ref[:, cut], do_ref[:, cut],
            lse_ref[0, h : h + 1, :], valid,
        )
        dq_ref[:, cut] = gq
        dk_ref[:, cut] = gk
        dv_ref[:, cut] = gv


def self_specs(row_len):
    seg = [
        pl.BlockSpec((1, 1, row_len), lambda r: (r, 0, 0)),
        pl.BlockSpec((1, row_len, 1), lambda r: (r, 0, 0)),
    ]
    row = pl.BlockSpec((row_len, D), lambda r: (r, 0))
    lse = pl.BlockSpec((1, PAIRS, 2 * row_len), lambda r: (r, 0, 0))
    return seg, row, lse


def self_forward(seg, queries, keys, values):
    rows, row_len = seg.shape
    seg_specs, row, lse = self_specs(row_len)
    return pl.pallas_call(
        self_fwd_kernel,
        grid=(rows,),
        in_specs=seg_specs + [row] * 3,
        out_specs=[row, lse],
        out_shape=[
            jax.ShapeDtypeStruct(queries.shape, BF16),
            jax.ShapeDtypeStruct((rows, PAIRS, 2 * row_len), F32),
        ],
        cost_estimate=pl.CostEstimate(flops=rows * 2 * 10**8, bytes_accessed=2 * 10**6, transcendentals=rows * 3 * 10**5),
        name="self_forward",
    )(seg[:, None, :], seg[:, :, None], queries, keys, values)


def self_backward(seg, queries, keys, values, grad_mixed, lse_rows):
    rows, row_len = seg.shape
    seg_specs, row, lse = self_specs(row_len)
    return pl.pallas_call(
        self_bwd_kernel,
        grid=(rows,),
        in_specs=seg_specs + [row] * 4 + [lse],
        out_specs=[row] * 3,
        out_shape=[jax.ShapeDtypeStruct(queries.shape, BF16)] * 3,
        cost_estimate=pl.CostEstimate(flops=rows * 5 * 10**8, bytes_accessed=4 * 10**6, transcendentals=rows * 3 * 10**5),
        name="self_backward",
    )(seg[:, None, :], seg[:, :, None], queries, keys, values, grad_mixed, lse_rows)


def cross_fwd_kernel(map_ref, len_ref, seg_row, seg_col, q_ref, k_ref, v_ref, o_ref, lse_ref):
    r, page = pl.program_id(0), pl.program_id(1)
    keys, toks = k_ref.shape[1], q_ref.shape[0]
    valid = lax.broadcasted_iota(jnp.int32, (keys, 2 * toks), 0) < len_ref[r * 2 + page]
    mine_col = (seg_col[0] == page) | (page == 0)
    mine_row = (seg_row[0] == page) | (page == 0)
    mine_row = jnp.concatenate((mine_row, mine_row), axis=1)
    for h in range(PAIRS):
        cut = slice(128 * h, 128 * h + 128)
        mixed, lse = pair_forward(q_ref[:, cut], k_ref[0, :, cut], v_ref[0, :, cut], valid)
        o_ref[:, cut] = jnp.where(mine_col, mixed, o_ref[:, cut])
        lse_ref[0, h : h + 1, :] = jnp.where(mine_row, lse, lse_ref[0, h : h + 1, :])


def cross_bwd_kernel(
    map_ref, len_ref, seg_row, seg_col, q_ref, k_ref, v_ref, do_ref, lse_ref, dq_ref, dk_ref, dv_ref
):
    r, page = pl.program_id(0), pl.program_id(1)
    keys, toks = k_ref.shape[1], q_ref.shape[0]
    valid = lax.broadcasted_iota(jnp.int32, (keys, 2 * toks), 0) < len_ref[r * 2 + page]
    mine_col = (seg_col[0] == page) | (page == 0)
    mine_row = seg_row[0] == page
    mine_row = jnp.concatenate((mine_row, mine_row), axis=1)
    for h in range(PAIRS):
        cut = slice(128 * h, 128 * h + 128)
        lse = jnp.where(mine_row, lse_ref[0, h : h + 1, :], -NEG_FILL)
        gq, gk, gv = pair_backward(
            q_ref[:, cut], k_ref[0, :, cut], v_ref[0, :, cut], do_ref[:, cut], lse, valid
        )
        dq_ref[:, cut] = jnp.where(mine_col, gq, dq_ref[:, cut])
        dk_ref[0, :, cut] = gk
        dv_ref[0, :, cut] = gv


def cross_specs(row_len, mem_len):
    seg = [
        pl.BlockSpec((1, 1, row_len), lambda r, p, *_: (r, 0, 0)),
        pl.BlockSpec((1, row_len, 1), lambda r, p, *_: (r, 0, 0)),
    ]
    row = pl.BlockSpec((row_len, D), lambda r, p, *_: (r, 0))
    mem = pl.BlockSpec((1, mem_len, D), lambda r, p, mp, ln: (mp[r * 2 + p], 0, 0))
    lse = pl.BlockSpec((1, PAIRS, 2 * row_len), lambda r, p, *_: (r, 0, 0))
    return seg, row, mem, lse


CROSS_PARAMS = pltpu.CompilerParams(
    dimension_semantics=("arbitrary", "arbitrary"), vmem_limit_bytes=40 * 2**20
)


def cross_forward(local_map, lengths, seg, queries, keys, values):
    rows, row_len = seg.shape
    mem_len = keys.shape[1]
    seg_specs, row, mem, lse = cross_specs(row_len, mem_len)
    return pl.pallas_call(
        cross_fwd_kernel,
        grid_spec=pltpu.PrefetchScalarGridSpec(
            num_scalar_prefetch=2,
            grid=(rows, 2),
            in_specs=seg_specs + [row, mem, mem],
            out_specs=[row, lse],
        ),
        out_shape=[
            jax.ShapeDtypeStruct(queries.shape, BF16),
            jax.ShapeDtypeStruct((rows, PAIRS, 2 * row_len), F32),
        ],
        compiler_params=CROSS_PARAMS,
        cost_estimate=pl.CostEstimate(flops=5 * 10**9, bytes_accessed=11 * 10**6, transcendentals=5 * 10**6),
        name="cross_forward",
    )(local_map, lengths, seg[:, None, :], seg[:, :, None], queries, keys, values)


def cross_backward(local_map, lengths, seg, queries, keys, values, grad_mixed, lse_rows):
    rows, row_len = seg.shape
    mem_len = keys.shape[1]
    seg_specs, row, mem, lse = cross_specs(row_len, mem_len)
    return pl.pallas_call(
        cross_bwd_kernel,
        grid_spec=pltpu.PrefetchScalarGridSpec(
            num_scalar_prefetch=2,
            grid=(rows, 2),
            in_specs=seg_specs + [row, mem, mem, row, lse],
            out_specs=[row, mem, mem],
        ),
        out_shape=[
            jax.ShapeDtypeStruct(queries.shape, BF16),
            jax.ShapeDtypeStruct(keys.shape, BF16),
            jax.ShapeDtypeStruct(values.shape, BF16),
        ],
        compiler_params=CROSS_PARAMS,
        cost_estimate=pl.CostEstimate(flops=12 * 10**9, bytes_accessed=22 * 10**6, transcendentals=5 * 10**6),
        name="cross_backward",
    )(local_map, lengths, seg[:, None, :], seg[:, :, None], queries, keys, values, grad_mixed, lse_rows)


SMALL_ROWS = 16


def tie(values, *after):
    return lax.optimization_barrier((values, after))[0]


class Clock:
    def __init__(self):
        self.last = ()

    def now(self, values):
        return tie(values, *self.last) if self.last else values

    def tick(self, *arrays):
        self.last = arrays


class Grid:
    def __init__(self, wide, narrow):
        self.wide, self.narrow, self.ring = wide, narrow, wide // 2
        self.devices = wide * narrow
        moves = {
            "z": lambda w, n: ((w + 2) % wide, n),
            "x": lambda w, n: (w ^ 1, n),
            "y": lambda w, n: (w, n ^ 2),
            "c": lambda w, n: (w, n ^ 1),
        }
        self.perms = {}
        for name, move in moves.items():
            pairs = []
            for w in range(wide):
                for n in range(narrow):
                    w2, n2 = move(w, n)
                    pairs.append((w * narrow + n, w2 * narrow + n2))
            self.perms[name] = pairs
        self.clock = Clock()

    def send(self, name, array):
        return lax.ppermute(self.clock.now(array), AXES, self.perms[name])


CHEAP = pl.CostEstimate(flops=10**6, bytes_accessed=10**5, transcendentals=0)
BIG_VMEM = pltpu.CompilerParams(vmem_limit_bytes=48 * 2**20)


def half_kernel(labels, ring, wide, g, rows, place, *refs):
    n = len(labels)
    pieces, (out, sems) = refs[:n], refs[n:]
    z, x, y = place[0], place[1], place[2]
    height = wide * rows
    copies = []

    def copy(src, dst):
        copies.append(pltpu.make_async_copy(src, dst, sems.at[len(copies)]))

    for piece, piece_labels in zip(pieces, labels):
        for i, (dz, dx, dy) in enumerate(piece_labels):
            row = 2 * lax.rem(z + (ring - dz), ring) + (x + dx - 2 * x * dx)
            col = y + dy - 2 * y * dy
            for k in range(g):
                first = pl.multiple_of(row * rows, 16)
                copy(piece.at[i, pl.ds(k * rows, rows)], out.at[col, pl.ds(k * height + first, rows)])
            if piece.shape[1] > g * rows:
                first = pl.multiple_of(g * height + row * SMALL_ROWS, 16)
                copy(piece.at[i, pl.ds(g * rows, SMALL_ROWS)], out.at[col, pl.ds(first, SMALL_ROWS)])
    for one in copies:
        one.start()
    for one in copies:
        one.wait()


def anywhere(count):
    return [pl.BlockSpec(memory_space=pl.ANY)] * count


PLACE = pl.BlockSpec(memory_space=pltpu.SMEM)


class Gather:
    def __init__(self, grid, place, shard, g, small=False):
        self.grid, self.place, self.g, self.small, self.shard = grid, place, g, small, shard
        self.rows = (shard.shape[0] - (SMALL_ROWS if small else 0)) // g
        self.parts = [([(0, 0, 0)], shard[None])]

    def set_ring(self, arrays):
        labels = self.parts[0][0]
        self.parts = [([(step, dx, dy) for _, dx, dy in labels], a) for step, a in enumerate(arrays)]

    def join(self):
        labels = [l for ls, _ in self.parts for l in ls]
        self.parts = [(labels, jnp.concatenate([a for _, a in self.parts], axis=0))]
        return self.parts[0][1]

    def array(self):
        return self.parts[0][1]

    def pairs(self):
        labels, array = self.parts[0]
        self.from_x, self.from_y = self.grid.send("x", array), self.grid.send("y", array)
        self.parts.append(([(dz, 1, dy) for dz, _, dy in labels], self.from_x))
        self.parts.append(([(dz, dx, 1) for dz, dx, _ in labels], self.from_y))
        return self.from_x, self.from_y

    def corner(self):
        labels, array = self.parts[0]
        cut = self.corner_cut(array.shape[1])
        over_x = self.grid.send("x", self.from_y[:, :cut])
        over_y = self.grid.send("y", self.from_x[:, cut:])
        self.corner_parts = ([(dz, 1, 1) for dz, _, _ in labels], cut, over_x, over_y)
        return over_x, over_y

    def corner_cut(self, height):
        return height // 32 * 16

    def close(self):
        labels, cut, over_x, over_y = self.corner_parts
        self.parts.append((labels, jnp.concatenate((over_x, over_y), axis=1)))

    def half(self):
        grid, g, rows = self.grid, self.g, self.rows
        height, cols = self.shard.shape
        n = (g + (height > g * rows)) * grid.devices // 2
        self.own = pl.pallas_call(
            functools.partial(half_kernel, [l for l, _ in self.parts], grid.ring, grid.wide, g, rows),
            in_specs=[PLACE] + anywhere(len(self.parts)),
            out_specs=pl.BlockSpec(memory_space=pltpu.VMEM),
            out_shape=jax.ShapeDtypeStruct((2, grid.wide * height, cols), self.shard.dtype),
            scratch_shapes=[pltpu.SemaphoreType.DMA((n,))],
            compiler_params=BIG_VMEM,
            cost_estimate=CHEAP,
            name="half_weights",
        )(self.place, *[array for _, array in self.parts])
        return self.own

    def swap(self):
        self.other = self.grid.send("c", self.own)
        return self.other

    def small_rows(self):
        own, other = (a[:, self.g * self.grid.wide * self.rows :] for a in (self.own, self.other))
        both = jnp.where(self.place[3] == 0, jnp.stack((own, other)), jnp.stack((other, own)))
        both = both.reshape(2, 2, self.grid.wide, -1)
        return both.transpose(2, 1, 0, 3).reshape(self.grid.devices, -1)


def corners(place):
    y, c = place[2], place[3]
    return (2 * y + 1 - c, 2 * (1 - y) + 1 - c), (2 * y + c, 2 * (1 - y) + c)


def column(ref, n, cols):
    return ref[:, pl.ds(pl.multiple_of(n * cols, 128), cols)]


def far_kernel(place, *refs):
    out = refs[-1]
    cols = out.shape[-1]
    for i in range(out.shape[0]):
        a, d = refs[2 * i], refs[2 * i + 1]
        for j, n in enumerate(corners(place)[0]):
            out[i, j] = dot_tn(a[...], column(d, n, cols)).astype(BF16)


def put_quadrants(x, scratch, k, i, here, outs):
    dx, dy, qx, qy, own = outs
    rows = own.shape[2]
    if here:
        own[i, k] = scratch[k, x]
        qx[i, k] = scratch[k, 1 - x]
    else:
        qy[i, k] = scratch[k, x]
        dx[i, k] = scratch[k, 1 - x, pl.ds(0, rows // 2)].astype(BF16)
        dy[i, k] = scratch[k, 1 - x, pl.ds(rows // 2, rows // 2)].astype(BF16)


def near_kernel(place, *refs):
    from_c, *outs, scratch = refs[-7:]
    units, zs, rows, cols = outs[-1].shape
    for i in range(units):
        a, d = refs[2 * i], refs[2 * i + 1]
        for j, n in enumerate(corners(place)[1]):
            term = dot_tn(a[...], column(d, n, cols)) + from_c[i, j].astype(F32)
            scratch[...] = term.reshape(scratch.shape)
            for k in range(zs):
                put_quadrants(place[1], scratch, k, i, j == 0, outs)


def quadrant_shapes(units, ring, rows, cols):
    return [jax.ShapeDtypeStruct((units, ring, rows // 2, cols), BF16)] * 2 + [
        jax.ShapeDtypeStruct((units, ring, rows, cols), F32)
    ] * 3


def quadrant_specs(units, zs, rows, cols, stepped):
    def at(s, *_):
        return (0, s if stepped else 0, 0, 0)

    half = pl.BlockSpec((units, zs, rows // 2, cols), at)
    full = pl.BlockSpec((units, zs, rows, cols), at)
    return [half] * 2 + [full] * 3


def token_terms(grid, place, pairs, rows, cols, from_c=None):
    units, tokens = len(pairs), pairs[0][0].shape[0]
    height = grid.wide * rows
    zs = max(1, 128 // (2 * rows))
    if 2 * rows >= 128 and height // (2 * rows) > 1 and rows * cols <= 128 * 256:
        zs = min(grid.ring, 2)
    tall = zs * 2 * rows
    in_specs, args = [], []
    for a, d in pairs:
        in_specs += [
            pl.BlockSpec((tokens, tall), lambda s, *_: (0, s)),
            pl.BlockSpec(d.shape, lambda s, *_: (0, 0)),
        ]
        args += [a, d]
    block = pl.BlockSpec((units, 2, tall, cols), lambda s, *_: (0, 0, s, 0))
    scratch = []
    if from_c is None:
        kernel, out_specs = far_kernel, block
        out_shape = jax.ShapeDtypeStruct((units, 2, height, cols), BF16)
    else:
        in_specs.append(block)
        args.append(from_c)
        kernel = near_kernel
        out_specs = quadrant_specs(units, zs, rows, cols, True)
        out_shape = quadrant_shapes(units, grid.ring, rows, cols)
        scratch = [pltpu.VMEM((zs, 2, rows, cols), F32)]
    return pl.pallas_call(
        kernel,
        grid_spec=pltpu.PrefetchScalarGridSpec(
            num_scalar_prefetch=1,
            grid=(height // tall,),
            in_specs=in_specs,
            out_specs=out_specs,
            scratch_shapes=scratch,
        ),
        out_shape=out_shape,
        compiler_params=BIG_VMEM,
        cost_estimate=CHEAP,
        name="weight_terms",
    )(place, *args)


def memory_terms_kernel(near, place, mem, *refs):
    if near:
        *ds, from_c, dx, dy, qx, qy, own, acc = refs
    else:
        *ds, out, acc = refs
    cols = acc.shape[-1]
    m = pl.program_id(0)

    @pl.when(m == 0)
    def _():
        acc[...] = from_c[...].astype(F32).reshape(acc.shape) if near else jnp.zeros_like(acc)

    for i, d in enumerate(ds):
        for j, n in enumerate(corners(place)[1 if near else 0]):
            term = dot_tn(mem[0], d[0, :, pl.ds(pl.multiple_of(n * cols, 128), cols)])
            acc[i, j] += term.reshape(acc.shape[2:])

    @pl.when(m == pl.num_programs(0) - 1)
    def _():
        if near:
            x = place[1]
            zs, rows = own.shape[1], own.shape[2]
            for i in range(len(ds)):
                for j in range(2):
                    for k in range(zs):
                        put_quadrants(x, acc.at[i, j], k, i, j == 0, (dx, dy, qx, qy, own))
        else:
            out[...] = acc[...].reshape(out.shape).astype(BF16)


def memory_terms(grid, place, memory, grads, rows, cols, from_c=None):
    units, (mems, length, wide_cols) = len(grads), memory.shape
    height = grid.wide * rows
    near = from_c is not None
    one = pl.BlockSpec((1, length, wide_cols), lambda m, *_: (m, 0, 0))
    term = pl.BlockSpec((units, 2, height, cols), lambda m, *_: (0, 0, 0, 0))
    return pl.pallas_call(
        functools.partial(memory_terms_kernel, near),
        grid_spec=pltpu.PrefetchScalarGridSpec(
            num_scalar_prefetch=1,
            grid=(mems,),
            in_specs=[one] * (1 + units) + ([term] if near else []),
            out_specs=quadrant_specs(units, grid.ring, rows, cols, False) if near else term,
            scratch_shapes=[pltpu.VMEM((units, 2, grid.ring, 2, rows, cols), F32)],
        ),
        out_shape=quadrant_shapes(units, grid.ring, rows, cols)
        if near
        else jax.ShapeDtypeStruct((units, 2, height, cols), BF16),
        compiler_params=BIG_VMEM,
        cost_estimate=CHEAP,
        name="memory_terms",
    )(place, memory, *grads, *([from_c] if near else []))


def add_corners_kernel(qx, qy, from_x, from_y, sx, sy):
    half = from_x.shape[2]
    first, second = pl.ds(0, half), pl.ds(half, half)
    sx[0, 0, first] = qx[0, 0, first].astype(BF16)
    sx[0, 0, second] = (qx[0, 0, second] + from_y[0, 0].astype(F32)).astype(BF16)
    sy[0, 0, first] = (qy[0, 0, first] + from_x[0, 0].astype(F32)).astype(BF16)
    sy[0, 0, second] = qy[0, 0, second].astype(BF16)


def add_corners(qx, qy, from_x, from_y):
    units, ring, rows, cols = qx.shape
    full = pl.BlockSpec((1, 1, rows, cols), lambda i, k: (i, k, 0, 0))
    half = pl.BlockSpec((1, 1, rows // 2, cols), lambda i, k: (i, k, 0, 0))
    return pl.pallas_call(
        add_corners_kernel,
        grid=(units, ring),
        in_specs=[full, full, half, half],
        out_specs=[full, full],
        out_shape=[jax.ShapeDtypeStruct(qx.shape, BF16)] * 2,
        compiler_params=BIG_VMEM,
        cost_estimate=CHEAP,
        name="add_corners",
    )(qx, qy, from_x, from_y)


class Reduce:
    def __init__(self, grid, place, terms, rows):
        self.grid, self.place, self.terms, self.rows = grid, place, terms, rows

    def far(self):
        self.out = self.terms(None)
        return self.out

    def swap(self):
        self.from_c = self.grid.send("c", self.out)
        return self.from_c

    def near(self):
        self.dx, self.dy, self.qx, self.qy, self.own = self.terms(self.grid.clock.now(self.from_c))
        return self.dx

    def across(self):
        self.from_x, self.from_y = self.grid.send("x", self.dx), self.grid.send("y", self.dy)
        return self.from_x, self.from_y

    def add(self):
        from_x = self.grid.clock.now(self.from_x)
        self.sx, self.sy = add_corners(self.qx, self.qy, from_x, self.from_y)
        return self.sx

    def pairs(self):
        self.back_x, self.back_y = self.grid.send("x", self.sx), self.grid.send("y", self.sy)
        return self.back_x, self.back_y

    def chunk(self, step):
        index = lax.rem(self.place[0] + (self.grid.ring - step), self.grid.ring)
        parts = [
            lax.dynamic_index_in_dim(a, index, 1, keepdims=False) for a in (self.own, self.back_x, self.back_y)
        ]
        return parts[0] + parts[1].astype(F32) + parts[2].astype(F32)


class RingSum:
    def __init__(self, grid, reduces):
        self.grid, self.reduces, self.done, self.came = grid, reduces, 0, None

    def step(self):
        self.done += 1
        total = jnp.concatenate([r.chunk(self.done % self.grid.ring) for r in self.reduces], axis=0)
        if self.came is not None:
            total = total + self.came.astype(F32)
        if self.done == self.grid.ring:
            self.came = total
        else:
            self.came = self.grid.send("z", total.astype(BF16))
        return self.came


class SmallSum:
    def __init__(self, grid, place, terms):
        self.grid, self.place, self.done = grid, place, 0
        self.mine = terms.reshape(grid.ring, 2, 2, 2, -1)

    def step(self):
        grid, place = self.grid, self.place
        if self.done < 3:
            name, axis, at = ("c", "y", "x")[self.done], 3 - self.done, place[3 - self.done]
            far = lax.dynamic_index_in_dim(self.mine, 1 - at, axis, keepdims=False)
            near = lax.dynamic_index_in_dim(self.mine, at, axis, keepdims=False)
            self.mine = near + grid.send(name, far)
        else:
            index = lax.rem(place[0] + (grid.ring - (self.done - 2)), grid.ring)
            total = lax.dynamic_index_in_dim(self.mine, index, 0, keepdims=False)
            self.came = grid.send("z", total if self.done == 3 else total + self.came)
        self.done += 1
        return self.mine if self.done <= 3 else self.came

    def result(self):
        return lax.dynamic_index_in_dim(self.mine, self.place[0], 0, keepdims=False) + self.came


def halves(place, own, other):
    c = place[3]
    return [(2 * y + core, y, half) for half, core in ((own, c), (other, 1 - c)) for y in range(2)]


def at_block(n, cols):
    return pl.ds(pl.multiple_of(n * cols, 128), cols)


def times_t(place, d, own, other):
    cols = own.shape[-1]
    return sum(dot_nt(d[:, at_block(n, cols)], half[y]) for n, y, half in halves(place, own, other))


def norm_parts(values):
    centre = values - jnp.mean(values, axis=-1, keepdims=True)
    scale = lax.rsqrt(jnp.mean(centre * centre, axis=-1, keepdims=True) + EPSILON)
    return centre * scale, scale


def norm_back(normed, scale, gain, grad):
    inner = grad * gain
    back = scale * (
        inner
        - jnp.mean(inner, axis=-1, keepdims=True)
        - normed * jnp.mean(inner * normed, axis=-1, keepdims=True)
    )
    return back, jnp.sum(grad * normed, axis=0, keepdims=True), jnp.sum(grad, axis=0, keepdims=True)


def column_sum(values):
    return jnp.sum(values.astype(F32), axis=0, keepdims=True)


GAIN, BIAS = 0, 3


def row(vectors, i):
    return vectors[i : i + 1, :]


def memory_kernel(place, mem, vectors, k_own, k_other, v_own, v_other, keys, values):
    cols = k_own.shape[-1]
    for n, y, half in halves(place, k_own, k_other):
        keys[0, :, at_block(n, cols)] = dot_nn(mem[0], half[y]).astype(BF16)
    for n, y, half in halves(place, v_own, v_other):
        bias = vectors[BIAS + 6 : BIAS + 7, at_block(n, cols)]
        values[0, :, at_block(n, cols)] = (dot_nn(mem[0], half[y]) + bias).astype(BF16)


def qkv_kernel(place, tokens, vectors, *refs):
    weights, (normed, q, k, v) = refs[:6], refs[6:]
    n, _ = norm_parts(tokens[...].astype(F32))
    normed[...] = (n * row(vectors, GAIN) + row(vectors, BIAS)).astype(BF16)
    cols = weights[0].shape[-1]
    for i, (out, bias_at) in enumerate(((q, 1), (k, None), (v, 2))):
        for n, y, half in halves(place, weights[2 * i], weights[2 * i + 1]):
            term = dot_nn(normed[...], half[y])
            if bias_at is not None:
                term = term + vectors[BIAS + bias_at : BIAS + bias_at + 1, at_block(n, cols)]
            out[:, at_block(n, cols)] = term.astype(BF16)


def middle_kernel(place, tokens, mixed, vectors, so_own, so_other, cq_own, cq_other, after, normed, queries):
    cols = so_own.shape[-1]
    for n, y, half in halves(place, so_own, so_other):
        at = at_block(n, cols)
        after[:, at] = tokens[:, at].astype(F32) + dot_nn(mixed[...], half[y]) + vectors[BIAS + 3 : BIAS + 4, at]
    n, _ = norm_parts(after[...])
    normed[...] = (n * row(vectors, GAIN + 1) + row(vectors, BIAS + 4)).astype(BF16)
    for n, y, half in halves(place, cq_own, cq_other):
        at = at_block(n, cols)
        queries[:, at] = (dot_nn(normed[...], half[y]) + vectors[BIAS + 5 : BIAS + 6, at]).astype(BF16)


def cross_out_kernel(place, before, mixed, vectors, own, other, after, normed):
    cols = own.shape[-1]
    for n, y, half in halves(place, own, other):
        at = at_block(n, cols)
        after[:, at] = before[:, at] + dot_nn(mixed[...], half[y]) + vectors[BIAS + 7 : BIAS + 8, at]
    n, _ = norm_parts(after[...])
    normed[...] = (n * row(vectors, GAIN + 2) + row(vectors, BIAS + 8)).astype(BF16)


def up_kernel(place, normed, bias, own, other, act, slope):
    c = place[3]
    cols = own.shape[-1]

    def block(n, half):
        at = at_block(n, cols)
        u = dot_nn(normed[...], half[0]) + bias[:, at]
        below = 0.5 * (1.0 + lax.erf(u * (1.0 / math.sqrt(2.0))))
        act[:, at] = (u * below).astype(BF16)
        slope[:, at] = below + u * jnp.exp(-0.5 * u * u) * (1.0 / math.sqrt(2.0 * math.pi))

    y = pl.program_id(0)
    block(2 * y + c, own)
    block(2 * y + 1 - c, other)


def down_kernel(place, after, act, vectors, own, other, out):
    c, y = place[3], pl.program_id(0)
    cols = own.shape[-1]
    for n, half in ((2 * y + c, own), (2 * y + 1 - c, other)):
        at = at_block(n, cols)
        total = after[:, at] + dot_nn(act[...], half[0]) + vectors[BIAS + 9 : BIAS + 10, at]
        out[:, at] = total.astype(BF16)


def down_back_kernel(place, grad, slope, own, other, grad_pre, bias_grad):
    back = (times_t(place, grad, own, other) * slope[...]).astype(BF16)
    grad_pre[...] = back
    bias_grad[...] = column_sum(back)


def up_back_kernel(
    place, grad_pre, grad_out, after, vectors, own, other, co_own, co_other,
    grad, branch, mixed, gain_grad, shift_grad, out_grad, last_grad, total,
):
    c, y = place[3], pl.program_id(0)
    cols = own.shape[-1]
    term = dot_nt(grad_pre[:, at_block(2 * y + c, cols)], own[0])
    term = term + dot_nt(grad_pre[:, at_block(2 * y + 1 - c, cols)], other[0])

    @pl.when(y == 0)
    def _():
        total[...] = term

    @pl.when(y == 1)
    def _():
        n, scale = norm_parts(after[...])
        back, gain_grad[...], shift_grad[...] = norm_back(n, scale, row(vectors, GAIN + 2), total[...] + term)
        out = grad_out[...].astype(F32) + back
        grad[...] = out
        branch[...] = out.astype(BF16)
        out_grad[...] = column_sum(branch[...])
        last_grad[...] = column_sum(grad_out[...])
        mixed[...] = times_t(place, branch, co_own, co_other).astype(BF16)


def middle_back_kernel(
    place, grad_queries, grad_after, after, vectors, cq_own, cq_other, so_own, so_other,
    grad, branch, mixed, gain_grad, shift_grad, out_grad, query_grad,
):
    n, scale = norm_parts(after[...])
    dense = times_t(place, grad_queries, cq_own, cq_other)
    back, gain_grad[...], shift_grad[...] = norm_back(n, scale, row(vectors, GAIN + 1), dense)
    out = grad_after[...] + back
    grad[...] = out
    branch[...] = out.astype(BF16)
    out_grad[...] = column_sum(branch[...])
    query_grad[...] = column_sum(grad_queries[...])
    mixed[...] = times_t(place, branch, so_own, so_other).astype(BF16)


def first_back_kernel(place, tokens, grad_after, gq, gk, gv, vectors, *refs):
    weights, (grad, gain_grad, shift_grad, query_grad, value_grad) = refs[:6], refs[6:]
    n, scale = norm_parts(tokens[...].astype(F32))
    dense = sum(
        times_t(place, d, weights[2 * i], weights[2 * i + 1]) for i, d in enumerate((gq, gk, gv))
    )
    back, gain_grad[...], shift_grad[...] = norm_back(n, scale, row(vectors, GAIN), dense)
    grad[...] = (grad_after[...] + back).astype(BF16)
    query_grad[...] = column_sum(gq[...])
    value_grad[...] = column_sum(gv[...])


def memory_back_kernel(place, gk, gv, k_own, k_other, v_own, v_other, grad, value_grad):
    total = times_t(place, gk.at[0], k_own, k_other) + times_t(place, gv.at[0], v_own, v_other)
    grad[0] = total.astype(BF16)

    @pl.when(pl.program_id(0) == 0)
    def _():
        value_grad[...] = jnp.zeros_like(value_grad)

    value_grad[...] += column_sum(gv[0])


def dense_call(kernel, name, place, ins, outs, grid=(1,), scratch=()):
    def spec(array, block, index):
        block = block or array.shape
        zeros = (0,) * len(block)
        return pl.BlockSpec(block, index or (lambda *_: zeros))

    return pl.pallas_call(
        kernel,
        grid_spec=pltpu.PrefetchScalarGridSpec(
            num_scalar_prefetch=1,
            grid=grid,
            in_specs=[spec(*one) for one in ins],
            out_specs=[spec(*one) for one in outs],
            scratch_shapes=scratch,
        ),
        out_shape=[one[0] for one in outs],
        compiler_params=BIG_VMEM,
        cost_estimate=CHEAP,
        name=name,
    )(place, *[one[0] for one in ins])


def full(array):
    return (array, None, None)


def result(shape, dtype):
    return (jax.ShapeDtypeStruct(shape, dtype), None, None)


def matrix(gathered, i, height=D):
    block = (2, height, gathered.own.shape[-1])
    return [(half, block, lambda *_: (0, i, 0)) for half in (gathered.own, gathered.other)]


def by_y(gathered):
    block = (1,) + gathered.own.shape[1:]
    return [(half, block, lambda y, *_: (y, 0, 0)) for half in (gathered.own, gathered.other)]


def by_rows(gathered, rows):
    block = (2, rows, gathered.own.shape[-1])
    return [(half, block, lambda s, *_: (0, s, 0)) for half in (gathered.own, gathered.other)]


def local(
    shape,
    tokens,
    memory,
    segment_ids,
    page_map,
    mem_lengths,
    gains,
    biases,
    fc1_bias,
    self_qkv,
    self_out,
    cross_q,
    cross_kv,
    cross_out,
    fc1,
    fc2,
    cotangent,
):
    grid = Grid(*shape)
    wide_at, narrow_at = lax.axis_index("wide"), lax.axis_index("narrow")
    place = jnp.stack((wide_at // 2, wide_at % 2, narrow_at // 2, narrow_at % 2)).astype(jnp.int32)
    devices = grid.devices
    mem_count, token_count = memory.shape[0], tokens.shape[0]
    rows, cols = self_out.shape

    small = jnp.concatenate((gains.reshape(-1), biases.reshape(-1), fc1_bias))
    small = jnp.pad(small, (0, SMALL_ROWS * cols - small.size)).reshape(SMALL_ROWS, cols)
    n_gain, n_bias, n_fc1 = gains.size, biases.size, fc1_bias.size
    gather = functools.partial(Gather, grid, place)
    g_ckv = gather(jnp.concatenate((cross_kv[0], cross_kv[1], small), axis=0), 2, True)
    g_qkv = gather(self_qkv.reshape(3 * rows, cols), 3)
    g_mix = gather(jnp.concatenate((self_out, cross_q, cross_out), axis=0), 3)
    g_fc1 = gather(fc1, 1)
    g_fc2 = gather(fc2, 1)
    send, clock = grid.send, grid.clock
    now, tick = clock.now, clock.tick
    steps = grid.ring - 1

    ring_ckv = [g_ckv.array()]
    ring_ckv.append(send("z", ring_ckv[-1]))
    tick(ring_ckv[-1], *g_fc2.pairs())
    ring_ckv.append(send("z", ring_ckv[-1]))
    tick(ring_ckv[-1], *g_fc2.corner())
    for _ in range(steps - 2):
        ring_ckv.append(send("z", ring_ckv[-1]))
        tick(ring_ckv[-1])
    g_fc2.close()
    fc2_all = g_fc2.join()
    fc2_cut = fc2_all.shape[1] // 2
    g_ckv.set_ring(ring_ckv)
    g_ckv.join()

    ring_two = [jnp.concatenate((g_qkv.array(), g_mix.array()), axis=1)]
    ring_two.append(send("z", ring_two[-1]))
    tick(ring_two[-1], *g_ckv.pairs())
    ring_two.append(send("z", ring_two[-1]))
    tick(ring_two[-1], *g_ckv.corner())
    g_ckv.close()
    for _ in range(steps - 2):
        ring_two.append(send("z", ring_two[-1]))
        tick(ring_two[-1], g_ckv.half())
    cut = 3 * rows
    g_qkv.set_ring([a[:, :cut] for a in ring_two])
    g_mix.set_ring([a[:, cut:] for a in ring_two])
    g_qkv.join()
    g_mix.join()

    ring_fc1 = [g_fc1.array()]
    for _ in range(steps - 1):
        ring_fc1.append(send("z", ring_fc1[-1]))
    tick(ring_fc1[-1], g_ckv.swap(), *g_qkv.pairs())

    ring_fc1.append(send("z", ring_fc1[-1]))
    small_all = g_ckv.small_rows().astype(F32)
    vectors = small_all[:, : n_gain + n_bias].reshape(devices, 13, -1).transpose(1, 0, 2).reshape(13, D)
    up_bias = small_all[:, n_gain + n_bias : n_gain + n_bias + n_fc1].reshape(1, -1)
    mem_block = (1,) + memory.shape[1:]
    mem_shape = jax.ShapeDtypeStruct(memory.shape, BF16)

    def by_memory(array):
        return (array, mem_block, lambda m, *_: (m, 0, 0))

    mem_keys, mem_values = dense_call(
        memory_kernel, "memory_keys_values", place,
        [by_memory(now(memory)), full(vectors)] + matrix(g_ckv, 0) + matrix(g_ckv, 1),
        [by_memory(mem_shape), by_memory(mem_shape)], grid=(mem_count,),
    )
    tick(ring_fc1[-1], mem_keys, *g_qkv.corner())
    g_qkv.close()
    g_fc1.set_ring(ring_fc1)
    g_fc1.join()

    ring_a, ring_b = [fc2_all[:, :fc2_cut]], [fc2_all[:, fc2_cut:]]
    ring_a.append(send("z", ring_a[-1]))
    tick(ring_a[-1], g_qkv.half(), *g_mix.pairs())
    ring_b.append(send("z", ring_b[-1]))
    tick(g_qkv.swap(), ring_b[-1], *g_mix.corner())
    g_mix.close()

    ring_a.append(send("z", ring_a[-1]))
    ring_b.append(send("z", ring_b[-1]))
    wide_row = (token_count, D)
    normed_one, self_queries, self_keys, self_values = dense_call(
        qkv_kernel, "self_qkv", place,
        [full(now(tokens)), full(vectors)] + matrix(g_qkv, 0) + matrix(g_qkv, 1) + matrix(g_qkv, 2),
        [result(wide_row, BF16)] * 4,
    )
    self_mixed, self_lse = self_forward(segment_ids, self_queries, self_keys, self_values)
    g_mix.half()
    tick(ring_a[-1], ring_b[-1], self_mixed, g_mix.swap(), *g_fc1.pairs())

    for _ in range(steps - 2):
        ring_a.append(send("z", ring_a[-1]))
    after_self, normed_two, cross_queries = dense_call(
        middle_kernel, "self_out_cross_q", place,
        [full(tokens), full(now(self_mixed)), full(vectors)] + matrix(g_mix, 0) + matrix(g_mix, 1),
        [result(wide_row, F32), result(wide_row, BF16), result(wide_row, BF16)],
    )
    first_mem = lax.axis_index(AXES) * mem_count
    local_map = (page_map - first_mem).reshape(-1).astype(jnp.int32)
    picks = local_map[:, None] == jnp.arange(mem_count, dtype=jnp.int32)[None, :]
    row_lengths = jnp.sum(jnp.where(picks, mem_lengths[None, :], 0), axis=-1).astype(jnp.int32)
    cross_mixed, cross_lse = cross_forward(
        local_map, row_lengths, segment_ids, cross_queries, mem_keys, mem_values
    )
    tick(cross_mixed, ring_a[-1], *g_fc1.corner())
    g_fc1.close()
    after_cross, normed_three = dense_call(
        cross_out_kernel, "cross_out", place,
        [full(after_self), full(now(cross_mixed)), full(vectors)] + matrix(g_mix, 2),
        [result(wide_row, F32), result(wide_row, BF16)],
    )

    g_fc1.half()
    for _ in range(steps - 2):
        ring_b.append(send("z", ring_b[-1]))
    tick(g_fc1.swap(), normed_three, ring_b[-1])
    g_fc2.set_ring([jnp.concatenate(ab, axis=1) for ab in zip(ring_a, ring_b)])
    g_fc2.half()
    hidden = up_bias.shape[1]
    activated, slope = dense_call(
        up_kernel, "fc1_gelu", place,
        [full(now(normed_three)), full(up_bias)] + by_y(g_fc1),
        [result((token_count, hidden), BF16), result((token_count, hidden), F32)], grid=(2,),
    )
    tick(activated, g_fc2.swap())

    def settle(pairs, shard):
        part_rows, part_cols = shard.shape
        return Reduce(
            grid, place,
            lambda from_c: token_terms(grid, place, pairs, part_rows, part_cols, from_c),
            part_rows,
        )

    one_row = result((1, D), F32)
    r_fc2 = settle([(now(activated), cotangent)], fc2)
    tick(r_fc2.far())
    slab = hidden // 4
    some = lambda array: (array, (token_count, slab), lambda s, *_: (0, s))
    grad_pre, grad_up_bias = dense_call(
        down_back_kernel, "fc2_gelu_back", place,
        [full(now(cotangent)), some(slope)] + by_rows(g_fc2, slab),
        [
            some(jax.ShapeDtypeStruct((token_count, hidden), BF16)),
            (jax.ShapeDtypeStruct((1, hidden), F32), (1, slab), lambda s, *_: (0, s)),
        ],
        grid=(4,),
    )
    tick(r_fc2.swap(), grad_pre)
    grad_pre = now(grad_pre)
    r_fc1 = settle([(normed_three, grad_pre)], fc1)
    tick(r_fc2.near(), r_fc1.far())
    (
        grad_after_cross, grad_branch_two, grad_cross_mixed,
        grad_gain_three, grad_bias_eight, grad_bias_seven, grad_bias_nine,
    ) = dense_call(
        up_back_kernel, "fc1_norm_back", place,
        [full(now(grad_pre)), full(cotangent), full(after_cross), full(vectors)]
        + by_y(g_fc1) + matrix(g_mix, 2),
        [result(wide_row, F32), result(wide_row, BF16), result(wide_row, BF16)] + [one_row] * 4,
        grid=(2,), scratch=[pltpu.VMEM(wide_row, F32)],
    )
    tick(r_fc1.swap(), grad_cross_mixed, *r_fc2.across())
    tick(r_fc1.near(), r_fc2.add())

    grad_cq, grad_ck, grad_cv = cross_backward(
        local_map, row_lengths, segment_ids, cross_queries, mem_keys, mem_values,
        now(grad_cross_mixed), cross_lse,
    )
    tick(grad_cq, *r_fc2.pairs())
    ring_fc2 = RingSum(grid, [r_fc2])
    grad_cq = now(grad_cq)
    r_mem = Reduce(
        grid, place,
        lambda from_c: memory_terms(grid, place, memory, now((grad_ck, grad_cv)), rows, cols, from_c),
        rows,
    )
    r_cross = settle([(cross_mixed, grad_branch_two), (normed_two, grad_cq)], cross_q)
    tick(ring_fc2.step(), r_cross.far(), r_mem.far(), *r_fc1.across())
    tick(r_fc1.add())

    ring_fc2.step()
    (
        grad_after_self, grad_branch_one, grad_self_mixed,
        grad_gain_two, grad_bias_four, grad_bias_three, grad_bias_five,
    ) = dense_call(
        middle_back_kernel, "cross_q_norm_back", place,
        [full(now(grad_cq)), full(grad_after_cross), full(after_self), full(vectors)]
        + matrix(g_mix, 1) + matrix(g_mix, 0),
        [result(wide_row, F32), result(wide_row, BF16), result(wide_row, BF16)] + [one_row] * 4,
    )
    grad_sq, grad_sk, grad_sv = self_backward(
        segment_ids, self_queries, self_keys, self_values, grad_self_mixed, self_lse
    )
    r_self = settle(
        [(normed_one, grad_sq), (normed_one, grad_sk), (normed_one, grad_sv), (self_mixed, grad_branch_one)],
        cross_q,
    )
    tick(r_cross.swap(), r_mem.swap(), r_self.far(), ring_fc2.step(), *r_fc1.pairs())
    ring_fc2.step()
    ring_fc1 = RingSum(grid, [r_fc1])
    tick(r_cross.near(), r_mem.near())
    grad_tokens, grad_gain_one, grad_bias_zero, grad_bias_one, grad_bias_two = dense_call(
        first_back_kernel, "self_qkv_norm_back", place,
        [full(tokens), full(grad_after_self)] + [full(d) for d in now((grad_sq, grad_sk, grad_sv))]
        + [full(vectors)] + matrix(g_qkv, 0) + matrix(g_qkv, 1) + matrix(g_qkv, 2),
        [result(wide_row, BF16)] + [one_row] * 4,
    )
    tick(r_self.swap(), ring_fc1.step(), grad_tokens, *r_cross.across(), *r_mem.across())
    tick(r_cross.add(), r_mem.add(), r_self.near())
    ring_fc1.step()
    grad_memory, grad_bias_six = dense_call(
        memory_back_kernel, "memory_back", place,
        [by_memory(a) for a in now((grad_ck, grad_cv))] + matrix(g_ckv, 0) + matrix(g_ckv, 1),
        [by_memory(mem_shape), one_row], grid=(mem_count,),
    )
    tick(ring_fc1.step(), grad_memory, *r_cross.pairs(), *r_mem.pairs())
    ring_fc1.step()
    ring_cross = RingSum(grid, [r_cross, r_mem])

    def by_device(array):
        return array.reshape(array.shape[0], devices, -1).transpose(1, 0, 2).reshape(devices, -1)

    small_grads = jnp.concatenate(
        (
            by_device(
                jnp.concatenate(
                    (
                        grad_gain_one, grad_gain_two, grad_gain_three,
                        grad_bias_zero, grad_bias_one, grad_bias_two, grad_bias_three, grad_bias_four,
                        grad_bias_five, grad_bias_six, grad_bias_seven, grad_bias_eight, grad_bias_nine,
                    ),
                    axis=0,
                )
            ),
            by_device(grad_up_bias),
        ),
        axis=1,
    )
    small_sum = SmallSum(grid, place, now(small_grads))
    (layer_out,) = dense_call(
        down_kernel, "fc2", place,
        [full(after_cross), full(now(activated)), full(vectors)] + by_y(g_fc2),
        [result(wide_row, BF16)], grid=(2,),
    )
    tick(ring_cross.step(), layer_out, small_sum.step(), *r_self.across())
    tick(r_self.add())
    ring_cross.step()
    tick(ring_cross.step(), small_sum.step(), *r_self.pairs())
    for _ in range(steps - 3):
        ring_cross.step()
    ring_cross.step()
    ring_self = RingSum(grid, [r_self])
    for _ in range(steps):
        tick(ring_self.step(), small_sum.step())
    ring_self.step()
    while small_sum.done < steps + 3:
        tick(small_sum.step())
    for ring in (ring_fc2, ring_fc1):
        while ring.done < grid.ring:
            ring.step()
    small_shard = small_sum.result()
    came_cross, came_self = ring_cross.came, ring_self.came
    return (
        layer_out,
        grad_tokens,
        grad_memory,
        small_shard[:n_gain].reshape(gains.shape),
        small_shard[n_gain : n_gain + n_bias].reshape(biases.shape),
        small_shard[n_gain + n_bias :],
        came_self[:3],
        came_self[3],
        came_cross[1],
        came_cross[2:],
        came_cross[0],
        ring_fc1.came[0],
        ring_fc2.came[0],
    )


def solution(mesh):
    shape = (mesh.shape["wide"], mesh.shape["narrow"])
    in_specs = (
        P(AXES, None),
        P(AXES, None, None),
        P(AXES, None),
        P(AXES, None),
        P(AXES),
        P(None, AXES),
        P(None, AXES),
        P(AXES),
        P(None, "wide", "narrow"),
        P("wide", "narrow"),
        P("wide", "narrow"),
        P(None, "wide", "narrow"),
        P("wide", "narrow"),
        P("wide", "narrow"),
        P("wide", "narrow"),
        P(AXES, None),
    )
    out_specs = (
        P(AXES, None),
        P(AXES, None),
        P(AXES, None, None),
        P(None, AXES),
        P(None, AXES),
        P(AXES),
        P(None, "wide", "narrow"),
        P("wide", "narrow"),
        P("wide", "narrow"),
        P(None, "wide", "narrow"),
        P("wide", "narrow"),
        P("wide", "narrow"),
        P("wide", "narrow"),
    )
    return jax.shard_map(
        functools.partial(local, shape), mesh=mesh, in_specs=in_specs, out_specs=out_specs, check_vma=False
    )
```

time: 900 us -> 594 us (0.66)
  matrix products: 173 us -> 0 us
  Pallas kernels: 67.1 us -> 235 us
  waiting for transfers between devices: 320 us -> 160 us
  blocking collectives: 51.4 us -> 0 us
  local copies, waits for them, and re-layouts: 134 us -> 84.5 us
  other arithmetic: 73.6 us -> 42.8 us
  starting transfers between devices: 69.6 us -> 58.5 us
    dot_general x48 -> x0, matrix products: 173 us -> none  [the longest x32 95.7 us: term(): out = jnp.einsum(spec, a, cut, preferred_element_type=F32)]
    pallas_call x7 -> x31, Pallas kernels: 17 us -> 186 us  [the longest x11 85.2 us: dense_call(): pl.pallas_call(kernel, grid_spec=pltpu.PrefetchScalarGridSpec(num_scalar_...]
    ppermute x132 -> x83, waiting for transfers between devices: 320 us -> 160 us  [send(): return lax.ppermute(self.clock.now(array), AXES, self.perms[name])]
    unnamed x1 -> x0, blocking collectives: 51.4 us -> none
    dynamic_slice x19 -> x4, local copies, waits for them, and re-layouts: 36.6 us -> 0.17 us  [the longest x3 0.14 us: step(): near = lax.dynamic_index_in_dim(self.mine, at, axis, keepdims=False)]
    reshape x7, local copies, waits for them, and re-layouts: 21.3 us -> 2.3 us  [the longest x2 1.87 us: local(): small_all[:, :n_gain + n_bias].reshape(devices, 13, -1).transpose(1, 0, 2)]
    add x22 -> x11, other arithmetic: 23.1 us -> 7.14 us  [the longest x3 5.86 us: chunk(): return parts[0] + parts[1].astype(F32) + parts[2].astype(F32)]
    reduce_sum x14 -> x0, other arithmetic: 13.1 us -> none  [the longest x1 3.58 us: local(): grad_bias_nine = jnp.sum(grad_out, axis=0)]
  transfers between devices with their start and end apart: 132 -> 83, of which waited for: 55 -> 33; matrix products, arithmetic and copies ran while one was open for 30% -> 16% of each run, Pallas kernels for 4% -> 30%
where the time goes in v2:
time: 594 us; the launch traced here: 584 us
  Pallas kernels  235 us (40%)
  waiting for transfers between devices  160 us (27%)
  local copies, waits for them, and re-layouts  84.5 us (14%)
  starting transfers between devices  58.5 us (10%)
  other arithmetic  42.8 us (7%)
    ppermute x83, waiting for transfers between devices, send(): return lax.ppermute(self.clock.now(array), AXES, self.perms[name])  160 us
    pallas_call x11, Pallas kernels, dense_call(): pl.pallas_call(kernel, grid_spec=pltpu.PrefetchScalarGridSpec(num_scalar_...  85.2 us
    ppermute x83, starting transfers between devices, send(): return lax.ppermute(self.clock.now(array), AXES, self.perms[name])  58.5 us
    unnamed x175, local copies, waits for them, and re-layouts  43 us
    pallas_call x8, Pallas kernels, token_terms(): pl.pallas_call(kernel, grid_spec=pltpu.PrefetchScalarGridSpec(num_scalar_...  38 us
    pallas_call x2, Pallas kernels, memory_terms(): pl.pallas_call(functools.partial(memory_terms_kernel, near), grid_spec=pl...  24.1 us
    pallas_call x5, Pallas kernels, half(): pl.pallas_call(functools.partial(half_kernel, [l for l, _ in self.parts],...  23.5 us
    pallas_call x1, Pallas kernels, cross_backward(): pl.pallas_call(cross_bwd_kernel, grid_spec=pltpu.PrefetchScalarGridSpec(n...  21.2 us
  transfers between devices with their start and end apart: 83, of which 33 were waited for; matrix products, arithmetic and copies ran while one was open for 16% of the time, Pallas kernels for 30%

profile of v2, /device:TPU:0, one launch (start us, length us, event | category | flops | bytes accessed | tf_op | source)
XLA Modules:
  0.0 583.6 jit_solution(5659734736166738979)
XLA Ops:
  0.7 3.0 collective-permute-start.2
  10.0 5.3 collective-permute-done
  16.5 4.0 collective-permute-done.4
  23.1 6.0 %collective-permute-done.6 = bf16[1,272,256]{2,1,0:T(8,128)(2,1)S(1)} collective-permute-done((bf16[1,272,256]{2,1,0:T(8,128)(2,1)S(1)}, bf16[1,272,256]{2,1,0:T(8,128)(2,1)S(1)}, u32[]{:S(2)}, u32[]{:S(2)}) %collective-permute-start.6) | collective-permute-done | bytes 139296 | tf_op jit(solution)/shard_map/ppermute | solution.py:282
  30.9 10.8 %collective-permute-done.7 = bf16[1,768,256]{2,1,0:T(8,128)(2,1)S(1)} collective-permute-done((bf16[1,768,256]{2,1,0:T(8,128)(2,1)S(1)}, bf16[1,768,256]{2,1,0:T(8,128)(2,1)S(1)}, u32[]{:S(2)}, u32[]{:S(2)}) %collective-permute-start.7) | collective-permute-done | bytes 393248 | tf_op jit(solution)/shard_map/ppermute | solution.py:282
  44.9 5.3 collective-permute-done.11
  50.1 5.4 collective-permute-done.10
  56.8 4.5 half_weights.5.k_own.v_own
  61.3 4.1 collective-permute-done.13
  72.0 10.3 %collective-permute-done.16 = bf16[1,128,1024]{2,1,0:T(8,128)(2,1)} collective-permute-done((bf16[1,128,1024]{2,1,0:T(8,128)(2,1)S(1)}, bf16[1,128,1024]{2,1,0:T(8,128)(2,1)}, u32[]{:S(2)}, u32[]{:S(2)}) %collective-permute-start.16) | collective-permute-done | bytes 262176 | tf_op jit(solution)/shard_map/ppermute | solution.py:282
  86.2 2.2 pad_maximum_fusion.7.refs_0_
  88.5 2.4 collective-permute-done.15.refs_2_
  99.0 2.9 convert_bitcast_fusion
  108.5 6.1 %copy.100.mem = bf16[4,588,1024]{2,1,0:T(8,128)(2,1)} copy(bf16[4,588,1024]{2,0,1:T(4,128)(2,1)} %param.17) | data formatting | bytes 9633792 | tf_op jit(solution)/shard_map/optimization_barrier | solution.py:247
  114.6 15.4 %memory_keys_values.1 = (bf16[4,588,1024]{2,1,0:T(8,128)(2,1)}, bf16[4,588,1024]{2,1,0:T(8,128)(2,1)}) custom-call(s32[4]{0:T(128)S(1)} %pad_add_fusion.place, bf16[4,588,1024]{2,1,0:T(8,128)(2,1)} %copy.100.mem, f32[13,1024]{1,0:T(8,128)S(1)} %reshape.505.vectors, bf16[2,2176,256]{2,1,0:T(8,128)(2,1)S(1)} %half_weights.5.k_own.v_own, ...), custom_call_target="tpu_custom_call" | custom-call | flops 1000000 | bytes 100000 | tf_op jit(solution)/shard_map/memory_keys_values/pallas_call | solution.py:827
  133.8 4.3 half_weights.6.refs_0_.refs_2_.refs_4_
  138.1 8.9 %collective-permute-done.22 = bf16[4,256,256]{2,1,0:T(8,128)(2,1)} collective-permute-done((bf16[4,256,256]{2,1,0:T(8,128)(2,1)S(1)}, bf16[4,256,256]{2,1,0:T(8,128)(2,1)}, u32[]{:S(2)}, u32[]{:S(2)}) %collective-permute-start.22) | collective-permute-done | bytes 524320 | tf_op jit(solution)/shard_map/ppermute | solution.py:282
  152.6 8.3 %collective-permute-done.28 = bf16[4,192,256]{2,1,0:T(8,128)(2,1)S(1)} collective-permute-done((bf16[4,192,256]{2,1,0:T(8,128)(2,1)S(1)}, bf16[4,192,256]{2,1,0:T(8,128)(2,1)S(1)}, u32[]{:S(2)}, u32[]{:S(2)}) %collective-permute-start.28) | collective-permute-done | bytes 393248 | tf_op jit(solution)/shard_map/ppermute | solution.py:282
  162.3 7.2 %half_weights.7.so_own.cq_own.own.co_own = bf16[2,3072,256]{2,1,0:T(8,128)(2,1)} custom-call(s32[4]{0:T(128)S(1)} %pad_add_fusion.place, bf16[4,384,256]{2,1,0:T(8,128)(2,1)S(1)} %copy-done.25, bf16[4,384,256]{2,1,0:T(8,128)(2,1)S(1)} %collective-permute-done.23.refs_1_, bf16[4,384,256]{2,1,0:T(8,128)(2,1)S(1)} %collective-permute-done.24.refs_2_, ...), custom_call_target="tpu_custom_call" | custom-call | flops 1000000 | bytes 100000 | tf_op jit(solution)/shard_map/half_weights/pallas_call | solution.py:366
  169.6 2.3 pad_maximum_fusion.refs_0_
  177.5 4.7 self_qkv.1
  185.4 3.9 self_forward.1
  189.3 8.4 %collective-permute-done.32.refs_1_ = bf16[4,128,1024]{2,1,0:T(8,128)(2,1)} collective-permute-done((bf16[4,128,1024]{2,1,0:T(8,128)(2,1)}, bf16[4,128,1024]{2,1,0:T(8,128)(2,1)}, u32[]{:S(2)}, u32[]{:S(2)}) %collective-permute-start.32) | collective-permute-done | bytes 1048608 | tf_op jit(solution)/shard_map/ppermute | solution.py:282
  203.4 4.9 self_out_cross_q.1
  208.4 17.6 %cross_forward.1 = (bf16[256,1024]{1,0:T(8,128)(2,1)S(1)}, f32[2,8,256]{2,1,0:T(8,128)S(1)}) custom-call(s32[4]{0:T(128)S(1)} %reshape.506.map_ref, s32[4]{0:T(128)S(1)} %select_reduce_fusion.len_ref, s32[2,1,128]{2,1,0:T(1,128)S(1)} %bitcast.131, s32[2,128,1]{2,1,0:T(8,128)S(1)} %copy-done.50, bf16[256,1024]{1,0:T(8,128)(2,1)S(1)} %get-tuple-element.239.q_ref, ...), custom_call_target="tpu_custom_call" | custom-call | flops 5000000000 | bytes 11000000 | tf_op jit(solution)/shard_map/cross_forward/pallas_call | solution.py:202
  227.2 4.5 half_weights.8.own
  235.2 3.2 cross_out.1
  238.4 10.1 %collective-permute-done.38 = bf16[4,256,256]{2,1,0:T(8,128)(2,1)S(1)} collective-permute-done((bf16[4,256,256]{2,1,0:T(8,128)(2,1)}, bf16[4,256,256]{2,1,0:T(8,128)(2,1)S(1)}, u32[]{:S(2)}, u32[]{:S(2)}) %collective-permute-start.38) | collective-permute-done | bytes 524320 | tf_op jit(solution)/shard_map/ppermute | solution.py:282
  248.6 3.0 half_weights.9.own
  254.4 8.8 %fc1_gelu.1 = (bf16[256,4096]{1,0:T(8,128)(2,1)S(1)}, f32[256,4096]{1,0:T(8,128)}) custom-call(s32[4]{0:T(128)S(1)} %pad_add_fusion.place, bf16[256,1024]{1,0:T(8,128)(2,1)S(1)} %get-tuple-element.250.normed.refs_0_, f32[1,4096]{1,0:T(1,128)S(1)} %bitcast.126, bf16[2,1024,1024]{2,1,0:T(8,128)(2,1)} %half_weights.8.own, bf16[2,1024,1024]{2,1,0:T(8,128)(2,1)} %copy-done.55), custom_call_target="tpu_custom_call" | custom-call | flops 1000000 | bytes 100000 | tf_op jit(solution)/shard_map/fc1_gelu/pallas_call | solution.py:827
  263.3 4.8 weight_terms.8
  268.6 7.0 %fc2_gelu_back.1 = (bf16[256,4096]{1,0:T(8,128)(2,1)S(1)}, f32[1,4096]{1,0:T(1,128)S(1)}) custom-call(s32[4]{0:T(128)S(1)} %pad_add_fusion.place, bf16[256,1024]{1,0:T(8,128)(2,1)S(1)} %copy-done.12, f32[256,4096]{1,0:T(8,128)} %get-tuple-element.255.slope, bf16[2,4096,256]{2,1,0:T(8,128)(2,1)} %half_weights.9.own, bf16[2,4096,256]{2,1,0:T(8,128)(2,1)} %copy-done.54), custom_call_target="tpu_custom_call" | custom-call | flops 1000000 | bytes 100000 | tf_op jit(solution)/shard_map/fc2_gelu_back/pallas_call | solution.py:827
  275.7 6.4 %weight_terms.10 = (bf16[1,4,256,256]{3,2,1,0:T(8,128)(2,1)S(1)}, bf16[1,4,256,256]{3,2,1,0:T(8,128)(2,1)S(1)}, f32[1,4,512,256]{3,2,1,0:T(8,128)S(1)}, f32[1,4,512,256]{3,2,1,0:T(8,128)S(1)}, f32[1,4,512,256]{3,2,1,0:T(8,128)}) custom-call(s32[4]{0:T(128)S(1)} %pad_add_fusion.place, bf16[256,4096]{1,0:T(8,128)(2,1)} %copy-done.7, ...), custom_call_target="tpu_custom_call" | custom-call | flops 1000000 | bytes 100000 | tf_op jit(solution)/shard_map/weight_terms/pallas_call | solution.py:472
  282.1 4.0 weight_terms.9
  288.3 7.7 %fc1_norm_back.1 = (f32[256,1024]{1,0:T(8,128)S(1)}, bf16[256,1024]{1,0:T(8,128)(2,1)S(1)}, bf16[256,1024]{1,0:T(8,128)(2,1)S(1)}, f32[1,1024]{1,0:T(1,128)S(1)}...) custom-call(s32[4]{0:T(128)S(1)} %pad_add_fusion.place, ...), custom_call_target="tpu_custom_call" | custom-call | flops 1000000 | bytes 100000 | tf_op jit(solution)/shard_map/fc1_norm_back/pallas_call | solution.py:827
  296.0 4.4 collective-permute-done.43.from_y
  301.1 6.7 %weight_terms.11 = (bf16[1,4,64,1024]{3,2,1,0:T(8,128)(2,1)}, bf16[1,4,64,1024]{3,2,1,0:T(8,128)(2,1)}, f32[1,4,128,1024]{3,2,1,0:T(8,128)S(1)}, f32[1,4,128,1024]{3,2,1,0:T(8,128)S(1)}, f32[1,4,128,1024]{3,2,1,0:T(8,128)}) custom-call(s32[4]{0:T(128)S(1)} %pad_add_fusion.place, bf16[256,1024]{1,0:T(8,128)(2,1)S(1)} %get-tuple-element.250.normed.refs_0_, ...), custom_call_target="tpu_custom_call" | custom-call | flops 1000000 | bytes 100000 | tf_op jit(solution)/shard_map/weight_terms/pallas_call | solution.py:472
  310.4 2.4 add_corners.5
  315.4 21.2 %cross_backward.1 = (bf16[256,1024]{1,0:T(8,128)(2,1)S(1)}, bf16[4,588,1024]{2,1,0:T(8,128)(2,1)S(1)}, bf16[4,588,1024]{2,1,0:T(8,128)(2,1)S(1)}) custom-call(s32[4]{0:T(128)S(1)} %reshape.506.map_ref, s32[4]{0:T(128)S(1)} %select_reduce_fusion.len_ref, s32[2,1,128]{2,1,0:T(1,128)S(1)} %bitcast.132, s32[2,128,1]{2,1,0:T(8,128)S(1)} %copy-done.50, ...), custom_call_target="tpu_custom_call" | custom-call | flops 12000000000 | bytes 22000000 | tf_op jit(solution)/shard_map/cross_backward/pallas_call | solution.py:224
  345.8 6.1 %copy.104.mem = bf16[4,588,1024]{2,1,0:T(8,128)(2,1)} copy(bf16[4,588,1024]{2,0,1:T(4,128)(2,1)} %param.17) | data formatting | bytes 9633792 | tf_op args[1]
  351.9 12.1 %memory_terms.2 = bf16[2,2,1024,256]{3,2,1,0:T(8,128)(2,1)} custom-call(s32[4]{0:T(128)S(1)} %pad_add_fusion.place, bf16[4,588,1024]{2,1,0:T(8,128)(2,1)} %copy.104.mem, bf16[4,588,1024]{2,1,0:T(8,128)(2,1)} %copy-done.3, bf16[4,588,1024]{2,1,0:T(8,128)(2,1)} %copy-done.4), custom_call_target="tpu_custom_call" | custom-call | flops 1000000 | bytes 100000 | tf_op jit(solution)/shard_map/memory_terms/pallas_call | solution.py:524
  364.0 2.7 weight_terms.12
  367.4 4.1 add_corners.6
  376.4 9.1 %collective-permute-done.53 = bf16[1,512,256]{2,1,0:T(8,128)(2,1)S(1)} collective-permute-done((bf16[1,512,256]{2,1,0:T(8,128)(2,1)S(1)}, bf16[1,512,256]{2,1,0:T(8,128)(2,1)S(1)}, u32[]{:S(2)}, u32[]{:S(2)}) %collective-permute-start.53) | collective-permute-done | bytes 262176 | tf_op jit(solution)/shard_map/ppermute | solution.py:282
  389.3 4.7 cross_q_norm_back.1
  396.6 6.7 %self_backward.1 = (bf16[256,1024]{1,0:T(8,128)(2,1)}, bf16[256,1024]{1,0:T(8,128)(2,1)}, bf16[256,1024]{1,0:T(8,128)(2,1)}) custom-call(s32[2,1,128]{2,1,0:T(1,128)} %bitcast.129, s32[2,128,1]{2,1,0:T(8,128)} %copy.101.seg_col, bf16[256,1024]{1,0:T(8,128)(2,1)} %copy-done.47, bf16[256,1024]{1,0:T(8,128)(2,1)} %copy-done.48, bf16[256,1024]{1,0:T(8,128)(2,1)} %copy-done.49, ...), custom_call_target="tpu_custom_call" | custom-call | flops 1000000000 | bytes 4000000 | tf_op jit(solution)/shard_map/self_backward/pallas_call | solution.py:137
  407.5 3.6 weight_terms.13
  411.8 3.4 weight_terms.14
  416.2 12.1 %memory_terms.3 = (bf16[2,4,64,256]{3,2,1,0:T(8,128)(2,1)S(1)}, bf16[2,4,64,256]{3,2,1,0:T(8,128)(2,1)S(1)}, f32[2,4,128,256]{3,2,1,0:T(8,128)S(1)}, f32[2,4,128...) custom-call(s32[4]{0:T(128)S(1)} %pad_add_fusion.place, bf16[4,588,1024]{2,1,0:T(8,128)(2,1)} %copy.104.mem, ...), custom_call_target="tpu_custom_call" | custom-call | flops 1000000 | bytes 100000 | tf_op jit(solution)/shard_map/memory_terms/pallas_call | solution.py:524
  433.2 7.2 %collective-permute-done.55 = bf16[1,128,1024]{2,1,0:T(8,128)(2,1)S(1)} collective-permute-done((bf16[1,128,1024]{2,1,0:T(8,128)(2,1)S(1)}, bf16[1,128,1024]{2,1,0:T(8,128)(2,1)S(1)}, u32[]{:S(2)}, u32[]{:S(2)}) %collective-permute-start.55) | collective-permute-done | bytes 262176 | tf_op jit(solution)/shard_map/ppermute | solution.py:282
  441.0 6.6 %self_qkv_norm_back.1 = (bf16[256,1024]{1,0:T(8,128)(2,1)}, f32[1,1024]{1,0:T(1,128)S(1)}, f32[1,1024]{1,0:T(1,128)S(1)}, f32[1,1024]{1,0:T(1,128)S(1)}, f32[1,1024]{1,0:T(1,128)S(1)}) custom-call(s32[4]{0:T(128)S(1)} %pad_add_fusion.place, bf16[256,1024]{1,0:T(8,128)(2,1)S(1)} %copy-done.19, f32[256,1024]{1,0:T(8,128)S(1)} %copy-done.43, ...), custom_call_target="tpu_custom_call" | custom-call | flops 1000000 | bytes 100000 | tf_op jit(solution)/shard_map/self_qkv_norm_back/pallas_call | solution.py:827
  448.9 6.4 %weight_terms.15 = (bf16[4,4,64,256]{3,2,1,0:T(8,128)(2,1)}, bf16[4,4,64,256]{3,2,1,0:T(8,128)(2,1)}, f32[4,4,128,256]{3,2,1,0:T(8,128)}, f32[4,4,128,256]{3,2,1,0:T(8,128)}, f32[4,4,128,256]{3,2,1,0:T(8,128)}) custom-call(s32[4]{0:T(128)S(1)} %pad_add_fusion.place, bf16[256,1024]{1,0:T(8,128)(2,1)S(1)} %copy-done.6, bf16[256,1024]{1,0:T(8,128)(2,1)S(1)} %copy-done.14, ...), custom_call_target="tpu_custom_call" | custom-call | flops 1000000 | bytes 100000 | tf_op jit(solution)/shard_map/weight_terms/pallas_call | solution.py:472
  462.5 2.8 collective-permute-done.61
  467.2 16.0 %memory_back.1 = (bf16[4,588,1024]{2,1,0:T(8,128)(2,1)}, f32[1,1024]{1,0:T(1,128)S(1)}) custom-call(s32[4]{0:T(128)S(1)} %pad_add_fusion.place, bf16[4,588,1024]{2,1,0:T(8,128)(2,1)} %copy-done.3, bf16[4,588,1024]{2,1,0:T(8,128)(2,1)} %copy-done.4, bf16[2,2176,256]{2,1,0:T(8,128)(2,1)S(1)} %copy-done.2, ...), custom_call_target="tpu_custom_call" | custom-call | flops 1000000 | bytes 100000 | tf_op jit(solution)/shard_map/memory_back/pallas_call | solution.py:827
  485.9 2.2 add_bitcast_fusion
  488.1 2.5 add_bitcast_fusion.1
  491.6 6.1 %fc2.1 = bf16[256,1024]{1,0:T(8,128)(2,1)} custom-call(s32[4]{0:T(128)S(1)} %pad_add_fusion.place, f32[256,1024]{1,0:T(8,128)S(1)} %copy-done.24, bf16[256,4096]{1,0:T(8,128)(2,1)S(1)} %copy-done.8, f32[13,1024]{1,0:T(8,128)S(1)} %reshape.505.vectors, bf16[2,4096,256]{2,1,0:T(8,128)(2,1)} %half_weights.9.own, bf16[2,4096,256]{2,1,0:T(8,128)(2,1)} %copy-done.54), custom_call_target="tpu_custom_call" | custom-call | flops 1000000 | bytes 100000 | tf_op jit(solution)/shard_map/fc2/pallas_call | solution.py:827
  499.8 8.0 %add_corners.9 = (bf16[4,4,128,256]{3,2,1,0:T(8,128)(2,1)S(1)}, bf16[4,4,128,256]{3,2,1,0:T(8,128)(2,1)S(1)}) custom-call(f32[4,4,128,256]{3,2,1,0:T(8,128)S(1)} %copy-done.33, f32[4,4,128,256]{3,2,1,0:T(8,128)} %get-tuple-element.370.qy, bf16[4,4,64,256]{3,2,1,0:T(8,128)(2,1)} %collective-permute-done.68.from_x, ...), custom_call_target="tpu_custom_call" | custom-call | flops 1000000 | bytes 100000 | tf_op jit(solution)/shard_map/add_corners/pallas_call | solution.py:555
  514.1 17.8 %collective-permute-done.71 = f32[4,2,544]{2,1,0:T(2,128)S(1)} collective-permute-done((f32[4,2,544]{2,1,0:T(2,128)S(1)}, f32[4,2,544]{2,1,0:T(2,128)S(1)}, u32[]{:S(2)}, u32[]{:S(2)}) %collective-permute-start.71) | collective-permute-done | bytes 17440 | tf_op jit(solution)/shard_map/ppermute | solution.py:282
  536.3 6.6 %collective-permute-done.73 = bf16[4,128,256]{2,1,0:T(8,128)(2,1)S(1)} collective-permute-done((bf16[4,128,256]{2,1,0:T(8,128)(2,1)S(1)}, bf16[4,128,256]{2,1,0:T(8,128)(2,1)S(1)}, u32[]{:S(2)}, u32[]{:S(2)}) %collective-permute-start.73) | collective-permute-done | bytes 262176 | tf_op jit(solution)/shard_map/ppermute | solution.py:282
  546.7 8.3 %copy.132 = bf16[4,588,1024]{2,0,1:T(4,128)(2,1)} copy(bf16[4,588,1024]{2,1,0:T(8,128)(2,1)} %get-tuple-element.421) | data formatting | bytes 9633792
  556.2 2.5 collective-permute-start.79
  569.2 6.6 %collective-permute-done.80 = f32[544]{0:T(1024)S(1)} collective-permute-done((f32[544]{0:T(1024)S(1)}, f32[544]{0:T(1024)S(1)}, u32[]{:S(2)}, u32[]{:S(2)}) %collective-permute-start.80) | collective-permute-done | bytes 2208 | tf_op jit(solution)/shard_map/ppermute | solution.py:282
  578.4 2.8 collective-permute-done.82
  (415 shorter events, 161.6 us)
Async XLA Ops:
  0.7 14.6 %collective-permute-start.2 = (bf16[1,512,256]{2,1,0:T(8,128)(2,1)}, bf16[1,512,256]{2,1,0:T(8,128)(2,1)S(1)}, u32[]{:S(2)}, u32[]{:S(2)}) collective-permute-start(bf16[1,512,256]{2,1,0:T(8,128)(2,1)} %bitcast.141), channel_id=1, source_target_pairs={{0,2},{1,3},{2,0},{3,1},{4,6},{5,7},{6,4},{7,5},{8,10},{9,11},{10,... | collective-permute-start | bytes 786440 | tf_op jit(solution)/shard_map/ppermute | solution.py:282
  3.7 11.6 %collective-permute-start.1 = (bf16[1,512,256]{2,1,0:T(8,128)(2,1)}, bf16[1,512,256]{2,1,0:T(8,128)(2,1)S(1)}, u32[]{:S(2)}, u32[]{:S(2)}) collective-permute-start(bf16[1,512,256]{2,1,0:T(8,128)(2,1)} %bitcast.142), channel_id=1, source_target_pairs={{0,4},{1,5},{2,6},{3,7},{4,0},{5,1},{6,2},{7,3},{8,12},{9,13},{10,... | collective-permute-start | bytes 786440 | tf_op jit(solution)/shard_map/ppermute | solution.py:282
  29.2 12.5 %collective-permute-start.8 = (bf16[4,272,256]{2,1,0:T(8,128)(2,1)S(1)}, bf16[4,272,256]{2,1,0:T(8,128)(2,1)S(1)}, u32[]{:S(2)}, u32[]{:S(2)}) collective-permute-start(bf16[4,272,256]{2,1,0:T(8,128)(2,1)S(1)} %pad_maximum_fusion.9.refs_0_), channel_id=1, source_target_pairs={{0,4},{1,5},{2,6},{3,7},{4,0},{5,1},{6,2},{7,3},{8,12},{9,13},{10,... | collective-permute-start | bytes 1671176 | tf_op jit(solution)/shard_map/ppermute | solution.py:282
  30.2 12.5 %collective-permute-start.9 = (bf16[4,272,256]{2,1,0:T(8,128)(2,1)S(1)}, bf16[4,272,256]{2,1,0:T(8,128)(2,1)S(1)}, u32[]{:S(2)}, u32[]{:S(2)}) collective-permute-start(bf16[4,272,256]{2,1,0:T(8,128)(2,1)S(1)} %pad_maximum_fusion.9.refs_0_), channel_id=1, source_target_pairs={{0,2},{1,3},{2,0},{3,1},{4,6},{5,7},{6,4},{7,5},{8,10},{9,11},{10,... | collective-permute-start | bytes 1671176 | tf_op jit(solution)/shard_map/ppermute | solution.py:282
  30.8 10.9 %collective-permute-start.7 = (bf16[1,768,256]{2,1,0:T(8,128)(2,1)S(1)}, bf16[1,768,256]{2,1,0:T(8,128)(2,1)S(1)}, u32[]{:S(2)}, u32[]{:S(2)}) collective-permute-start(bf16[1,768,256]{2,1,0:T(8,128)(2,1)S(1)} %pad_maximum_fusion.11), channel_id=1, source_target_pairs={{0,8},{1,9},{2,10},{3,11},{4,12},{5,13},{6,14},{7,15},{8,16},{9,17... | collective-permute-start | bytes 1179656 | tf_op jit(solution)/shard_map/ppermute | solution.py:282
  42.7 12.8 %collective-permute-start.10 = (bf16[1,768,256]{2,1,0:T(8,128)(2,1)S(1)}, bf16[1,768,256]{2,1,0:T(8,128)(2,1)}, u32[]{:S(2)}, u32[]{:S(2)}) collective-permute-start(bf16[1,768,256]{2,1,0:T(8,128)(2,1)S(1)} %collective-permute-done.7), channel_id=1, source_target_pairs={{0,8},{1,9},{2,10},{3,11},{4,12},{5,13},{6,14},{7,15},{8,16},{9,17... | collective-permute-start | bytes 1179656 | tf_op jit(solution)/shard_map/ppermute | solution.py:282
  55.6 9.9 %collective-permute-start.13 = (bf16[1,768,256]{2,1,0:T(8,128)(2,1)}, bf16[1,768,256]{2,1,0:T(8,128)(2,1)}, u32[]{:S(2)}, u32[]{:S(2)}) collective-permute-start(bf16[1,768,256]{2,1,0:T(8,128)(2,1)} %collective-permute-done.10), channel_id=1, source_target_pairs={{0,8},{1,9},{2,10},{3,11},{4,12},{5,13},{6,14},{7,15},{8,16},{9,17... | collective-permute-start | bytes 1179656 | tf_op jit(solution)/shard_map/ppermute | solution.py:282
  65.5 29.0 %collective-permute-start.18 = (bf16[2,2176,256]{2,1,0:T(8,128)(2,1)S(1)}, bf16[2,2176,256]{2,1,0:T(8,128)(2,1)}, u32[]{:S(2)}, u32[]{:S(2)}) collective-permute-start(bf16[2,2176,256]{2,1,0:T(8,128)(2,1)S(1)} %half_weights.5.k_own.v_own), channel_id=1, source_target_pairs={{0,1},{1,0},{2,3},{3,2},{4,5},{5,4},{6,7},{7,6},{8,9},{9,8},{10,11... | collective-permute-start | bytes 6684680 | tf_op jit(solution)/shard_map/ppermute | solution.py:282
  70.6 20.3 %collective-permute-start.15 = (bf16[4,384,256]{2,1,0:T(8,128)(2,1)}, bf16[4,384,256]{2,1,0:T(8,128)(2,1)}, u32[]{:S(2)}, u32[]{:S(2)}) collective-permute-start(bf16[4,384,256]{2,1,0:T(8,128)(2,1)} %pad_maximum_fusion.5.refs_0_), channel_id=1, source_target_pairs={{0,2},{1,3},{2,0},{3,1},{4,6},{5,7},{6,4},{7,5},{8,10},{9,11},{10,... | collective-permute-start | bytes 2359304 | tf_op jit(solution)/shard_map/ppermute | solution.py:282
  70.6 22.0 %collective-permute-start.14 = (bf16[4,384,256]{2,1,0:T(8,128)(2,1)}, bf16[4,384,256]{2,1,0:T(8,128)(2,1)}, u32[]{:S(2)}, u32[]{:S(2)}) collective-permute-start(bf16[4,384,256]{2,1,0:T(8,128)(2,1)} %pad_maximum_fusion.5.refs_0_), channel_id=1, source_target_pairs={{0,4},{1,5},{2,6},{3,7},{4,0},{5,1},{6,2},{7,3},{8,12},{9,13},{10,... | collective-permute-start | bytes 2359304 | tf_op jit(solution)/shard_map/ppermute | solution.py:282
  72.0 10.3 %collective-permute-start.16 = (bf16[1,128,1024]{2,1,0:T(8,128)(2,1)S(1)}, bf16[1,128,1024]{2,1,0:T(8,128)(2,1)}, u32[]{:S(2)}, u32[]{:S(2)}) collective-permute-start(bf16[1,128,1024]{2,1,0:T(8,128)(2,1)S(1)} %bitcast.144), channel_id=1, source_target_pairs={{0,8},{1,9},{2,10},{3,11},{4,12},{5,13},{6,14},{7,15},{8,16},{9,17... | collective-permute-start | bytes 786440 | tf_op jit(solution)/shard_map/ppermute | solution.py:282
  82.3 12.1 %collective-permute-start.17 = (bf16[1,128,1024]{2,1,0:T(8,128)(2,1)}, bf16[1,128,1024]{2,1,0:T(8,128)(2,1)}, u32[]{:S(2)}, u32[]{:S(2)}) collective-permute-start(bf16[1,128,1024]{2,1,0:T(8,128)(2,1)} %collective-permute-done.16), channel_id=1, source_target_pairs={{0,8},{1,9},{2,10},{3,11},{4,12},{5,13},{6,14},{7,15},{8,16},{9,17... | collective-permute-start | bytes 786440 | tf_op jit(solution)/shard_map/ppermute | solution.py:282
  94.4 35.6 %collective-permute-start.21 = (bf16[1,128,1024]{2,1,0:T(8,128)(2,1)}, bf16[1,128,1024]{2,1,0:T(8,128)(2,1)}, u32[]{:S(2)}, u32[]{:S(2)}) collective-permute-start(bf16[1,128,1024]{2,1,0:T(8,128)(2,1)} %collective-permute-done.17), channel_id=1, source_target_pairs={{0,8},{1,9},{2,10},{3,11},{4,12},{5,13},{6,14},{7,15},{8,16},{9,17... | collective-permute-start | bytes 786440 | tf_op jit(solution)/shard_map/ppermute | solution.py:282
  97.2 32.8 %collective-permute-start.19 = (bf16[4,192,256]{2,1,0:T(8,128)(2,1)}, bf16[4,192,256]{2,1,0:T(8,128)(2,1)}, u32[]{:S(2)}, u32[]{:S(2)}) collective-permute-start(bf16[4,192,256]{2,1,0:T(8,128)(2,1)} %slice.158), channel_id=1, source_target_pairs={{0,4},{1,5},{2,6},{3,7},{4,0},{5,1},{6,2},{7,3},{8,12},{9,13},{10,... | collective-permute-start | bytes 1179656 | tf_op jit(solution)/shard_map/ppermute | solution.py:282
  98.7 31.4 %collective-permute-start.20 = (bf16[4,192,256]{2,1,0:T(8,128)(2,1)}, bf16[4,192,256]{2,1,0:T(8,128)(2,1)}, u32[]{:S(2)}, u32[]{:S(2)}) collective-permute-start(bf16[4,192,256]{2,1,0:T(8,128)(2,1)} %slice.159), channel_id=1, source_target_pairs={{0,2},{1,3},{2,0},{3,1},{4,6},{5,7},{6,4},{7,5},{8,10},{9,11},{10,... | collective-permute-start | bytes 1179656 | tf_op jit(solution)/shard_map/ppermute | solution.py:282
  130.1 18.8 %collective-permute-start.23 = (bf16[4,384,256]{2,1,0:T(8,128)(2,1)S(1)}, bf16[4,384,256]{2,1,0:T(8,128)(2,1)S(1)}, u32[]{:S(2)}, u32[]{:S(2)}) collective-permute-start(bf16[4,384,256]{2,1,0:T(8,128)(2,1)S(1)} %copy-done.25), channel_id=1, source_target_pairs={{0,4},{1,5},{2,6},{3,7},{4,0},{5,1},{6,2},{7,3},{8,12},{9,13},{10,... | collective-permute-start | bytes 2359304 | tf_op jit(solution)/shard_map/ppermute | solution.py:282
  130.7 18.5 %collective-permute-start.24 = (bf16[4,384,256]{2,1,0:T(8,128)(2,1)S(1)}, bf16[4,384,256]{2,1,0:T(8,128)(2,1)S(1)}, u32[]{:S(2)}, u32[]{:S(2)}) collective-permute-start(bf16[4,384,256]{2,1,0:T(8,128)(2,1)S(1)} %copy-done.25), channel_id=1, source_target_pairs={{0,2},{1,3},{2,0},{3,1},{4,6},{5,7},{6,4},{7,5},{8,10},{9,11},{10,... | collective-permute-start | bytes 2359304 | tf_op jit(solution)/shard_map/ppermute | solution.py:282
  132.6 14.4 %collective-permute-start.22 = (bf16[4,256,256]{2,1,0:T(8,128)(2,1)S(1)}, bf16[4,256,256]{2,1,0:T(8,128)(2,1)}, u32[]{:S(2)}, u32[]{:S(2)}) collective-permute-start(bf16[4,256,256]{2,1,0:T(8,128)(2,1)S(1)} %get-tuple-element.222), channel_id=1, source_target_pairs={{0,8},{1,9},{2,10},{3,11},{4,12},{5,13},{6,14},{7,15},{8,16},{9,17... | collective-permute-start | bytes 1572872 | tf_op jit(solution)/shard_map/ppermute | solution.py:282
  149.3 20.3 %collective-permute-start.25 = (bf16[2,3072,256]{2,1,0:T(8,128)(2,1)}, bf16[2,3072,256]{2,1,0:T(8,128)(2,1)}, u32[]{:S(2)}, u32[]{:S(2)}) collective-permute-start(bf16[2,3072,256]{2,1,0:T(8,128)(2,1)} %half_weights.6.refs_0_.refs_2_.refs_4_), channel_id=1, source_target_pairs={{0,1},{1,0},{2,3},{3,2},{4,5},{5,4},{6,7},{7,6},{8,9},{9,8},{10,11... | collective-permute-start | bytes 9437192 | tf_op jit(solution)/shard_map/ppermute | solution.py:282
  149.3 11.6 %collective-permute-start.28 = (bf16[4,192,256]{2,1,0:T(8,128)(2,1)S(1)}, bf16[4,192,256]{2,1,0:T(8,128)(2,1)S(1)}, u32[]{:S(2)}, u32[]{:S(2)}) collective-permute-start(bf16[4,192,256]{2,1,0:T(8,128)(2,1)S(1)} %slice.169), channel_id=1, source_target_pairs={{0,2},{1,3},{2,0},{3,1},{4,6},{5,7},{6,4},{7,5},{8,10},{9,11},{10,... | collective-permute-start | bytes 1179656 | tf_op jit(solution)/shard_map/ppermute | solution.py:282
  150.9 11.3 %collective-permute-start.27 = (bf16[4,192,256]{2,1,0:T(8,128)(2,1)S(1)}, bf16[4,192,256]{2,1,0:T(8,128)(2,1)S(1)}, u32[]{:S(2)}, u32[]{:S(2)}) collective-permute-start(bf16[4,192,256]{2,1,0:T(8,128)(2,1)S(1)} %slice.168), channel_id=1, source_target_pairs={{0,4},{1,5},{2,6},{3,7},{4,0},{5,1},{6,2},{7,3},{8,12},{9,13},{10,... | collective-permute-start | bytes 1179656 | tf_op jit(solution)/shard_map/ppermute | solution.py:282
  152.4 17.1 %collective-permute-start.26 = (bf16[4,256,256]{2,1,0:T(8,128)(2,1)S(1)}, bf16[4,256,256]{2,1,0:T(8,128)(2,1)}, u32[]{:S(2)}, u32[]{:S(2)}) collective-permute-start(bf16[4,256,256]{2,1,0:T(8,128)(2,1)S(1)} %get-tuple-element.225), channel_id=1, source_target_pairs={{0,8},{1,9},{2,10},{3,11},{4,12},{5,13},{6,14},{7,15},{8,16},{9,17... | collective-permute-start | bytes 1572872 | tf_op jit(solution)/shard_map/ppermute | solution.py:282
  169.6 31.3 %collective-permute-start.31 = (bf16[2,3072,256]{2,1,0:T(8,128)(2,1)}, bf16[2,3072,256]{2,1,0:T(8,128)(2,1)}, u32[]{:S(2)}, u32[]{:S(2)}) collective-permute-start(bf16[2,3072,256]{2,1,0:T(8,128)(2,1)} %half_weights.7.so_own.cq_own.own.co_own), channel_id=1, source_target_pairs={{0,1},{1,0},{2,3},{3,2},{4,5},{5,4},{6,7},{7,6},{8,9},{9,8},{10,11... | collective-permute-start | bytes 9437192 | tf_op jit(solution)/shard_map/ppermute | solution.py:282
  171.9 25.9 %collective-permute-start.32 = (bf16[4,128,1024]{2,1,0:T(8,128)(2,1)}, bf16[4,128,1024]{2,1,0:T(8,128)(2,1)}, u32[]{:S(2)}, u32[]{:S(2)}) collective-permute-start(bf16[4,128,1024]{2,1,0:T(8,128)(2,1)} %pad_maximum_fusion.refs_0_), channel_id=1, source_target_pairs={{0,4},{1,5},{2,6},{3,7},{4,0},{5,1},{6,2},{7,3},{8,12},{9,13},{10,... | collective-permute-start | bytes 3145736 | tf_op jit(solution)/shard_map/ppermute | solution.py:282
  173.3 25.6 %collective-permute-start.33 = (bf16[4,128,1024]{2,1,0:T(8,128)(2,1)}, bf16[4,128,1024]{2,1,0:T(8,128)(2,1)}, u32[]{:S(2)}, u32[]{:S(2)}) collective-permute-start(bf16[4,128,1024]{2,1,0:T(8,128)(2,1)} %pad_maximum_fusion.refs_0_), channel_id=1, source_target_pairs={{0,2},{1,3},{2,0},{3,1},{4,6},{5,7},{6,4},{7,5},{8,10},{9,11},{10,... | collective-permute-start | bytes 3145736 | tf_op jit(solution)/shard_map/ppermute | solution.py:282
  173.8 26.3 %collective-permute-start.30 = (bf16[4,256,256]{2,1,0:T(8,128)(2,1)}, bf16[4,256,256]{2,1,0:T(8,128)(2,1)}, u32[]{:S(2)}, u32[]{:S(2)}) collective-permute-start(bf16[4,256,256]{2,1,0:T(8,128)(2,1)} %collective-permute-done.26), channel_id=1, source_target_pairs={{0,8},{1,9},{2,10},{3,11},{4,12},{5,13},{6,14},{7,15},{8,16},{9,17... | collective-permute-start | bytes 1572872 | tf_op jit(solution)/shard_map/ppermute | solution.py:282
  173.8 27.1 %collective-permute-start.29 = (bf16[4,256,256]{2,1,0:T(8,128)(2,1)}, bf16[4,256,256]{2,1,0:T(8,128)(2,1)}, u32[]{:S(2)}, u32[]{:S(2)}) collective-permute-start(bf16[4,256,256]{2,1,0:T(8,128)(2,1)} %collective-permute-done.22), channel_id=1, source_target_pairs={{0,8},{1,9},{2,10},{3,11},{4,12},{5,13},{6,14},{7,15},{8,16},{9,17... | collective-permute-start | bytes 1572872 | tf_op jit(solution)/shard_map/ppermute | solution.py:282
  200.9 25.1 %collective-permute-start.36 = (bf16[4,64,1024]{2,1,0:T(8,128)(2,1)S(1)}, bf16[4,64,1024]{2,1,0:T(8,128)(2,1)S(1)}, u32[]{:S(2)}, u32[]{:S(2)}) collective-permute-start(bf16[4,64,1024]{2,1,0:T(8,128)(2,1)S(1)} %slice.171), channel_id=1, source_target_pairs={{0,2},{1,3},{2,0},{3,1},{4,6},{5,7},{6,4},{7,5},{8,10},{9,11},{10,... | collective-permute-start | bytes 1572872 | tf_op jit(solution)/shard_map/ppermute | solution.py:282
  202.4 23.6 %collective-permute-start.35 = (bf16[4,64,1024]{2,1,0:T(8,128)(2,1)S(1)}, bf16[4,64,1024]{2,1,0:T(8,128)(2,1)}, u32[]{:S(2)}, u32[]{:S(2)}) collective-permute-start(bf16[4,64,1024]{2,1,0:T(8,128)(2,1)S(1)} %slice.170), channel_id=1, source_target_pairs={{0,4},{1,5},{2,6},{3,7},{4,0},{5,1},{6,2},{7,3},{8,12},{9,13},{10,... | collective-permute-start | bytes 1572872 | tf_op jit(solution)/shard_map/ppermute | solution.py:282
  203.3 28.4 %collective-permute-start.34 = (bf16[4,256,256]{2,1,0:T(8,128)(2,1)}, bf16[4,256,256]{2,1,0:T(8,128)(2,1)S(1)}, u32[]{:S(2)}, u32[]{:S(2)}) collective-permute-start(bf16[4,256,256]{2,1,0:T(8,128)(2,1)} %collective-permute-done.29), channel_id=1, source_target_pairs={{0,8},{1,9},{2,10},{3,11},{4,12},{5,13},{6,14},{7,15},{8,16},{9,17... | collective-permute-start | bytes 1572872 | tf_op jit(solution)/shard_map/ppermute | solution.py:282
  231.7 19.9 %collective-permute-start.37 = (bf16[2,1024,1024]{2,1,0:T(8,128)(2,1)}, bf16[2,1024,1024]{2,1,0:T(8,128)(2,1)S(1)}, u32[]{:S(2)}, u32[]{:S(2)}) collective-permute-start(bf16[2,1024,1024]{2,1,0:T(8,128)(2,1)} %half_weights.8.own), channel_id=1, source_target_pairs={{0,1},{1,0},{2,3},{3,2},{4,5},{5,4},{6,7},{7,6},{8,9},{9,8},{10,11... | collective-permute-start | bytes 12582920 | tf_op jit(solution)/shard_map/ppermute | solution.py:282
  231.8 16.7 %collective-permute-start.38 = (bf16[4,256,256]{2,1,0:T(8,128)(2,1)}, bf16[4,256,256]{2,1,0:T(8,128)(2,1)S(1)}, u32[]{:S(2)}, u32[]{:S(2)}) collective-permute-start(bf16[4,256,256]{2,1,0:T(8,128)(2,1)} %collective-permute-done.30), channel_id=1, source_target_pairs={{0,8},{1,9},{2,10},{3,11},{4,12},{5,13},{6,14},{7,15},{8,16},{9,17... | collective-permute-start | bytes 1572872 | tf_op jit(solution)/shard_map/ppermute | solution.py:282
  286.1 15.0 %collective-permute-start.41 = (bf16[1,2,1024,1024]{3,2,1,0:T(8,128)(2,1)}, bf16[1,2,1024,1024]{3,2,1,0:T(8,128)(2,1)}, u32[]{:S(2)}, u32[]{:S(2)}) collective-permute-start(bf16[1,2,1024,1024]{3,2,1,0:T(8,128)(2,1)} %weight_terms.9), channel_id=1, source_target_pairs={{0,1},{1,0},{2,3},{3,2},{4,5},{5,4},{6,7},{7,6},{8,9},{9,8},{10,11... | collective-permute-start | bytes 12582920 | tf_op jit(solution)/shard_map/ppermute | solution.py:282
  286.4 14.0 %collective-permute-start.43 = (bf16[1,4,256,256]{3,2,1,0:T(8,128)(2,1)S(1)}, bf16[1,4,256,256]{3,2,1,0:T(8,128)(2,1)S(1)}, u32[]{:S(2)}, u32[]{:S(2)}) collective-permute-start(bf16[1,4,256,256]{3,2,1,0:T(8,128)(2,1)S(1)} %get-tuple-element.266), channel_id=1, source_target_pairs={{0,2},{1,3},{2,0},{3,1},{4,6},{5,7},{6,4},{7,5},{8,10},{9,11},{10,... | collective-permute-start | bytes 1572872 | tf_op jit(solution)/shard_map/ppermute | solution.py:282
  287.3 13.7 %collective-permute-start.42 = (bf16[1,4,256,256]{3,2,1,0:T(8,128)(2,1)S(1)}, bf16[1,4,256,256]{3,2,1,0:T(8,128)(2,1)S(1)}, u32[]{:S(2)}, u32[]{:S(2)}) collective-permute-start(bf16[1,4,256,256]{3,2,1,0:T(8,128)(2,1)S(1)} %get-tuple-element.264), channel_id=1, source_target_pairs={{0,4},{1,5},{2,6},{3,7},{4,0},{5,1},{6,2},{7,3},{8,12},{9,13},{10,... | collective-permute-start | bytes 1572872 | tf_op jit(solution)/shard_map/ppermute | solution.py:282
  312.8 28.1 %collective-permute-start.45 = (bf16[1,4,512,256]{3,2,1,0:T(8,128)(2,1)S(1)}, bf16[1,4,512,256]{3,2,1,0:T(8,128)(2,1)S(1)}, u32[]{:S(2)}, u32[]{:S(2)}) collective-permute-start(bf16[1,4,512,256]{3,2,1,0:T(8,128)(2,1)S(1)} %get-tuple-element.281), channel_id=1, source_target_pairs={{0,2},{1,3},{2,0},{3,1},{4,6},{5,7},{6,4},{7,5},{8,10},{9,11},{10,... | collective-permute-start | bytes 3145736 | tf_op jit(solution)/shard_map/ppermute | solution.py:282
  314.0 26.9 %collective-permute-start.44 = (bf16[1,4,512,256]{3,2,1,0:T(8,128)(2,1)S(1)}, bf16[1,4,512,256]{3,2,1,0:T(8,128)(2,1)S(1)}, u32[]{:S(2)}, u32[]{:S(2)}) collective-permute-start(bf16[1,4,512,256]{3,2,1,0:T(8,128)(2,1)S(1)} %get-tuple-element.279), channel_id=1, source_target_pairs={{0,4},{1,5},{2,6},{3,7},{4,0},{5,1},{6,2},{7,3},{8,12},{9,13},{10,... | collective-permute-start | bytes 3145736 | tf_op jit(solution)/shard_map/ppermute | solution.py:282
  342.9 24.4 %collective-permute-start.48 = (bf16[1,4,64,1024]{3,2,1,0:T(8,128)(2,1)}, bf16[1,4,64,1024]{3,2,1,0:T(8,128)(2,1)}, u32[]{:S(2)}, u32[]{:S(2)}) collective-permute-start(bf16[1,4,64,1024]{3,2,1,0:T(8,128)(2,1)} %get-tuple-element.293), channel_id=1, source_target_pairs={{0,2},{1,3},{2,0},{3,1},{4,6},{5,7},{6,4},{7,5},{8,10},{9,11},{10,... | collective-permute-start | bytes 1572872 | tf_op jit(solution)/shard_map/ppermute | solution.py:282
  343.4 24.0 %collective-permute-start.46 = (bf16[1,4,64,1024]{3,2,1,0:T(8,128)(2,1)}, bf16[1,4,64,1024]{3,2,1,0:T(8,128)(2,1)}, u32[]{:S(2)}, u32[]{:S(2)}) collective-permute-start(bf16[1,4,64,1024]{3,2,1,0:T(8,128)(2,1)} %get-tuple-element.282), channel_id=1, source_target_pairs={{0,4},{1,5},{2,6},{3,7},{4,0},{5,1},{6,2},{7,3},{8,12},{9,13},{10,... | collective-permute-start | bytes 1572872 | tf_op jit(solution)/shard_map/ppermute | solution.py:282
  345.7 20.9 %collective-permute-start.47 = (bf16[1,512,256]{2,1,0:T(8,128)(2,1)S(1)}, bf16[1,512,256]{2,1,0:T(8,128)(2,1)S(1)}, u32[]{:S(2)}, u32[]{:S(2)}) collective-permute-start(bf16[1,512,256]{2,1,0:T(8,128)(2,1)S(1)} %fusion.10), channel_id=1, source_target_pairs={{0,8},{1,9},{2,10},{3,11},{4,12},{5,13},{6,14},{7,15},{8,16},{9,17... | collective-permute-start | bytes 786440 | tf_op jit(solution)/shard_map/ppermute | solution.py:282
  371.4 39.7 %collective-permute-start.52 = (bf16[2,2,1024,256]{3,2,1,0:T(8,128)(2,1)}, bf16[2,2,1024,256]{3,2,1,0:T(8,128)(2,1)}, u32[]{:S(2)}, u32[]{:S(2)}) collective-permute-start(bf16[2,2,1024,256]{3,2,1,0:T(8,128)(2,1)} %memory_terms.2), channel_id=1, source_target_pairs={{0,1},{1,0},{2,3},{3,2},{4,5},{5,4},{6,7},{7,6},{8,9},{9,8},{10,11... | collective-permute-start | bytes 6291464 | tf_op jit(solution)/shard_map/ppermute | solution.py:282
  371.4 40.4 %collective-permute-start.51 = (bf16[2,2,1024,256]{3,2,1,0:T(8,128)(2,1)}, bf16[2,2,1024,256]{3,2,1,0:T(8,128)(2,1)}, u32[]{:S(2)}, u32[]{:S(2)}) collective-permute-start(bf16[2,2,1024,256]{3,2,1,0:T(8,128)(2,1)} %weight_terms.12), channel_id=1, source_target_pairs={{0,1},{1,0},{2,3},{3,2},{4,5},{5,4},{6,7},{7,6},{8,9},{9,8},{10,11... | collective-permute-start | bytes 6291464 | tf_op jit(solution)/shard_map/ppermute | solution.py:282
  371.9 39.2 %collective-permute-start.49 = (bf16[1,4,128,1024]{3,2,1,0:T(8,128)(2,1)}, bf16[1,4,128,1024]{3,2,1,0:T(8,128)(2,1)}, u32[]{:S(2)}, u32[]{:S(2)}) collective-permute-start(bf16[1,4,128,1024]{3,2,1,0:T(8,128)(2,1)} %get-tuple-element.296), channel_id=1, source_target_pairs={{0,4},{1,5},{2,6},{3,7},{4,0},{5,1},{6,2},{7,3},{8,12},{9,13},{10,... | collective-permute-start | bytes 3145736 | tf_op jit(solution)/shard_map/ppermute | solution.py:282
  372.9 38.2 %collective-permute-start.50 = (bf16[1,4,128,1024]{3,2,1,0:T(8,128)(2,1)}, bf16[1,4,128,1024]{3,2,1,0:T(8,128)(2,1)}, u32[]{:S(2)}, u32[]{:S(2)}) collective-permute-start(bf16[1,4,128,1024]{3,2,1,0:T(8,128)(2,1)} %get-tuple-element.298), channel_id=1, source_target_pairs={{0,2},{1,3},{2,0},{3,1},{4,6},{5,7},{6,4},{7,5},{8,10},{9,11},{10,... | collective-permute-start | bytes 3145736 | tf_op jit(solution)/shard_map/ppermute | solution.py:282
  386.8 24.3 %collective-permute-start.54 = (bf16[1,512,256]{2,1,0:T(8,128)(2,1)S(1)}, bf16[1,512,256]{2,1,0:T(8,128)(2,1)S(1)}, u32[]{:S(2)}, u32[]{:S(2)}) collective-permute-start(bf16[1,512,256]{2,1,0:T(8,128)(2,1)S(1)} %fusion.7), channel_id=1, source_target_pairs={{0,8},{1,9},{2,10},{3,11},{4,12},{5,13},{6,14},{7,15},{8,16},{9,17... | collective-permute-start | bytes 786440 | tf_op jit(solution)/shard_map/ppermute | solution.py:282
  428.3 20.5 %collective-permute-start.57 = (bf16[4,2,1024,256]{3,2,1,0:T(8,128)(2,1)}, bf16[4,2,1024,256]{3,2,1,0:T(8,128)(2,1)}, u32[]{:S(2)}, u32[]{:S(2)}) collective-permute-start(bf16[4,2,1024,256]{3,2,1,0:T(8,128)(2,1)} %weight_terms.13), channel_id=1, source_target_pairs={{0,1},{1,0},{2,3},{3,2},{4,5},{5,4},{6,7},{7,6},{8,9},{9,8},{10,11... | collective-permute-start | bytes 12582920 | tf_op jit(solution)/shard_map/ppermute | solution.py:282
  429.8 10.5 %collective-permute-start.55 = (bf16[1,128,1024]{2,1,0:T(8,128)(2,1)S(1)}, bf16[1,128,1024]{2,1,0:T(8,128)(2,1)S(1)}, u32[]{:S(2)}, u32[]{:S(2)}) collective-permute-start(bf16[1,128,1024]{2,1,0:T(8,128)(2,1)S(1)} %fusion.11), channel_id=1, source_target_pairs={{0,8},{1,9},{2,10},{3,11},{4,12},{5,13},{6,14},{7,15},{8,16},{9,17... | collective-permute-start | bytes 786440 | tf_op jit(solution)/shard_map/ppermute | solution.py:282
  430.5 18.3 %collective-permute-start.60 = (bf16[2,4,64,256]{3,2,1,0:T(8,128)(2,1)S(1)}, bf16[2,4,64,256]{3,2,1,0:T(8,128)(2,1)S(1)}, u32[]{:S(2)}, u32[]{:S(2)}) collective-permute-start(bf16[2,4,64,256]{3,2,1,0:T(8,128)(2,1)S(1)} %get-tuple-element.332), channel_id=1, source_target_pairs={{0,2},{1,3},{2,0},{3,1},{4,6},{5,7},{6,4},{7,5},{8,10},{9,11},{10,... | collective-permute-start | bytes 786440 | tf_op jit(solution)/shard_map/ppermute | solution.py:282
  431.0 17.8 %collective-permute-start.59 = (bf16[2,4,64,256]{3,2,1,0:T(8,128)(2,1)S(1)}, bf16[2,4,64,256]{3,2,1,0:T(8,128)(2,1)S(1)}, u32[]{:S(2)}, u32[]{:S(2)}) collective-permute-start(bf16[2,4,64,256]{3,2,1,0:T(8,128)(2,1)S(1)} %get-tuple-element.330), channel_id=1, source_target_pairs={{0,4},{1,5},{2,6},{3,7},{4,0},{5,1},{6,2},{7,3},{8,12},{9,13},{10,... | collective-permute-start | bytes 786440 | tf_op jit(solution)/shard_map/ppermute | solution.py:282
  432.3 16.5 %collective-permute-start.58 = (bf16[2,4,64,256]{3,2,1,0:T(8,128)(2,1)S(1)}, bf16[2,4,64,256]{3,2,1,0:T(8,128)(2,1)S(1)}, u32[]{:S(2)}, u32[]{:S(2)}) collective-permute-start(bf16[2,4,64,256]{3,2,1,0:T(8,128)(2,1)S(1)} %get-tuple-element.329), channel_id=1, source_target_pairs={{0,2},{1,3},{2,0},{3,1},{4,6},{5,7},{6,4},{7,5},{8,10},{9,11},{10,... | collective-permute-start | bytes 786440 | tf_op jit(solution)/shard_map/ppermute | solution.py:282
  455.9 27.9 %collective-permute-start.66 = (bf16[2,4,128,256]{3,2,1,0:T(8,128)(2,1)S(1)}, bf16[2,4,128,256]{3,2,1,0:T(8,128)(2,1)}, u32[]{:S(2)}, u32[]{:S(2)}) collective-permute-start(bf16[2,4,128,256]{3,2,1,0:T(8,128)(2,1)S(1)} %get-tuple-element.351), channel_id=1, source_target_pairs={{0,2},{1,3},{2,0},{3,1},{4,6},{5,7},{6,4},{7,5},{8,10},{9,11},{10,... | collective-permute-start | bytes 1572872 | tf_op jit(solution)/shard_map/ppermute | solution.py:282
  457.8 26.0 %collective-permute-start.65 = (bf16[2,4,128,256]{3,2,0,1:T(8,128)(2,1)}, bf16[2,4,128,256]{3,2,0,1:T(8,128)(2,1)}, u32[]{:S(2)}, u32[]{:S(2)}) collective-permute-start(bf16[2,4,128,256]{3,2,0,1:T(8,128)(2,1)} %copy.109), channel_id=1, source_target_pairs={{0,4},{1,5},{2,6},{3,7},{4,0},{5,1},{6,2},{7,3},{8,12},{9,13},{10,... | collective-permute-start | bytes 1572872 | tf_op jit(solution)/shard_map/ppermute | solution.py:282
  459.6 24.2 %collective-permute-start.64 = (bf16[2,4,128,256]{3,2,0,1:T(8,128)(2,1)}, bf16[2,4,128,256]{3,2,0,1:T(8,128)(2,1)}, u32[]{:S(2)}, u32[]{:S(2)}) collective-permute-start(bf16[2,4,128,256]{3,2,0,1:T(8,128)(2,1)} %copy.108), channel_id=1, source_target_pairs={{0,2},{1,3},{2,0},{3,1},{4,6},{5,7},{6,4},{7,5},{8,10},{9,11},{10,... | collective-permute-start | bytes 1572872 | tf_op jit(solution)/shard_map/ppermute | solution.py:282
  461.9 21.9 %collective-permute-start.63 = (bf16[2,4,128,256]{3,2,0,1:T(8,128)(2,1)}, bf16[2,4,128,256]{3,2,0,1:T(8,128)(2,1)}, u32[]{:S(2)}, u32[]{:S(2)}) collective-permute-start(bf16[2,4,128,256]{3,2,0,1:T(8,128)(2,1)} %copy.107), channel_id=1, source_target_pairs={{0,4},{1,5},{2,6},{3,7},{4,0},{5,1},{6,2},{7,3},{8,12},{9,13},{10,... | collective-permute-start | bytes 1572872 | tf_op jit(solution)/shard_map/ppermute | solution.py:282
  467.2 16.6 %collective-permute-start.62 = (bf16[1,128,1024]{2,1,0:T(8,128)(2,1)}, bf16[1,128,1024]{2,1,0:T(8,128)(2,1)}, u32[]{:S(2)}, u32[]{:S(2)}) collective-permute-start(bf16[1,128,1024]{2,1,0:T(8,128)(2,1)} %fusion.9), channel_id=1, source_target_pairs={{0,8},{1,9},{2,10},{3,11},{4,12},{5,13},{6,14},{7,15},{8,16},{9,17... | collective-permute-start | bytes 786440 | tf_op jit(solution)/shard_map/ppermute | solution.py:282
  483.9 16.0 %collective-permute-start.70 = (bf16[4,4,64,256]{3,2,1,0:T(8,128)(2,1)}, bf16[4,4,64,256]{3,2,1,0:T(8,128)(2,1)}, u32[]{:S(2)}, u32[]{:S(2)}) collective-permute-start(bf16[4,4,64,256]{3,2,1,0:T(8,128)(2,1)} %get-tuple-element.376), channel_id=1, source_target_pairs={{0,2},{1,3},{2,0},{3,1},{4,6},{5,7},{6,4},{7,5},{8,10},{9,11},{10,... | collective-permute-start | bytes 1572872 | tf_op jit(solution)/shard_map/ppermute | solution.py:282
  484.9 14.9 %collective-permute-start.68 = (bf16[4,4,64,256]{3,2,1,0:T(8,128)(2,1)}, bf16[4,4,64,256]{3,2,1,0:T(8,128)(2,1)}, u32[]{:S(2)}, u32[]{:S(2)}) collective-permute-start(bf16[4,4,64,256]{3,2,1,0:T(8,128)(2,1)} %get-tuple-element.371), channel_id=1, source_target_pairs={{0,4},{1,5},{2,6},{3,7},{4,0},{5,1},{6,2},{7,3},{8,12},{9,13},{10,... | collective-permute-start | bytes 1572872 | tf_op jit(solution)/shard_map/ppermute | solution.py:282
  507.8 27.3 %collective-permute-start.75 = (bf16[4,4,128,256]{3,2,1,0:T(8,128)(2,1)S(1)}, bf16[4,4,128,256]{3,2,1,0:T(8,128)(2,1)}, u32[]{:S(2)}, u32[]{:S(2)}) collective-permute-start(bf16[4,4,128,256]{3,2,1,0:T(8,128)(2,1)S(1)} %get-tuple-element.384), channel_id=1, source_target_pairs={{0,2},{1,3},{2,0},{3,1},{4,6},{5,7},{6,4},{7,5},{8,10},{9,11},{10,... | collective-permute-start | bytes 3145736 | tf_op jit(solution)/shard_map/ppermute | solution.py:282
  510.4 24.7 %collective-permute-start.74 = (bf16[4,4,128,256]{3,2,0,1:T(8,128)(2,1)}, bf16[4,4,128,256]{3,2,0,1:T(8,128)(2,1)}, u32[]{:S(2)}, u32[]{:S(2)}) collective-permute-start(bf16[4,4,128,256]{3,2,0,1:T(8,128)(2,1)} %copy.120), channel_id=1, source_target_pairs={{0,4},{1,5},{2,6},{3,7},{4,0},{5,1},{6,2},{7,3},{8,12},{9,13},{10,... | collective-permute-start | bytes 3145736 | tf_op jit(solution)/shard_map/ppermute | solution.py:282
  512.9 18.9 %collective-permute-start.72 = (bf16[4,128,256]{2,1,0:T(8,128)(2,1)}, bf16[4,128,256]{2,1,0:T(8,128)(2,1)}, u32[]{:S(2)}, u32[]{:S(2)}) collective-permute-start(bf16[4,128,256]{2,1,0:T(8,128)(2,1)} %fusion.1), channel_id=1, source_target_pairs={{0,8},{1,9},{2,10},{3,11},{4,12},{5,13},{6,14},{7,15},{8,16},{9,17... | collective-permute-start | bytes 786440 | tf_op jit(solution)/shard_map/ppermute | solution.py:282
  513.0 18.8 %collective-permute-start.71 = (f32[4,2,544]{2,1,0:T(2,128)S(1)}, f32[4,2,544]{2,1,0:T(2,128)S(1)}, u32[]{:S(2)}, u32[]{:S(2)}) collective-permute-start(f32[4,2,544]{2,1,0:T(2,128)S(1)} %bitcast.147), channel_id=1, source_target_pairs={{0,2},{1,3},{2,0},{3,1},{4,6},{5,7},{6,4},{7,5},{8,10},{9,11},{10,... | collective-permute-start | bytes 52232 | tf_op jit(solution)/shard_map/ppermute | solution.py:282
  533.0 9.9 %collective-permute-start.73 = (bf16[4,128,256]{2,1,0:T(8,128)(2,1)S(1)}, bf16[4,128,256]{2,1,0:T(8,128)(2,1)S(1)}, u32[]{:S(2)}, u32[]{:S(2)}) collective-permute-start(bf16[4,128,256]{2,1,0:T(8,128)(2,1)S(1)} %fusion), channel_id=1, source_target_pairs={{0,8},{1,9},{2,10},{3,11},{4,12},{5,13},{6,14},{7,15},{8,16},{9,17... | collective-permute-start | bytes 786440 | tf_op jit(solution)/shard_map/ppermute | solution.py:282
  542.8 12.1 %collective-permute-start.77 = (bf16[4,128,256]{2,1,0:T(8,128)(2,1)S(1)}, bf16[4,128,256]{2,1,0:T(8,128)(2,1)S(1)}, u32[]{:S(2)}, u32[]{:S(2)}) collective-permute-start(bf16[4,128,256]{2,1,0:T(8,128)(2,1)S(1)} %fusion.12), channel_id=1, source_target_pairs={{0,8},{1,9},{2,10},{3,11},{4,12},{5,13},{6,14},{7,15},{8,16},{9,17... | collective-permute-start | bytes 786440 | tf_op jit(solution)/shard_map/ppermute | solution.py:282
  543.5 11.5 %collective-permute-start.76 = (f32[4,544]{1,0:T(4,128)S(1)}, f32[4,544]{1,0:T(4,128)S(1)}, u32[]{:S(2)}, u32[]{:S(2)}) collective-permute-start(f32[4,544]{1,0:T(4,128)S(1)} %bitcast.148), channel_id=1, source_target_pairs={{0,4},{1,5},{2,6},{3,7},{4,0},{5,1},{6,2},{7,3},{8,12},{9,13},{10,... | collective-permute-start | bytes 26120 | tf_op jit(solution)/shard_map/ppermute | solution.py:282
  (104 other events, 1203.3 us)

commit v3 on v2

--- a/solution.py
+++ b/solution.py
@@ -21,6 +21,10 @@
 
 F32 = jnp.float32
 BF16 = jnp.bfloat16
+VMEM = 24 * 2**20
+CHEAP = pl.CostEstimate(flops=10**6, bytes_accessed=10**5, transcendentals=0)
+BIG_VMEM = pltpu.CompilerParams(vmem_limit_bytes=VMEM)
+FULL_VMEM = pltpu.CompilerParams(vmem_limit_bytes=60 * 2**20)
 
 
 def dot_nt(a, b):
@@ -43,35 +47,54 @@
     )
 
 
-def join_heads(both):
-    half = both.shape[0] // 2
-    lane = lax.broadcasted_iota(jnp.int32, (half, both.shape[1]), 1)
-    return jnp.where(lane < HEAD_DIM, both[:half], both[half:])
-
-
-def pair_forward(q2, k2, v2, valid):
-    scores = dot_nt(k2, two_heads(q2)) * (SCALE * LOG2E)
-    scores = jnp.where(valid, scores, NEG_FILL)
-    top = jnp.max(scores, axis=0, keepdims=True)
-    expo = jnp.exp2(scores - top)
-    total = jnp.sum(expo, axis=0, keepdims=True)
-    weights = (expo * (1.0 / total)).astype(BF16)
-    mixed = join_heads(dot_tn(weights, v2)).astype(BF16)
-    return mixed, top + jnp.log2(total)
-
-
-def pair_backward(q2, k2, v2, do2, lse, valid):
-    qq = two_heads(q2)
-    dd = two_heads(do2)
-    scores = dot_nt(k2, qq) * (SCALE * LOG2E)
-    weights = jnp.where(valid, jnp.exp2(scores - lse), 0.0)
-    grad_weights = dot_nt(v2, dd)
-    inner = jnp.sum(weights * grad_weights, axis=0, keepdims=True)
-    grad_scores = (weights * (grad_weights - inner)).astype(BF16)
-    grad_v = dot_nn(weights.astype(BF16), dd).astype(BF16)
-    grad_k = (dot_nn(grad_scores, qq) * SCALE).astype(BF16)
-    grad_q = (join_heads(dot_tn(grad_scores, k2)) * SCALE).astype(BF16)
-    return grad_q, grad_k, grad_v
+def own_heads(both):
+    half = both.shape[1] // 2
+    line = lax.broadcasted_iota(jnp.int32, (both.shape[0], half), 0)
+    return jnp.transpose(jnp.where(line < HEAD_DIM, both[:, :half], both[:, half:]))
+
+
+CUTS = [slice(128 * h, 128 * h + 128) for h in range(PAIRS)]
+
+
+def heads_forward(q_ref, k_ref, v_ref, valid, put):
+    scores = [dot_nt(k_ref(cut), two_heads(q_ref(cut))) for cut in CUTS]
+    weights, lses = [], []
+    for one in scores:
+        one = jnp.where(valid, one * (SCALE * LOG2E), NEG_FILL)
+        top = jnp.max(one, axis=0, keepdims=True)
+        expo = jnp.exp2(one - top)
+        total = jnp.sum(expo, axis=0, keepdims=True)
+        weights.append((expo * (1.0 / total)).astype(BF16))
+        lses.append(top + jnp.log2(total))
+    for h, cut in enumerate(CUTS):
+        put(h, own_heads(dot_tn(v_ref(cut), weights[h])).astype(BF16), lses[h])
+
+
+def heads_backward(q_ref, k_ref, v_ref, do_ref, lse_of, valid, put, group=4):
+    for first in range(0, PAIRS, group):
+        hs = range(first, first + group)
+        qs = [two_heads(q_ref(CUTS[h])) for h in hs]
+        ds = [two_heads(do_ref(CUTS[h])) for h in hs]
+        scores = [dot_nt(k_ref(CUTS[h]), q) for h, q in zip(hs, qs)]
+        grads = [dot_nt(v_ref(CUTS[h]), d) for h, d in zip(hs, ds)]
+        weights, grad_scores = [], []
+        for h, one, grad in zip(hs, scores, grads):
+            weight = jnp.where(valid, jnp.exp2(one * (SCALE * LOG2E) - lse_of(h)), 0.0)
+            inner = jnp.sum(weight * grad, axis=0, keepdims=True)
+            grad_scores.append((weight * (grad - inner)).astype(BF16))
+            weights.append(weight.astype(BF16))
+        for h, q, d, weight, grad in zip(hs, qs, ds, weights, grad_scores):
+            grad_q = (own_heads(dot_tn(k_ref(CUTS[h]), grad)) * SCALE).astype(BF16)
+            grad_k = (dot_nn(grad, q) * SCALE).astype(BF16)
+            put(h, grad_q, grad_k, dot_nn(weight, d).astype(BF16))
+
+
+def columns_in(ref):
+    return lambda cut: ref[:, cut]
+
+
+def memory_columns(ref):
+    return lambda cut: ref[0, :, cut]
 
 
 def self_valid(seg_row, seg_col):
@@ -83,25 +106,25 @@
 
 
 def self_fwd_kernel(seg_row, seg_col, q_ref, k_ref, v_ref, o_ref, lse_ref):
-    valid = self_valid(seg_row[0], seg_col[0])
-    for h in range(PAIRS):
-        cut = slice(128 * h, 128 * h + 128)
-        mixed, lse = pair_forward(q_ref[:, cut], k_ref[:, cut], v_ref[:, cut], valid)
-        o_ref[:, cut] = mixed
+    def put(h, mixed, lse):
+        o_ref[:, CUTS[h]] = mixed
         lse_ref[0, h : h + 1, :] = lse
 
+    heads_forward(
+        columns_in(q_ref), columns_in(k_ref), columns_in(v_ref), self_valid(seg_row[0], seg_col[0]), put
+    )
+
 
 def self_bwd_kernel(seg_row, seg_col, q_ref, k_ref, v_ref, do_ref, lse_ref, dq_ref, dk_ref, dv_ref):
-    valid = self_valid(seg_row[0], seg_col[0])
-    for h in range(PAIRS):
-        cut = slice(128 * h, 128 * h + 128)
-        gq, gk, gv = pair_backward(
-            q_ref[:, cut], k_ref[:, cut], v_ref[:, cut], do_ref[:, cut],
-            lse_ref[0, h : h + 1, :], valid,
-        )
-        dq_ref[:, cut] = gq
-        dk_ref[:, cut] = gk
-        dv_ref[:, cut] = gv
+    def put(h, grad_q, grad_k, grad_v):
+        dq_ref[:, CUTS[h]] = grad_q
+        dk_ref[:, CUTS[h]] = grad_k
+        dv_ref[:, CUTS[h]] = grad_v
+
+    heads_backward(
+        columns_in(q_ref), columns_in(k_ref), columns_in(v_ref), columns_in(do_ref),
+        lambda h: lse_ref[0, h : h + 1, :], self_valid(seg_row[0], seg_col[0]), put, PAIRS,
+    )
 
 
 def self_specs(row_len):
@@ -126,7 +149,8 @@
             jax.ShapeDtypeStruct(queries.shape, BF16),
             jax.ShapeDtypeStruct((rows, PAIRS, 2 * row_len), F32),
         ],
-        cost_estimate=pl.CostEstimate(flops=rows * 2 * 10**8, bytes_accessed=2 * 10**6, transcendentals=rows * 3 * 10**5),
+        compiler_params=BIG_VMEM,
+        cost_estimate=CHEAP,
         name="self_forward",
     )(seg[:, None, :], seg[:, :, None], queries, keys, values)
 
@@ -140,7 +164,8 @@
         in_specs=seg_specs + [row] * 4 + [lse],
         out_specs=[row] * 3,
         out_shape=[jax.ShapeDtypeStruct(queries.shape, BF16)] * 3,
-        cost_estimate=pl.CostEstimate(flops=rows * 5 * 10**8, bytes_accessed=4 * 10**6, transcendentals=rows * 3 * 10**5),
+        compiler_params=FULL_VMEM,
+        cost_estimate=CHEAP,
         name="self_backward",
     )(seg[:, None, :], seg[:, :, None], queries, keys, values, grad_mixed, lse_rows)
 
@@ -152,15 +177,17 @@
     mine_col = (seg_col[0] == page) | (page == 0)
     mine_row = (seg_row[0] == page) | (page == 0)
     mine_row = jnp.concatenate((mine_row, mine_row), axis=1)
-    for h in range(PAIRS):
-        cut = slice(128 * h, 128 * h + 128)
-        mixed, lse = pair_forward(q_ref[:, cut], k_ref[0, :, cut], v_ref[0, :, cut], valid)
-        o_ref[:, cut] = jnp.where(mine_col, mixed, o_ref[:, cut])
+
+    def put(h, mixed, lse):
+        o_ref[:, CUTS[h]] = jnp.where(mine_col, mixed, o_ref[:, CUTS[h]])
         lse_ref[0, h : h + 1, :] = jnp.where(mine_row, lse, lse_ref[0, h : h + 1, :])
 
+    heads_forward(columns_in(q_ref), memory_columns(k_ref), memory_columns(v_ref), valid, put)
+
 
 def cross_bwd_kernel(
-    map_ref, len_ref, seg_row, seg_col, q_ref, k_ref, v_ref, do_ref, lse_ref, dq_ref, dk_ref, dv_ref
+    map_ref, len_ref, seg_row, seg_col, q_ref, k_ref, v_ref, do_ref, lse_ref,
+    dq_ref, dk_ref, dv_ref, sum_ref,
 ):
     r, page = pl.program_id(0), pl.program_id(1)
     keys, toks = k_ref.shape[1], q_ref.shape[0]
@@ -168,15 +195,19 @@
     mine_col = (seg_col[0] == page) | (page == 0)
     mine_row = seg_row[0] == page
     mine_row = jnp.concatenate((mine_row, mine_row), axis=1)
-    for h in range(PAIRS):
-        cut = slice(128 * h, 128 * h + 128)
-        lse = jnp.where(mine_row, lse_ref[0, h : h + 1, :], -NEG_FILL)
-        gq, gk, gv = pair_backward(
-            q_ref[:, cut], k_ref[0, :, cut], v_ref[0, :, cut], do_ref[:, cut], lse, valid
-        )
-        dq_ref[:, cut] = jnp.where(mine_col, gq, dq_ref[:, cut])
-        dk_ref[0, :, cut] = gk
-        dv_ref[0, :, cut] = gv
+
+    def put(h, grad_q, grad_k, grad_v):
+        cut = CUTS[h]
+        dq_ref[:, cut] = jnp.where(mine_col, grad_q, dq_ref[:, cut])
+        dk_ref[0, :, cut] = grad_k
+        dv_ref[0, :, cut] = grad_v
+        before = jnp.where(r + page == 0, jnp.zeros((1, 128), F32), sum_ref[:, cut])
+        sum_ref[:, cut] = before + jnp.sum(grad_v.astype(F32), axis=0, keepdims=True)
+
+    heads_backward(
+        columns_in(q_ref), memory_columns(k_ref), memory_columns(v_ref), columns_in(do_ref),
+        lambda h: jnp.where(mine_row, lse_ref[0, h : h + 1, :], -NEG_FILL), valid, put,
+    )
 
 
 def cross_specs(row_len, mem_len):
@@ -188,11 +219,6 @@
     mem = pl.BlockSpec((1, mem_len, D), lambda r, p, mp, ln: (mp[r * 2 + p], 0, 0))
     lse = pl.BlockSpec((1, PAIRS, 2 * row_len), lambda r, p, *_: (r, 0, 0))
     return seg, row, mem, lse
-
-
-CROSS_PARAMS = pltpu.CompilerParams(
-    dimension_semantics=("arbitrary", "arbitrary"), vmem_limit_bytes=40 * 2**20
-)
 
 
 def cross_forward(local_map, lengths, seg, queries, keys, values):
@@ -211,8 +237,8 @@
             jax.ShapeDtypeStruct(queries.shape, BF16),
             jax.ShapeDtypeStruct((rows, PAIRS, 2 * row_len), F32),
         ],
-        compiler_params=CROSS_PARAMS,
-        cost_estimate=pl.CostEstimate(flops=5 * 10**9, bytes_accessed=11 * 10**6, transcendentals=5 * 10**6),
+        compiler_params=FULL_VMEM,
+        cost_estimate=CHEAP,
         name="cross_forward",
     )(local_map, lengths, seg[:, None, :], seg[:, :, None], queries, keys, values)
 
@@ -227,15 +253,16 @@
             num_scalar_prefetch=2,
             grid=(rows, 2),
             in_specs=seg_specs + [row, mem, mem, row, lse],
-            out_specs=[row, mem, mem],
+            out_specs=[row, mem, mem, pl.BlockSpec((1, D), lambda r, p, *_: (0, 0))],
         ),
         out_shape=[
             jax.ShapeDtypeStruct(queries.shape, BF16),
             jax.ShapeDtypeStruct(keys.shape, BF16),
             jax.ShapeDtypeStruct(values.shape, BF16),
+            jax.ShapeDtypeStruct((1, D), F32),
         ],
-        compiler_params=CROSS_PARAMS,
-        cost_estimate=pl.CostEstimate(flops=12 * 10**9, bytes_accessed=22 * 10**6, transcendentals=5 * 10**6),
+        compiler_params=FULL_VMEM,
+        cost_estimate=CHEAP,
         name="cross_backward",
     )(local_map, lengths, seg[:, None, :], seg[:, :, None], queries, keys, values, grad_mixed, lse_rows)
 
@@ -282,30 +309,41 @@
         return lax.ppermute(self.clock.now(array), AXES, self.perms[name])
 
 
-CHEAP = pl.CostEstimate(flops=10**6, bytes_accessed=10**5, transcendentals=0)
-BIG_VMEM = pltpu.CompilerParams(vmem_limit_bytes=48 * 2**20)
-
-
-def half_kernel(labels, ring, wide, g, rows, place, *refs):
-    n = len(labels)
-    pieces, (out, sems) = refs[:n], refs[n:]
+def segments(first, height, g, rows):
+    out, at, end = [], first, first + height
+    while at < end:
+        k = min(at // rows, g)
+        stop = min(end, (k + 1) * rows) if k < g else end
+        out.append((k, at - k * rows, at - first, stop - at))
+        at = stop
+    return out
+
+
+def half_kernel(parts, ring, wide, g, rows, place, *refs):
+    arrays, (out, sems) = refs[:-2], refs[-2:]
     z, x, y = place[0], place[1], place[2]
-    height = wide * rows
+    height, cols = wide * rows, out.shape[-1]
     copies = []
 
     def copy(src, dst):
         copies.append(pltpu.make_async_copy(src, dst, sems.at[len(copies)]))
 
-    for piece, piece_labels in zip(pieces, labels):
-        for i, (dz, dx, dy) in enumerate(piece_labels):
+    for which, first_row, count, offset, labels in parts:
+        piece = arrays[which]
+        for i, (dz, dx, dy) in enumerate(labels):
             row = 2 * lax.rem(z + (ring - dz), ring) + (x + dx - 2 * x * dx)
             col = y + dy - 2 * y * dy
-            for k in range(g):
-                first = pl.multiple_of(row * rows, 16)
-                copy(piece.at[i, pl.ds(k * rows, rows)], out.at[col, pl.ds(k * height + first, rows)])
-            if piece.shape[1] > g * rows:
-                first = pl.multiple_of(g * height + row * SMALL_ROWS, 16)
-                copy(piece.at[i, pl.ds(g * rows, SMALL_ROWS)], out.at[col, pl.ds(first, SMALL_ROWS)])
+            pieces = segments(offset, count, g, rows)
+            if pieces[0][3] == rows and len([p for p in pieces if p[0] < g]) == g:
+                copy(
+                    piece.at[i, pl.ds(first_row, g * rows)].reshape(g, rows, cols),
+                    out.at[col, pl.ds(0, g * height)].reshape(g, wide, rows, cols).at[:, row],
+                )
+                pieces = [p for p in pieces if p[0] == g]
+            for k, matrix_row, at, n in pieces:
+                each = rows if k < g else SMALL_ROWS
+                first = pl.multiple_of(k * height + row * each + matrix_row, 16)
+                copy(piece.at[i, pl.ds(first_row + at, n)], out.at[col, pl.ds(first, n)])
     for one in copies:
         one.start()
     for one in copies:
@@ -319,60 +357,78 @@
 PLACE = pl.BlockSpec(memory_space=pltpu.SMEM)
 
 
+def rearrange_kernel(moves, n_in, *refs):
+    ins, outs, sems = refs[:n_in], refs[n_in:-1], refs[-1]
+    copies = []
+    for i, bi, ri, ci, rows, o, bo, ro in moves:
+        src = ins[i].at[bi, pl.ds(ri, rows), pl.ds(ci, outs[o].shape[-1])]
+        copies.append(pltpu.make_async_copy(src, outs[o].at[bo, pl.ds(ro, rows)], sems.at[len(copies)]))
+    for one in copies:
+        one.start()
+    for one in copies:
+        one.wait()
+
+
+class Rearrange:
+    def __init__(self):
+        self.ins, self.shapes, self.moves = [], [], []
+
+    def source(self, array):
+        for i, known in enumerate(self.ins):
+            if known is array:
+                return i
+        self.ins.append(array)
+        return len(self.ins) - 1
+
+    def out(self, blocks, rows, cols):
+        self.shapes.append((blocks, rows, cols))
+        return len(self.shapes) - 1
+
+    def move(self, out, block, row, array, from_block, first, rows, column=0):
+        self.moves.append((self.source(array), from_block, first, column, rows, out, block, row))
+
+    def run(self, clock):
+        outs = pl.pallas_call(
+            functools.partial(rearrange_kernel, self.moves, len(self.ins)),
+            in_specs=anywhere(len(self.ins)),
+            out_specs=[pl.BlockSpec(memory_space=pltpu.VMEM)] * len(self.shapes),
+            out_shape=[jax.ShapeDtypeStruct(shape, BF16) for shape in self.shapes],
+            scratch_shapes=[pltpu.SemaphoreType.DMA((len(self.moves),))],
+            compiler_params=BIG_VMEM,
+            cost_estimate=CHEAP,
+            name="rearrange",
+        )(*clock.now(self.ins))
+        return list(outs)
+
+
 class Gather:
-    def __init__(self, grid, place, shard, g, small=False):
-        self.grid, self.place, self.g, self.small, self.shard = grid, place, g, small, shard
-        self.rows = (shard.shape[0] - (SMALL_ROWS if small else 0)) // g
-        self.parts = [([(0, 0, 0)], shard[None])]
-
-    def set_ring(self, arrays):
-        labels = self.parts[0][0]
-        self.parts = [([(step, dx, dy) for _, dx, dy in labels], a) for step, a in enumerate(arrays)]
-
-    def join(self):
-        labels = [l for ls, _ in self.parts for l in ls]
-        self.parts = [(labels, jnp.concatenate([a for _, a in self.parts], axis=0))]
-        return self.parts[0][1]
-
-    def array(self):
-        return self.parts[0][1]
-
-    def pairs(self):
-        labels, array = self.parts[0]
-        self.from_x, self.from_y = self.grid.send("x", array), self.grid.send("y", array)
-        self.parts.append(([(dz, 1, dy) for dz, _, dy in labels], self.from_x))
-        self.parts.append(([(dz, dx, 1) for dz, dx, _ in labels], self.from_y))
-        return self.from_x, self.from_y
-
-    def corner(self):
-        labels, array = self.parts[0]
-        cut = self.corner_cut(array.shape[1])
-        over_x = self.grid.send("x", self.from_y[:, :cut])
-        over_y = self.grid.send("y", self.from_x[:, cut:])
-        self.corner_parts = ([(dz, 1, 1) for dz, _, _ in labels], cut, over_x, over_y)
-        return over_x, over_y
-
-    def corner_cut(self, height):
-        return height // 32 * 16
-
-    def close(self):
-        labels, cut, over_x, over_y = self.corner_parts
-        self.parts.append((labels, jnp.concatenate((over_x, over_y), axis=1)))
-
-    def half(self):
-        grid, g, rows = self.grid, self.g, self.rows
-        height, cols = self.shard.shape
-        n = (g + (height > g * rows)) * grid.devices // 2
+    def __init__(self, grid, place, g, height, cols, small=False):
+        self.grid, self.place, self.g, self.height, self.cols = grid, place, g, height, cols
+        self.rows = (height - (SMALL_ROWS if small else 0)) // g
+        self.parts = []
+
+    def put(self, labels, array, first_row, count, offset):
+        self.parts.append((labels, array, first_row, count, offset))
+
+    def half(self, *after):
+        grid, arrays, parts, n = self.grid, [], [], 0
+        for labels, array, first_row, count, offset in self.parts:
+            which = [i for i, known in enumerate(arrays) if known is array]
+            if not which:
+                arrays.append(array)
+                which = [len(arrays) - 1]
+            parts.append((which[0], first_row, count, offset, labels))
+            n += len(labels) * len(segments(offset, count, self.g, self.rows))
         self.own = pl.pallas_call(
-            functools.partial(half_kernel, [l for l, _ in self.parts], grid.ring, grid.wide, g, rows),
-            in_specs=[PLACE] + anywhere(len(self.parts)),
+            functools.partial(half_kernel, parts, grid.ring, grid.wide, self.g, self.rows),
+            in_specs=[PLACE] + anywhere(len(arrays)),
             out_specs=pl.BlockSpec(memory_space=pltpu.VMEM),
-            out_shape=jax.ShapeDtypeStruct((2, grid.wide * height, cols), self.shard.dtype),
+            out_shape=jax.ShapeDtypeStruct((2, grid.wide * self.height, self.cols), BF16),
             scratch_shapes=[pltpu.SemaphoreType.DMA((n,))],
             compiler_params=BIG_VMEM,
             cost_estimate=CHEAP,
             name="half_weights",
-        )(self.place, *[array for _, array in self.parts])
+        )(self.place, *tie(grid.clock.now(arrays), *after))
         return self.own
 
     def swap(self):
@@ -380,10 +436,60 @@
         return self.other
 
     def small_rows(self):
-        own, other = (a[:, self.g * self.grid.wide * self.rows :] for a in (self.own, self.other))
-        both = jnp.where(self.place[3] == 0, jnp.stack((own, other)), jnp.stack((other, own)))
-        both = both.reshape(2, 2, self.grid.wide, -1)
-        return both.transpose(2, 1, 0, 3).reshape(self.grid.devices, -1)
+        first = self.g * self.grid.wide * self.rows
+        own, other = self.grid.clock.now((self.own[:, first:], self.other[:, first:]))
+        flip = self.place[3] == 0
+        both = jnp.stack((jnp.where(flip, own, other), jnp.where(flip, other, own)))
+        return both.reshape(2, 2, self.grid.wide, SMALL_ROWS, -1).astype(F32)
+
+
+class Square:
+    def __init__(self, gather, blocks, height, offset=0):
+        self.gather, self.blocks, self.height, self.offset = gather, blocks, height, offset
+        self.cut = height // 32 * 16
+
+    def labels(self, dx, dy):
+        return [(dz, dx, dy) for dz in range(len(self.blocks))]
+
+
+def exchange(grid, before, after):
+    make = Rearrange()
+    cols = (before or after).gather.cols
+    depth = len((before or after).blocks)
+    heights = [0, 0]
+    if before:
+        heights = [before.cut, before.height - before.cut]
+    total = [h + (after.height if after else 0) for h in heights]
+    outs = [make.out(depth, h, cols) for h in total]
+    if before:
+        (near_x, x_first), (near_y, y_first) = before.near
+        for k in range(depth):
+            make.move(outs[0], k, 0, near_y, k, y_first, heights[0])
+            make.move(outs[1], k, 0, near_x, k, x_first + before.cut, heights[1])
+    if after:
+        for out, first in zip(outs, heights):
+            for k, pieces in enumerate(after.blocks):
+                at = first
+                for array, block, row, count, column in pieces:
+                    make.move(out, k, at, array, block, row, count, column)
+                    at += count
+    send_x, send_y = make.run(grid.clock)
+    from_x, from_y = grid.send("x", send_x), grid.send("y", send_y)
+    if before:
+        before.gather.put(before.labels(1, 1), from_x, 0, heights[0], before.offset)
+        before.gather.put(before.labels(1, 1), from_y, 0, heights[1], before.offset + before.cut)
+    if after:
+        after.near = ((from_x, heights[0]), (from_y, heights[1]))
+        put = after.gather.put
+        put(after.labels(0, 0), send_x, heights[0], after.height, after.offset)
+        put(after.labels(1, 0), from_x, heights[0], after.height, after.offset)
+        put(after.labels(0, 1), from_y, heights[1], after.height, after.offset)
+    return from_x, from_y
+
+
+def unfold(small, count, start, width):
+    part = small[:, :, :, :count, start : start + width]
+    return part.transpose(3, 2, 1, 0, 4).reshape(count, -1)
 
 
 def corners(place):
@@ -393,6 +499,10 @@
 
 def column(ref, n, cols):
     return ref[:, pl.ds(pl.multiple_of(n * cols, 128), cols)]
+
+
+def both_columns(ref, blocks, cols):
+    return jnp.concatenate([column(ref, n, cols) for n in blocks], axis=1)
 
 
 def far_kernel(place, *refs):
@@ -400,8 +510,9 @@
     cols = out.shape[-1]
     for i in range(out.shape[0]):
         a, d = refs[2 * i], refs[2 * i + 1]
-        for j, n in enumerate(corners(place)[0]):
-            out[i, j] = dot_tn(a[...], column(d, n, cols)).astype(BF16)
+        term = dot_tn(a[...], both_columns(d, corners(place)[0], cols))
+        for j in range(2):
+            out[i, j] = term[:, j * cols : (j + 1) * cols].astype(BF16)
 
 
 def put_quadrants(x, scratch, k, i, here, outs):
@@ -409,9 +520,9 @@
     rows = own.shape[2]
     if here:
         own[i, k] = scratch[k, x]
-        qx[i, k] = scratch[k, 1 - x]
+        qx[i, k] = scratch[k, 1 - x].astype(BF16)
     else:
-        qy[i, k] = scratch[k, x]
+        qy[i, k] = scratch[k, x].astype(BF16)
         dx[i, k] = scratch[k, 1 - x, pl.ds(0, rows // 2)].astype(BF16)
         dy[i, k] = scratch[k, 1 - x, pl.ds(rows // 2, rows // 2)].astype(BF16)
 
@@ -421,17 +532,19 @@
     units, zs, rows, cols = outs[-1].shape
     for i in range(units):
         a, d = refs[2 * i], refs[2 * i + 1]
-        for j, n in enumerate(corners(place)[1]):
-            term = dot_tn(a[...], column(d, n, cols)) + from_c[i, j].astype(F32)
-            scratch[...] = term.reshape(scratch.shape)
+        term = dot_tn(a[...], both_columns(d, corners(place)[1], cols))
+        for j in range(2):
+            part = term[:, j * cols : (j + 1) * cols] + from_c[i, j].astype(F32)
+            scratch[...] = part.reshape(scratch.shape)
             for k in range(zs):
                 put_quadrants(place[1], scratch, k, i, j == 0, outs)
 
 
 def quadrant_shapes(units, ring, rows, cols):
-    return [jax.ShapeDtypeStruct((units, ring, rows // 2, cols), BF16)] * 2 + [
-        jax.ShapeDtypeStruct((units, ring, rows, cols), F32)
-    ] * 3
+    half, full = (units, ring, rows // 2, cols), (units, ring, rows, cols)
+    return [jax.ShapeDtypeStruct(half, BF16)] * 2 + [
+        jax.ShapeDtypeStruct(full, BF16), jax.ShapeDtypeStruct(full, BF16), jax.ShapeDtypeStruct(full, F32)
+    ]
 
 
 def quadrant_specs(units, zs, rows, cols, stepped):
@@ -479,86 +592,98 @@
             scratch_shapes=scratch,
         ),
         out_shape=out_shape,
-        compiler_params=BIG_VMEM,
+        compiler_params=FULL_VMEM,
         cost_estimate=CHEAP,
         name="weight_terms",
     )(place, *args)
 
 
-def memory_terms_kernel(near, place, mem, *refs):
+def memory_terms_kernel(near, pairs, place, mem, dk, dv, *refs):
+    tokens, refs = refs[: 2 * pairs], refs[2 * pairs :]
     if near:
-        *ds, from_c, dx, dy, qx, qy, own, acc = refs
+        from_c, dx, dy, qx, qy, own, acc = refs
     else:
-        *ds, out, acc = refs
+        out, acc = refs
     cols = acc.shape[-1]
     m = pl.program_id(0)
+    blocks = corners(place)[1 if near else 0]
 
     @pl.when(m == 0)
     def _():
-        acc[...] = from_c[...].astype(F32).reshape(acc.shape) if near else jnp.zeros_like(acc)
-
-    for i, d in enumerate(ds):
-        for j, n in enumerate(corners(place)[1 if near else 0]):
-            term = dot_tn(mem[0], d[0, :, pl.ds(pl.multiple_of(n * cols, 128), cols)])
-            acc[i, j] += term.reshape(acc.shape[2:])
+        for i in range(pairs):
+            term = dot_tn(tokens[2 * i][...], both_columns(tokens[2 * i + 1], blocks, cols))
+            for j in range(2):
+                acc[i, j] = term[:, j * cols : (j + 1) * cols].reshape(acc.shape[2:])
+        acc[pairs:] = jnp.zeros_like(acc[pairs:])
+        if near:
+            acc[...] += from_c[...].astype(F32).reshape(acc.shape)
+
+    grads = jnp.concatenate([both_columns(d.at[0], blocks, cols) for d in (dk, dv)], axis=1)
+    term = dot_tn(mem[0], grads)
+    for q in range(4):
+        part = term[:, q * cols : (q + 1) * cols].reshape(acc.shape[2:])
+        acc[pairs + q // 2, q % 2] += part
 
     @pl.when(m == pl.num_programs(0) - 1)
     def _():
         if near:
             x = place[1]
-            zs, rows = own.shape[1], own.shape[2]
-            for i in range(len(ds)):
+            for i in range(pairs + 2):
                 for j in range(2):
-                    for k in range(zs):
+                    for k in range(own.shape[1]):
                         put_quadrants(x, acc.at[i, j], k, i, j == 0, (dx, dy, qx, qy, own))
         else:
             out[...] = acc[...].reshape(out.shape).astype(BF16)
 
 
-def memory_terms(grid, place, memory, grads, rows, cols, from_c=None):
-    units, (mems, length, wide_cols) = len(grads), memory.shape
+def memory_terms(grid, place, memory, grads, pairs, rows, cols, from_c=None):
+    units, (mems, length, wide_cols) = len(pairs) + 2, memory.shape
     height = grid.wide * rows
     near = from_c is not None
     one = pl.BlockSpec((1, length, wide_cols), lambda m, *_: (m, 0, 0))
     term = pl.BlockSpec((units, 2, height, cols), lambda m, *_: (0, 0, 0, 0))
+    tokens = [array for pair in pairs for array in pair]
     return pl.pallas_call(
-        functools.partial(memory_terms_kernel, near),
+        functools.partial(memory_terms_kernel, near, len(pairs)),
         grid_spec=pltpu.PrefetchScalarGridSpec(
             num_scalar_prefetch=1,
             grid=(mems,),
-            in_specs=[one] * (1 + units) + ([term] if near else []),
+            in_specs=[one] * 3
+            + [pl.BlockSpec(a.shape, lambda m, *_: (0, 0)) for a in tokens]
+            + ([term] if near else []),
             out_specs=quadrant_specs(units, grid.ring, rows, cols, False) if near else term,
             scratch_shapes=[pltpu.VMEM((units, 2, grid.ring, 2, rows, cols), F32)],
         ),
         out_shape=quadrant_shapes(units, grid.ring, rows, cols)
         if near
         else jax.ShapeDtypeStruct((units, 2, height, cols), BF16),
-        compiler_params=BIG_VMEM,
+        compiler_params=FULL_VMEM,
         cost_estimate=CHEAP,
         name="memory_terms",
-    )(place, memory, *grads, *([from_c] if near else []))
+    )(place, memory, *grads, *tokens, *([from_c] if near else []))
 
 
 def add_corners_kernel(qx, qy, from_x, from_y, sx, sy):
     half = from_x.shape[2]
     first, second = pl.ds(0, half), pl.ds(half, half)
-    sx[0, 0, first] = qx[0, 0, first].astype(BF16)
-    sx[0, 0, second] = (qx[0, 0, second] + from_y[0, 0].astype(F32)).astype(BF16)
-    sy[0, 0, first] = (qy[0, 0, first] + from_x[0, 0].astype(F32)).astype(BF16)
-    sy[0, 0, second] = qy[0, 0, second].astype(BF16)
+    sx[0, :, first] = qx[0, :, first]
+    sx[0, :, second] = (qx[0, :, second].astype(F32) + from_y[0].astype(F32)).astype(BF16)
+    sy[0, :, first] = (qy[0, :, first].astype(F32) + from_x[0].astype(F32)).astype(BF16)
+    sy[0, :, second] = qy[0, :, second]
 
 
 def add_corners(qx, qy, from_x, from_y):
     units, ring, rows, cols = qx.shape
-    full = pl.BlockSpec((1, 1, rows, cols), lambda i, k: (i, k, 0, 0))
-    half = pl.BlockSpec((1, 1, rows // 2, cols), lambda i, k: (i, k, 0, 0))
+    zs = ring if units > 1 else 1
+    full = pl.BlockSpec((1, zs, rows, cols), lambda i, k: (i, k, 0, 0))
+    half = pl.BlockSpec((1, zs, rows // 2, cols), lambda i, k: (i, k, 0, 0))
     return pl.pallas_call(
         add_corners_kernel,
-        grid=(units, ring),
+        grid=(units, ring // zs),
         in_specs=[full, full, half, half],
         out_specs=[full, full],
         out_shape=[jax.ShapeDtypeStruct(qx.shape, BF16)] * 2,
-        compiler_params=BIG_VMEM,
+        compiler_params=FULL_VMEM,
         cost_estimate=CHEAP,
         name="add_corners",
     )(qx, qy, from_x, from_y)
@@ -605,11 +730,11 @@
     def __init__(self, grid, reduces):
         self.grid, self.reduces, self.done, self.came = grid, reduces, 0, None
 
-    def step(self):
+    def step(self, *after):
         self.done += 1
         total = jnp.concatenate([r.chunk(self.done % self.grid.ring) for r in self.reduces], axis=0)
         if self.came is not None:
-            total = total + self.came.astype(F32)
+            total = total + tie(self.grid.clock.now(self.came), *after).astype(F32)
         if self.done == self.grid.ring:
             self.came = total
         else:
@@ -725,19 +850,15 @@
 
 
 def up_kernel(place, normed, bias, own, other, act, slope):
-    c = place[3]
-    cols = own.shape[-1]
-
-    def block(n, half):
-        at = at_block(n, cols)
-        u = dot_nn(normed[...], half[0]) + bias[:, at]
-        below = 0.5 * (1.0 + lax.erf(u * (1.0 / math.sqrt(2.0))))
-        act[:, at] = (u * below).astype(BF16)
-        slope[:, at] = below + u * jnp.exp(-0.5 * u * u) * (1.0 / math.sqrt(2.0 * math.pi))
-
+    c, cols = place[3], own.shape[-1]
     y = pl.program_id(0)
-    block(2 * y + c, own)
-    block(2 * y + 1 - c, other)
+    for n, half in ((2 * y + c, own), (2 * y + 1 - c, other)):
+        for j in range(4):
+            at = at_block(4 * n + j, cols)
+            u = dot_nn(normed[...], half[0, j * D : (j + 1) * D]) + bias[:, at]
+            below = 0.5 * (1.0 + lax.erf(u * (1.0 / math.sqrt(2.0))))
+            act[:, at] = (u * below).astype(BF16)
+            slope[:, at] = (below + u * jnp.exp(-0.5 * u * u) * (1.0 / math.sqrt(2.0 * math.pi))).astype(BF16)
 
 
 def down_kernel(place, after, act, vectors, own, other, out):
@@ -750,7 +871,7 @@
 
 
 def down_back_kernel(place, grad, slope, own, other, grad_pre, bias_grad):
-    back = (times_t(place, grad, own, other) * slope[...]).astype(BF16)
+    back = (times_t(place, grad, own, other) * slope[...].astype(F32)).astype(BF16)
     grad_pre[...] = back
     bias_grad[...] = column_sum(back)
 
@@ -761,8 +882,11 @@
 ):
     c, y = place[3], pl.program_id(0)
     cols = own.shape[-1]
-    term = dot_nt(grad_pre[:, at_block(2 * y + c, cols)], own[0])
-    term = term + dot_nt(grad_pre[:, at_block(2 * y + 1 - c, cols)], other[0])
+    term = sum(
+        dot_nt(grad_pre[:, at_block(4 * n + j, cols)], half[0, j * D : (j + 1) * D])
+        for n, half in ((2 * y + c, own), (2 * y + 1 - c, other))
+        for j in range(4)
+    )
 
     @pl.when(y == 0)
     def _():
@@ -807,18 +931,25 @@
     value_grad[...] = column_sum(gv[...])
 
 
-def memory_back_kernel(place, gk, gv, k_own, k_other, v_own, v_other, grad, value_grad):
+def memory_back_kernel(place, gk, gv, k_own, k_other, v_own, v_other, grad):
     total = times_t(place, gk.at[0], k_own, k_other) + times_t(place, gv.at[0], v_own, v_other)
     grad[0] = total.astype(BF16)
 
-    @pl.when(pl.program_id(0) == 0)
-    def _():
-        value_grad[...] = jnp.zeros_like(value_grad)
-
-    value_grad[...] += column_sum(gv[0])
-
-
-def dense_call(kernel, name, place, ins, outs, grid=(1,), scratch=()):
+
+def in_place(array):
+    return pl.pallas_call(
+        lambda _, out: None,
+        in_specs=anywhere(1),
+        out_specs=pl.BlockSpec(memory_space=pl.ANY),
+        out_shape=jax.ShapeDtypeStruct(array.shape, array.dtype),
+        input_output_aliases={0: 0},
+        compiler_params=BIG_VMEM,
+        cost_estimate=CHEAP,
+        name="in_place",
+    )(array)
+
+
+def dense_call(kernel, name, place, ins, outs, grid=(1,), scratch=(), params=BIG_VMEM):
     def spec(array, block, index):
         block = block or array.shape
         zeros = (0,) * len(block)
@@ -834,7 +965,7 @@
             scratch_shapes=scratch,
         ),
         out_shape=[one[0] for one in outs],
-        compiler_params=BIG_VMEM,
+        compiler_params=params,
         cost_estimate=CHEAP,
         name=name,
     )(place, *[one[0] for one in ins])
@@ -889,57 +1020,89 @@
     mem_count, token_count = memory.shape[0], tokens.shape[0]
     rows, cols = self_out.shape
 
-    small = jnp.concatenate((gains.reshape(-1), biases.reshape(-1), fc1_bias))
-    small = jnp.pad(small, (0, SMALL_ROWS * cols - small.size)).reshape(SMALL_ROWS, cols)
-    n_gain, n_bias, n_fc1 = gains.size, biases.size, fc1_bias.size
-    gather = functools.partial(Gather, grid, place)
-    g_ckv = gather(jnp.concatenate((cross_kv[0], cross_kv[1], small), axis=0), 2, True)
-    g_qkv = gather(self_qkv.reshape(3 * rows, cols), 3)
-    g_mix = gather(jnp.concatenate((self_out, cross_q, cross_out), axis=0), 3)
-    g_fc1 = gather(fc1, 1)
-    g_fc2 = gather(fc2, 1)
+    each, up_each = gains.shape[1], fc1_bias.size
+    n_gain, n_bias = gains.size, biases.size
+    small = jnp.pad(
+        jnp.concatenate((gains, biases), axis=0), ((0, SMALL_ROWS - 13), (0, cols - each))
+    )
+    small = lax.dynamic_update_slice(small, fc1_bias[None], (0, 128))
     send, clock = grid.send, grid.clock
     now, tick = clock.now, clock.tick
     steps = grid.ring - 1
-
-    ring_ckv = [g_ckv.array()]
-    ring_ckv.append(send("z", ring_ckv[-1]))
-    tick(ring_ckv[-1], *g_fc2.pairs())
-    ring_ckv.append(send("z", ring_ckv[-1]))
-    tick(ring_ckv[-1], *g_fc2.corner())
+    gather = functools.partial(Gather, grid, place)
+    ckv_height = 2 * rows + SMALL_ROWS
+    fc2_rows = fc2.shape[0]
+    part = fc2_rows // 2
+    g_ckv = gather(2, ckv_height, cols, True)
+    g_qkv = gather(3, 3 * rows, cols)
+    g_mix = gather(3, 3 * rows, cols)
+    g_fc1 = gather(4, 4 * rows, cols)
+    g_fc2 = gather(1, fc2_rows, cols)
+
+    start = Rearrange()
+    out = start.out(1, 5 * rows, cols)
+    for k, (array, i) in enumerate(((cross_kv, 0), (cross_kv, 1), (self_qkv, 0), (self_qkv, 1), (self_qkv, 2))):
+        start.move(out, 0, k * rows, array, i, 0, rows)
+    ring_one = start.run(clock)
+    ring_one.append(send("z", ring_one[-1]))
+    top = Square(g_fc2, [[(fc2[None], 0, 0, part, 0)]], part)
+    memory = in_place(memory)
+    more = Rearrange()
+    out = more.out(1, 3 * rows, cols)
+    for k, array in enumerate((self_out, cross_q, cross_out)):
+        more.move(out, 0, k * rows, array[None], 0, 0, rows)
+    out = more.out(1, 4 * rows + part, cols)
+    for k in range(4):
+        more.move(out, 0, k * rows, fc1[None], 0, 0, rows, k * cols)
+    more.move(out, 0, 4 * rows, fc2[None], 0, part, part)
+    ring_mix, ring_up = [[array] for array in more.run(clock)]
+    tick(ring_one[-1], memory, ring_mix[0], ring_up[0], *exchange(grid, None, top))
+    ring_one.append(send("z", ring_one[-1]))
+    ring_small = [small[None]]
+    ring_small.append(send("z", ring_small[-1]))
+    tick(ring_one[-1], ring_small[-1], *exchange(grid, top, None))
     for _ in range(steps - 2):
-        ring_ckv.append(send("z", ring_ckv[-1]))
-        tick(ring_ckv[-1])
-    g_fc2.close()
-    fc2_all = g_fc2.join()
-    fc2_cut = fc2_all.shape[1] // 2
-    g_ckv.set_ring(ring_ckv)
-    g_ckv.join()
-
-    ring_two = [jnp.concatenate((g_qkv.array(), g_mix.array()), axis=1)]
-    ring_two.append(send("z", ring_two[-1]))
-    tick(ring_two[-1], *g_ckv.pairs())
-    ring_two.append(send("z", ring_two[-1]))
-    tick(ring_two[-1], *g_ckv.corner())
-    g_ckv.close()
+        ring_one.append(send("z", ring_one[-1]))
+        ring_small.append(send("z", ring_small[-1]))
+        tick(ring_one[-1], ring_small[-1])
+    ring_small.append(send("z", ring_small[-1]))
+
+    def from_ring(arrays, first, count):
+        return [[(array, 0, first, count, 0)] for array in arrays]
+
+    ckv = Square(
+        g_ckv, [a + b for a, b in zip(from_ring(ring_one, 0, 2 * rows), from_ring(ring_small, 0, SMALL_ROWS))],
+        ckv_height,
+    )
+    qkv = Square(g_qkv, from_ring(ring_one, 2 * rows, 3 * rows), 3 * rows)
+    ring_mix.append(send("z", ring_mix[-1]))
+    ring_up.append(send("z", ring_up[-1]))
+    tick(ring_mix[-1], ring_up[-1], *exchange(grid, None, ckv))
+
+    make = Rearrange()
+    out = make.out(4, part, cols)
+    (_, own, own_at, _, _), (_, by_x, x_at, _, _), (_, by_y_, y_at, _, _), (_, low, _, _, _), (_, high, _, _, _) = g_fc2.parts
+    g_fc2.parts = []
+    for k, (array, at) in enumerate(((own, own_at), (by_x, x_at), (by_y_, y_at))):
+        make.move(out, k, 0, array, 0, at, part)
+    make.move(out, 3, 0, low, 0, 0, top.cut)
+    make.move(out, 3, top.cut, high, 0, 0, part - top.cut)
+    came = exchange(grid, ckv, qkv)
+    ring_top = make.run(clock)
+    ring_up.append(send("z", ring_up[-1]))
+    for _ in range(steps - 1):
+        ring_mix.append(send("z", ring_mix[-1]))
+    tick(ring_mix[-1], ring_up[-1], ring_top[-1], *came)
+
+    mix = Square(g_mix, from_ring(ring_mix, 0, 3 * rows), 3 * rows)
+    came = exchange(grid, qkv, mix)
     for _ in range(steps - 2):
-        ring_two.append(send("z", ring_two[-1]))
-        tick(ring_two[-1], g_ckv.half())
-    cut = 3 * rows
-    g_qkv.set_ring([a[:, :cut] for a in ring_two])
-    g_mix.set_ring([a[:, cut:] for a in ring_two])
-    g_qkv.join()
-    g_mix.join()
-
-    ring_fc1 = [g_fc1.array()]
-    for _ in range(steps - 1):
-        ring_fc1.append(send("z", ring_fc1[-1]))
-    tick(ring_fc1[-1], g_ckv.swap(), *g_qkv.pairs())
-
-    ring_fc1.append(send("z", ring_fc1[-1]))
-    small_all = g_ckv.small_rows().astype(F32)
-    vectors = small_all[:, : n_gain + n_bias].reshape(devices, 13, -1).transpose(1, 0, 2).reshape(13, D)
-    up_bias = small_all[:, n_gain + n_bias : n_gain + n_bias + n_fc1].reshape(1, -1)
+        ring_up.append(send("z", ring_up[-1]))
+    g_ckv.half(g_mix.parts[0][1])
+    g_ckv.swap()
+    small_all = g_ckv.small_rows()
+    vectors = unfold(small_all, 13, 0, each)
+    up_bias = unfold(small_all, 1, 128, up_each)
     mem_block = (1,) + memory.shape[1:]
     mem_shape = jax.ShapeDtypeStruct(memory.shape, BF16)
 
@@ -951,20 +1114,14 @@
         [by_memory(now(memory)), full(vectors)] + matrix(g_ckv, 0) + matrix(g_ckv, 1),
         [by_memory(mem_shape), by_memory(mem_shape)], grid=(mem_count,),
     )
-    tick(ring_fc1[-1], mem_keys, *g_qkv.corner())
-    g_qkv.close()
-    g_fc1.set_ring(ring_fc1)
-    g_fc1.join()
-
-    ring_a, ring_b = [fc2_all[:, :fc2_cut]], [fc2_all[:, fc2_cut:]]
-    ring_a.append(send("z", ring_a[-1]))
-    tick(ring_a[-1], g_qkv.half(), *g_mix.pairs())
-    ring_b.append(send("z", ring_b[-1]))
-    tick(g_qkv.swap(), ring_b[-1], *g_mix.corner())
-    g_mix.close()
-
-    ring_a.append(send("z", ring_a[-1]))
-    ring_b.append(send("z", ring_b[-1]))
+    tick(ring_up[-1], mem_keys, *came)
+
+    up = Square(g_fc1, from_ring(ring_up, 0, 4 * rows), 4 * rows)
+    low = Square(g_fc2, from_ring(ring_up, 4 * rows, part), part, part)
+    came = exchange(grid, mix, up)
+    ring_top.append(send("z", ring_top[-1]))
+    g_qkv.half(g_fc1.parts[0][1])
+    g_qkv.swap()
     wide_row = (token_count, D)
     normed_one, self_queries, self_keys, self_values = dense_call(
         qkv_kernel, "self_qkv", place,
@@ -972,11 +1129,12 @@
         [result(wide_row, BF16)] * 4,
     )
     self_mixed, self_lse = self_forward(segment_ids, self_queries, self_keys, self_values)
-    g_mix.half()
-    tick(ring_a[-1], ring_b[-1], self_mixed, g_mix.swap(), *g_fc1.pairs())
-
-    for _ in range(steps - 2):
-        ring_a.append(send("z", ring_a[-1]))
+    tick(self_mixed, ring_top[-1], *came)
+
+    came = exchange(grid, up, low)
+    g_mix.half(g_fc2.parts[0][1])
+    g_mix.swap()
+    ring_top.append(send("z", ring_top[-1]))
     after_self, normed_two, cross_queries = dense_call(
         middle_kernel, "self_out_cross_q", place,
         [full(tokens), full(now(self_mixed)), full(vectors)] + matrix(g_mix, 0) + matrix(g_mix, 1),
@@ -989,27 +1147,28 @@
     cross_mixed, cross_lse = cross_forward(
         local_map, row_lengths, segment_ids, cross_queries, mem_keys, mem_values
     )
-    tick(cross_mixed, ring_a[-1], *g_fc1.corner())
-    g_fc1.close()
+    tick(cross_mixed, ring_top[-1], *came)
+
+    came = exchange(grid, low, None)
+    for _ in range(steps - 2):
+        ring_top.append(send("z", ring_top[-1]))
+    g_fc1.half()
+    g_fc1.swap()
     after_cross, normed_three = dense_call(
         cross_out_kernel, "cross_out", place,
         [full(after_self), full(now(cross_mixed)), full(vectors)] + matrix(g_mix, 2),
         [result(wide_row, F32), result(wide_row, BF16)],
     )
-
-    g_fc1.half()
-    for _ in range(steps - 2):
-        ring_b.append(send("z", ring_b[-1]))
-    tick(g_fc1.swap(), normed_three, ring_b[-1])
-    g_fc2.set_ring([jnp.concatenate(ab, axis=1) for ab in zip(ring_a, ring_b)])
-    g_fc2.half()
     hidden = up_bias.shape[1]
     activated, slope = dense_call(
         up_kernel, "fc1_gelu", place,
-        [full(now(normed_three)), full(up_bias)] + by_y(g_fc1),
-        [result((token_count, hidden), BF16), result((token_count, hidden), F32)], grid=(2,),
-    )
-    tick(activated, g_fc2.swap())
+        [full(normed_three), full(up_bias)] + by_y(g_fc1),
+        [result((token_count, hidden), BF16)] * 2, grid=(2,),
+    )
+    tick(activated, ring_top[-1], *came)
+    spread = [(0, 0), (1, 0), (0, 1), (1, 1)]
+    for step, array in enumerate(ring_top):
+        g_fc2.put([(step, dx, dy) for dx, dy in spread], array, 0, part, 0)
 
     def settle(pairs, shard):
         part_rows, part_cols = shard.shape
@@ -1021,7 +1180,11 @@
 
     one_row = result((1, D), F32)
     r_fc2 = settle([(now(activated), cotangent)], fc2)
-    tick(r_fc2.far())
+    r_fc2.far()
+    r_fc2.swap()
+    g_fc2.half()
+    g_fc2.swap()
+    tick(r_fc2.near(), g_fc2.other)
     slab = hidden // 4
     some = lambda array: (array, (token_count, slab), lambda s, *_: (0, s))
     grad_pre, grad_up_bias = dense_call(
@@ -1031,12 +1194,12 @@
             some(jax.ShapeDtypeStruct((token_count, hidden), BF16)),
             (jax.ShapeDtypeStruct((1, hidden), F32), (1, slab), lambda s, *_: (0, s)),
         ],
-        grid=(4,),
-    )
-    tick(r_fc2.swap(), grad_pre)
-    grad_pre = now(grad_pre)
+        grid=(4,), params=FULL_VMEM,
+    )
     r_fc1 = settle([(normed_three, grad_pre)], fc1)
-    tick(r_fc2.near(), r_fc1.far())
+    tick(r_fc1.far(), *r_fc2.across())
+    r_fc2.add()
+    r_fc1.swap()
     (
         grad_after_cross, grad_branch_two, grad_cross_mixed,
         grad_gain_three, grad_bias_eight, grad_bias_seven, grad_bias_nine,
@@ -1045,65 +1208,63 @@
         [full(now(grad_pre)), full(cotangent), full(after_cross), full(vectors)]
         + by_y(g_fc1) + matrix(g_mix, 2),
         [result(wide_row, F32), result(wide_row, BF16), result(wide_row, BF16)] + [one_row] * 4,
-        grid=(2,), scratch=[pltpu.VMEM(wide_row, F32)],
-    )
-    tick(r_fc1.swap(), grad_cross_mixed, *r_fc2.across())
-    tick(r_fc1.near(), r_fc2.add())
-
-    grad_cq, grad_ck, grad_cv = cross_backward(
+        grid=(2,), scratch=[pltpu.VMEM(wide_row, F32)], params=FULL_VMEM,
+    )
+    tick(r_fc1.near(), grad_cross_mixed, *r_fc2.pairs())
+    ring_fc2 = RingSum(grid, [r_fc2])
+
+    grad_cq, grad_ck, grad_cv, grad_bias_six = cross_backward(
         local_map, row_lengths, segment_ids, cross_queries, mem_keys, mem_values,
         now(grad_cross_mixed), cross_lse,
     )
-    tick(grad_cq, *r_fc2.pairs())
-    ring_fc2 = RingSum(grid, [r_fc2])
+    tick(grad_cq, ring_fc2.step(), *r_fc1.across())
+    r_fc1.add()
     grad_cq = now(grad_cq)
-    r_mem = Reduce(
+    cross_pairs = [(cross_mixed, grad_branch_two), (normed_two, grad_cq)]
+    r_cross = Reduce(
         grid, place,
-        lambda from_c: memory_terms(grid, place, memory, now((grad_ck, grad_cv)), rows, cols, from_c),
+        lambda from_c: memory_terms(
+            grid, place, memory, (grad_ck, grad_cv), cross_pairs, rows, cols, from_c
+        ),
         rows,
     )
-    r_cross = settle([(cross_mixed, grad_branch_two), (normed_two, grad_cq)], cross_q)
-    tick(ring_fc2.step(), r_cross.far(), r_mem.far(), *r_fc1.across())
-    tick(r_fc1.add())
-
-    ring_fc2.step()
+    r_cross.far()
+    r_cross.swap()
     (
         grad_after_self, grad_branch_one, grad_self_mixed,
         grad_gain_two, grad_bias_four, grad_bias_three, grad_bias_five,
     ) = dense_call(
         middle_back_kernel, "cross_q_norm_back", place,
-        [full(now(grad_cq)), full(grad_after_cross), full(after_self), full(vectors)]
+        [full(grad_cq), full(grad_after_cross), full(after_self), full(vectors)]
         + matrix(g_mix, 1) + matrix(g_mix, 0),
         [result(wide_row, F32), result(wide_row, BF16), result(wide_row, BF16)] + [one_row] * 4,
-    )
+        params=FULL_VMEM,
+    )
+    tick(r_cross.near(), grad_self_mixed, ring_fc2.step(), *r_fc1.pairs())
+    ring_fc1 = RingSum(grid, [r_fc1])
+
     grad_sq, grad_sk, grad_sv = self_backward(
-        segment_ids, self_queries, self_keys, self_values, grad_self_mixed, self_lse
+        segment_ids, self_queries, self_keys, self_values, now(grad_self_mixed), self_lse
     )
     r_self = settle(
         [(normed_one, grad_sq), (normed_one, grad_sk), (normed_one, grad_sv), (self_mixed, grad_branch_one)],
         cross_q,
     )
-    tick(r_cross.swap(), r_mem.swap(), r_self.far(), ring_fc2.step(), *r_fc1.pairs())
+    tick(r_self.far(), ring_fc2.step(), *r_cross.across())
     ring_fc2.step()
-    ring_fc1 = RingSum(grid, [r_fc1])
-    tick(r_cross.near(), r_mem.near())
+    r_cross.add()
+    r_self.swap()
     grad_tokens, grad_gain_one, grad_bias_zero, grad_bias_one, grad_bias_two = dense_call(
         first_back_kernel, "self_qkv_norm_back", place,
         [full(tokens), full(grad_after_self)] + [full(d) for d in now((grad_sq, grad_sk, grad_sv))]
         + [full(vectors)] + matrix(g_qkv, 0) + matrix(g_qkv, 1) + matrix(g_qkv, 2),
         [result(wide_row, BF16)] + [one_row] * 4,
-    )
-    tick(r_self.swap(), ring_fc1.step(), grad_tokens, *r_cross.across(), *r_mem.across())
-    tick(r_cross.add(), r_mem.add(), r_self.near())
+        params=FULL_VMEM,
+    )
     ring_fc1.step()
-    grad_memory, grad_bias_six = dense_call(
-        memory_back_kernel, "memory_back", place,
-        [by_memory(a) for a in now((grad_ck, grad_cv))] + matrix(g_ckv, 0) + matrix(g_ckv, 1),
-        [by_memory(mem_shape), one_row], grid=(mem_count,),
-    )
-    tick(ring_fc1.step(), grad_memory, *r_cross.pairs(), *r_mem.pairs())
-    ring_fc1.step()
-    ring_cross = RingSum(grid, [r_cross, r_mem])
+    ring_fc1.step(grad_tokens)
+    tick(r_self.near(), grad_tokens, ring_fc1.came, *r_cross.pairs())
+    ring_cross = RingSum(grid, [r_cross])
 
     def by_device(array):
         return array.reshape(array.shape[0], devices, -1).transpose(1, 0, 2).reshape(devices, -1)
@@ -1125,27 +1286,31 @@
         axis=1,
     )
     small_sum = SmallSum(grid, place, now(small_grads))
+    (grad_memory,) = dense_call(
+        memory_back_kernel, "memory_back", place,
+        [by_memory(a) for a in now((grad_ck, grad_cv))] + matrix(g_ckv, 0) + matrix(g_ckv, 1),
+        [by_memory(mem_shape)], grid=(mem_count,), params=FULL_VMEM,
+    )
+    ring_fc1.step()
+    tick(grad_memory, ring_fc1.came, ring_cross.step(), small_sum.step(), *r_self.across())
+    r_self.add()
     (layer_out,) = dense_call(
         down_kernel, "fc2", place,
         [full(after_cross), full(now(activated)), full(vectors)] + by_y(g_fc2),
-        [result(wide_row, BF16)], grid=(2,),
-    )
-    tick(ring_cross.step(), layer_out, small_sum.step(), *r_self.across())
-    tick(r_self.add())
+        [result(wide_row, BF16)], grid=(2,), params=FULL_VMEM,
+    )
     ring_cross.step()
-    tick(ring_cross.step(), small_sum.step(), *r_self.pairs())
-    for _ in range(steps - 3):
-        ring_cross.step()
-    ring_cross.step()
+    ring_cross.step(layer_out)
+    tick(layer_out, ring_cross.came, small_sum.step(), *r_self.pairs())
+    ring_fc1.step()
     ring_self = RingSum(grid, [r_self])
     for _ in range(steps):
         tick(ring_self.step(), small_sum.step())
-    ring_self.step()
+    for ring in (ring_fc2, ring_fc1, ring_cross, ring_self):
+        while ring.done < grid.ring:
+            ring.step()
     while small_sum.done < steps + 3:
         tick(small_sum.step())
-    for ring in (ring_fc2, ring_fc1):
-        while ring.done < grid.ring:
-            ring.step()
     small_shard = small_sum.result()
     came_cross, came_self = ring_cross.came, ring_self.came
     return (

time: 594 us -> 531 us (0.89)
  waiting for transfers between devices: 160 us -> 128 us
  local copies, waits for them, and re-layouts: 84.5 us -> 57.5 us
  other arithmetic: 42.8 us -> 25.1 us
  Pallas kernels: 235 us -> 252 us
    ppermute x83 -> x74, waiting for transfers between devices: 160 us -> 128 us  [send(): return lax.ppermute(self.clock.now(array), AXES, self.perms[name])]
    pallas_call x12 -> x23, Pallas kernels: 62.7 us -> 88.1 us  [the longest x2 31.2 us: memory_terms(): pl.pallas_call(functools.partial(memory_terms_kernel, near, len(pairs)),...]
    concatenate x15 -> x0, other arithmetic: 13.3 us -> none  [the longest x5 6.78 us: join(): self.parts = [(labels, jnp.concatenate([a for _, a in self.parts], axis=0))]]
    slice x18 -> x2, local copies, waits for them, and re-layouts: 14.1 us -> 0.92 us  [the longest x1 0.91 us: small_rows(): self.other[:, first:]]
    optimization_barrier x5 -> x2, local copies, waits for them, and re-layouts: 9.66 us -> 2.58 us  [tie(): return lax.optimization_barrier((values, after))[0]]
    convert_element_type x11 -> x12, other arithmetic: 14.8 us -> 17.4 us  [step(): self.came = self.grid.send('z', total.astype(BF16))]
    pallas_call x8 -> x6, Pallas kernels: 38 us -> 40.2 us  [token_terms(): pl.pallas_call(kernel, grid_spec=pltpu.PrefetchScalarGridSpec(num_scalar_...]
    ppermute x83 -> x74, starting transfers between devices: 58.5 us -> 56.9 us  [send(): return lax.ppermute(self.clock.now(array), AXES, self.perms[name])]
  transfers between devices with their start and end apart: 83 -> 74, of which waited for: 33 -> 29; matrix products, arithmetic and copies ran while one was open for 16% -> 9% of each run, Pallas kernels for 30% -> 38%
where the time goes in v3:
time: 531 us; the launch traced here: 521 us
  Pallas kernels  252 us (47%)
  waiting for transfers between devices  128 us (24%)
  local copies, waits for them, and re-layouts  57.5 us (11%)
  starting transfers between devices  56.9 us (11%)
  other arithmetic  25.1 us (5%)
    ppermute x74, waiting for transfers between devices, send(): return lax.ppermute(self.clock.now(array), AXES, self.perms[name])  128 us
    pallas_call x11, Pallas kernels, dense_call(): pl.pallas_call(kernel, grid_spec=pltpu.PrefetchScalarGridSpec(num_scalar_...  85.2 us
    ppermute x74, starting transfers between devices, send(): return lax.ppermute(self.clock.now(array), AXES, self.perms[name])  56.9 us
    unnamed x207, local copies, waits for them, and re-layouts  44.1 us
    pallas_call x6, Pallas kernels, token_terms(): pl.pallas_call(kernel, grid_spec=pltpu.PrefetchScalarGridSpec(num_scalar_...  40.2 us
    pallas_call x2, Pallas kernels, memory_terms(): pl.pallas_call(functools.partial(memory_terms_kernel, near, len(pairs)),...  31.2 us
    pallas_call x11, Pallas kernels, run(): pl.pallas_call(functools.partial(rearrange_kernel, self.moves, len(self.i...  23.4 us
    pallas_call x1, Pallas kernels, cross_backward(): pl.pallas_call(cross_bwd_kernel, grid_spec=pltpu.PrefetchScalarGridSpec(n...  19.9 us
  transfers between devices with their start and end apart: 74, of which 29 were waited for; matrix products, arithmetic and copies ran while one was open for 9% of the time, Pallas kernels for 38%

profile of v3, /device:TPU:0, one launch (start us, length us, event | category | flops | bytes accessed | tf_op | source)
XLA Modules:
  0.0 521.4 jit_solution(6823288380393326402)
XLA Ops:
  2.9 3.1 collective-permute-start
  10.4 3.9 copy.79._
  14.4 2.1 copy-done.2
  21.9 5.9 %collective-permute-done.4.refs_3_ = bf16[1,16,256]{2,1,0:T(8,128)(2,1)S(1)} collective-permute-done((bf16[1,16,256]{2,1,0:T(8,128)(2,1)S(1)}, bf16[1,16,256]{2,1,0:T(8,128)(2,1)S(1)}, u32[]{:S(2)}, u32[]{:S(2)}) %collective-permute-start.4) | collective-permute-done | bytes 8224 | tf_op jit(solution)/shard_map/ppermute | solution.py:309
  29.3 8.3 %collective-permute-done.8.refs_5_ = bf16[1,16,256]{2,1,0:T(8,128)(2,1)S(1)} collective-permute-done((bf16[1,16,256]{2,1,0:T(8,128)(2,1)S(1)}, bf16[1,16,256]{2,1,0:T(8,128)(2,1)S(1)}, u32[]{:S(2)}, u32[]{:S(2)}) %collective-permute-start.8) | collective-permute-done | bytes 8224 | tf_op jit(solution)/shard_map/ppermute | solution.py:309
  37.6 5.4 %collective-permute-done.11.refs_7_ = bf16[1,16,256]{2,1,0:T(8,128)(2,1)S(1)} collective-permute-done((bf16[1,16,256]{2,1,0:T(8,128)(2,1)S(1)}, bf16[1,16,256]{2,1,0:T(8,128)(2,1)S(1)}, u32[]{:S(2)}, u32[]{:S(2)}) %collective-permute-start.11) | collective-permute-done | bytes 8224 | tf_op jit(solution)/shard_map/ppermute | solution.py:309
  47.1 12.5 %collective-permute-done.10.refs_3_ = bf16[1,384,256]{2,1,0:T(8,128)(2,1)S(1)} collective-permute-done((bf16[1,384,256]{2,1,0:T(8,128)(2,1)S(1)}, bf16[1,384,256]{2,1,0:T(8,128)(2,1)S(1)}, u32[]{:S(2)}, u32[]{:S(2)}) %collective-permute-start.10) | collective-permute-done | bytes 196640 | tf_op jit(solution)/shard_map/ppermute | solution.py:309
  59.6 4.2 rearrange.17
  66.4 8.9 %collective-permute-done.15.refs_4_ = bf16[1,384,256]{2,1,0:T(8,128)(2,1)S(1)} collective-permute-done((bf16[1,384,256]{2,1,0:T(8,128)(2,1)S(1)}, bf16[1,384,256]{2,1,0:T(8,128)(2,1)S(1)}, u32[]{:S(2)}, u32[]{:S(2)}) %collective-permute-start.15) | collective-permute-done | bytes 196640 | tf_op jit(solution)/shard_map/ppermute | solution.py:309
  79.6 3.3 collective-permute-done.16.refs_5_
  86.6 5.0 rearrange.18
  93.9 3.2 half_weights.5.k_own.v_own
  99.4 2.2 collective-permute-done.20.k_other.v_other
  106.4 2.4 copy-done.3
  108.8 13.9 %memory_keys_values.1 = (bf16[4,588,1024]{2,1,0:T(8,128)(2,1)S(1)}, bf16[4,588,1024]{2,1,0:T(8,128)(2,1)S(1)}) custom-call(s32[4]{0:T(128)S(1)} %pad_add_fusion.place, bf16[4,588,1024]{2,1,0:T(8,128)(2,1)S(1)} %copy-done.3, f32[13,1024]{1,0:T(8,128)S(1)} %reshape.468.vectors, bf16[2,2176,256]{2,1,0:T(8,128)(2,1)S(1)} %half_weights.5.k_own.v_own, ...), custom_call_target="tpu_custom_call" | custom-call | flops 1000000 | bytes 100000 | tf_op jit(solution)/shard_map/memory_keys_values/pallas_call | solution.py:958
  122.7 3.1 collective-permute-done.21.refs_1_.refs_3_
  127.1 3.5 rearrange.19
  132.9 3.4 half_weights.6.refs_0_.refs_2_.refs_4_
  138.8 3.4 collective-permute-done.23.refs_1_.refs_3_.refs_5_
  143.2 4.7 self_qkv.1
  151.9 2.5 collective-permute-done.24.refs_6_
  154.4 16.3 %collective-permute-done.25.refs_1_.refs_3_ = bf16[4,704,256]{2,1,0:T(8,128)(2,1)} collective-permute-done((bf16[4,704,256]{2,1,0:T(8,128)(2,1)}, bf16[4,704,256]{2,1,0:T(8,128)(2,1)}, u32[]{:S(2)}, u32[]{:S(2)}) %collective-permute-start.25) | collective-permute-done | bytes 1441824 | tf_op jit(solution)/shard_map/ppermute | solution.py:309
  171.0 3.2 rearrange.20
  174.3 2.8 half_weights.7.so_own.cq_own.own.co_own
  180.2 2.8 collective-permute-done.27.so_other.cq_other.other.co_other
  185.1 3.9 self_out_cross_q.1
  191.6 12.5 %cross_forward.1 = (bf16[256,1024]{1,0:T(8,128)(2,1)}, f32[2,8,256]{2,1,0:T(8,128)}) custom-call(s32[4]{0:T(128)} %copy-done.96, s32[4]{0:T(128)} %select_reduce_fusion.len_ref, s32[2,1,128]{2,1,0:T(1,128)} %bitcast.132, s32[2,128,1]{2,1,0:T(8,128)} %copy-done.30, bf16[256,1024]{1,0:T(8,128)(2,1)} %copy-done.36, bf16[4,588,1024]{2,1,0:T(8,128)(2,1)} %copy-done.6, ...), custom_call_target="tpu_custom_call" | custom-call | flops 1000000 | bytes 100000 | tf_op jit(solution)/shard_map/cross_forward/pallas_call | solution.py:228
  204.3 3.2 half_weights.8.own
  207.9 2.8 rearrange.21
  212.9 2.9 cross_out.1
  215.9 4.9 fc1_gelu.1
  225.1 6.0 %weight_terms.6 = bf16[1,2,4096,256]{3,2,1,0:T(8,128)(2,1)} custom-call(s32[4]{0:T(128)} %copy-done.53, bf16[256,4096]{1,0:T(8,128)(2,1)} %copy-done.9, bf16[256,1024]{1,0:T(8,128)(2,1)} %grad_out.1), custom_call_target="tpu_custom_call" | custom-call | flops 1000000 | bytes 100000 | tf_op jit(solution)/shard_map/weight_terms/pallas_call | solution.py:585
  231.1 5.2 half_weights.9.own
  238.6 7.7 %weight_terms.7 = (bf16[1,4,256,256]{3,2,1,0:T(8,128)(2,1)}, bf16[1,4,256,256]{3,2,1,0:T(8,128)(2,1)}, bf16[1,4,512,256]{3,2,1,0:T(8,128)(2,1)}, bf16[1,4,512,256]{3,2,1,0:T(8,128)(2,1)}, f32[1,4,512,256]{3,2,1,0:T(8,128)}) custom-call(s32[4]{0:T(128)} %copy-done.53, bf16[256,4096]{1,0:T(8,128)(2,1)} %copy-done.9, bf16[256,1024]{1,0:T(8,128)(2,1)} %grad_out.1, ...), custom_call_target="tpu_custom_call" | custom-call | flops 1000000 | bytes 100000 | tf_op jit(solution)/shard_map/weight_terms/pallas_call | solution.py:585
  248.4 8.0 %fc2_gelu_back.1 = (bf16[256,4096]{1,0:T(8,128)(2,1)}, f32[1,4096]{1,0:T(1,128)}) custom-call(s32[4]{0:T(128)} %copy-done.53, bf16[256,1024]{1,0:T(8,128)(2,1)} %grad_out.1, bf16[256,4096]{1,0:T(8,128)(2,1)} %copy-done.40, bf16[2,4096,256]{2,1,0:T(8,128)(2,1)} %half_weights.9.own, bf16[2,4096,256]{2,1,0:T(8,128)(2,1)} %collective-permute-done.36.other), custom_call_target="tpu_custom_call" | custom-call | flops 1000000 | bytes 100000 | tf_op jit(solution)/shard_map/fc2_gelu_back/pallas_call | solution.py:958
  256.3 6.1 %weight_terms.8 = bf16[1,2,1024,1024]{3,2,1,0:T(8,128)(2,1)} custom-call(s32[4]{0:T(128)} %copy-done.53, bf16[256,1024]{1,0:T(8,128)(2,1)} %copy-done.25, bf16[256,4096]{1,0:T(8,128)(2,1)} %get-tuple-element.493.refs_1_.grad_pre), custom_call_target="tpu_custom_call" | custom-call | flops 1000000 | bytes 100000 | tf_op jit(solution)/shard_map/weight_terms/pallas_call | solution.py:585
  263.4 3.9 add_corners.4
  269.5 10.2 %fc1_norm_back.1 = (f32[256,1024]{1,0:T(8,128)}, bf16[256,1024]{1,0:T(8,128)(2,1)}, bf16[256,1024]{1,0:T(8,128)(2,1)}, f32[1,1024]{1,0:T(1,128)}, f32[1,1024]{1,...) custom-call(s32[4]{0:T(128)} %copy-done.53, bf16[256,4096]{1,0:T(8,128)(2,1)} %get-tuple-element.493.refs_1_.grad_pre, ...), custom_call_target="tpu_custom_call" | custom-call | flops 1000000 | bytes 100000 | tf_op jit(solution)/shard_map/fc1_norm_back/pallas_call | solution.py:958
  279.7 7.8 %weight_terms.9 = (bf16[1,4,64,1024]{3,2,1,0:T(8,128)(2,1)}, bf16[1,4,64,1024]{3,2,1,0:T(8,128)(2,1)}, bf16[1,4,128,1024]{3,2,1,0:T(8,128)(2,1)}, bf16[1,4,128,1024]{3,2,1,0:T(8,128)(2,1)}, f32[1,4,128,1024]{3,2,1,0:T(8,128)}) custom-call(s32[4]{0:T(128)} %copy-done.53, bf16[256,1024]{1,0:T(8,128)(2,1)} %copy-done.25, ...), custom_call_target="tpu_custom_call" | custom-call | flops 1000000 | bytes 100000 | tf_op jit(solution)/shard_map/weight_terms/pallas_call | solution.py:585
  287.5 4.8 collective-permute-done.41
  296.9 19.9 %cross_backward.1 = (bf16[256,1024]{1,0:T(8,128)(2,1)}, bf16[4,588,1024]{2,1,0:T(8,128)(2,1)}, bf16[4,588,1024]{2,1,0:T(8,128)(2,1)}, f32[1,1024]{1,0:T(1,128)}) custom-call(s32[4]{0:T(128)} %copy-done.96, s32[4]{0:T(128)} %select_reduce_fusion.len_ref, s32[2,1,128]{2,1,0:T(1,128)} %bitcast.133, s32[2,128,1]{2,1,0:T(8,128)} %copy-done.30, ...), custom_call_target="tpu_custom_call" | custom-call | flops 1000000 | bytes 100000 | tf_op jit(solution)/shard_map/cross_backward/pallas_call | solution.py:250
  316.8 14.7 %memory_terms.2 = bf16[4,2,1024,256]{3,2,1,0:T(8,128)(2,1)} custom-call(s32[4]{0:T(128)} %copy-done.53, bf16[4,588,1024]{2,1,0:T(8,128)(2,1)} %copy-done.2, bf16[4,588,1024]{2,1,0:T(8,128)(2,1)} %get-tuple-element.564.dk.gk, bf16[4,588,1024]{2,1,0:T(8,128)(2,1)} %get-tuple-element.565.dv.gv, bf16[256,1024]{1,0:T(8,128)(2,1)} %get-tuple-element.442.mixed.refs_0_, ...), custom_call_target="tpu_custom_call" | custom-call | flops 1000000 | bytes 100000 | tf_op jit(solution)/shard_map/memory_terms/pallas_call | solution.py:646
  331.5 4.0 add_corners.5
  339.3 6.4 %cross_q_norm_back.1 = (f32[256,1024]{1,0:T(8,128)}, bf16[256,1024]{1,0:T(8,128)(2,1)}, bf16[256,1024]{1,0:T(8,128)(2,1)}, f32[1,1024]{1,0:T(1,128)}, f32[1,1024...) custom-call(s32[4]{0:T(128)} %copy-done.53, bf16[256,1024]{1,0:T(8,128)(2,1)} %get-tuple-element.516.grad_queries.refs_3_, ...), custom_call_target="tpu_custom_call" | custom-call | flops 1000000 | bytes 100000 | tf_op jit(solution)/shard_map/cross_q_norm_back/pallas_call | solution.py:958
  345.7 16.5 %memory_terms.3 = (bf16[4,4,64,256]{3,2,1,0:T(8,128)(2,1)}, bf16[4,4,64,256]{3,2,1,0:T(8,128)(2,1)}, bf16[4,4,128,256]{3,2,1,0:T(8,128)(2,1)}, bf16[4,4,128,256]{3,2,1,0:T(8,128)(2,1)}, f32[4,4,128,256]{3,2,1,0:T(8,128)}) custom-call(s32[4]{0:T(128)} %copy-done.53, bf16[4,588,1024]{2,1,0:T(8,128)(2,1)} %copy-done.2, ...), custom_call_target="tpu_custom_call" | custom-call | flops 1000000 | bytes 100000 | tf_op jit(solution)/shard_map/memory_terms/pallas_call | solution.py:646
  365.1 3.3 collective-permute-start.49
  368.3 4.1 self_backward.1
  372.5 5.5 %weight_terms.10 = bf16[4,2,1024,256]{3,2,1,0:T(8,128)(2,1)} custom-call(s32[4]{0:T(128)} %copy-done.53, bf16[256,1024]{1,0:T(8,128)(2,1)} %copy-done.8, bf16[256,1024]{1,0:T(8,128)(2,1)} %get-tuple-element.548.refs_1_.gq, bf16[256,1024]{1,0:T(8,128)(2,1)} %copy-done.8, bf16[256,1024]{1,0:T(8,128)(2,1)} %get-tuple-element.549.refs_3_.gk, ...), custom_call_target="tpu_custom_call" | custom-call | flops 1000000 | bytes 100000 | tf_op jit(solution)/shard_map/weight_terms/pallas_call | solution.py:585
  378.1 4.0 add_corners.6
  389.1 7.5 %self_qkv_norm_back.1 = (bf16[256,1024]{1,0:T(8,128)(2,1)}, f32[1,1024]{1,0:T(1,128)}, f32[1,1024]{1,0:T(1,128)}, f32[1,1024]{1,0:T(1,128)}, f32[1,1024]{1,0:T(1,128)}) custom-call(s32[4]{0:T(128)} %copy-done.53, bf16[256,1024]{1,0:T(8,128)(2,1)} %tokens.4, f32[256,1024]{1,0:T(8,128)} %get-tuple-element.547.grad_after, ...), custom_call_target="tpu_custom_call" | custom-call | flops 1000000 | bytes 100000 | tf_op jit(solution)/shard_map/self_qkv_norm_back/pallas_call | solution.py:958
  402.7 6.6 %collective-permute-done.56 = bf16[4,4,128,256]{3,2,1,0:T(8,128)(2,1)} collective-permute-done((bf16[4,4,128,256]{3,2,1,0:T(8,128)(2,1)}, bf16[4,4,128,256]{3,2,1,0:T(8,128)(2,1)}, u32[]{:S(2)}, u32[]{:S(2)}) %collective-permute-start.56) | collective-permute-done | bytes 1048608 | tf_op jit(solution)/shard_map/ppermute | solution.py:309
  410.8 7.1 %weight_terms.11 = (bf16[4,4,64,256]{3,2,1,0:T(8,128)(2,1)}, bf16[4,4,64,256]{3,2,1,0:T(8,128)(2,1)}, bf16[4,4,128,256]{3,2,1,0:T(8,128)(2,1)}, bf16[4,4,128,256]{3,2,1,0:T(8,128)(2,1)}, f32[4,4,128,256]{3,2,1,0:T(8,128)}) custom-call(s32[4]{0:T(128)} %copy-done.53, bf16[256,1024]{1,0:T(8,128)(2,1)} %copy-done.8, ...), custom_call_target="tpu_custom_call" | custom-call | flops 1000000 | bytes 100000 | tf_op jit(solution)/shard_map/weight_terms/pallas_call | solution.py:585
  420.8 2.1 fusion.6
  426.5 15.7 %memory_back.1 = bf16[4,588,1024]{2,1,0:T(8,128)(2,1)} custom-call(s32[4]{0:T(128)} %copy-done.53, bf16[4,588,1024]{2,1,0:T(8,128)(2,1)} %get-tuple-element.564.dk.gk, bf16[4,588,1024]{2,1,0:T(8,128)(2,1)} %get-tuple-element.565.dv.gv, bf16[2,2176,256]{2,1,0:T(8,128)(2,1)} %copy-done.4, bf16[2,2176,256]{2,1,0:T(8,128)(2,1)} %collective-permute-done.20.k_other.v_other, ...), custom_call_target="tpu_custom_call" | custom-call | flops 1000000 | bytes 100000 | tf_op jit(solution)/shard_map/memory_back/pallas_call | solution.py:958
  443.3 4.0 add_corners.7
  450.8 2.1 fusion.4
  454.1 7.1 %fc2.1 = bf16[256,1024]{1,0:T(8,128)(2,1)} custom-call(s32[4]{0:T(128)} %copy-done.53, f32[256,1024]{1,0:T(8,128)} %copy-done.29, bf16[256,4096]{1,0:T(8,128)(2,1)} %copy-done.9, f32[13,1024]{1,0:T(8,128)} %copy-done.19, bf16[2,4096,256]{2,1,0:T(8,128)(2,1)} %half_weights.9.own, bf16[2,4096,256]{2,1,0:T(8,128)(2,1)} %collective-permute-done.36.other), custom_call_target="tpu_custom_call" | custom-call | flops 1000000 | bytes 100000 | tf_op jit(solution)/shard_map/fc2/pallas_call | solution.py:958
  464.6 10.2 %collective-permute-done.62 = f32[4,2,544]{2,1,0:T(2,128)S(1)} collective-permute-done((f32[4,2,544]{2,1,0:T(2,128)S(1)}, f32[4,2,544]{2,1,0:T(2,128)S(1)}, u32[]{:S(2)}, u32[]{:S(2)}) %collective-permute-start.62) | collective-permute-done | bytes 17440 | tf_op jit(solution)/shard_map/ppermute | solution.py:309
  478.0 2.4 collective-permute-done.67
  480.4 5.8 %collective-permute-done.68 = bf16[4,128,256]{2,1,0:T(8,128)(2,1)S(1)} collective-permute-done((bf16[4,128,256]{2,1,0:T(8,128)(2,1)S(1)}, bf16[4,128,256]{2,1,0:T(8,128)(2,1)S(1)}, u32[]{:S(2)}, u32[]{:S(2)}) %collective-permute-start.68) | collective-permute-done | bytes 262176 | tf_op jit(solution)/shard_map/ppermute | solution.py:309
  487.7 8.9 %collective-permute-done.69 = f32[544]{0:T(1024)S(1)} collective-permute-done((f32[544]{0:T(1024)S(1)}, f32[544]{0:T(1024)S(1)}, u32[]{:S(2)}, u32[]{:S(2)}) %collective-permute-start.69) | collective-permute-done | bytes 2208 | tf_op jit(solution)/shard_map/ppermute | solution.py:309
  500.0 8.3 %copy.105 = bf16[4,588,1024]{2,0,1:T(4,128)(2,1)} copy(bf16[4,588,1024]{2,1,0:T(8,128)(2,1)} %memory_back.1) | data formatting | bytes 9633792
  508.4 2.1 fusion.1
  510.5 3.3 collective-permute-done.71
  (392 shorter events, 127.2 us)
Async XLA Ops:
  2.9 14.3 %collective-permute-start = (bf16[1,640,256]{2,1,0:T(8,128)(2,1)S(1)}, bf16[1,640,256]{2,1,0:T(8,128)(2,1)S(1)}, u32[]{:S(2)}, u32[]{:S(2)}) collective-permute-start(bf16[1,640,256]{2,1,0:T(8,128)(2,1)S(1)} %rearrange.12.refs_0_.refs_2_), channel_id=1, source_target_pairs={{0,8},{1,9},{2,10},{3,11},{4,12},{5,13},{6,14},{7,15},{8,16},{9,17... | collective-permute-start | bytes 983048 | tf_op jit(solution)/shard_map/ppermute | solution.py:309
  7.3 9.9 %collective-permute-start.2 = (bf16[1,256,256]{2,1,0:T(8,128)(2,1)S(1)}, bf16[1,256,256]{2,1,0:T(8,128)(2,1)S(1)}, u32[]{:S(2)}, u32[]{:S(2)}) collective-permute-start(bf16[1,256,256]{2,1,0:T(8,128)(2,1)S(1)} %get-tuple-element.318), channel_id=1, source_target_pairs={{0,2},{1,3},{2,0},{3,1},{4,6},{5,7},{6,4},{7,5},{8,10},{9,11},{10,... | collective-permute-start | bytes 393224 | tf_op jit(solution)/shard_map/ppermute | solution.py:309
  8.9 8.3 %collective-permute-start.1 = (bf16[1,256,256]{2,1,0:T(8,128)(2,1)S(1)}, bf16[1,256,256]{2,1,0:T(8,128)(2,1)S(1)}, u32[]{:S(2)}, u32[]{:S(2)}) collective-permute-start(bf16[1,256,256]{2,1,0:T(8,128)(2,1)S(1)} %get-tuple-element.347.refs_0_), channel_id=1, source_target_pairs={{0,4},{1,5},{2,6},{3,7},{4,0},{5,1},{6,2},{7,3},{8,12},{9,13},{10,... | collective-permute-start | bytes 393224 | tf_op jit(solution)/shard_map/ppermute | solution.py:309
  17.2 10.7 %collective-permute-start.3 = (bf16[1,640,256]{2,1,0:T(8,128)(2,1)S(1)}, bf16[1,640,256]{2,1,0:T(8,128)(2,1)S(1)}, u32[]{:S(2)}, u32[]{:S(2)}) collective-permute-start(bf16[1,640,256]{2,1,0:T(8,128)(2,1)S(1)} %collective-permute-done.refs_2_.refs_3_), channel_id=1, source_target_pairs={{0,8},{1,9},{2,10},{3,11},{4,12},{5,13},{6,14},{7,15},{8,16},{9,17... | collective-permute-start | bytes 983048 | tf_op jit(solution)/shard_map/ppermute | solution.py:309
  19.0 8.8 %collective-permute-start.6 = (bf16[1,128,256]{2,1,0:T(8,128)(2,1)S(1)}, bf16[1,128,256]{2,1,0:T(8,128)(2,1)S(1)}, u32[]{:S(2)}, u32[]{:S(2)}) collective-permute-start(bf16[1,128,256]{2,1,0:T(8,128)(2,1)S(1)} %get-tuple-element.326), channel_id=1, source_target_pairs={{0,2},{1,3},{2,0},{3,1},{4,6},{5,7},{6,4},{7,5},{8,10},{9,11},{10,... | collective-permute-start | bytes 196616 | tf_op jit(solution)/shard_map/ppermute | solution.py:309
  19.6 8.3 %collective-permute-start.5 = (bf16[1,128,256]{2,1,0:T(8,128)(2,1)S(1)}, bf16[1,128,256]{2,1,0:T(8,128)(2,1)S(1)}, u32[]{:S(2)}, u32[]{:S(2)}) collective-permute-start(bf16[1,128,256]{2,1,0:T(8,128)(2,1)S(1)} %get-tuple-element.324), channel_id=1, source_target_pairs={{0,4},{1,5},{2,6},{3,7},{4,0},{5,1},{6,2},{7,3},{8,12},{9,13},{10,... | collective-permute-start | bytes 196616 | tf_op jit(solution)/shard_map/ppermute | solution.py:309
  27.9 9.7 %collective-permute-start.7 = (bf16[1,640,256]{2,1,0:T(8,128)(2,1)S(1)}, bf16[1,640,256]{2,1,0:T(8,128)(2,1)S(1)}, u32[]{:S(2)}, u32[]{:S(2)}) collective-permute-start(bf16[1,640,256]{2,1,0:T(8,128)(2,1)S(1)} %collective-permute-done.3.refs_4_), channel_id=1, source_target_pairs={{0,8},{1,9},{2,10},{3,11},{4,12},{5,13},{6,14},{7,15},{8,16},{9,17... | collective-permute-start | bytes 983048 | tf_op jit(solution)/shard_map/ppermute | solution.py:309
  27.9 9.6 %collective-permute-start.8 = (bf16[1,16,256]{2,1,0:T(8,128)(2,1)S(1)}, bf16[1,16,256]{2,1,0:T(8,128)(2,1)S(1)}, u32[]{:S(2)}, u32[]{:S(2)}) collective-permute-start(bf16[1,16,256]{2,1,0:T(8,128)(2,1)S(1)} %collective-permute-done.4.refs_3_), channel_id=1, source_target_pairs={{0,8},{1,9},{2,10},{3,11},{4,12},{5,13},{6,14},{7,15},{8,16},{9,17... | collective-permute-start | bytes 24584 | tf_op jit(solution)/shard_map/ppermute | solution.py:309
  44.6 15.0 %collective-permute-start.12 = (bf16[4,272,256]{2,1,0:T(8,128)(2,1)S(1)}, bf16[4,272,256]{2,1,0:T(8,128)(2,1)S(1)}, u32[]{:S(2)}, u32[]{:S(2)}) collective-permute-start(bf16[4,272,256]{2,1,0:T(8,128)(2,1)S(1)} %get-tuple-element.376.refs_0_), channel_id=1, source_target_pairs={{0,4},{1,5},{2,6},{3,7},{4,0},{5,1},{6,2},{7,3},{8,12},{9,13},{10,... | collective-permute-start | bytes 1671176 | tf_op jit(solution)/shard_map/ppermute | solution.py:309
  46.0 13.6 %collective-permute-start.13 = (bf16[4,272,256]{2,1,0:T(8,128)(2,1)S(1)}, bf16[4,272,256]{2,1,0:T(8,128)(2,1)S(1)}, u32[]{:S(2)}, u32[]{:S(2)}) collective-permute-start(bf16[4,272,256]{2,1,0:T(8,128)(2,1)S(1)} %get-tuple-element.343), channel_id=1, source_target_pairs={{0,2},{1,3},{2,0},{3,1},{4,6},{5,7},{6,4},{7,5},{8,10},{9,11},{10,... | collective-permute-start | bytes 1671176 | tf_op jit(solution)/shard_map/ppermute | solution.py:309
  47.1 12.5 %collective-permute-start.9 = (bf16[1,768,256]{2,1,0:T(8,128)(2,1)S(1)}, bf16[1,768,256]{2,1,0:T(8,128)(2,1)S(1)}, u32[]{:S(2)}, u32[]{:S(2)}) collective-permute-start(bf16[1,768,256]{2,1,0:T(8,128)(2,1)S(1)} %get-tuple-element.423.refs_2_), channel_id=1, source_target_pairs={{0,8},{1,9},{2,10},{3,11},{4,12},{5,13},{6,14},{7,15},{8,16},{9,17... | collective-permute-start | bytes 1179656 | tf_op jit(solution)/shard_map/ppermute | solution.py:309
  47.1 12.5 %collective-permute-start.10 = (bf16[1,384,256]{2,1,0:T(8,128)(2,1)S(1)}, bf16[1,384,256]{2,1,0:T(8,128)(2,1)S(1)}, u32[]{:S(2)}, u32[]{:S(2)}) collective-permute-start(bf16[1,384,256]{2,1,0:T(8,128)(2,1)S(1)} %get-tuple-element.371.refs_2_), channel_id=1, source_target_pairs={{0,8},{1,9},{2,10},{3,11},{4,12},{5,13},{6,14},{7,15},{8,16},{9,17... | collective-permute-start | bytes 589832 | tf_op jit(solution)/shard_map/ppermute | solution.py:309
  63.9 20.6 %collective-permute-start.18 = (bf16[4,528,256]{2,1,0:T(8,128)(2,1)}, bf16[4,528,256]{2,1,0:T(8,128)(2,1)S(1)}, u32[]{:S(2)}, u32[]{:S(2)}) collective-permute-start(bf16[4,528,256]{2,1,0:T(8,128)(2,1)} %get-tuple-element.361), channel_id=1, source_target_pairs={{0,2},{1,3},{2,0},{3,1},{4,6},{5,7},{6,4},{7,5},{8,10},{9,11},{10,... | collective-permute-start | bytes 3244040 | tf_op jit(solution)/shard_map/ppermute | solution.py:309
  64.9 19.6 %collective-permute-start.17 = (bf16[4,512,256]{2,1,0:T(8,128)(2,1)}, bf16[4,512,256]{2,1,0:T(8,128)(2,1)S(1)}, u32[]{:S(2)}, u32[]{:S(2)}) collective-permute-start(bf16[4,512,256]{2,1,0:T(8,128)(2,1)} %get-tuple-element.401.refs_0_), channel_id=1, source_target_pairs={{0,4},{1,5},{2,6},{3,7},{4,0},{5,1},{6,2},{7,3},{8,12},{9,13},{10,... | collective-permute-start | bytes 3145736 | tf_op jit(solution)/shard_map/ppermute | solution.py:309
  66.4 8.9 %collective-permute-start.15 = (bf16[1,384,256]{2,1,0:T(8,128)(2,1)S(1)}, bf16[1,384,256]{2,1,0:T(8,128)(2,1)S(1)}, u32[]{:S(2)}, u32[]{:S(2)}) collective-permute-start(bf16[1,384,256]{2,1,0:T(8,128)(2,1)S(1)} %collective-permute-done.10.refs_3_), channel_id=1, source_target_pairs={{0,8},{1,9},{2,10},{3,11},{4,12},{5,13},{6,14},{7,15},{8,16},{9,17... | collective-permute-start | bytes 589832 | tf_op jit(solution)/shard_map/ppermute | solution.py:309
  66.4 13.2 %collective-permute-start.14 = (bf16[1,768,256]{2,1,0:T(8,128)(2,1)S(1)}, bf16[1,768,256]{2,1,0:T(8,128)(2,1)}, u32[]{:S(2)}, u32[]{:S(2)}) collective-permute-start(bf16[1,768,256]{2,1,0:T(8,128)(2,1)S(1)} %collective-permute-done.9.refs_3_), channel_id=1, source_target_pairs={{0,8},{1,9},{2,10},{3,11},{4,12},{5,13},{6,14},{7,15},{8,16},{9,17... | collective-permute-start | bytes 1179656 | tf_op jit(solution)/shard_map/ppermute | solution.py:309
  97.2 28.6 %collective-permute-start.21 = (bf16[4,576,256]{2,1,0:T(8,128)(2,1)}, bf16[4,576,256]{2,1,0:T(8,128)(2,1)S(1)}, u32[]{:S(2)}, u32[]{:S(2)}) collective-permute-start(bf16[4,576,256]{2,1,0:T(8,128)(2,1)} %get-tuple-element.428.refs_0_), channel_id=1, source_target_pairs={{0,4},{1,5},{2,6},{3,7},{4,0},{5,1},{6,2},{7,3},{8,12},{9,13},{10,... | collective-permute-start | bytes 3538952 | tf_op jit(solution)/shard_map/ppermute | solution.py:309
  98.7 28.4 %collective-permute-start.22 = (bf16[4,576,256]{2,1,0:T(8,128)(2,1)}, bf16[4,576,256]{2,1,0:T(8,128)(2,1)}, u32[]{:S(2)}, u32[]{:S(2)}) collective-permute-start(bf16[4,576,256]{2,1,0:T(8,128)(2,1)} %get-tuple-element.387), channel_id=1, source_target_pairs={{0,2},{1,3},{2,0},{3,1},{4,6},{5,7},{6,4},{7,5},{8,10},{9,11},{10,... | collective-permute-start | bytes 3538952 | tf_op jit(solution)/shard_map/ppermute | solution.py:309
  99.4 23.3 %collective-permute-start.19 = (bf16[1,768,256]{2,1,0:T(8,128)(2,1)}, bf16[1,768,256]{2,1,0:T(8,128)(2,1)}, u32[]{:S(2)}, u32[]{:S(2)}) collective-permute-start(bf16[1,768,256]{2,1,0:T(8,128)(2,1)} %collective-permute-done.14.refs_4_), channel_id=1, source_target_pairs={{0,8},{1,9},{2,10},{3,11},{4,12},{5,13},{6,14},{7,15},{8,16},{9,17... | collective-permute-start | bytes 1179656 | tf_op jit(solution)/shard_map/ppermute | solution.py:309
  136.4 34.3 %collective-permute-start.25 = (bf16[4,704,256]{2,1,0:T(8,128)(2,1)}, bf16[4,704,256]{2,1,0:T(8,128)(2,1)}, u32[]{:S(2)}, u32[]{:S(2)}) collective-permute-start(bf16[4,704,256]{2,1,0:T(8,128)(2,1)} %get-tuple-element.450.refs_0_), channel_id=1, source_target_pairs={{0,4},{1,5},{2,6},{3,7},{4,0},{5,1},{6,2},{7,3},{8,12},{9,13},{10,... | collective-permute-start | bytes 4325384 | tf_op jit(solution)/shard_map/ppermute | solution.py:309
  137.1 33.9 %collective-permute-start.26 = (bf16[4,704,256]{2,1,0:T(8,128)(2,1)}, bf16[4,704,256]{2,1,0:T(8,128)(2,1)}, u32[]{:S(2)}, u32[]{:S(2)}) collective-permute-start(bf16[4,704,256]{2,1,0:T(8,128)(2,1)} %get-tuple-element.414), channel_id=1, source_target_pairs={{0,2},{1,3},{2,0},{3,1},{4,6},{5,7},{6,4},{7,5},{8,10},{9,11},{10,... | collective-permute-start | bytes 4325384 | tf_op jit(solution)/shard_map/ppermute | solution.py:309
  138.1 16.3 %collective-permute-start.24 = (bf16[4,256,256]{2,1,0:T(8,128)(2,1)}, bf16[4,256,256]{2,1,0:T(8,128)(2,1)}, u32[]{:S(2)}, u32[]{:S(2)}) collective-permute-start(bf16[4,256,256]{2,1,0:T(8,128)(2,1)} %rearrange.16.refs_5_), channel_id=1, source_target_pairs={{0,8},{1,9},{2,10},{3,11},{4,12},{5,13},{6,14},{7,15},{8,16},{9,17... | collective-permute-start | bytes 1572872 | tf_op jit(solution)/shard_map/ppermute | solution.py:309
  177.2 26.9 %collective-permute-start.29 = (bf16[4,512,256]{2,1,0:T(8,128)(2,1)}, bf16[4,512,256]{2,1,0:T(8,128)(2,1)}, u32[]{:S(2)}, u32[]{:S(2)}) collective-permute-start(bf16[4,512,256]{2,1,0:T(8,128)(2,1)} %get-tuple-element.477.refs_0_), channel_id=1, source_target_pairs={{0,4},{1,5},{2,6},{3,7},{4,0},{5,1},{6,2},{7,3},{8,12},{9,13},{10,... | collective-permute-start | bytes 3145736 | tf_op jit(solution)/shard_map/ppermute | solution.py:309
  178.7 25.5 %collective-permute-start.30 = (bf16[4,512,256]{2,1,0:T(8,128)(2,1)}, bf16[4,512,256]{2,1,0:T(8,128)(2,1)}, u32[]{:S(2)}, u32[]{:S(2)}) collective-permute-start(bf16[4,512,256]{2,1,0:T(8,128)(2,1)} %get-tuple-element.441), channel_id=1, source_target_pairs={{0,2},{1,3},{2,0},{3,1},{4,6},{5,7},{6,4},{7,5},{8,10},{9,11},{10,... | collective-permute-start | bytes 3145736 | tf_op jit(solution)/shard_map/ppermute | solution.py:309
  179.4 24.7 %collective-permute-start.28 = (bf16[4,256,256]{2,1,0:T(8,128)(2,1)}, bf16[4,256,256]{2,1,0:T(8,128)(2,1)}, u32[]{:S(2)}, u32[]{:S(2)}) collective-permute-start(bf16[4,256,256]{2,1,0:T(8,128)(2,1)} %collective-permute-done.24.refs_6_), channel_id=1, source_target_pairs={{0,8},{1,9},{2,10},{3,11},{4,12},{5,13},{6,14},{7,15},{8,16},{9,17... | collective-permute-start | bytes 1572872 | tf_op jit(solution)/shard_map/ppermute | solution.py:309
  207.5 8.4 %collective-permute-start.31 = (bf16[2,4096,256]{2,1,0:T(8,128)(2,1)S(1)}, bf16[2,4096,256]{2,1,0:T(8,128)(2,1)S(1)}, u32[]{:S(2)}, u32[]{:S(2)}) collective-permute-start(bf16[2,4096,256]{2,1,0:T(8,128)(2,1)S(1)} %half_weights.8.own), channel_id=1, source_target_pairs={{0,1},{1,0},{2,3},{3,2},{4,5},{5,4},{6,7},{7,6},{8,9},{9,8},{10,11... | collective-permute-start | bytes 12582920 | tf_op jit(solution)/shard_map/ppermute | solution.py:309
  207.6 16.7 %collective-permute-start.32 = (bf16[4,256,256]{2,1,0:T(8,128)(2,1)}, bf16[4,256,256]{2,1,0:T(8,128)(2,1)S(1)}, u32[]{:S(2)}, u32[]{:S(2)}) collective-permute-start(bf16[4,256,256]{2,1,0:T(8,128)(2,1)} %collective-permute-done.28.refs_7_), channel_id=1, source_target_pairs={{0,8},{1,9},{2,10},{3,11},{4,12},{5,13},{6,14},{7,15},{8,16},{9,17... | collective-permute-start | bytes 1572872 | tf_op jit(solution)/shard_map/ppermute | solution.py:309
  210.7 12.9 %collective-permute-start.34 = (bf16[4,128,256]{2,1,0:T(8,128)(2,1)S(1)}, bf16[4,128,256]{2,1,0:T(8,128)(2,1)S(1)}, u32[]{:S(2)}, u32[]{:S(2)}) collective-permute-start(bf16[4,128,256]{2,1,0:T(8,128)(2,1)S(1)} %get-tuple-element.463), channel_id=1, source_target_pairs={{0,2},{1,3},{2,0},{3,1},{4,6},{5,7},{6,4},{7,5},{8,10},{9,11},{10,... | collective-permute-start | bytes 786440 | tf_op jit(solution)/shard_map/ppermute | solution.py:309
  211.8 11.8 %collective-permute-start.33 = (bf16[4,128,256]{2,1,0:T(8,128)(2,1)S(1)}, bf16[4,128,256]{2,1,0:T(8,128)(2,1)S(1)}, u32[]{:S(2)}, u32[]{:S(2)}) collective-permute-start(bf16[4,128,256]{2,1,0:T(8,128)(2,1)S(1)} %get-tuple-element.461), channel_id=1, source_target_pairs={{0,4},{1,5},{2,6},{3,7},{4,0},{5,1},{6,2},{7,3},{8,12},{9,13},{10,... | collective-permute-start | bytes 786440 | tf_op jit(solution)/shard_map/ppermute | solution.py:309
  236.3 10.0 %collective-permute-start.36 = (bf16[2,4096,256]{2,1,0:T(8,128)(2,1)}, bf16[2,4096,256]{2,1,0:T(8,128)(2,1)}, u32[]{:S(2)}, u32[]{:S(2)}) collective-permute-start(bf16[2,4096,256]{2,1,0:T(8,128)(2,1)} %half_weights.9.own), channel_id=1, source_target_pairs={{0,1},{1,0},{2,3},{3,2},{4,5},{5,4},{6,7},{7,6},{8,9},{9,8},{10,11... | collective-permute-start | bytes 12582920 | tf_op jit(solution)/shard_map/ppermute | solution.py:309
  246.4 16.1 %collective-permute-start.37 = (bf16[1,4,256,256]{3,2,1,0:T(8,128)(2,1)}, bf16[1,4,256,256]{3,2,1,0:T(8,128)(2,1)S(1)}, u32[]{:S(2)}, u32[]{:S(2)}) collective-permute-start(bf16[1,4,256,256]{3,2,1,0:T(8,128)(2,1)} %get-tuple-element.490), channel_id=1, source_target_pairs={{0,4},{1,5},{2,6},{3,7},{4,0},{5,1},{6,2},{7,3},{8,12},{9,13},{10,... | collective-permute-start | bytes 1572872 | tf_op jit(solution)/shard_map/ppermute | solution.py:309
  247.6 14.9 %collective-permute-start.38 = (bf16[1,4,256,256]{3,2,1,0:T(8,128)(2,1)}, bf16[1,4,256,256]{3,2,1,0:T(8,128)(2,1)S(1)}, u32[]{:S(2)}, u32[]{:S(2)}) collective-permute-start(bf16[1,4,256,256]{3,2,1,0:T(8,128)(2,1)} %get-tuple-element.492), channel_id=1, source_target_pairs={{0,2},{1,3},{2,0},{3,1},{4,6},{5,7},{6,4},{7,5},{8,10},{9,11},{10,... | collective-permute-start | bytes 1572872 | tf_op jit(solution)/shard_map/ppermute | solution.py:309
  262.5 17.2 %collective-permute-start.39 = (bf16[1,2,1024,1024]{3,2,1,0:T(8,128)(2,1)}, bf16[1,2,1024,1024]{3,2,1,0:T(8,128)(2,1)}, u32[]{:S(2)}, u32[]{:S(2)}) collective-permute-start(bf16[1,2,1024,1024]{3,2,1,0:T(8,128)(2,1)} %weight_terms.8), channel_id=1, source_target_pairs={{0,1},{1,0},{2,3},{3,2},{4,5},{5,4},{6,7},{7,6},{8,9},{9,8},{10,11... | collective-permute-start | bytes 12582920 | tf_op jit(solution)/shard_map/ppermute | solution.py:309
  267.4 24.9 %collective-permute-start.41 = (bf16[1,4,512,256]{3,2,1,0:T(8,128)(2,1)}, bf16[1,4,512,256]{3,2,1,0:T(8,128)(2,1)S(1)}, u32[]{:S(2)}, u32[]{:S(2)}) collective-permute-start(bf16[1,4,512,256]{3,2,1,0:T(8,128)(2,1)} %get-tuple-element.504), channel_id=1, source_target_pairs={{0,2},{1,3},{2,0},{3,1},{4,6},{5,7},{6,4},{7,5},{8,10},{9,11},{10,... | collective-permute-start | bytes 3145736 | tf_op jit(solution)/shard_map/ppermute | solution.py:309
  268.6 24.7 %collective-permute-start.40 = (bf16[1,4,512,256]{3,2,1,0:T(8,128)(2,1)}, bf16[1,4,512,256]{3,2,1,0:T(8,128)(2,1)}, u32[]{:S(2)}, u32[]{:S(2)}) collective-permute-start(bf16[1,4,512,256]{3,2,1,0:T(8,128)(2,1)} %get-tuple-element.502), channel_id=1, source_target_pairs={{0,4},{1,5},{2,6},{3,7},{4,0},{5,1},{6,2},{7,3},{8,12},{9,13},{10,... | collective-permute-start | bytes 3145736 | tf_op jit(solution)/shard_map/ppermute | solution.py:309
  293.4 23.4 %collective-permute-start.43 = (bf16[1,4,64,1024]{3,2,1,0:T(8,128)(2,1)}, bf16[1,4,64,1024]{3,2,1,0:T(8,128)(2,1)}, u32[]{:S(2)}, u32[]{:S(2)}) collective-permute-start(bf16[1,4,64,1024]{3,2,1,0:T(8,128)(2,1)} %get-tuple-element.513), channel_id=1, source_target_pairs={{0,4},{1,5},{2,6},{3,7},{4,0},{5,1},{6,2},{7,3},{8,12},{9,13},{10,... | collective-permute-start | bytes 1572872 | tf_op jit(solution)/shard_map/ppermute | solution.py:309
  294.2 22.6 %collective-permute-start.44 = (bf16[1,4,64,1024]{3,2,1,0:T(8,128)(2,1)}, bf16[1,4,64,1024]{3,2,1,0:T(8,128)(2,1)}, u32[]{:S(2)}, u32[]{:S(2)}) collective-permute-start(bf16[1,4,64,1024]{3,2,1,0:T(8,128)(2,1)} %get-tuple-element.515), channel_id=1, source_target_pairs={{0,2},{1,3},{2,0},{3,1},{4,6},{5,7},{6,4},{7,5},{8,10},{9,11},{10,... | collective-permute-start | bytes 1572872 | tf_op jit(solution)/shard_map/ppermute | solution.py:309
  296.6 20.2 %collective-permute-start.42 = (bf16[1,512,256]{2,1,0:T(8,128)(2,1)S(1)}, bf16[1,512,256]{2,1,0:T(8,128)(2,1)S(1)}, u32[]{:S(2)}, u32[]{:S(2)}) collective-permute-start(bf16[1,512,256]{2,1,0:T(8,128)(2,1)S(1)} %fusion.10), channel_id=1, source_target_pairs={{0,8},{1,9},{2,10},{3,11},{4,12},{5,13},{6,14},{7,15},{8,16},{9,17... | collective-permute-start | bytes 786440 | tf_op jit(solution)/shard_map/ppermute | solution.py:309
  331.5 14.2 %collective-permute-start.45 = (bf16[4,2,1024,256]{3,2,1,0:T(8,128)(2,1)}, bf16[4,2,1024,256]{3,2,1,0:T(8,128)(2,1)}, u32[]{:S(2)}, u32[]{:S(2)}) collective-permute-start(bf16[4,2,1024,256]{3,2,1,0:T(8,128)(2,1)} %memory_terms.2), channel_id=1, source_target_pairs={{0,1},{1,0},{2,3},{3,2},{4,5},{5,4},{6,7},{7,6},{8,9},{9,8},{10,11... | collective-permute-start | bytes 12582920 | tf_op jit(solution)/shard_map/ppermute | solution.py:309
  335.5 26.7 %collective-permute-start.48 = (bf16[1,4,128,1024]{3,2,1,0:T(8,128)(2,1)}, bf16[1,4,128,1024]{3,2,1,0:T(8,128)(2,1)}, u32[]{:S(2)}, u32[]{:S(2)}) collective-permute-start(bf16[1,4,128,1024]{3,2,1,0:T(8,128)(2,1)} %get-tuple-element.532), channel_id=1, source_target_pairs={{0,2},{1,3},{2,0},{3,1},{4,6},{5,7},{6,4},{7,5},{8,10},{9,11},{10,... | collective-permute-start | bytes 3145736 | tf_op jit(solution)/shard_map/ppermute | solution.py:309
  336.2 26.0 %collective-permute-start.47 = (bf16[1,4,128,1024]{3,2,1,0:T(8,128)(2,1)}, bf16[1,4,128,1024]{3,2,1,0:T(8,128)(2,1)}, u32[]{:S(2)}, u32[]{:S(2)}) collective-permute-start(bf16[1,4,128,1024]{3,2,1,0:T(8,128)(2,1)} %get-tuple-element.530), channel_id=1, source_target_pairs={{0,4},{1,5},{2,6},{3,7},{4,0},{5,1},{6,2},{7,3},{8,12},{9,13},{10,... | collective-permute-start | bytes 3145736 | tf_op jit(solution)/shard_map/ppermute | solution.py:309
  338.3 23.8 %collective-permute-start.46 = (bf16[1,512,256]{2,1,0:T(8,128)(2,1)S(1)}, bf16[1,512,256]{2,1,0:T(8,128)(2,1)S(1)}, u32[]{:S(2)}, u32[]{:S(2)}) collective-permute-start(bf16[1,512,256]{2,1,0:T(8,128)(2,1)S(1)} %fusion.9), channel_id=1, source_target_pairs={{0,8},{1,9},{2,10},{3,11},{4,12},{5,13},{6,14},{7,15},{8,16},{9,17... | collective-permute-start | bytes 786440 | tf_op jit(solution)/shard_map/ppermute | solution.py:309
  362.2 15.8 %collective-permute-start.50 = (bf16[4,4,64,256]{3,2,1,0:T(8,128)(2,1)}, bf16[4,4,64,256]{3,2,1,0:T(8,128)(2,1)}, u32[]{:S(2)}, u32[]{:S(2)}) collective-permute-start(bf16[4,4,64,256]{3,2,1,0:T(8,128)(2,1)} %get-tuple-element.541), channel_id=1, source_target_pairs={{0,4},{1,5},{2,6},{3,7},{4,0},{5,1},{6,2},{7,3},{8,12},{9,13},{10,... | collective-permute-start | bytes 1572872 | tf_op jit(solution)/shard_map/ppermute | solution.py:309
  362.9 15.1 %collective-permute-start.51 = (bf16[4,4,64,256]{3,2,1,0:T(8,128)(2,1)}, bf16[4,4,64,256]{3,2,1,0:T(8,128)(2,1)}, u32[]{:S(2)}, u32[]{:S(2)}) collective-permute-start(bf16[4,4,64,256]{3,2,1,0:T(8,128)(2,1)} %get-tuple-element.543), channel_id=1, source_target_pairs={{0,2},{1,3},{2,0},{3,1},{4,6},{5,7},{6,4},{7,5},{8,10},{9,11},{10,... | collective-permute-start | bytes 1572872 | tf_op jit(solution)/shard_map/ppermute | solution.py:309
  365.1 12.9 %collective-permute-start.49 = (bf16[1,512,256]{2,1,0:T(8,128)(2,1)S(1)}, bf16[1,512,256]{2,1,0:T(8,128)(2,1)S(1)}, u32[]{:S(2)}, u32[]{:S(2)}) collective-permute-start(bf16[1,512,256]{2,1,0:T(8,128)(2,1)S(1)} %fusion.8), channel_id=1, source_target_pairs={{0,8},{1,9},{2,10},{3,11},{4,12},{5,13},{6,14},{7,15},{8,16},{9,17... | collective-permute-start | bytes 786440 | tf_op jit(solution)/shard_map/ppermute | solution.py:309
  378.0 32.8 %collective-permute-start.52 = (bf16[4,2,1024,256]{3,2,1,0:T(8,128)(2,1)}, bf16[4,2,1024,256]{3,2,1,0:T(8,128)(2,1)}, u32[]{:S(2)}, u32[]{:S(2)}) collective-permute-start(bf16[4,2,1024,256]{3,2,1,0:T(8,128)(2,1)} %weight_terms.10), channel_id=1, source_target_pairs={{0,1},{1,0},{2,3},{3,2},{4,5},{5,4},{6,7},{7,6},{8,9},{9,8},{10,11... | collective-permute-start | bytes 12582920 | tf_op jit(solution)/shard_map/ppermute | solution.py:309
  383.4 25.9 %collective-permute-start.56 = (bf16[4,4,128,256]{3,2,1,0:T(8,128)(2,1)}, bf16[4,4,128,256]{3,2,1,0:T(8,128)(2,1)}, u32[]{:S(2)}, u32[]{:S(2)}) collective-permute-start(bf16[4,4,128,256]{3,2,1,0:T(8,128)(2,1)} %get-tuple-element.563), channel_id=1, source_target_pairs={{0,2},{1,3},{2,0},{3,1},{4,6},{5,7},{6,4},{7,5},{8,10},{9,11},{10,... | collective-permute-start | bytes 3145736 | tf_op jit(solution)/shard_map/ppermute | solution.py:309
  384.1 25.4 %collective-permute-start.55 = (bf16[4,4,128,256]{3,2,0,1:T(8,128)(2,1)S(1)}, bf16[4,4,128,256]{3,2,0,1:T(8,128)(2,1)}, u32[]{:S(2)}, u32[]{:S(2)}) collective-permute-start(bf16[4,4,128,256]{3,2,0,1:T(8,128)(2,1)S(1)} %copy.86), channel_id=1, source_target_pairs={{0,4},{1,5},{2,6},{3,7},{4,0},{5,1},{6,2},{7,3},{8,12},{9,13},{10,... | collective-permute-start | bytes 3145736 | tf_op jit(solution)/shard_map/ppermute | solution.py:309
  387.1 12.4 %collective-permute-start.53 = (bf16[1,128,1024]{2,1,0:T(8,128)(2,1)}, bf16[1,128,1024]{2,1,0:T(8,128)(2,1)}, u32[]{:S(2)}, u32[]{:S(2)}) collective-permute-start(bf16[1,128,1024]{2,1,0:T(8,128)(2,1)} %fusion.11), channel_id=1, source_target_pairs={{0,8},{1,9},{2,10},{3,11},{4,12},{5,13},{6,14},{7,15},{8,16},{9,17... | collective-permute-start | bytes 786440 | tf_op jit(solution)/shard_map/ppermute | solution.py:309
  400.9 16.9 %collective-permute-start.54 = (bf16[1,128,1024]{2,1,0:T(8,128)(2,1)S(1)}, bf16[1,128,1024]{2,1,0:T(8,128)(2,1)S(1)}, u32[]{:S(2)}, u32[]{:S(2)}) collective-permute-start(bf16[1,128,1024]{2,1,0:T(8,128)(2,1)S(1)} %fusion.7), channel_id=1, source_target_pairs={{0,8},{1,9},{2,10},{3,11},{4,12},{5,13},{6,14},{7,15},{8,16},{9,17... | collective-permute-start | bytes 786440 | tf_op jit(solution)/shard_map/ppermute | solution.py:309
  418.6 23.7 %collective-permute-start.60 = (bf16[4,4,64,256]{3,2,1,0:T(8,128)(2,1)}, bf16[4,4,64,256]{3,2,1,0:T(8,128)(2,1)S(1)}, u32[]{:S(2)}, u32[]{:S(2)}) collective-permute-start(bf16[4,4,64,256]{3,2,1,0:T(8,128)(2,1)} %get-tuple-element.586), channel_id=1, source_target_pairs={{0,4},{1,5},{2,6},{3,7},{4,0},{5,1},{6,2},{7,3},{8,12},{9,13},{10,... | collective-permute-start | bytes 1572872 | tf_op jit(solution)/shard_map/ppermute | solution.py:309
  419.7 22.6 %collective-permute-start.61 = (bf16[4,4,64,256]{3,2,1,0:T(8,128)(2,1)}, bf16[4,4,64,256]{3,2,1,0:T(8,128)(2,1)S(1)}, u32[]{:S(2)}, u32[]{:S(2)}) collective-permute-start(bf16[4,4,64,256]{3,2,1,0:T(8,128)(2,1)} %get-tuple-element.588), channel_id=1, source_target_pairs={{0,2},{1,3},{2,0},{3,1},{4,6},{5,7},{6,4},{7,5},{8,10},{9,11},{10,... | collective-permute-start | bytes 1572872 | tf_op jit(solution)/shard_map/ppermute | solution.py:309
  423.0 19.3 %collective-permute-start.57 = (bf16[1,128,1024]{2,1,0:T(8,128)(2,1)}, bf16[1,128,1024]{2,1,0:T(8,128)(2,1)S(1)}, u32[]{:S(2)}, u32[]{:S(2)}) collective-permute-start(bf16[1,128,1024]{2,1,0:T(8,128)(2,1)} %fusion.6), channel_id=1, source_target_pairs={{0,8},{1,9},{2,10},{3,11},{4,12},{5,13},{6,14},{7,15},{8,16},{9,17... | collective-permute-start | bytes 786440 | tf_op jit(solution)/shard_map/ppermute | solution.py:309
  424.7 17.6 %collective-permute-start.58 = (bf16[4,128,256]{2,1,0:T(8,128)(2,1)S(1)}, bf16[4,128,256]{2,1,0:T(8,128)(2,1)}, u32[]{:S(2)}, u32[]{:S(2)}) collective-permute-start(bf16[4,128,256]{2,1,0:T(8,128)(2,1)S(1)} %fusion.12), channel_id=1, source_target_pairs={{0,8},{1,9},{2,10},{3,11},{4,12},{5,13},{6,14},{7,15},{8,16},{9,17... | collective-permute-start | bytes 786440 | tf_op jit(solution)/shard_map/ppermute | solution.py:309
  426.5 15.7 %collective-permute-start.59 = (f32[4,2,2,544]{3,2,1,0:T(2,128)S(1)}, f32[4,2,2,544]{3,2,1,0:T(2,128)S(1)}, u32[]{:S(2)}, u32[]{:S(2)}) collective-permute-start(f32[4,2,2,544]{3,2,1,0:T(2,128)S(1)} %bitcast.140), channel_id=1, source_target_pairs={{0,1},{1,0},{2,3},{3,2},{4,5},{5,4},{6,7},{7,6},{8,9},{9,8},{10,11... | collective-permute-start | bytes 104456 | tf_op jit(solution)/shard_map/ppermute | solution.py:309
  448.5 26.3 %collective-permute-start.66 = (bf16[4,4,128,256]{3,2,1,0:T(8,128)(2,1)}, bf16[4,4,128,256]{3,2,1,0:T(8,128)(2,1)}, u32[]{:S(2)}, u32[]{:S(2)}) collective-permute-start(bf16[4,4,128,256]{3,2,1,0:T(8,128)(2,1)} %get-tuple-element.602), channel_id=1, source_target_pairs={{0,2},{1,3},{2,0},{3,1},{4,6},{5,7},{6,4},{7,5},{8,10},{9,11},{10,... | collective-permute-start | bytes 3145736 | tf_op jit(solution)/shard_map/ppermute | solution.py:309
  449.4 25.5 %collective-permute-start.65 = (bf16[4,4,128,256]{3,2,0,1:T(8,128)(2,1)S(1)}, bf16[4,4,128,256]{3,2,0,1:T(8,128)(2,1)}, u32[]{:S(2)}, u32[]{:S(2)}) collective-permute-start(bf16[4,4,128,256]{3,2,0,1:T(8,128)(2,1)S(1)} %copy.94), channel_id=1, source_target_pairs={{0,4},{1,5},{2,6},{3,7},{4,0},{5,1},{6,2},{7,3},{8,12},{9,13},{10,... | collective-permute-start | bytes 3145736 | tf_op jit(solution)/shard_map/ppermute | solution.py:309
  452.9 10.3 %collective-permute-start.63 = (bf16[4,128,256]{2,1,0:T(8,128)(2,1)}, bf16[4,128,256]{2,1,0:T(8,128)(2,1)}, u32[]{:S(2)}, u32[]{:S(2)}) collective-permute-start(bf16[4,128,256]{2,1,0:T(8,128)(2,1)} %fusion.4), channel_id=1, source_target_pairs={{0,8},{1,9},{2,10},{3,11},{4,12},{5,13},{6,14},{7,15},{8,16},{9,17... | collective-permute-start | bytes 786440 | tf_op jit(solution)/shard_map/ppermute | solution.py:309
  453.2 21.6 %collective-permute-start.62 = (f32[4,2,544]{2,1,0:T(2,128)S(1)}, f32[4,2,544]{2,1,0:T(2,128)S(1)}, u32[]{:S(2)}, u32[]{:S(2)}) collective-permute-start(f32[4,2,544]{2,1,0:T(2,128)S(1)} %bitcast.141), channel_id=1, source_target_pairs={{0,2},{1,3},{2,0},{3,1},{4,6},{5,7},{6,4},{7,5},{8,10},{9,11},{10,... | collective-permute-start | bytes 52232 | tf_op jit(solution)/shard_map/ppermute | solution.py:309
  464.6 11.7 %collective-permute-start.64 = (bf16[4,128,256]{2,1,0:T(8,128)(2,1)S(1)}, bf16[4,128,256]{2,1,0:T(8,128)(2,1)S(1)}, u32[]{:S(2)}, u32[]{:S(2)}) collective-permute-start(bf16[4,128,256]{2,1,0:T(8,128)(2,1)S(1)} %fusion.5), channel_id=1, source_target_pairs={{0,8},{1,9},{2,10},{3,11},{4,12},{5,13},{6,14},{7,15},{8,16},{9,17... | collective-permute-start | bytes 786440 | tf_op jit(solution)/shard_map/ppermute | solution.py:309
  476.3 9.9 %collective-permute-start.68 = (bf16[4,128,256]{2,1,0:T(8,128)(2,1)S(1)}, bf16[4,128,256]{2,1,0:T(8,128)(2,1)S(1)}, u32[]{:S(2)}, u32[]{:S(2)}) collective-permute-start(bf16[4,128,256]{2,1,0:T(8,128)(2,1)S(1)} %fusion.13), channel_id=1, source_target_pairs={{0,8},{1,9},{2,10},{3,11},{4,12},{5,13},{6,14},{7,15},{8,16},{9,17... | collective-permute-start | bytes 786440 | tf_op jit(solution)/shard_map/ppermute | solution.py:309
  487.5 9.1 %collective-permute-start.70 = (bf16[4,128,256]{2,1,0:T(8,128)(2,1)S(1)}, bf16[4,128,256]{2,1,0:T(8,128)(2,1)S(1)}, u32[]{:S(2)}, u32[]{:S(2)}) collective-permute-start(bf16[4,128,256]{2,1,0:T(8,128)(2,1)S(1)} %fusion.3), channel_id=1, source_target_pairs={{0,8},{1,9},{2,10},{3,11},{4,12},{5,13},{6,14},{7,15},{8,16},{9,17... | collective-permute-start | bytes 786440 | tf_op jit(solution)/shard_map/ppermute | solution.py:309
  487.6 9.0 %collective-permute-start.69 = (f32[544]{0:T(1024)S(1)}, f32[544]{0:T(1024)S(1)}, u32[]{:S(2)}, u32[]{:S(2)}) collective-permute-start(f32[544]{0:T(1024)S(1)} %get-tuple-element.606), channel_id=1, source_target_pairs={{0,8},{1,9},{2,10},{3,11},{4,12},{5,13},{6,14},{7,15},{8,16},{9,17... | collective-permute-start | bytes 6536 | tf_op jit(solution)/shard_map/ppermute | solution.py:309
  498.0 15.8 %collective-permute-start.72 = (bf16[4,128,256]{2,1,0:T(8,128)(2,1)S(1)}, bf16[4,128,256]{2,1,0:T(8,128)(2,1)S(1)}, u32[]{:S(2)}, u32[]{:S(2)}) collective-permute-start(bf16[4,128,256]{2,1,0:T(8,128)(2,1)S(1)} %fusion.2), channel_id=1, source_target_pairs={{0,8},{1,9},{2,10},{3,11},{4,12},{5,13},{6,14},{7,15},{8,16},{9,17... | collective-permute-start | bytes 786440 | tf_op jit(solution)/shard_map/ppermute | solution.py:309
  (111 other events, 1130.2 us)

commit v4 on v3

--- a/solution.py
+++ b/solution.py
@@ -519,17 +519,17 @@
     dx, dy, qx, qy, own = outs
     rows = own.shape[2]
     if here:
-        own[i, k] = scratch[k, x]
-        qx[i, k] = scratch[k, 1 - x].astype(BF16)
+        own[k, i] = scratch[k, x]
+        qx[k, i] = scratch[k, 1 - x].astype(BF16)
     else:
-        qy[i, k] = scratch[k, x].astype(BF16)
-        dx[i, k] = scratch[k, 1 - x, pl.ds(0, rows // 2)].astype(BF16)
-        dy[i, k] = scratch[k, 1 - x, pl.ds(rows // 2, rows // 2)].astype(BF16)
+        qy[k, i] = scratch[k, x].astype(BF16)
+        dx[k, i] = scratch[k, 1 - x, pl.ds(0, rows // 2)].astype(BF16)
+        dy[k, i] = scratch[k, 1 - x, pl.ds(rows // 2, rows // 2)].astype(BF16)
 
 
 def near_kernel(place, *refs):
     from_c, *outs, scratch = refs[-7:]
-    units, zs, rows, cols = outs[-1].shape
+    zs, units, rows, cols = outs[-1].shape
     for i in range(units):
         a, d = refs[2 * i], refs[2 * i + 1]
         term = dot_tn(a[...], both_columns(d, corners(place)[1], cols))
@@ -541,7 +541,7 @@
 
 
 def quadrant_shapes(units, ring, rows, cols):
-    half, full = (units, ring, rows // 2, cols), (units, ring, rows, cols)
+    half, full = (ring, units, rows // 2, cols), (ring, units, rows, cols)
     return [jax.ShapeDtypeStruct(half, BF16)] * 2 + [
         jax.ShapeDtypeStruct(full, BF16), jax.ShapeDtypeStruct(full, BF16), jax.ShapeDtypeStruct(full, F32)
     ]
@@ -549,14 +549,14 @@
 
 def quadrant_specs(units, zs, rows, cols, stepped):
     def at(s, *_):
-        return (0, s if stepped else 0, 0, 0)
-
-    half = pl.BlockSpec((units, zs, rows // 2, cols), at)
-    full = pl.BlockSpec((units, zs, rows, cols), at)
+        return (s if stepped else 0, 0, 0, 0)
+
+    half = pl.BlockSpec((zs, units, rows // 2, cols), at)
+    full = pl.BlockSpec((zs, units, rows, cols), at)
     return [half] * 2 + [full] * 3
 
 
-def token_terms(grid, place, pairs, rows, cols, from_c=None):
+def token_terms(grid, place, pairs, rows, cols, from_c=None, params=FULL_VMEM):
     units, tokens = len(pairs), pairs[0][0].shape[0]
     height = grid.wide * rows
     zs = max(1, 128 // (2 * rows))
@@ -592,7 +592,7 @@
             scratch_shapes=scratch,
         ),
         out_shape=out_shape,
-        compiler_params=FULL_VMEM,
+        compiler_params=params,
         cost_estimate=CHEAP,
         name="weight_terms",
     )(place, *args)
@@ -630,7 +630,7 @@
             x = place[1]
             for i in range(pairs + 2):
                 for j in range(2):
-                    for k in range(own.shape[1]):
+                    for k in range(own.shape[0]):
                         put_quadrants(x, acc.at[i, j], k, i, j == 0, (dx, dy, qx, qy, own))
         else:
             out[...] = acc[...].reshape(out.shape).astype(BF16)
@@ -673,13 +673,12 @@
 
 
 def add_corners(qx, qy, from_x, from_y):
-    units, ring, rows, cols = qx.shape
-    zs = ring if units > 1 else 1
-    full = pl.BlockSpec((1, zs, rows, cols), lambda i, k: (i, k, 0, 0))
-    half = pl.BlockSpec((1, zs, rows // 2, cols), lambda i, k: (i, k, 0, 0))
+    ring, units, rows, cols = qx.shape
+    full = pl.BlockSpec((1, units, rows, cols), lambda k: (k, 0, 0, 0))
+    half = pl.BlockSpec((1, units, rows // 2, cols), lambda k: (k, 0, 0, 0))
     return pl.pallas_call(
         add_corners_kernel,
-        grid=(units, ring // zs),
+        grid=(ring,),
         in_specs=[full, full, half, half],
         out_specs=[full, full],
         out_shape=[jax.ShapeDtypeStruct(qx.shape, BF16)] * 2,
@@ -721,7 +720,8 @@
     def chunk(self, step):
         index = lax.rem(self.place[0] + (self.grid.ring - step), self.grid.ring)
         parts = [
-            lax.dynamic_index_in_dim(a, index, 1, keepdims=False) for a in (self.own, self.back_x, self.back_y)
+            lax.dynamic_index_in_dim(a, index, 0, keepdims=False)
+            for a in self.grid.clock.now((self.own, self.back_x, self.back_y))
         ]
         return parts[0] + parts[1].astype(F32) + parts[2].astype(F32)
 
@@ -744,25 +744,44 @@
 
 class SmallSum:
     def __init__(self, grid, place, terms):
-        self.grid, self.place, self.done = grid, place, 0
+        self.grid, self.place, self.done, self.came = grid, place, 0, None
         self.mine = terms.reshape(grid.ring, 2, 2, 2, -1)
-
-    def step(self):
+        self.steps = grid.ring + 2
+
+    def pair(self, name, axis, at):
+        far = lax.dynamic_index_in_dim(self.mine, 1 - at, axis, keepdims=False)
+        self.came = self.grid.send(name, far)
+        self.near = lax.dynamic_index_in_dim(self.mine, at, axis, keepdims=False)
+
+    def settle(self, *after):
+        if self.came is not None:
+            came = tie(self.came, *after) if after else self.came
+            self.mine = self.near + came
+
+    def step(self, *after):
         grid, place = self.grid, self.place
-        if self.done < 3:
-            name, axis, at = ("c", "y", "x")[self.done], 3 - self.done, place[3 - self.done]
-            far = lax.dynamic_index_in_dim(self.mine, 1 - at, axis, keepdims=False)
-            near = lax.dynamic_index_in_dim(self.mine, at, axis, keepdims=False)
-            self.mine = near + grid.send(name, far)
+        if self.done == 0:
+            self.pair("c", 3, place[3])
+        elif self.done < grid.ring:
+            if self.done == 1:
+                self.settle(*after)
+            index = lax.rem(place[0] + (grid.ring - self.done), grid.ring)
+            total = lax.dynamic_index_in_dim(self.mine, index, 0, keepdims=False)
+            if self.done > 1:
+                total = total + (tie(self.came, *after) if after else self.came)
+            self.came = grid.send("z", total)
+            self.near = lax.dynamic_index_in_dim(self.mine, place[0], 0, keepdims=False)
         else:
-            index = lax.rem(place[0] + (grid.ring - (self.done - 2)), grid.ring)
-            total = lax.dynamic_index_in_dim(self.mine, index, 0, keepdims=False)
-            self.came = grid.send("z", total if self.done == 3 else total + self.came)
+            self.settle(*after)
+            if self.done == grid.ring:
+                self.pair("y", 1, place[2])
+            else:
+                self.pair("x", 0, place[1])
         self.done += 1
-        return self.mine if self.done <= 3 else self.came
+        return self.came
 
     def result(self):
-        return lax.dynamic_index_in_dim(self.mine, self.place[0], 0, keepdims=False) + self.came
+        return self.near + self.came
 
 
 def halves(place, own, other):
@@ -1045,8 +1064,9 @@
         start.move(out, 0, k * rows, array, i, 0, rows)
     ring_one = start.run(clock)
     ring_one.append(send("z", ring_one[-1]))
+    ring_small = [small[None]]
+    ring_small.append(send("z", ring_small[-1]))
     top = Square(g_fc2, [[(fc2[None], 0, 0, part, 0)]], part)
-    memory = in_place(memory)
     more = Rearrange()
     out = more.out(1, 3 * rows, cols)
     for k, array in enumerate((self_out, cross_q, cross_out)):
@@ -1056,16 +1076,15 @@
         more.move(out, 0, k * rows, fc1[None], 0, 0, rows, k * cols)
     more.move(out, 0, 4 * rows, fc2[None], 0, part, part)
     ring_mix, ring_up = [[array] for array in more.run(clock)]
-    tick(ring_one[-1], memory, ring_mix[0], ring_up[0], *exchange(grid, None, top))
+    tick(ring_one[-1], ring_small[-1], ring_mix[0], ring_up[0], *exchange(grid, None, top))
     ring_one.append(send("z", ring_one[-1]))
-    ring_small = [small[None]]
     ring_small.append(send("z", ring_small[-1]))
-    tick(ring_one[-1], ring_small[-1], *exchange(grid, top, None))
+    memory = in_place(now(memory))
+    tick(ring_one[-1], ring_small[-1], memory, *exchange(grid, top, None))
     for _ in range(steps - 2):
         ring_one.append(send("z", ring_one[-1]))
         ring_small.append(send("z", ring_small[-1]))
         tick(ring_one[-1], ring_small[-1])
-    ring_small.append(send("z", ring_small[-1]))
 
     def from_ring(arrays, first, count):
         return [[(array, 0, first, count, 0)] for array in arrays]
@@ -1170,16 +1189,16 @@
     for step, array in enumerate(ring_top):
         g_fc2.put([(step, dx, dy) for dx, dy in spread], array, 0, part, 0)
 
-    def settle(pairs, shard):
+    def settle(pairs, shard, params=FULL_VMEM):
         part_rows, part_cols = shard.shape
         return Reduce(
             grid, place,
-            lambda from_c: token_terms(grid, place, pairs, part_rows, part_cols, from_c),
+            lambda from_c: token_terms(grid, place, pairs, part_rows, part_cols, from_c, params),
             part_rows,
         )
 
     one_row = result((1, D), F32)
-    r_fc2 = settle([(now(activated), cotangent)], fc2)
+    r_fc2 = settle([(now(activated), cotangent)], fc2, BIG_VMEM)
     r_fc2.far()
     r_fc2.swap()
     g_fc2.half()
@@ -1210,26 +1229,24 @@
         [result(wide_row, F32), result(wide_row, BF16), result(wide_row, BF16)] + [one_row] * 4,
         grid=(2,), scratch=[pltpu.VMEM(wide_row, F32)], params=FULL_VMEM,
     )
-    tick(r_fc1.near(), grad_cross_mixed, *r_fc2.pairs())
-    ring_fc2 = RingSum(grid, [r_fc2])
-
+    tick(r_fc1.near(), r_fc2.sx, grad_cross_mixed)
+
+    came = [*r_fc2.pairs(), *r_fc1.across()]
     grad_cq, grad_ck, grad_cv, grad_bias_six = cross_backward(
         local_map, row_lengths, segment_ids, cross_queries, mem_keys, mem_values,
         now(grad_cross_mixed), cross_lse,
     )
-    tick(grad_cq, ring_fc2.step(), *r_fc1.across())
+    r_mem = Reduce(
+        grid, place,
+        lambda from_c: memory_terms(grid, place, memory, (grad_ck, grad_cv), [], rows, cols, from_c),
+        rows,
+    )
+    tick(grad_cq, r_mem.far(), *came)
+    ring_fc2 = RingSum(grid, [r_fc2])
     r_fc1.add()
-    grad_cq = now(grad_cq)
-    cross_pairs = [(cross_mixed, grad_branch_two), (normed_two, grad_cq)]
-    r_cross = Reduce(
-        grid, place,
-        lambda from_c: memory_terms(
-            grid, place, memory, (grad_ck, grad_cv), cross_pairs, rows, cols, from_c
-        ),
-        rows,
-    )
-    r_cross.far()
-    r_cross.swap()
+    r_mem.swap()
+    ring_fc2.step()
+    grad_cq = tie(now(grad_cq), r_fc1.sx)
     (
         grad_after_self, grad_branch_one, grad_self_mixed,
         grad_gain_two, grad_bias_four, grad_bias_three, grad_bias_five,
@@ -1240,20 +1257,22 @@
         [result(wide_row, F32), result(wide_row, BF16), result(wide_row, BF16)] + [one_row] * 4,
         params=FULL_VMEM,
     )
-    tick(r_cross.near(), grad_self_mixed, ring_fc2.step(), *r_fc1.pairs())
+    grad_sq, grad_sk, grad_sv = self_backward(
+        segment_ids, self_queries, self_keys, self_values, grad_self_mixed, self_lse
+    )
+    r_rest = settle(
+        [
+            (normed_one, grad_sq), (normed_one, grad_sk), (normed_one, grad_sv),
+            (self_mixed, grad_branch_one), (normed_two, grad_cq), (cross_mixed, grad_branch_two),
+        ],
+        cross_q,
+    )
+    tick(r_rest.far(), r_mem.near(), ring_fc2.came, *r_fc1.pairs())
     ring_fc1 = RingSum(grid, [r_fc1])
-
-    grad_sq, grad_sk, grad_sv = self_backward(
-        segment_ids, self_queries, self_keys, self_values, now(grad_self_mixed), self_lse
-    )
-    r_self = settle(
-        [(normed_one, grad_sq), (normed_one, grad_sk), (normed_one, grad_sv), (self_mixed, grad_branch_one)],
-        cross_q,
-    )
-    tick(r_self.far(), ring_fc2.step(), *r_cross.across())
+    came = r_mem.across()
+    r_rest.swap()
     ring_fc2.step()
-    r_cross.add()
-    r_self.swap()
+    ring_fc1.step()
     grad_tokens, grad_gain_one, grad_bias_zero, grad_bias_one, grad_bias_two = dense_call(
         first_back_kernel, "self_qkv_norm_back", place,
         [full(tokens), full(grad_after_self)] + [full(d) for d in now((grad_sq, grad_sk, grad_sv))]
@@ -1261,10 +1280,7 @@
         [result(wide_row, BF16)] + [one_row] * 4,
         params=FULL_VMEM,
     )
-    ring_fc1.step()
-    ring_fc1.step(grad_tokens)
-    tick(r_self.near(), grad_tokens, ring_fc1.came, *r_cross.pairs())
-    ring_cross = RingSum(grid, [r_cross])
+    tick(r_rest.near(), grad_tokens, ring_fc2.came, ring_fc1.came, *came)
 
     def by_device(array):
         return array.reshape(array.shape[0], devices, -1).transpose(1, 0, 2).reshape(devices, -1)
@@ -1286,33 +1302,48 @@
         axis=1,
     )
     small_sum = SmallSum(grid, place, now(small_grads))
+    r_mem.add()
+    ring_fc2.step()
     (grad_memory,) = dense_call(
         memory_back_kernel, "memory_back", place,
-        [by_memory(a) for a in now((grad_ck, grad_cv))] + matrix(g_ckv, 0) + matrix(g_ckv, 1),
+        [by_memory(a) for a in tie(now((grad_ck, grad_cv)), r_mem.sx)] + matrix(g_ckv, 0) + matrix(g_ckv, 1),
         [by_memory(mem_shape)], grid=(mem_count,), params=FULL_VMEM,
     )
-    ring_fc1.step()
-    tick(grad_memory, ring_fc1.came, ring_cross.step(), small_sum.step(), *r_self.across())
-    r_self.add()
     (layer_out,) = dense_call(
         down_kernel, "fc2", place,
-        [full(after_cross), full(now(activated)), full(vectors)] + by_y(g_fc2),
+        [full(after_cross), full(tie(now(activated), r_mem.sx)), full(vectors)] + by_y(g_fc2),
         [result(wide_row, BF16)], grid=(2,), params=FULL_VMEM,
     )
-    ring_cross.step()
-    ring_cross.step(layer_out)
-    tick(layer_out, ring_cross.came, small_sum.step(), *r_self.pairs())
+    tick(grad_memory, layer_out, ring_fc2.came, *r_mem.pairs(), *r_rest.across())
+    small_sum.step()
+    ring_mem = RingSum(grid, [r_mem])
+    r_rest.add()
+    turned_memory = in_place(tie(now(grad_memory).transpose(1, 0, 2), r_rest.sx))
+    grad_memory = turned_memory.transpose(1, 0, 2)
     ring_fc1.step()
-    ring_self = RingSum(grid, [r_self])
+    ring_mem.step()
     for _ in range(steps):
-        tick(ring_self.step(), small_sum.step())
-    for ring in (ring_fc2, ring_fc1, ring_cross, ring_self):
+        small_sum.step()
+    ring_fc1.step(turned_memory)
+    tick(turned_memory, small_sum.came, ring_fc1.came, ring_mem.came, *r_rest.pairs())
+    ring_fc2.step()
+    ring_rest = RingSum(grid, [r_rest])
+    ring_rest.step()
+    ring_fc1.step()
+    ring_mem.step()
+    small_sum.step()
+    tick(ring_rest.came, ring_mem.came, small_sum.came)
+    for _ in range(steps - 1):
+        ring_mem.step() if ring_mem.done < grid.ring else None
+        small_sum.step() if small_sum.done < small_sum.steps else None
+        tick(ring_rest.step(), ring_mem.came, small_sum.came)
+    for ring in (ring_fc2, ring_fc1, ring_mem, ring_rest):
         while ring.done < grid.ring:
             ring.step()
-    while small_sum.done < steps + 3:
-        tick(small_sum.step())
+    while small_sum.done < small_sum.steps:
+        small_sum.step()
+    came_mem, came_rest = ring_mem.came, ring_rest.came
     small_shard = small_sum.result()
-    came_cross, came_self = ring_cross.came, ring_self.came
     return (
         layer_out,
         grad_tokens,
@@ -1320,11 +1351,11 @@
         small_shard[:n_gain].reshape(gains.shape),
         small_shard[n_gain : n_gain + n_bias].reshape(biases.shape),
         small_shard[n_gain + n_bias :],
-        came_self[:3],
-        came_self[3],
-        came_cross[1],
-        came_cross[2:],
-        came_cross[0],
+        came_rest[:3],
+        came_rest[3],
+        came_rest[4],
+        came_mem,
+        came_rest[5],
         ring_fc1.came[0],
         ring_fc2.came[0],
     )

time: 531 us -> 509 us (0.959)
  Pallas kernels: 252 us -> 242 us
    optimization_barrier x2, local copies, waits for them, and re-layouts: 2.58 us -> 12.3 us  [tie(): return lax.optimization_barrier((values, after))[0]]
    unnamed x207 -> x212, local copies, waits for them, and re-layouts: 44.1 us -> 34.8 us
    pallas_call x2, Pallas kernels: 31.2 us -> 25.7 us  [memory_terms(): pl.pallas_call(functools.partial(memory_terms_kernel, near, len(pairs)),...]
    convert_element_type x12, other arithmetic: 17.4 us -> 12 us  [step(): self.came = self.grid.send('z', total.astype(BF16))]
  transfers between devices with their start and end apart: 74 -> 74, of which waited for: 29 -> 29; matrix products, arithmetic and copies ran while one was open for 9% -> 8% of each run, Pallas kernels for 38% -> 40%
where the time goes in v4:
time: 509 us; the launch traced here: 501 us
  Pallas kernels  242 us (48%)
  waiting for transfers between devices  124 us (24%)
  starting transfers between devices  56.4 us (11%)
  local copies, waits for them, and re-layouts  55.2 us (11%)
  other arithmetic  20.8 us (4%)
    ppermute x74, waiting for transfers between devices, send(): return lax.ppermute(self.clock.now(array), AXES, self.perms[name])  124 us
    pallas_call x11, Pallas kernels, dense_call(): pl.pallas_call(kernel, grid_spec=pltpu.PrefetchScalarGridSpec(num_scalar_...  85.3 us
    ppermute x74, starting transfers between devices, send(): return lax.ppermute(self.clock.now(array), AXES, self.perms[name])  56.4 us
    pallas_call x6, Pallas kernels, token_terms(): pl.pallas_call(kernel, grid_spec=pltpu.PrefetchScalarGridSpec(num_scalar_...  36.8 us
    unnamed x212, local copies, waits for them, and re-layouts  34.8 us
    pallas_call x2, Pallas kernels, memory_terms(): pl.pallas_call(functools.partial(memory_terms_kernel, near, len(pairs)),...  25.7 us
    pallas_call x11, Pallas kernels, run(): pl.pallas_call(functools.partial(rearrange_kernel, self.moves, len(self.i...  23.1 us
    pallas_call x1, Pallas kernels, cross_backward(): pl.pallas_call(cross_bwd_kernel, grid_spec=pltpu.PrefetchScalarGridSpec(n...  20.1 us
  transfers between devices with their start and end apart: 74, of which 29 were waited for; matrix products, arithmetic and copies ran while one was open for 8% of the time, Pallas kernels for 40%

profile of v4, /device:TPU:0, one launch (start us, length us, event | category | flops | bytes accessed | tf_op | source)
XLA Modules:
  0.0 500.5 jit_solution(1035493102110434696)
XLA Ops:
  2.9 3.1 collective-permute-start
  21.5 3.9 copy.44._
  25.4 2.1 copy-done.2
  31.0 7.3 %collective-permute-done.9.refs_7_ = bf16[1,16,256]{2,1,0:T(8,128)(2,1)S(1)} collective-permute-done((bf16[1,16,256]{2,1,0:T(8,128)(2,1)S(1)}, bf16[1,16,256]{2,1,0:T(8,128)(2,1)S(1)}, u32[]{:S(2)}, u32[]{:S(2)}) %collective-permute-start.9) | collective-permute-done | bytes 8224 | tf_op jit(solution)/shard_map/ppermute | solution.py:309
  43.8 12.0 %collective-permute-done.11.refs_3_ = bf16[1,384,256]{2,1,0:T(8,128)(2,1)S(1)} collective-permute-done((bf16[1,384,256]{2,1,0:T(8,128)(2,1)S(1)}, bf16[1,384,256]{2,1,0:T(8,128)(2,1)S(1)}, u32[]{:S(2)}, u32[]{:S(2)}) %collective-permute-start.11) | collective-permute-done | bytes 196640 | tf_op jit(solution)/shard_map/ppermute | solution.py:309
  55.9 4.2 rearrange.17
  62.6 9.5 %collective-permute-done.15.refs_4_ = bf16[1,384,256]{2,1,0:T(8,128)(2,1)} collective-permute-done((bf16[1,384,256]{2,1,0:T(8,128)(2,1)S(1)}, bf16[1,384,256]{2,1,0:T(8,128)(2,1)}, u32[]{:S(2)}, u32[]{:S(2)}) %collective-permute-start.15) | collective-permute-done | bytes 196640 | tf_op jit(solution)/shard_map/ppermute | solution.py:309
  73.7 2.8 collective-permute-done.14.refs_4_
  76.5 3.4 collective-permute-done.16.refs_5_
  83.5 4.6 rearrange.18
  90.5 3.2 half_weights.5.k_own.v_own
  96.2 2.1 collective-permute-done.20.k_other.v_other
  102.0 2.4 copy-done.3
  104.4 13.8 %memory_keys_values.1 = (bf16[4,588,1024]{2,1,0:T(8,128)(2,1)S(1)}, bf16[4,588,1024]{2,1,0:T(8,128)(2,1)S(1)}) custom-call(s32[4]{0:T(128)S(1)} %pad_add_fusion.place, bf16[4,588,1024]{2,1,0:T(8,128)(2,1)S(1)} %copy-done.3, f32[13,1024]{1,0:T(8,128)S(1)} %reshape.468.vectors, bf16[2,2176,256]{2,1,0:T(8,128)(2,1)S(1)} %half_weights.5.k_own.v_own, ...), custom_call_target="tpu_custom_call" | custom-call | flops 1000000 | bytes 100000 | tf_op jit(solution)/shard_map/memory_keys_values/pallas_call | solution.py:977
  118.3 4.1 collective-permute-done.21.refs_1_.refs_3_
  123.7 3.4 rearrange.19
  129.4 3.4 half_weights.6.refs_0_.refs_2_.refs_4_
  135.2 3.5 collective-permute-done.23.refs_1_.refs_3_.refs_5_
  139.7 4.7 self_qkv.1
  148.4 2.5 collective-permute-done.24.refs_6_
  150.8 16.4 %collective-permute-done.25.refs_1_.refs_3_ = bf16[4,704,256]{2,1,0:T(8,128)(2,1)} collective-permute-done((bf16[4,704,256]{2,1,0:T(8,128)(2,1)}, bf16[4,704,256]{2,1,0:T(8,128)(2,1)}, u32[]{:S(2)}, u32[]{:S(2)}) %collective-permute-start.25) | collective-permute-done | bytes 1441824 | tf_op jit(solution)/shard_map/ppermute | solution.py:309
  167.5 3.4 rearrange.20
  171.0 2.8 half_weights.7.so_own.cq_own.own.co_own
  176.9 2.7 collective-permute-done.27.so_other.cq_other.other.co_other
  181.7 3.9 self_out_cross_q.1
  188.2 12.5 %cross_forward.1 = (bf16[256,1024]{1,0:T(8,128)(2,1)}, f32[2,8,256]{2,1,0:T(8,128)}) custom-call(s32[4]{0:T(128)} %copy-done.102, s32[4]{0:T(128)} %select_reduce_fusion.len_ref, s32[2,1,128]{2,1,0:T(1,128)} %bitcast.125, s32[2,128,1]{2,1,0:T(8,128)} %copy-done.32, bf16[256,1024]{1,0:T(8,128)(2,1)} %copy-done.38, bf16[4,588,1024]{2,1,0:T(8,128)(2,1)} %copy-done.7, ...), custom_call_target="tpu_custom_call" | custom-call | flops 1000000 | bytes 100000 | tf_op jit(solution)/shard_map/cross_forward/pallas_call | solution.py:228
  200.9 3.2 half_weights.8.own
  204.5 2.9 rearrange.21
  209.6 2.9 cross_out.1
  212.7 4.8 fc1_gelu.1
  218.9 1.9 collective-permute-done.32.refs_8_
  220.8 2.9 weight_terms.6
  223.8 3.2 half_weights.9.own
  227.6 3.4 collective-permute-done.35.refs_2_
  230.9 3.9 weight_terms.7
  240.3 7.9 %fc2_gelu_back.1 = (bf16[256,4096]{1,0:T(8,128)(2,1)}, f32[1,4096]{1,0:T(1,128)}) custom-call(s32[4]{0:T(128)} %copy-done.60, bf16[256,1024]{1,0:T(8,128)(2,1)} %grad_out.1, bf16[256,4096]{1,0:T(8,128)(2,1)} %copy-done.44, bf16[2,4096,256]{2,1,0:T(8,128)(2,1)} %copy-done.5, bf16[2,4096,256]{2,1,0:T(8,128)(2,1)} %copy-done.72), custom_call_target="tpu_custom_call" | custom-call | flops 1000000 | bytes 100000 | tf_op jit(solution)/shard_map/fc2_gelu_back/pallas_call | solution.py:977
  248.2 6.2 %weight_terms.8 = bf16[1,2,1024,1024]{3,2,1,0:T(8,128)(2,1)} custom-call(s32[4]{0:T(128)} %copy-done.60, bf16[256,1024]{1,0:T(8,128)(2,1)} %copy-done.27, bf16[256,4096]{1,0:T(8,128)(2,1)} %get-tuple-element.543.refs_1_.grad_pre), custom_call_target="tpu_custom_call" | custom-call | flops 1000000 | bytes 100000 | tf_op jit(solution)/shard_map/weight_terms/pallas_call | solution.py:585
  254.5 10.2 %fc1_norm_back.1 = (f32[256,1024]{1,0:T(8,128)}, bf16[256,1024]{1,0:T(8,128)(2,1)}, bf16[256,1024]{1,0:T(8,128)(2,1)}, f32[1,1024]{1,0:T(1,128)}, f32[1,1024]{1,...) custom-call(s32[4]{0:T(128)} %copy-done.60, bf16[256,4096]{1,0:T(8,128)(2,1)} %get-tuple-element.543.refs_1_.grad_pre, ...), custom_call_target="tpu_custom_call" | custom-call | flops 1000000 | bytes 100000 | tf_op jit(solution)/shard_map/fc1_norm_back/pallas_call | solution.py:977
  264.7 4.0 add_corners.4
  268.6 7.6 %weight_terms.9 = (bf16[4,1,64,1024]{3,2,1,0:T(8,128)(2,1)}, bf16[4,1,64,1024]{3,2,1,0:T(8,128)(2,1)}, bf16[4,1,128,1024]{3,2,1,0:T(8,128)(2,1)}, bf16[4,1,128,1024]{3,2,1,0:T(8,128)(2,1)}, f32[4,1,128,1024]{3,2,1,0:T(8,128)}) custom-call(s32[4]{0:T(128)} %copy-done.60, bf16[256,1024]{1,0:T(8,128)(2,1)} %copy-done.27, ...), custom_call_target="tpu_custom_call" | custom-call | flops 1000000 | bytes 100000 | tf_op jit(solution)/shard_map/weight_terms/pallas_call | solution.py:585
  280.4 20.1 %cross_backward.1 = (bf16[256,1024]{1,0:T(8,128)(2,1)}, bf16[4,588,1024]{2,1,0:T(8,128)(2,1)}, bf16[4,588,1024]{2,1,0:T(8,128)(2,1)}, f32[1,1024]{1,0:T(1,128)}) custom-call(s32[4]{0:T(128)} %copy-done.102, s32[4]{0:T(128)} %select_reduce_fusion.len_ref, s32[2,1,128]{2,1,0:T(1,128)} %bitcast.126, s32[2,128,1]{2,1,0:T(8,128)} %copy-done.32, ...), custom_call_target="tpu_custom_call" | custom-call | flops 1000000 | bytes 100000 | tf_op jit(solution)/shard_map/cross_backward/pallas_call | solution.py:250
  300.5 12.1 %memory_terms.2 = bf16[2,2,1024,256]{3,2,1,0:T(8,128)(2,1)} custom-call(s32[4]{0:T(128)} %copy-done.60, bf16[4,588,1024]{2,1,0:T(8,128)(2,1)} %copy-done.2, bf16[4,588,1024]{2,1,0:T(8,128)(2,1)} %get-tuple-element.618.dk.gk, bf16[4,588,1024]{2,1,0:T(8,128)(2,1)} %get-tuple-element.619.dv.gv), custom_call_target="tpu_custom_call" | custom-call | flops 1000000 | bytes 100000 | tf_op jit(solution)/shard_map/memory_terms/pallas_call | solution.py:646
  314.4 4.2 add_corners.5
  321.9 6.4 %cross_q_norm_back.1 = (f32[256,1024]{1,0:T(8,128)}, bf16[256,1024]{1,0:T(8,128)(2,1)}, bf16[256,1024]{1,0:T(8,128)(2,1)}, f32[1,1024]{1,0:T(1,128)}, f32[1,1024...) custom-call(s32[4]{0:T(128)} %copy-done.60, bf16[256,1024]{1,0:T(8,128)(2,1)} %get-tuple-element.568.grad_queries.refs_9_, ...), custom_call_target="tpu_custom_call" | custom-call | flops 1000000 | bytes 100000 | tf_op jit(solution)/shard_map/cross_q_norm_back/pallas_call | solution.py:977
  328.2 4.6 self_backward.1
  332.8 6.9 %weight_terms.10 = bf16[6,2,1024,256]{3,2,1,0:T(8,128)(2,1)} custom-call(s32[4]{0:T(128)} %copy-done.60, bf16[256,1024]{1,0:T(8,128)(2,1)} %copy-done.9, bf16[256,1024]{1,0:T(8,128)(2,1)} %get-tuple-element.593.refs_1_.gq, bf16[256,1024]{1,0:T(8,128)(2,1)} %copy-done.9, bf16[256,1024]{1,0:T(8,128)(2,1)} %get-tuple-element.594.refs_3_.gk, ...), custom_call_target="tpu_custom_call" | custom-call | flops 1000000 | bytes 100000 | tf_op jit(solution)/shard_map/weight_terms/pallas_call | solution.py:585
  339.7 13.6 %memory_terms.3 = (bf16[4,2,64,256]{3,2,1,0:T(8,128)(2,1)}, bf16[4,2,64,256]{3,2,1,0:T(8,128)(2,1)}, bf16[4,2,128,256]{3,2,1,0:T(8,128)(2,1)}, bf16[4,2,128,256]{3,2,1,0:T(8,128)(2,1)}, f32[4,2,128,256]{3,2,1,0:T(8,128)}) custom-call(s32[4]{0:T(128)} %copy-done.60, bf16[4,588,1024]{2,1,0:T(8,128)(2,1)} %copy-done.2, ...), custom_call_target="tpu_custom_call" | custom-call | flops 1000000 | bytes 100000 | tf_op jit(solution)/shard_map/memory_terms/pallas_call | solution.py:646
  359.8 7.5 %self_qkv_norm_back.1 = (bf16[256,1024]{1,0:T(8,128)(2,1)}, f32[1,1024]{1,0:T(1,128)}, f32[1,1024]{1,0:T(1,128)}, f32[1,1024]{1,0:T(1,128)}, f32[1,1024]{1,0:T(1,128)}) custom-call(s32[4]{0:T(128)} %copy-done.60, bf16[256,1024]{1,0:T(8,128)(2,1)} %tokens.4, f32[256,1024]{1,0:T(8,128)} %get-tuple-element.592.grad_after, ...), custom_call_target="tpu_custom_call" | custom-call | flops 1000000 | bytes 100000 | tf_op jit(solution)/shard_map/self_qkv_norm_back/pallas_call | solution.py:977
  367.3 9.3 %weight_terms.11 = (bf16[4,6,64,256]{3,2,1,0:T(8,128)(2,1)}, bf16[4,6,64,256]{3,2,1,0:T(8,128)(2,1)}, bf16[4,6,128,256]{3,2,1,0:T(8,128)(2,1)}, bf16[4,6,128,256]{3,2,1,0:T(8,128)(2,1)}, f32[4,6,128,256]{3,2,1,0:T(8,128)}) custom-call(s32[4]{0:T(128)} %copy-done.60, bf16[256,1024]{1,0:T(8,128)(2,1)} %copy-done.9, ...), custom_call_target="tpu_custom_call" | custom-call | flops 1000000 | bytes 100000 | tf_op jit(solution)/shard_map/weight_terms/pallas_call | solution.py:585
  379.5 3.5 add_corners.6
  386.8 3.6 collective-permute-start.53
  391.2 7.3 %fc2.1 = bf16[256,1024]{1,0:T(8,128)(2,1)} custom-call(s32[4]{0:T(128)} %copy-done.60, f32[256,1024]{1,0:T(8,128)} %copy-done.31, bf16[256,4096]{1,0:T(8,128)(2,1)} %copy-done.10, f32[13,1024]{1,0:T(8,128)} %copy-done.21, bf16[2,4096,256]{2,1,0:T(8,128)(2,1)} %copy-done.5, bf16[2,4096,256]{2,1,0:T(8,128)(2,1)} %copy-done.72), custom_call_target="tpu_custom_call" | custom-call | flops 1000000 | bytes 100000 | tf_op jit(solution)/shard_map/fc2/pallas_call | solution.py:977
  398.5 15.8 %memory_back.1 = bf16[4,588,1024]{2,1,0:T(8,128)(2,1)} custom-call(s32[4]{0:T(128)} %copy-done.60, bf16[4,588,1024]{2,1,0:T(8,128)(2,1)} %get-tuple-element.618.dk.gk, bf16[4,588,1024]{2,1,0:T(8,128)(2,1)} %get-tuple-element.619.dv.gv, bf16[2,2176,256]{2,1,0:T(8,128)(2,1)} %copy-done.4, bf16[2,2176,256]{2,1,0:T(8,128)(2,1)} %collective-permute-done.20.k_other.v_other, ...), custom_call_target="tpu_custom_call" | custom-call | flops 1000000 | bytes 100000 | tf_op jit(solution)/shard_map/memory_back/pallas_call | solution.py:977
  414.5 4.6 add_corners.7
  422.9 3.9 collective-permute-done.59
  428.8 8.3 %copy.63 = bf16[4,588,1024]{2,0,1:T(4,128)(2,1)} copy(bf16[4,588,1024]{2,1,0:T(8,128)(2,1)} %memory_back.1) | data formatting | bytes 9633792 | tf_op jit(solution)/shard_map/optimization_barrier | solution.py:274
  439.9 2.6 collective-permute-start.63
  442.7 6.0 %collective-permute-done.63 = bf16[1,128,1024]{2,1,0:T(8,128)(2,1)S(1)} collective-permute-done((bf16[1,128,1024]{2,1,0:T(8,128)(2,1)S(1)}, bf16[1,128,1024]{2,1,0:T(8,128)(2,1)S(1)}, u32[]{:S(2)}, u32[]{:S(2)}) %collective-permute-start.63) | collective-permute-done | bytes 262176 | tf_op jit(solution)/shard_map/ppermute | solution.py:309
  448.7 7.4 %collective-permute-done.65 = bf16[4,6,128,256]{3,2,1,0:T(8,128)(2,1)S(1)} collective-permute-done((bf16[4,6,128,256]{3,2,1,0:T(8,128)(2,1)}, bf16[4,6,128,256]{3,2,1,0:T(8,128)(2,1)S(1)}, u32[]{:S(2)}, u32[]{:S(2)}) %collective-permute-start.65) | collective-permute-done | bytes 1572896 | tf_op jit(solution)/shard_map/ppermute | solution.py:309
  460.3 12.5 %collective-permute-done.69 = bf16[2,128,256]{2,1,0:T(8,128)(2,1)S(1)} collective-permute-done((bf16[2,128,256]{2,1,0:T(8,128)(2,1)S(1)}, bf16[2,128,256]{2,1,0:T(8,128)(2,1)S(1)}, u32[]{:S(2)}, u32[]{:S(2)}) %collective-permute-start.69) | collective-permute-done | bytes 131104 | tf_op jit(solution)/shard_map/ppermute | solution.py:309
  474.9 1.9 fusion.2
  476.8 10.4 %collective-permute-done.72 = bf16[2,128,256]{2,1,0:T(8,128)(2,1)S(1)} collective-permute-done((bf16[2,128,256]{2,1,0:T(8,128)(2,1)S(1)}, bf16[2,128,256]{2,1,0:T(8,128)(2,1)S(1)}, u32[]{:S(2)}, u32[]{:S(2)}) %collective-permute-start.72) | collective-permute-done | bytes 131104 | tf_op jit(solution)/shard_map/ppermute | solution.py:309
  487.6 2.0 fusion.3
  493.2 4.1 collective-permute-done.73
  (398 shorter events, 116.7 us)
Async XLA Ops:
  2.9 15.6 %collective-permute-start = (bf16[1,640,256]{2,1,0:T(8,128)(2,1)S(1)}, bf16[1,640,256]{2,1,0:T(8,128)(2,1)S(1)}, u32[]{:S(2)}, u32[]{:S(2)}) collective-permute-start(bf16[1,640,256]{2,1,0:T(8,128)(2,1)S(1)} %rearrange.12.refs_0_.refs_2_), channel_id=1, source_target_pairs={{0,8},{1,9},{2,10},{3,11},{4,12},{5,13},{6,14},{7,15},{8,16},{9,17... | collective-permute-start | bytes 983048 | tf_op jit(solution)/shard_map/ppermute | solution.py:309
  7.3 11.2 %collective-permute-start.3 = (bf16[1,256,256]{2,1,0:T(8,128)(2,1)S(1)}, bf16[1,256,256]{2,1,0:T(8,128)(2,1)S(1)}, u32[]{:S(2)}, u32[]{:S(2)}) collective-permute-start(bf16[1,256,256]{2,1,0:T(8,128)(2,1)S(1)} %get-tuple-element.367), channel_id=1, source_target_pairs={{0,2},{1,3},{2,0},{3,1},{4,6},{5,7},{6,4},{7,5},{8,10},{9,11},{10,... | collective-permute-start | bytes 393224 | tf_op jit(solution)/shard_map/ppermute | solution.py:309
  8.9 9.6 %collective-permute-start.2 = (bf16[1,256,256]{2,1,0:T(8,128)(2,1)S(1)}, bf16[1,256,256]{2,1,0:T(8,128)(2,1)S(1)}, u32[]{:S(2)}, u32[]{:S(2)}) collective-permute-start(bf16[1,256,256]{2,1,0:T(8,128)(2,1)S(1)} %get-tuple-element.396.refs_0_), channel_id=1, source_target_pairs={{0,4},{1,5},{2,6},{3,7},{4,0},{5,1},{6,2},{7,3},{8,12},{9,13},{10,... | collective-permute-start | bytes 393224 | tf_op jit(solution)/shard_map/ppermute | solution.py:309
  18.5 10.4 %collective-permute-start.4 = (bf16[1,640,256]{2,1,0:T(8,128)(2,1)S(1)}, bf16[1,640,256]{2,1,0:T(8,128)(2,1)S(1)}, u32[]{:S(2)}, u32[]{:S(2)}) collective-permute-start(bf16[1,640,256]{2,1,0:T(8,128)(2,1)S(1)} %collective-permute-done.refs_2_.refs_3_), channel_id=1, source_target_pairs={{0,8},{1,9},{2,10},{3,11},{4,12},{5,13},{6,14},{7,15},{8,16},{9,17... | collective-permute-start | bytes 983048 | tf_op jit(solution)/shard_map/ppermute | solution.py:309
  20.3 8.6 %collective-permute-start.7 = (bf16[1,128,256]{2,1,0:T(8,128)(2,1)S(1)}, bf16[1,128,256]{2,1,0:T(8,128)(2,1)S(1)}, u32[]{:S(2)}, u32[]{:S(2)}) collective-permute-start(bf16[1,128,256]{2,1,0:T(8,128)(2,1)S(1)} %get-tuple-element.376), channel_id=1, source_target_pairs={{0,2},{1,3},{2,0},{3,1},{4,6},{5,7},{6,4},{7,5},{8,10},{9,11},{10,... | collective-permute-start | bytes 196616 | tf_op jit(solution)/shard_map/ppermute | solution.py:309
  20.9 8.0 %collective-permute-start.6 = (bf16[1,128,256]{2,1,0:T(8,128)(2,1)S(1)}, bf16[1,128,256]{2,1,0:T(8,128)(2,1)S(1)}, u32[]{:S(2)}, u32[]{:S(2)}) collective-permute-start(bf16[1,128,256]{2,1,0:T(8,128)(2,1)S(1)} %get-tuple-element.374), channel_id=1, source_target_pairs={{0,4},{1,5},{2,6},{3,7},{4,0},{5,1},{6,2},{7,3},{8,12},{9,13},{10,... | collective-permute-start | bytes 196616 | tf_op jit(solution)/shard_map/ppermute | solution.py:309
  21.4 7.5 %collective-permute-start.5 = (bf16[1,16,256]{2,1,0:T(8,128)(2,1)S(1)}, bf16[1,16,256]{2,1,0:T(8,128)(2,1)S(1)}, u32[]{:S(2)}, u32[]{:S(2)}) collective-permute-start(bf16[1,16,256]{2,1,0:T(8,128)(2,1)S(1)} %collective-permute-done.1.refs_3_), channel_id=1, source_target_pairs={{0,8},{1,9},{2,10},{3,11},{4,12},{5,13},{6,14},{7,15},{8,16},{9,17... | collective-permute-start | bytes 24584 | tf_op jit(solution)/shard_map/ppermute | solution.py:309
  28.9 9.4 %collective-permute-start.8 = (bf16[1,640,256]{2,1,0:T(8,128)(2,1)S(1)}, bf16[1,640,256]{2,1,0:T(8,128)(2,1)S(1)}, u32[]{:S(2)}, u32[]{:S(2)}) collective-permute-start(bf16[1,640,256]{2,1,0:T(8,128)(2,1)S(1)} %collective-permute-done.4.refs_4_), channel_id=1, source_target_pairs={{0,8},{1,9},{2,10},{3,11},{4,12},{5,13},{6,14},{7,15},{8,16},{9,17... | collective-permute-start | bytes 983048 | tf_op jit(solution)/shard_map/ppermute | solution.py:309
  29.4 8.9 %collective-permute-start.9 = (bf16[1,16,256]{2,1,0:T(8,128)(2,1)S(1)}, bf16[1,16,256]{2,1,0:T(8,128)(2,1)S(1)}, u32[]{:S(2)}, u32[]{:S(2)}) collective-permute-start(bf16[1,16,256]{2,1,0:T(8,128)(2,1)S(1)} %collective-permute-done.5.refs_5_), channel_id=1, source_target_pairs={{0,8},{1,9},{2,10},{3,11},{4,12},{5,13},{6,14},{7,15},{8,16},{9,17... | collective-permute-start | bytes 24584 | tf_op jit(solution)/shard_map/ppermute | solution.py:309
  39.9 15.9 %collective-permute-start.12 = (bf16[4,272,256]{2,1,0:T(8,128)(2,1)S(1)}, bf16[4,272,256]{2,1,0:T(8,128)(2,1)S(1)}, u32[]{:S(2)}, u32[]{:S(2)}) collective-permute-start(bf16[4,272,256]{2,1,0:T(8,128)(2,1)S(1)} %get-tuple-element.425.refs_0_), channel_id=1, source_target_pairs={{0,4},{1,5},{2,6},{3,7},{4,0},{5,1},{6,2},{7,3},{8,12},{9,13},{10,... | collective-permute-start | bytes 1671176 | tf_op jit(solution)/shard_map/ppermute | solution.py:309
  41.3 14.5 %collective-permute-start.13 = (bf16[4,272,256]{2,1,0:T(8,128)(2,1)S(1)}, bf16[4,272,256]{2,1,0:T(8,128)(2,1)S(1)}, u32[]{:S(2)}, u32[]{:S(2)}) collective-permute-start(bf16[4,272,256]{2,1,0:T(8,128)(2,1)S(1)} %get-tuple-element.392), channel_id=1, source_target_pairs={{0,2},{1,3},{2,0},{3,1},{4,6},{5,7},{6,4},{7,5},{8,10},{9,11},{10,... | collective-permute-start | bytes 1671176 | tf_op jit(solution)/shard_map/ppermute | solution.py:309
  42.6 13.3 %collective-permute-start.10 = (bf16[1,768,256]{2,1,0:T(8,128)(2,1)S(1)}, bf16[1,768,256]{2,1,0:T(8,128)(2,1)S(1)}, u32[]{:S(2)}, u32[]{:S(2)}) collective-permute-start(bf16[1,768,256]{2,1,0:T(8,128)(2,1)S(1)} %get-tuple-element.472.refs_2_), channel_id=1, source_target_pairs={{0,8},{1,9},{2,10},{3,11},{4,12},{5,13},{6,14},{7,15},{8,16},{9,17... | collective-permute-start | bytes 1179656 | tf_op jit(solution)/shard_map/ppermute | solution.py:309
  42.6 13.2 %collective-permute-start.11 = (bf16[1,384,256]{2,1,0:T(8,128)(2,1)S(1)}, bf16[1,384,256]{2,1,0:T(8,128)(2,1)S(1)}, u32[]{:S(2)}, u32[]{:S(2)}) collective-permute-start(bf16[1,384,256]{2,1,0:T(8,128)(2,1)S(1)} %get-tuple-element.420.refs_2_), channel_id=1, source_target_pairs={{0,8},{1,9},{2,10},{3,11},{4,12},{5,13},{6,14},{7,15},{8,16},{9,17... | collective-permute-start | bytes 589832 | tf_op jit(solution)/shard_map/ppermute | solution.py:309
  60.1 21.3 %collective-permute-start.18 = (bf16[4,528,256]{2,1,0:T(8,128)(2,1)}, bf16[4,528,256]{2,1,0:T(8,128)(2,1)S(1)}, u32[]{:S(2)}, u32[]{:S(2)}) collective-permute-start(bf16[4,528,256]{2,1,0:T(8,128)(2,1)} %get-tuple-element.410), channel_id=1, source_target_pairs={{0,2},{1,3},{2,0},{3,1},{4,6},{5,7},{6,4},{7,5},{8,10},{9,11},{10,... | collective-permute-start | bytes 3244040 | tf_op jit(solution)/shard_map/ppermute | solution.py:309
  61.0 20.4 %collective-permute-start.17 = (bf16[4,512,256]{2,1,0:T(8,128)(2,1)}, bf16[4,512,256]{2,1,0:T(8,128)(2,1)S(1)}, u32[]{:S(2)}, u32[]{:S(2)}) collective-permute-start(bf16[4,512,256]{2,1,0:T(8,128)(2,1)} %get-tuple-element.450.refs_0_), channel_id=1, source_target_pairs={{0,4},{1,5},{2,6},{3,7},{4,0},{5,1},{6,2},{7,3},{8,12},{9,13},{10,... | collective-permute-start | bytes 3145736 | tf_op jit(solution)/shard_map/ppermute | solution.py:309
  62.5 9.5 %collective-permute-start.15 = (bf16[1,384,256]{2,1,0:T(8,128)(2,1)S(1)}, bf16[1,384,256]{2,1,0:T(8,128)(2,1)}, u32[]{:S(2)}, u32[]{:S(2)}) collective-permute-start(bf16[1,384,256]{2,1,0:T(8,128)(2,1)S(1)} %collective-permute-done.11.refs_3_), channel_id=1, source_target_pairs={{0,8},{1,9},{2,10},{3,11},{4,12},{5,13},{6,14},{7,15},{8,16},{9,17... | collective-permute-start | bytes 589832 | tf_op jit(solution)/shard_map/ppermute | solution.py:309
  62.5 14.0 %collective-permute-start.14 = (bf16[1,768,256]{2,1,0:T(8,128)(2,1)S(1)}, bf16[1,768,256]{2,1,0:T(8,128)(2,1)S(1)}, u32[]{:S(2)}, u32[]{:S(2)}) collective-permute-start(bf16[1,768,256]{2,1,0:T(8,128)(2,1)S(1)} %collective-permute-done.10.refs_3_), channel_id=1, source_target_pairs={{0,8},{1,9},{2,10},{3,11},{4,12},{5,13},{6,14},{7,15},{8,16},{9,17... | collective-permute-start | bytes 1179656 | tf_op jit(solution)/shard_map/ppermute | solution.py:309
  72.1 7.8 %collective-permute-start.16 = (bf16[1,384,256]{2,1,0:T(8,128)(2,1)}, bf16[1,384,256]{2,1,0:T(8,128)(2,1)}, u32[]{:S(2)}, u32[]{:S(2)}) collective-permute-start(bf16[1,384,256]{2,1,0:T(8,128)(2,1)} %collective-permute-done.15.refs_4_), channel_id=1, source_target_pairs={{0,8},{1,9},{2,10},{3,11},{4,12},{5,13},{6,14},{7,15},{8,16},{9,17... | collective-permute-start | bytes 589832 | tf_op jit(solution)/shard_map/ppermute | solution.py:309
  93.8 28.6 %collective-permute-start.21 = (bf16[4,576,256]{2,1,0:T(8,128)(2,1)}, bf16[4,576,256]{2,1,0:T(8,128)(2,1)S(1)}, u32[]{:S(2)}, u32[]{:S(2)}) collective-permute-start(bf16[4,576,256]{2,1,0:T(8,128)(2,1)} %get-tuple-element.477.refs_0_), channel_id=1, source_target_pairs={{0,4},{1,5},{2,6},{3,7},{4,0},{5,1},{6,2},{7,3},{8,12},{9,13},{10,... | collective-permute-start | bytes 3538952 | tf_op jit(solution)/shard_map/ppermute | solution.py:309
  95.3 28.4 %collective-permute-start.22 = (bf16[4,576,256]{2,1,0:T(8,128)(2,1)}, bf16[4,576,256]{2,1,0:T(8,128)(2,1)}, u32[]{:S(2)}, u32[]{:S(2)}) collective-permute-start(bf16[4,576,256]{2,1,0:T(8,128)(2,1)} %get-tuple-element.436), channel_id=1, source_target_pairs={{0,2},{1,3},{2,0},{3,1},{4,6},{5,7},{6,4},{7,5},{8,10},{9,11},{10,... | collective-permute-start | bytes 3538952 | tf_op jit(solution)/shard_map/ppermute | solution.py:309
  96.1 22.2 %collective-permute-start.19 = (bf16[1,768,256]{2,1,0:T(8,128)(2,1)}, bf16[1,768,256]{2,1,0:T(8,128)(2,1)}, u32[]{:S(2)}, u32[]{:S(2)}) collective-permute-start(bf16[1,768,256]{2,1,0:T(8,128)(2,1)} %copy-done.51), channel_id=1, source_target_pairs={{0,8},{1,9},{2,10},{3,11},{4,12},{5,13},{6,14},{7,15},{8,16},{9,17... | collective-permute-start | bytes 1179656 | tf_op jit(solution)/shard_map/ppermute | solution.py:309
  132.9 34.3 %collective-permute-start.25 = (bf16[4,704,256]{2,1,0:T(8,128)(2,1)}, bf16[4,704,256]{2,1,0:T(8,128)(2,1)}, u32[]{:S(2)}, u32[]{:S(2)}) collective-permute-start(bf16[4,704,256]{2,1,0:T(8,128)(2,1)} %get-tuple-element.499.refs_0_), channel_id=1, source_target_pairs={{0,4},{1,5},{2,6},{3,7},{4,0},{5,1},{6,2},{7,3},{8,12},{9,13},{10,... | collective-permute-start | bytes 4325384 | tf_op jit(solution)/shard_map/ppermute | solution.py:309
  133.5 34.0 %collective-permute-start.26 = (bf16[4,704,256]{2,1,0:T(8,128)(2,1)}, bf16[4,704,256]{2,1,0:T(8,128)(2,1)}, u32[]{:S(2)}, u32[]{:S(2)}) collective-permute-start(bf16[4,704,256]{2,1,0:T(8,128)(2,1)} %get-tuple-element.463), channel_id=1, source_target_pairs={{0,2},{1,3},{2,0},{3,1},{4,6},{5,7},{6,4},{7,5},{8,10},{9,11},{10,... | collective-permute-start | bytes 4325384 | tf_op jit(solution)/shard_map/ppermute | solution.py:309
  134.6 16.3 %collective-permute-start.24 = (bf16[4,256,256]{2,1,0:T(8,128)(2,1)}, bf16[4,256,256]{2,1,0:T(8,128)(2,1)}, u32[]{:S(2)}, u32[]{:S(2)}) collective-permute-start(bf16[4,256,256]{2,1,0:T(8,128)(2,1)} %rearrange.16.refs_5_), channel_id=1, source_target_pairs={{0,8},{1,9},{2,10},{3,11},{4,12},{5,13},{6,14},{7,15},{8,16},{9,17... | collective-permute-start | bytes 1572872 | tf_op jit(solution)/shard_map/ppermute | solution.py:309
  173.9 26.9 %collective-permute-start.29 = (bf16[4,512,256]{2,1,0:T(8,128)(2,1)}, bf16[4,512,256]{2,1,0:T(8,128)(2,1)}, u32[]{:S(2)}, u32[]{:S(2)}) collective-permute-start(bf16[4,512,256]{2,1,0:T(8,128)(2,1)} %get-tuple-element.527.refs_0_), channel_id=1, source_target_pairs={{0,4},{1,5},{2,6},{3,7},{4,0},{5,1},{6,2},{7,3},{8,12},{9,13},{10,... | collective-permute-start | bytes 3145736 | tf_op jit(solution)/shard_map/ppermute | solution.py:309
  175.4 25.5 %collective-permute-start.30 = (bf16[4,512,256]{2,1,0:T(8,128)(2,1)}, bf16[4,512,256]{2,1,0:T(8,128)(2,1)}, u32[]{:S(2)}, u32[]{:S(2)}) collective-permute-start(bf16[4,512,256]{2,1,0:T(8,128)(2,1)} %get-tuple-element.490), channel_id=1, source_target_pairs={{0,2},{1,3},{2,0},{3,1},{4,6},{5,7},{6,4},{7,5},{8,10},{9,11},{10,... | collective-permute-start | bytes 3145736 | tf_op jit(solution)/shard_map/ppermute | solution.py:309
  176.1 24.6 %collective-permute-start.28 = (bf16[4,256,256]{2,1,0:T(8,128)(2,1)}, bf16[4,256,256]{2,1,0:T(8,128)(2,1)}, u32[]{:S(2)}, u32[]{:S(2)}) collective-permute-start(bf16[4,256,256]{2,1,0:T(8,128)(2,1)} %collective-permute-done.24.refs_6_), channel_id=1, source_target_pairs={{0,8},{1,9},{2,10},{3,11},{4,12},{5,13},{6,14},{7,15},{8,16},{9,17... | collective-permute-start | bytes 1572872 | tf_op jit(solution)/shard_map/ppermute | solution.py:309
  204.2 8.4 %collective-permute-start.31 = (bf16[2,4096,256]{2,1,0:T(8,128)(2,1)S(1)}, bf16[2,4096,256]{2,1,0:T(8,128)(2,1)S(1)}, u32[]{:S(2)}, u32[]{:S(2)}) collective-permute-start(bf16[2,4096,256]{2,1,0:T(8,128)(2,1)S(1)} %half_weights.8.own), channel_id=1, source_target_pairs={{0,1},{1,0},{2,3},{3,2},{4,5},{5,4},{6,7},{7,6},{8,9},{9,8},{10,11... | collective-permute-start | bytes 12582920 | tf_op jit(solution)/shard_map/ppermute | solution.py:309
  204.3 16.5 %collective-permute-start.32 = (bf16[4,256,256]{2,1,0:T(8,128)(2,1)}, bf16[4,256,256]{2,1,0:T(8,128)(2,1)S(1)}, u32[]{:S(2)}, u32[]{:S(2)}) collective-permute-start(bf16[4,256,256]{2,1,0:T(8,128)(2,1)} %collective-permute-done.28.refs_7_), channel_id=1, source_target_pairs={{0,8},{1,9},{2,10},{3,11},{4,12},{5,13},{6,14},{7,15},{8,16},{9,17... | collective-permute-start | bytes 1572872 | tf_op jit(solution)/shard_map/ppermute | solution.py:309
  207.4 11.5 %collective-permute-start.34 = (bf16[4,128,256]{2,1,0:T(8,128)(2,1)S(1)}, bf16[4,128,256]{2,1,0:T(8,128)(2,1)S(1)}, u32[]{:S(2)}, u32[]{:S(2)}) collective-permute-start(bf16[4,128,256]{2,1,0:T(8,128)(2,1)S(1)} %get-tuple-element.513), channel_id=1, source_target_pairs={{0,2},{1,3},{2,0},{3,1},{4,6},{5,7},{6,4},{7,5},{8,10},{9,11},{10,... | collective-permute-start | bytes 786440 | tf_op jit(solution)/shard_map/ppermute | solution.py:309
  208.4 10.5 %collective-permute-start.33 = (bf16[4,128,256]{2,1,0:T(8,128)(2,1)S(1)}, bf16[4,128,256]{2,1,0:T(8,128)(2,1)S(1)}, u32[]{:S(2)}, u32[]{:S(2)}) collective-permute-start(bf16[4,128,256]{2,1,0:T(8,128)(2,1)S(1)} %get-tuple-element.511), channel_id=1, source_target_pairs={{0,4},{1,5},{2,6},{3,7},{4,0},{5,1},{6,2},{7,3},{8,12},{9,13},{10,... | collective-permute-start | bytes 786440 | tf_op jit(solution)/shard_map/ppermute | solution.py:309
  227.0 11.2 %collective-permute-start.36 = (bf16[2,4096,256]{2,1,0:T(8,128)(2,1)S(1)}, bf16[2,4096,256]{2,1,0:T(8,128)(2,1)S(1)}, u32[]{:S(2)}, u32[]{:S(2)}) collective-permute-start(bf16[2,4096,256]{2,1,0:T(8,128)(2,1)S(1)} %half_weights.9.own), channel_id=1, source_target_pairs={{0,1},{1,0},{2,3},{3,2},{4,5},{5,4},{6,7},{7,6},{8,9},{9,8},{10,11... | collective-permute-start | bytes 12582920 | tf_op jit(solution)/shard_map/ppermute | solution.py:309
  238.2 16.2 %collective-permute-start.37 = (bf16[4,1,256,256]{3,2,1,0:T(8,128)(2,1)S(1)}, bf16[4,1,256,256]{3,2,1,0:T(8,128)(2,1)S(1)}, u32[]{:S(2)}, u32[]{:S(2)}) collective-permute-start(bf16[4,1,256,256]{3,2,1,0:T(8,128)(2,1)S(1)} %get-tuple-element.540), channel_id=1, source_target_pairs={{0,4},{1,5},{2,6},{3,7},{4,0},{5,1},{6,2},{7,3},{8,12},{9,13},{10,... | collective-permute-start | bytes 1572872 | tf_op jit(solution)/shard_map/ppermute | solution.py:309
  239.5 14.9 %collective-permute-start.38 = (bf16[4,1,256,256]{3,2,1,0:T(8,128)(2,1)S(1)}, bf16[4,1,256,256]{3,2,1,0:T(8,128)(2,1)S(1)}, u32[]{:S(2)}, u32[]{:S(2)}) collective-permute-start(bf16[4,1,256,256]{3,2,1,0:T(8,128)(2,1)S(1)} %get-tuple-element.542), channel_id=1, source_target_pairs={{0,2},{1,3},{2,0},{3,1},{4,6},{5,7},{6,4},{7,5},{8,10},{9,11},{10,... | collective-permute-start | bytes 1572872 | tf_op jit(solution)/shard_map/ppermute | solution.py:309
  254.4 14.3 %collective-permute-start.39 = (bf16[1,2,1024,1024]{3,2,1,0:T(8,128)(2,1)}, bf16[1,2,1024,1024]{3,2,1,0:T(8,128)(2,1)}, u32[]{:S(2)}, u32[]{:S(2)}) collective-permute-start(bf16[1,2,1024,1024]{3,2,1,0:T(8,128)(2,1)} %weight_terms.8), channel_id=1, source_target_pairs={{0,1},{1,0},{2,3},{3,2},{4,5},{5,4},{6,7},{7,6},{8,9},{9,8},{10,11... | collective-permute-start | bytes 12582920 | tf_op jit(solution)/shard_map/ppermute | solution.py:309
  276.2 38.1 %collective-permute-start.40 = (bf16[4,1,512,256]{3,2,1,0:T(8,128)(2,1)}, bf16[4,1,512,256]{3,2,1,0:T(8,128)(2,1)S(1)}, u32[]{:S(2)}, u32[]{:S(2)}) collective-permute-start(bf16[4,1,512,256]{3,2,1,0:T(8,128)(2,1)} %get-tuple-element.557), channel_id=1, source_target_pairs={{0,4},{1,5},{2,6},{3,7},{4,0},{5,1},{6,2},{7,3},{8,12},{9,13},{10,... | collective-permute-start | bytes 3145736 | tf_op jit(solution)/shard_map/ppermute | solution.py:309
  277.6 36.7 %collective-permute-start.41 = (bf16[4,1,512,256]{3,2,1,0:T(8,128)(2,1)}, bf16[4,1,512,256]{3,2,1,0:T(8,128)(2,1)}, u32[]{:S(2)}, u32[]{:S(2)}) collective-permute-start(bf16[4,1,512,256]{3,2,1,0:T(8,128)(2,1)} %get-tuple-element.559), channel_id=1, source_target_pairs={{0,2},{1,3},{2,0},{3,1},{4,6},{5,7},{6,4},{7,5},{8,10},{9,11},{10,... | collective-permute-start | bytes 3145736 | tf_op jit(solution)/shard_map/ppermute | solution.py:309
  278.4 34.9 %collective-permute-start.42 = (bf16[4,1,64,1024]{3,2,1,0:T(8,128)(2,1)}, bf16[4,1,64,1024]{3,2,1,0:T(8,128)(2,1)S(1)}, u32[]{:S(2)}, u32[]{:S(2)}) collective-permute-start(bf16[4,1,64,1024]{3,2,1,0:T(8,128)(2,1)} %get-tuple-element.560), channel_id=1, source_target_pairs={{0,4},{1,5},{2,6},{3,7},{4,0},{5,1},{6,2},{7,3},{8,12},{9,13},{10,... | collective-permute-start | bytes 1572872 | tf_op jit(solution)/shard_map/ppermute | solution.py:309
  279.6 34.7 %collective-permute-start.43 = (bf16[4,1,64,1024]{3,2,1,0:T(8,128)(2,1)}, bf16[4,1,64,1024]{3,2,1,0:T(8,128)(2,1)}, u32[]{:S(2)}, u32[]{:S(2)}) collective-permute-start(bf16[4,1,64,1024]{3,2,1,0:T(8,128)(2,1)} %get-tuple-element.562), channel_id=1, source_target_pairs={{0,2},{1,3},{2,0},{3,1},{4,6},{5,7},{6,4},{7,5},{8,10},{9,11},{10,... | collective-permute-start | bytes 1572872 | tf_op jit(solution)/shard_map/ppermute | solution.py:309
  314.3 25.4 %collective-permute-start.44 = (bf16[2,2,1024,256]{3,2,1,0:T(8,128)(2,1)}, bf16[2,2,1024,256]{3,2,1,0:T(8,128)(2,1)}, u32[]{:S(2)}, u32[]{:S(2)}) collective-permute-start(bf16[2,2,1024,256]{3,2,1,0:T(8,128)(2,1)} %memory_terms.2), channel_id=1, source_target_pairs={{0,1},{1,0},{2,3},{3,2},{4,5},{5,4},{6,7},{7,6},{8,9},{9,8},{10,11... | collective-permute-start | bytes 6291464 | tf_op jit(solution)/shard_map/ppermute | solution.py:309
  318.7 34.7 %collective-permute-start.46 = (bf16[4,1,128,1024]{3,2,1,0:T(8,128)(2,1)}, bf16[4,1,128,1024]{3,2,1,0:T(8,128)(2,1)}, u32[]{:S(2)}, u32[]{:S(2)}) collective-permute-start(bf16[4,1,128,1024]{3,2,1,0:T(8,128)(2,1)} %get-tuple-element.586), channel_id=1, source_target_pairs={{0,4},{1,5},{2,6},{3,7},{4,0},{5,1},{6,2},{7,3},{8,12},{9,13},{10,... | collective-permute-start | bytes 3145736 | tf_op jit(solution)/shard_map/ppermute | solution.py:309
  319.5 33.8 %collective-permute-start.47 = (bf16[4,1,128,1024]{3,2,1,0:T(8,128)(2,1)}, bf16[4,1,128,1024]{3,2,1,0:T(8,128)(2,1)}, u32[]{:S(2)}, u32[]{:S(2)}) collective-permute-start(bf16[4,1,128,1024]{3,2,1,0:T(8,128)(2,1)} %get-tuple-element.588), channel_id=1, source_target_pairs={{0,2},{1,3},{2,0},{3,1},{4,6},{5,7},{6,4},{7,5},{8,10},{9,11},{10,... | collective-permute-start | bytes 3145736 | tf_op jit(solution)/shard_map/ppermute | solution.py:309
  321.8 31.5 %collective-permute-start.45 = (bf16[1,512,256]{2,1,0:T(8,128)(2,1)S(1)}, bf16[1,512,256]{2,1,0:T(8,128)(2,1)S(1)}, u32[]{:S(2)}, u32[]{:S(2)}) collective-permute-start(bf16[1,512,256]{2,1,0:T(8,128)(2,1)S(1)} %fusion.9), channel_id=1, source_target_pairs={{0,8},{1,9},{2,10},{3,11},{4,12},{5,13},{6,14},{7,15},{8,16},{9,17... | collective-permute-start | bytes 786440 | tf_op jit(solution)/shard_map/ppermute | solution.py:309
  353.3 14.0 %collective-permute-start.48 = (bf16[6,2,1024,256]{3,2,1,0:T(8,128)(2,1)}, bf16[6,2,1024,256]{3,2,1,0:T(8,128)(2,1)}, u32[]{:S(2)}, u32[]{:S(2)}) collective-permute-start(bf16[6,2,1024,256]{3,2,1,0:T(8,128)(2,1)} %weight_terms.10), channel_id=1, source_target_pairs={{0,1},{1,0},{2,3},{3,2},{4,5},{5,4},{6,7},{7,6},{8,9},{9,8},{10,11... | collective-permute-start | bytes 18874376 | tf_op jit(solution)/shard_map/ppermute | solution.py:309
  356.5 20.3 %collective-permute-start.50 = (bf16[1,128,1024]{2,1,0:T(8,128)(2,1)S(1)}, bf16[1,128,1024]{2,1,0:T(8,128)(2,1)S(1)}, u32[]{:S(2)}, u32[]{:S(2)}) collective-permute-start(bf16[1,128,1024]{2,1,0:T(8,128)(2,1)S(1)} %fusion.10), channel_id=1, source_target_pairs={{0,8},{1,9},{2,10},{3,11},{4,12},{5,13},{6,14},{7,15},{8,16},{9,17... | collective-permute-start | bytes 786440 | tf_op jit(solution)/shard_map/ppermute | solution.py:309
  356.5 21.0 %collective-permute-start.49 = (bf16[1,512,256]{2,1,0:T(8,128)(2,1)}, bf16[1,512,256]{2,1,0:T(8,128)(2,1)S(1)}, u32[]{:S(2)}, u32[]{:S(2)}) collective-permute-start(bf16[1,512,256]{2,1,0:T(8,128)(2,1)} %fusion.7), channel_id=1, source_target_pairs={{0,8},{1,9},{2,10},{3,11},{4,12},{5,13},{6,14},{7,15},{8,16},{9,17... | collective-permute-start | bytes 786440 | tf_op jit(solution)/shard_map/ppermute | solution.py:309
  357.7 19.8 %collective-permute-start.51 = (bf16[4,2,64,256]{3,2,1,0:T(8,128)(2,1)}, bf16[4,2,64,256]{3,2,1,0:T(8,128)(2,1)}, u32[]{:S(2)}, u32[]{:S(2)}) collective-permute-start(bf16[4,2,64,256]{3,2,1,0:T(8,128)(2,1)} %get-tuple-element.607), channel_id=1, source_target_pairs={{0,4},{1,5},{2,6},{3,7},{4,0},{5,1},{6,2},{7,3},{8,12},{9,13},{10,... | collective-permute-start | bytes 786440 | tf_op jit(solution)/shard_map/ppermute | solution.py:309
  358.5 19.0 %collective-permute-start.52 = (bf16[4,2,64,256]{3,2,1,0:T(8,128)(2,1)}, bf16[4,2,64,256]{3,2,1,0:T(8,128)(2,1)}, u32[]{:S(2)}, u32[]{:S(2)}) collective-permute-start(bf16[4,2,64,256]{3,2,1,0:T(8,128)(2,1)} %get-tuple-element.609), channel_id=1, source_target_pairs={{0,2},{1,3},{2,0},{3,1},{4,6},{5,7},{6,4},{7,5},{8,10},{9,11},{10,... | collective-permute-start | bytes 786440 | tf_op jit(solution)/shard_map/ppermute | solution.py:309
  377.5 36.9 %collective-permute-start.56 = (bf16[4,6,64,256]{3,2,1,0:T(8,128)(2,1)}, bf16[4,6,64,256]{3,2,1,0:T(8,128)(2,1)}, u32[]{:S(2)}, u32[]{:S(2)}) collective-permute-start(bf16[4,6,64,256]{3,2,1,0:T(8,128)(2,1)} %get-tuple-element.628), channel_id=1, source_target_pairs={{0,4},{1,5},{2,6},{3,7},{4,0},{5,1},{6,2},{7,3},{8,12},{9,13},{10,... | collective-permute-start | bytes 2359304 | tf_op jit(solution)/shard_map/ppermute | solution.py:309
  378.2 36.2 %collective-permute-start.57 = (bf16[4,6,64,256]{3,2,1,0:T(8,128)(2,1)}, bf16[4,6,64,256]{3,2,1,0:T(8,128)(2,1)}, u32[]{:S(2)}, u32[]{:S(2)}) collective-permute-start(bf16[4,6,64,256]{3,2,1,0:T(8,128)(2,1)} %get-tuple-element.630), channel_id=1, source_target_pairs={{0,2},{1,3},{2,0},{3,1},{4,6},{5,7},{6,4},{7,5},{8,10},{9,11},{10,... | collective-permute-start | bytes 2359304 | tf_op jit(solution)/shard_map/ppermute | solution.py:309
  383.0 31.4 %collective-permute-start.54 = (bf16[4,2,128,256]{3,2,1,0:T(8,128)(2,1)}, bf16[4,2,128,256]{3,2,1,0:T(8,128)(2,1)}, u32[]{:S(2)}, u32[]{:S(2)}) collective-permute-start(bf16[4,2,128,256]{3,2,1,0:T(8,128)(2,1)} %get-tuple-element.625), channel_id=1, source_target_pairs={{0,4},{1,5},{2,6},{3,7},{4,0},{5,1},{6,2},{7,3},{8,12},{9,13},{10,... | collective-permute-start | bytes 1572872 | tf_op jit(solution)/shard_map/ppermute | solution.py:309
  383.8 30.6 %collective-permute-start.55 = (bf16[4,2,128,256]{3,2,1,0:T(8,128)(2,1)}, bf16[4,2,128,256]{3,2,1,0:T(8,128)(2,1)}, u32[]{:S(2)}, u32[]{:S(2)}) collective-permute-start(bf16[4,2,128,256]{3,2,1,0:T(8,128)(2,1)} %get-tuple-element.627), channel_id=1, source_target_pairs={{0,2},{1,3},{2,0},{3,1},{4,6},{5,7},{6,4},{7,5},{8,10},{9,11},{10,... | collective-permute-start | bytes 1572872 | tf_op jit(solution)/shard_map/ppermute | solution.py:309
  386.8 27.5 %collective-permute-start.53 = (bf16[1,512,256]{2,1,0:T(8,128)(2,1)}, bf16[1,512,256]{2,1,0:T(8,128)(2,1)S(1)}, u32[]{:S(2)}, u32[]{:S(2)}) collective-permute-start(bf16[1,512,256]{2,1,0:T(8,128)(2,1)} %fusion.6), channel_id=1, source_target_pairs={{0,8},{1,9},{2,10},{3,11},{4,12},{5,13},{6,14},{7,15},{8,16},{9,17... | collective-permute-start | bytes 786440 | tf_op jit(solution)/shard_map/ppermute | solution.py:309
  419.1 37.0 %collective-permute-start.65 = (bf16[4,6,128,256]{3,2,1,0:T(8,128)(2,1)}, bf16[4,6,128,256]{3,2,1,0:T(8,128)(2,1)S(1)}, u32[]{:S(2)}, u32[]{:S(2)}) collective-permute-start(bf16[4,6,128,256]{3,2,1,0:T(8,128)(2,1)} %get-tuple-element.669), channel_id=1, source_target_pairs={{0,4},{1,5},{2,6},{3,7},{4,0},{5,1},{6,2},{7,3},{8,12},{9,13},{10,... | collective-permute-start | bytes 4718600 | tf_op jit(solution)/shard_map/ppermute | solution.py:309
  419.9 36.7 %collective-permute-start.66 = (bf16[4,6,128,256]{3,2,1,0:T(8,128)(2,1)}, bf16[4,6,128,256]{3,2,1,0:T(8,128)(2,1)S(1)}, u32[]{:S(2)}, u32[]{:S(2)}) collective-permute-start(bf16[4,6,128,256]{3,2,1,0:T(8,128)(2,1)} %get-tuple-element.671), channel_id=1, source_target_pairs={{0,2},{1,3},{2,0},{3,1},{4,6},{5,7},{6,4},{7,5},{8,10},{9,11},{10,... | collective-permute-start | bytes 4718600 | tf_op jit(solution)/shard_map/ppermute | solution.py:309
  422.7 14.5 %collective-permute-start.62 = (bf16[1,128,1024]{2,1,0:T(8,128)(2,1)S(1)}, bf16[1,128,1024]{2,1,0:T(8,128)(2,1)S(1)}, u32[]{:S(2)}, u32[]{:S(2)}) collective-permute-start(bf16[1,128,1024]{2,1,0:T(8,128)(2,1)S(1)} %fusion.4), channel_id=1, source_target_pairs={{0,8},{1,9},{2,10},{3,11},{4,12},{5,13},{6,14},{7,15},{8,16},{9,17... | collective-permute-start | bytes 786440 | tf_op jit(solution)/shard_map/ppermute | solution.py:309
  426.8 10.3 %collective-permute-start.60 = (f32[2,2,544]{2,1,0:T(2,128)S(1)}, f32[2,2,544]{2,1,0:T(2,128)S(1)}, u32[]{:S(2)}, u32[]{:S(2)}) collective-permute-start(f32[2,2,544]{2,1,0:T(2,128)S(1)} %fusion.24), channel_id=1, source_target_pairs={{0,8},{1,9},{2,10},{3,11},{4,12},{5,13},{6,14},{7,15},{8,16},{9,17... | collective-permute-start | bytes 26120 | tf_op jit(solution)/shard_map/ppermute | solution.py:309
  427.9 14.8 %collective-permute-start.64 = (bf16[2,128,256]{2,1,0:T(8,128)(2,1)S(1)}, bf16[2,128,256]{2,1,0:T(8,128)(2,1)S(1)}, u32[]{:S(2)}, u32[]{:S(2)}) collective-permute-start(bf16[2,128,256]{2,1,0:T(8,128)(2,1)S(1)} %fusion.13), channel_id=1, source_target_pairs={{0,8},{1,9},{2,10},{3,11},{4,12},{5,13},{6,14},{7,15},{8,16},{9,17... | collective-permute-start | bytes 393224 | tf_op jit(solution)/shard_map/ppermute | solution.py:309
  439.9 8.8 %collective-permute-start.63 = (bf16[1,128,1024]{2,1,0:T(8,128)(2,1)S(1)}, bf16[1,128,1024]{2,1,0:T(8,128)(2,1)S(1)}, u32[]{:S(2)}, u32[]{:S(2)}) collective-permute-start(bf16[1,128,1024]{2,1,0:T(8,128)(2,1)S(1)} %fusion.5), channel_id=1, source_target_pairs={{0,8},{1,9},{2,10},{3,11},{4,12},{5,13},{6,14},{7,15},{8,16},{9,17... | collective-permute-start | bytes 786440 | tf_op jit(solution)/shard_map/ppermute | solution.py:309
  458.1 14.7 %collective-permute-start.68 = (bf16[6,128,256]{2,1,0:T(8,128)(2,1)S(1)}, bf16[6,128,256]{2,1,0:T(8,128)(2,1)S(1)}, u32[]{:S(2)}, u32[]{:S(2)}) collective-permute-start(bf16[6,128,256]{2,1,0:T(8,128)(2,1)S(1)} %fusion.8), channel_id=1, source_target_pairs={{0,8},{1,9},{2,10},{3,11},{4,12},{5,13},{6,14},{7,15},{8,16},{9,17... | collective-permute-start | bytes 1179656 | tf_op jit(solution)/shard_map/ppermute | solution.py:309
  459.2 13.6 %collective-permute-start.69 = (bf16[2,128,256]{2,1,0:T(8,128)(2,1)S(1)}, bf16[2,128,256]{2,1,0:T(8,128)(2,1)S(1)}, u32[]{:S(2)}, u32[]{:S(2)}) collective-permute-start(bf16[2,128,256]{2,1,0:T(8,128)(2,1)S(1)} %fusion.12), channel_id=1, source_target_pairs={{0,8},{1,9},{2,10},{3,11},{4,12},{5,13},{6,14},{7,15},{8,16},{9,17... | collective-permute-start | bytes 393224 | tf_op jit(solution)/shard_map/ppermute | solution.py:309
  473.7 13.5 %collective-permute-start.71 = (bf16[6,128,256]{2,1,0:T(8,128)(2,1)S(1)}, bf16[6,128,256]{2,1,0:T(8,128)(2,1)S(1)}, u32[]{:S(2)}, u32[]{:S(2)}) collective-permute-start(bf16[6,128,256]{2,1,0:T(8,128)(2,1)S(1)} %fusion.1), channel_id=1, source_target_pairs={{0,8},{1,9},{2,10},{3,11},{4,12},{5,13},{6,14},{7,15},{8,16},{9,17... | collective-permute-start | bytes 1179656 | tf_op jit(solution)/shard_map/ppermute | solution.py:309
  474.8 12.4 %collective-permute-start.72 = (bf16[2,128,256]{2,1,0:T(8,128)(2,1)S(1)}, bf16[2,128,256]{2,1,0:T(8,128)(2,1)S(1)}, u32[]{:S(2)}, u32[]{:S(2)}) collective-permute-start(bf16[2,128,256]{2,1,0:T(8,128)(2,1)S(1)} %fusion.11), channel_id=1, source_target_pairs={{0,8},{1,9},{2,10},{3,11},{4,12},{5,13},{6,14},{7,15},{8,16},{9,17... | collective-permute-start | bytes 393224 | tf_op jit(solution)/shard_map/ppermute | solution.py:309
  487.5 9.8 %collective-permute-start.73 = (bf16[6,128,256]{2,1,0:T(8,128)(2,1)S(1)}, bf16[6,128,256]{2,1,0:T(8,128)(2,1)S(1)}, u32[]{:S(2)}, u32[]{:S(2)}) collective-permute-start(bf16[6,128,256]{2,1,0:T(8,128)(2,1)S(1)} %fusion), channel_id=1, source_target_pairs={{0,8},{1,9},{2,10},{3,11},{4,12},{5,13},{6,14},{7,15},{8,16},{9,17... | collective-permute-start | bytes 1179656 | tf_op jit(solution)/shard_map/ppermute | solution.py:309
  (115 other events, 1353.9 us)

commit v5 on v4

--- a/solution.py
+++ b/solution.py
@@ -320,34 +320,17 @@
 
 
 def half_kernel(parts, ring, wide, g, rows, place, *refs):
-    arrays, (out, sems) = refs[:-2], refs[-2:]
+    *arrays, out = refs
     z, x, y = place[0], place[1], place[2]
-    height, cols = wide * rows, out.shape[-1]
-    copies = []
-
-    def copy(src, dst):
-        copies.append(pltpu.make_async_copy(src, dst, sems.at[len(copies)]))
-
+    height = wide * rows
     for which, first_row, count, offset, labels in parts:
-        piece = arrays[which]
         for i, (dz, dx, dy) in enumerate(labels):
             row = 2 * lax.rem(z + (ring - dz), ring) + (x + dx - 2 * x * dx)
             col = y + dy - 2 * y * dy
-            pieces = segments(offset, count, g, rows)
-            if pieces[0][3] == rows and len([p for p in pieces if p[0] < g]) == g:
-                copy(
-                    piece.at[i, pl.ds(first_row, g * rows)].reshape(g, rows, cols),
-                    out.at[col, pl.ds(0, g * height)].reshape(g, wide, rows, cols).at[:, row],
-                )
-                pieces = [p for p in pieces if p[0] == g]
-            for k, matrix_row, at, n in pieces:
+            for k, matrix_row, at, n in segments(offset, count, g, rows):
                 each = rows if k < g else SMALL_ROWS
                 first = pl.multiple_of(k * height + row * each + matrix_row, 16)
-                copy(piece.at[i, pl.ds(first_row + at, n)], out.at[col, pl.ds(first, n)])
-    for one in copies:
-        one.start()
-    for one in copies:
-        one.wait()
+                out[col, pl.ds(first, n)] = arrays[which][i, pl.ds(first_row + at, n)]
 
 
 def anywhere(count):
@@ -358,15 +341,10 @@
 
 
 def rearrange_kernel(moves, n_in, *refs):
-    ins, outs, sems = refs[:n_in], refs[n_in:-1], refs[-1]
-    copies = []
+    ins, outs = refs[:n_in], refs[n_in:]
     for i, bi, ri, ci, rows, o, bo, ro in moves:
-        src = ins[i].at[bi, pl.ds(ri, rows), pl.ds(ci, outs[o].shape[-1])]
-        copies.append(pltpu.make_async_copy(src, outs[o].at[bo, pl.ds(ro, rows)], sems.at[len(copies)]))
-    for one in copies:
-        one.start()
-    for one in copies:
-        one.wait()
+        cols = outs[o].shape[-1]
+        outs[o][bo, pl.ds(ro, rows)] = ins[i][bi, pl.ds(ri, rows), pl.ds(ci, cols)]
 
 
 class Rearrange:
@@ -390,10 +368,9 @@
     def run(self, clock):
         outs = pl.pallas_call(
             functools.partial(rearrange_kernel, self.moves, len(self.ins)),
-            in_specs=anywhere(len(self.ins)),
+            in_specs=[pl.BlockSpec(memory_space=pltpu.VMEM)] * len(self.ins),
             out_specs=[pl.BlockSpec(memory_space=pltpu.VMEM)] * len(self.shapes),
             out_shape=[jax.ShapeDtypeStruct(shape, BF16) for shape in self.shapes],
-            scratch_shapes=[pltpu.SemaphoreType.DMA((len(self.moves),))],
             compiler_params=BIG_VMEM,
             cost_estimate=CHEAP,
             name="rearrange",
@@ -411,20 +388,18 @@
         self.parts.append((labels, array, first_row, count, offset))
 
     def half(self, *after):
-        grid, arrays, parts, n = self.grid, [], [], 0
+        grid, arrays, parts = self.grid, [], []
         for labels, array, first_row, count, offset in self.parts:
             which = [i for i, known in enumerate(arrays) if known is array]
             if not which:
                 arrays.append(array)
                 which = [len(arrays) - 1]
             parts.append((which[0], first_row, count, offset, labels))
-            n += len(labels) * len(segments(offset, count, self.g, self.rows))
         self.own = pl.pallas_call(
             functools.partial(half_kernel, parts, grid.ring, grid.wide, self.g, self.rows),
-            in_specs=[PLACE] + anywhere(len(arrays)),
+            in_specs=[PLACE] + [pl.BlockSpec(memory_space=pltpu.VMEM)] * len(arrays),
             out_specs=pl.BlockSpec(memory_space=pltpu.VMEM),
             out_shape=jax.ShapeDtypeStruct((2, grid.wide * self.height, self.cols), BF16),
-            scratch_shapes=[pltpu.SemaphoreType.DMA((n,))],
             compiler_params=BIG_VMEM,
             cost_estimate=CHEAP,
             name="half_weights",
@@ -889,10 +864,15 @@
         out[:, at] = total.astype(BF16)
 
 
-def down_back_kernel(place, grad, slope, own, other, grad_pre, bias_grad):
+def down_back_kernel(place, grad, slope, normed, own, other, grad_pre, bias_grad, far):
     back = (times_t(place, grad, own, other) * slope[...].astype(F32)).astype(BF16)
     grad_pre[...] = back
     bias_grad[...] = column_sum(back)
+    for i, n in enumerate(corners(place)[0]):
+
+        @pl.when(pl.program_id(0) == n)
+        def _():
+            far[0, i] = dot_tn(normed[...], back).astype(BF16)
 
 
 def up_back_kernel(
@@ -1203,20 +1183,22 @@
     r_fc2.swap()
     g_fc2.half()
     g_fc2.swap()
-    tick(r_fc2.near(), g_fc2.other)
+    tick(r_fc2.near())
     slab = hidden // 4
     some = lambda array: (array, (token_count, slab), lambda s, *_: (0, s))
-    grad_pre, grad_up_bias = dense_call(
+    grad_pre, grad_up_bias, far_fc1 = dense_call(
         down_back_kernel, "fc2_gelu_back", place,
-        [full(now(cotangent)), some(slope)] + by_rows(g_fc2, slab),
+        [full(now(cotangent)), some(slope), full(normed_three)] + by_rows(g_fc2, slab),
         [
             some(jax.ShapeDtypeStruct((token_count, hidden), BF16)),
             (jax.ShapeDtypeStruct((1, hidden), F32), (1, slab), lambda s, *_: (0, s)),
+            result((1, 2, D, slab), BF16),
         ],
         grid=(4,), params=FULL_VMEM,
     )
     r_fc1 = settle([(normed_three, grad_pre)], fc1)
-    tick(r_fc1.far(), *r_fc2.across())
+    r_fc1.out = far_fc1
+    tick(far_fc1, *r_fc2.across())
     r_fc2.add()
     r_fc1.swap()
     (

time: 509 us -> 502 us (0.986)
  Pallas kernels: 242 us -> 226 us
  starting transfers between devices: 56.4 us -> 68 us
    ppermute x74, starting transfers between devices: 56.4 us -> 68 us  [send(): return lax.ppermute(self.clock.now(array), AXES, self.perms[name])]
    pallas_call x11, Pallas kernels: 23.1 us -> 15.3 us  [run(): pl.pallas_call(functools.partial(rearrange_kernel, self.moves, len(self.i...]
    pallas_call x6 -> x5, Pallas kernels: 36.8 us -> 30.7 us  [token_terms(): pl.pallas_call(kernel, grid_spec=pltpu.PrefetchScalarGridSpec(num_scalar_...]
  transfers between devices with their start and end apart: 74 -> 74, of which waited for: 29 -> 28; matrix products, arithmetic and copies ran while one was open for 8% -> 8% of each run, Pallas kernels for 40% -> 40%
where the time goes in v5:
time: 502 us; the launch traced here: 495 us
  Pallas kernels  226 us (45%)
  waiting for transfers between devices  121 us (24%)
  starting transfers between devices  68 us (14%)
  local copies, waits for them, and re-layouts  56.7 us (11%)
  other arithmetic  20.8 us (4%)
    ppermute x74, waiting for transfers between devices, send(): return lax.ppermute(self.clock.now(array), AXES, self.perms[name])  121 us
    pallas_call x11, Pallas kernels, dense_call(): pl.pallas_call(kernel, grid_spec=pltpu.PrefetchScalarGridSpec(num_scalar_...  88.2 us
    ppermute x74, starting transfers between devices, send(): return lax.ppermute(self.clock.now(array), AXES, self.perms[name])  68 us
    unnamed x212, local copies, waits for them, and re-layouts  36.2 us
    pallas_call x5, Pallas kernels, token_terms(): pl.pallas_call(kernel, grid_spec=pltpu.PrefetchScalarGridSpec(num_scalar_...  30.7 us
    pallas_call x2, Pallas kernels, memory_terms(): pl.pallas_call(functools.partial(memory_terms_kernel, near, len(pairs)),...  25.7 us
    pallas_call x1, Pallas kernels, cross_backward(): pl.pallas_call(cross_bwd_kernel, grid_spec=pltpu.PrefetchScalarGridSpec(n...  20.1 us
    pallas_call x4, Pallas kernels, add_corners(): pl.pallas_call(add_corners_kernel, grid=(ring,), in_specs=[full, full, ha...  16.3 us
  transfers between devices with their start and end apart: 74, of which 28 were waited for; matrix products, arithmetic and copies ran while one was open for 8% of the time, Pallas kernels for 40%

profile of v5, /device:TPU:0, one launch (start us, length us, event | category | flops | bytes accessed | tf_op | source)
XLA Modules:
  0.0 495.3 jit_solution(1646995329869166966)
XLA Ops:
  2.5 3.1 collective-permute-start
  20.1 3.9 copy.44._
  24.0 2.1 copy-done.2
  28.0 1.8 collective-permute-start.9
  29.8 7.3 %collective-permute-done.9.refs_7_ = bf16[1,16,256]{2,1,0:T(8,128)(2,1)S(1)} collective-permute-done((bf16[1,16,256]{2,1,0:T(8,128)(2,1)S(1)}, bf16[1,16,256]{2,1,0:T(8,128)(2,1)S(1)}, u32[]{:S(2)}, u32[]{:S(2)}) %collective-permute-start.9) | collective-permute-done | bytes 8224 | tf_op jit(solution)/shard_map/ppermute | solution.py:309
  41.0 12.4 %collective-permute-done.11.refs_3_ = bf16[1,384,256]{2,1,0:T(8,128)(2,1)S(1)} collective-permute-done((bf16[1,384,256]{2,1,0:T(8,128)(2,1)S(1)}, bf16[1,384,256]{2,1,0:T(8,128)(2,1)S(1)}, u32[]{:S(2)}, u32[]{:S(2)}) %collective-permute-start.11) | collective-permute-done | bytes 196640 | tf_op jit(solution)/shard_map/ppermute | solution.py:309
  57.1 9.5 %collective-permute-done.15.refs_4_ = bf16[1,384,256]{2,1,0:T(8,128)(2,1)} collective-permute-done((bf16[1,384,256]{2,1,0:T(8,128)(2,1)S(1)}, bf16[1,384,256]{2,1,0:T(8,128)(2,1)}, u32[]{:S(2)}, u32[]{:S(2)}) %collective-permute-start.15) | collective-permute-done | bytes 196640 | tf_op jit(solution)/shard_map/ppermute | solution.py:309
  67.6 3.5 collective-permute-done.14.refs_4_
  71.1 3.4 collective-permute-done.16.refs_5_
  78.4 3.0 rearrange.18
  86.6 2.4 collective-permute-done.20.k_other.v_other
  92.6 2.4 copy-done.3
  95.0 13.8 %memory_keys_values.1 = (bf16[4,588,1024]{2,1,0:T(8,128)(2,1)S(1)}, bf16[4,588,1024]{2,1,0:T(8,128)(2,1)S(1)}) custom-call(s32[4]{0:T(128)S(1)} %pad_add_fusion.place, bf16[4,588,1024]{2,1,0:T(8,128)(2,1)S(1)} %copy-done.3, f32[13,1024]{1,0:T(8,128)S(1)} %reshape.468.vectors, bf16[2,2176,256]{2,1,0:T(8,128)(2,1)S(1)} %half_weights.5.k_own.v_own, ...), custom_call_target="tpu_custom_call" | custom-call | flops 1000000 | bytes 100000 | tf_op jit(solution)/shard_map/memory_keys_values/pallas_call | solution.py:957
  108.9 4.1 collective-permute-done.21.refs_1_.refs_3_
  114.1 3.1 rearrange.19
  119.5 1.8 half_weights.6.refs_0_.refs_2_.refs_4_
  123.8 3.4 collective-permute-done.23.refs_1_.refs_3_.refs_5_
  128.3 4.7 self_qkv.1
  137.0 2.5 collective-permute-done.24.refs_6_
  139.5 16.3 %collective-permute-done.25.refs_1_.refs_3_ = bf16[4,704,256]{2,1,0:T(8,128)(2,1)} collective-permute-done((bf16[4,704,256]{2,1,0:T(8,128)(2,1)}, bf16[4,704,256]{2,1,0:T(8,128)(2,1)}, u32[]{:S(2)}, u32[]{:S(2)}) %collective-permute-start.25) | collective-permute-done | bytes 1441824 | tf_op jit(solution)/shard_map/ppermute | solution.py:309
  156.4 3.4 rearrange.20
  159.8 2.7 half_weights.7.so_own.cq_own.own.co_own
  164.6 10.3 %collective-permute-start.28 = (bf16[4,256,256]{2,1,0:T(8,128)(2,1)}, bf16[4,256,256]{2,1,0:T(8,128)(2,1)}, u32[]{:S(2)}, u32[]{:S(2)}) collective-permute-start(bf16[4,256,256]{2,1,0:T(8,128)(2,1)} %collective-permute-done.24.refs_6_), channel_id=1, source_target_pairs={{0,8},{1,9},{2,10},{3,11},{4,12},{5,13},{6,14},{7,15},{8,16},{9,17... | collective-permute-start | bytes 1572872 | tf_op jit(solution)/shard_map/ppermute | solution.py:309
  177.8 3.9 self_out_cross_q.1
  184.3 12.5 %cross_forward.1 = (bf16[256,1024]{1,0:T(8,128)(2,1)}, f32[2,8,256]{2,1,0:T(8,128)}) custom-call(s32[4]{0:T(128)} %copy-done.102, s32[4]{0:T(128)} %select_reduce_fusion.len_ref, s32[2,1,128]{2,1,0:T(1,128)} %bitcast.125, s32[2,128,1]{2,1,0:T(8,128)} %copy-done.32, bf16[256,1024]{1,0:T(8,128)(2,1)} %copy-done.38, bf16[4,588,1024]{2,1,0:T(8,128)(2,1)} %copy-done.7, ...), custom_call_target="tpu_custom_call" | custom-call | flops 1000000 | bytes 100000 | tf_op jit(solution)/shard_map/cross_forward/pallas_call | solution.py:228
  196.9 3.1 half_weights.8.own
  200.2 3.2 rearrange.21
  205.7 2.9 cross_out.1
  208.8 4.8 fc1_gelu.1
  215.0 1.8 collective-permute-done.32.refs_8_
  216.8 2.9 weight_terms.5
  219.8 2.6 half_weights.9.own
  222.9 4.0 collective-permute-done.35.refs_2_
  226.9 3.9 weight_terms.6
  236.3 1.9 copy-done.72
  238.2 10.8 %fc2_gelu_back.1 = (bf16[256,4096]{1,0:T(8,128)(2,1)}, f32[1,4096]{1,0:T(1,128)}, bf16[1,2,1024,1024]{3,2,1,0:T(8,128)(2,1)}) custom-call(s32[4]{0:T(128)} %copy-done.60, bf16[256,1024]{1,0:T(8,128)(2,1)} %grad_out.1, bf16[256,4096]{1,0:T(8,128)(2,1)} %copy-done.44, bf16[256,1024]{1,0:T(8,128)(2,1)} %copy-done.23, bf16[2,4096,256]{2,1,0:T(8,128)(2,1)} %copy-done.5, ...), custom_call_target="tpu_custom_call" | custom-call | flops 1000000 | bytes 100000 | tf_op jit(solution)/shard_map/fc2_gelu_back/pallas_call | solution.py:957
  249.2 10.2 %fc1_norm_back.1 = (f32[256,1024]{1,0:T(8,128)}, bf16[256,1024]{1,0:T(8,128)(2,1)}, bf16[256,1024]{1,0:T(8,128)(2,1)}, f32[1,1024]{1,0:T(1,128)}, f32[1,1024]{1,...) custom-call(s32[4]{0:T(128)} %copy-done.60, bf16[256,4096]{1,0:T(8,128)(2,1)} %get-tuple-element.545.grad_pre.refs_1_, ...), custom_call_target="tpu_custom_call" | custom-call | flops 1000000 | bytes 100000 | tf_op jit(solution)/shard_map/fc1_norm_back/pallas_call | solution.py:957
  259.4 4.0 add_corners.4
  263.4 7.6 %weight_terms.7 = (bf16[4,1,64,1024]{3,2,1,0:T(8,128)(2,1)}, bf16[4,1,64,1024]{3,2,1,0:T(8,128)(2,1)}, bf16[4,1,128,1024]{3,2,1,0:T(8,128)(2,1)}, bf16[4,1,128,1024]{3,2,1,0:T(8,128)(2,1)}, f32[4,1,128,1024]{3,2,1,0:T(8,128)}) custom-call(s32[4]{0:T(128)} %copy-done.60, bf16[256,1024]{1,0:T(8,128)(2,1)} %copy-done.23, ...), custom_call_target="tpu_custom_call" | custom-call | flops 1000000 | bytes 100000 | tf_op jit(solution)/shard_map/weight_terms/pallas_call | solution.py:560
  275.1 20.1 %cross_backward.1 = (bf16[256,1024]{1,0:T(8,128)(2,1)}, bf16[4,588,1024]{2,1,0:T(8,128)(2,1)}, bf16[4,588,1024]{2,1,0:T(8,128)(2,1)}, f32[1,1024]{1,0:T(1,128)}) custom-call(s32[4]{0:T(128)} %copy-done.102, s32[4]{0:T(128)} %select_reduce_fusion.len_ref, s32[2,1,128]{2,1,0:T(1,128)} %bitcast.126, s32[2,128,1]{2,1,0:T(8,128)} %copy-done.32, ...), custom_call_target="tpu_custom_call" | custom-call | flops 1000000 | bytes 100000 | tf_op jit(solution)/shard_map/cross_backward/pallas_call | solution.py:250
  295.2 12.1 %memory_terms.2 = bf16[2,2,1024,256]{3,2,1,0:T(8,128)(2,1)} custom-call(s32[4]{0:T(128)} %copy-done.60, bf16[4,588,1024]{2,1,0:T(8,128)(2,1)} %copy-done.2, bf16[4,588,1024]{2,1,0:T(8,128)(2,1)} %get-tuple-element.620.dk.gk, bf16[4,588,1024]{2,1,0:T(8,128)(2,1)} %get-tuple-element.621.dv.gv), custom_call_target="tpu_custom_call" | custom-call | flops 1000000 | bytes 100000 | tf_op jit(solution)/shard_map/memory_terms/pallas_call | solution.py:621
  309.2 4.2 add_corners.5
  316.6 6.4 %cross_q_norm_back.1 = (f32[256,1024]{1,0:T(8,128)}, bf16[256,1024]{1,0:T(8,128)(2,1)}, bf16[256,1024]{1,0:T(8,128)(2,1)}, f32[1,1024]{1,0:T(1,128)}, f32[1,1024...) custom-call(s32[4]{0:T(128)} %copy-done.60, bf16[256,1024]{1,0:T(8,128)(2,1)} %get-tuple-element.570.grad_queries.refs_9_, ...), custom_call_target="tpu_custom_call" | custom-call | flops 1000000 | bytes 100000 | tf_op jit(solution)/shard_map/cross_q_norm_back/pallas_call | solution.py:957
  322.9 4.6 self_backward.1
  327.5 6.9 %weight_terms.8 = bf16[6,2,1024,256]{3,2,1,0:T(8,128)(2,1)} custom-call(s32[4]{0:T(128)} %copy-done.60, bf16[256,1024]{1,0:T(8,128)(2,1)} %copy-done.9, bf16[256,1024]{1,0:T(8,128)(2,1)} %get-tuple-element.595.refs_1_.gq, bf16[256,1024]{1,0:T(8,128)(2,1)} %copy-done.9, bf16[256,1024]{1,0:T(8,128)(2,1)} %get-tuple-element.596.refs_3_.gk, ...), custom_call_target="tpu_custom_call" | custom-call | flops 1000000 | bytes 100000 | tf_op jit(solution)/shard_map/weight_terms/pallas_call | solution.py:560
  334.5 13.6 %memory_terms.3 = (bf16[4,2,64,256]{3,2,1,0:T(8,128)(2,1)}, bf16[4,2,64,256]{3,2,1,0:T(8,128)(2,1)}, bf16[4,2,128,256]{3,2,1,0:T(8,128)(2,1)}, bf16[4,2,128,256]{3,2,1,0:T(8,128)(2,1)}, f32[4,2,128,256]{3,2,1,0:T(8,128)}) custom-call(s32[4]{0:T(128)} %copy-done.60, bf16[4,588,1024]{2,1,0:T(8,128)(2,1)} %copy-done.2, ...), custom_call_target="tpu_custom_call" | custom-call | flops 1000000 | bytes 100000 | tf_op jit(solution)/shard_map/memory_terms/pallas_call | solution.py:621
  356.3 7.5 %self_qkv_norm_back.1 = (bf16[256,1024]{1,0:T(8,128)(2,1)}, f32[1,1024]{1,0:T(1,128)}, f32[1,1024]{1,0:T(1,128)}, f32[1,1024]{1,0:T(1,128)}, f32[1,1024]{1,0:T(1,128)}) custom-call(s32[4]{0:T(128)} %copy-done.60, bf16[256,1024]{1,0:T(8,128)(2,1)} %tokens.4, f32[256,1024]{1,0:T(8,128)} %get-tuple-element.594.grad_after, ...), custom_call_target="tpu_custom_call" | custom-call | flops 1000000 | bytes 100000 | tf_op jit(solution)/shard_map/self_qkv_norm_back/pallas_call | solution.py:957
  363.8 9.3 %weight_terms.9 = (bf16[4,6,64,256]{3,2,1,0:T(8,128)(2,1)}, bf16[4,6,64,256]{3,2,1,0:T(8,128)(2,1)}, bf16[4,6,128,256]{3,2,1,0:T(8,128)(2,1)}, bf16[4,6,128,256]{3,2,1,0:T(8,128)(2,1)}, f32[4,6,128,256]{3,2,1,0:T(8,128)}) custom-call(s32[4]{0:T(128)} %copy-done.60, bf16[256,1024]{1,0:T(8,128)(2,1)} %copy-done.9, ...), custom_call_target="tpu_custom_call" | custom-call | flops 1000000 | bytes 100000 | tf_op jit(solution)/shard_map/weight_terms/pallas_call | solution.py:560
  376.0 3.5 add_corners.6
  381.5 1.8 fusion.6
  383.3 1.8 collective-permute-start.53
  386.0 7.3 %fc2.1 = bf16[256,1024]{1,0:T(8,128)(2,1)} custom-call(s32[4]{0:T(128)} %copy-done.60, f32[256,1024]{1,0:T(8,128)} %copy-done.31, bf16[256,4096]{1,0:T(8,128)(2,1)} %copy-done.10, f32[13,1024]{1,0:T(8,128)} %copy-done.21, bf16[2,4096,256]{2,1,0:T(8,128)(2,1)} %copy-done.5, bf16[2,4096,256]{2,1,0:T(8,128)(2,1)} %copy-done.72), custom_call_target="tpu_custom_call" | custom-call | flops 1000000 | bytes 100000 | tf_op jit(solution)/shard_map/fc2/pallas_call | solution.py:957
  393.3 15.8 %memory_back.1 = bf16[4,588,1024]{2,1,0:T(8,128)(2,1)} custom-call(s32[4]{0:T(128)} %copy-done.60, bf16[4,588,1024]{2,1,0:T(8,128)(2,1)} %get-tuple-element.620.dk.gk, bf16[4,588,1024]{2,1,0:T(8,128)(2,1)} %get-tuple-element.621.dv.gv, bf16[2,2176,256]{2,1,0:T(8,128)(2,1)} %copy-done.4, bf16[2,2176,256]{2,1,0:T(8,128)(2,1)} %collective-permute-done.20.k_other.v_other, ...), custom_call_target="tpu_custom_call" | custom-call | flops 1000000 | bytes 100000 | tf_op jit(solution)/shard_map/memory_back/pallas_call | solution.py:957
  409.3 4.6 add_corners.7
  418.7 2.8 collective-permute-done.59
  423.5 8.3 %copy.63 = bf16[4,588,1024]{2,0,1:T(4,128)(2,1)} copy(bf16[4,588,1024]{2,1,0:T(8,128)(2,1)} %memory_back.1) | data formatting | bytes 9633792 | tf_op jit(solution)/shard_map/optimization_barrier | solution.py:274
  434.6 2.6 collective-permute-start.63
  437.5 6.0 %collective-permute-done.63 = bf16[1,128,1024]{2,1,0:T(8,128)(2,1)S(1)} collective-permute-done((bf16[1,128,1024]{2,1,0:T(8,128)(2,1)S(1)}, bf16[1,128,1024]{2,1,0:T(8,128)(2,1)S(1)}, u32[]{:S(2)}, u32[]{:S(2)}) %collective-permute-start.63) | collective-permute-done | bytes 262176 | tf_op jit(solution)/shard_map/ppermute | solution.py:309
  443.4 7.4 %collective-permute-done.65 = bf16[4,6,128,256]{3,2,1,0:T(8,128)(2,1)S(1)} collective-permute-done((bf16[4,6,128,256]{3,2,1,0:T(8,128)(2,1)}, bf16[4,6,128,256]{3,2,1,0:T(8,128)(2,1)S(1)}, u32[]{:S(2)}, u32[]{:S(2)}) %collective-permute-start.65) | collective-permute-done | bytes 1572896 | tf_op jit(solution)/shard_map/ppermute | solution.py:309
  455.3 12.3 %collective-permute-done.69 = bf16[2,128,256]{2,1,0:T(8,128)(2,1)S(1)} collective-permute-done((bf16[2,128,256]{2,1,0:T(8,128)(2,1)S(1)}, bf16[2,128,256]{2,1,0:T(8,128)(2,1)S(1)}, u32[]{:S(2)}, u32[]{:S(2)}) %collective-permute-start.69) | collective-permute-done | bytes 131104 | tf_op jit(solution)/shard_map/ppermute | solution.py:309
  469.7 1.9 fusion.2
  471.6 10.4 %collective-permute-done.72 = bf16[2,128,256]{2,1,0:T(8,128)(2,1)S(1)} collective-permute-done((bf16[2,128,256]{2,1,0:T(8,128)(2,1)S(1)}, bf16[2,128,256]{2,1,0:T(8,128)(2,1)S(1)}, u32[]{:S(2)}, u32[]{:S(2)}) %collective-permute-start.72) | collective-permute-done | bytes 131104 | tf_op jit(solution)/shard_map/ppermute | solution.py:309
  482.3 2.0 fusion.3
  488.0 4.1 collective-permute-done.73
  (397 shorter events, 114.4 us)
Async XLA Ops:
  2.5 14.8 %collective-permute-start = (bf16[1,640,256]{2,1,0:T(8,128)(2,1)S(1)}, bf16[1,640,256]{2,1,0:T(8,128)(2,1)S(1)}, u32[]{:S(2)}, u32[]{:S(2)}) collective-permute-start(bf16[1,640,256]{2,1,0:T(8,128)(2,1)S(1)} %rearrange.12.refs_0_.refs_2_), channel_id=1, source_target_pairs={{0,8},{1,9},{2,10},{3,11},{4,12},{5,13},{6,14},{7,15},{8,16},{9,17... | collective-permute-start | bytes 983048 | tf_op jit(solution)/shard_map/ppermute | solution.py:309
  6.6 10.7 %collective-permute-start.3 = (bf16[1,256,256]{2,1,0:T(8,128)(2,1)S(1)}, bf16[1,256,256]{2,1,0:T(8,128)(2,1)S(1)}, u32[]{:S(2)}, u32[]{:S(2)}) collective-permute-start(bf16[1,256,256]{2,1,0:T(8,128)(2,1)S(1)} %get-tuple-element.368), channel_id=1, source_target_pairs={{0,2},{1,3},{2,0},{3,1},{4,6},{5,7},{6,4},{7,5},{8,10},{9,11},{10,... | collective-permute-start | bytes 393224 | tf_op jit(solution)/shard_map/ppermute | solution.py:309
  8.1 9.1 %collective-permute-start.2 = (bf16[1,256,256]{2,1,0:T(8,128)(2,1)S(1)}, bf16[1,256,256]{2,1,0:T(8,128)(2,1)S(1)}, u32[]{:S(2)}, u32[]{:S(2)}) collective-permute-start(bf16[1,256,256]{2,1,0:T(8,128)(2,1)S(1)} %get-tuple-element.397.refs_0_), channel_id=1, source_target_pairs={{0,4},{1,5},{2,6},{3,7},{4,0},{5,1},{6,2},{7,3},{8,12},{9,13},{10,... | collective-permute-start | bytes 393224 | tf_op jit(solution)/shard_map/ppermute | solution.py:309
  17.3 10.4 %collective-permute-start.4 = (bf16[1,640,256]{2,1,0:T(8,128)(2,1)S(1)}, bf16[1,640,256]{2,1,0:T(8,128)(2,1)S(1)}, u32[]{:S(2)}, u32[]{:S(2)}) collective-permute-start(bf16[1,640,256]{2,1,0:T(8,128)(2,1)S(1)} %collective-permute-done.refs_2_.refs_3_), channel_id=1, source_target_pairs={{0,8},{1,9},{2,10},{3,11},{4,12},{5,13},{6,14},{7,15},{8,16},{9,17... | collective-permute-start | bytes 983048 | tf_op jit(solution)/shard_map/ppermute | solution.py:309
  18.9 8.7 %collective-permute-start.7 = (bf16[1,128,256]{2,1,0:T(8,128)(2,1)S(1)}, bf16[1,128,256]{2,1,0:T(8,128)(2,1)S(1)}, u32[]{:S(2)}, u32[]{:S(2)}) collective-permute-start(bf16[1,128,256]{2,1,0:T(8,128)(2,1)S(1)} %get-tuple-element.377), channel_id=1, source_target_pairs={{0,2},{1,3},{2,0},{3,1},{4,6},{5,7},{6,4},{7,5},{8,10},{9,11},{10,... | collective-permute-start | bytes 196616 | tf_op jit(solution)/shard_map/ppermute | solution.py:309
  19.5 8.1 %collective-permute-start.6 = (bf16[1,128,256]{2,1,0:T(8,128)(2,1)S(1)}, bf16[1,128,256]{2,1,0:T(8,128)(2,1)S(1)}, u32[]{:S(2)}, u32[]{:S(2)}) collective-permute-start(bf16[1,128,256]{2,1,0:T(8,128)(2,1)S(1)} %get-tuple-element.375), channel_id=1, source_target_pairs={{0,4},{1,5},{2,6},{3,7},{4,0},{5,1},{6,2},{7,3},{8,12},{9,13},{10,... | collective-permute-start | bytes 196616 | tf_op jit(solution)/shard_map/ppermute | solution.py:309
  27.7 9.4 %collective-permute-start.8 = (bf16[1,640,256]{2,1,0:T(8,128)(2,1)S(1)}, bf16[1,640,256]{2,1,0:T(8,128)(2,1)S(1)}, u32[]{:S(2)}, u32[]{:S(2)}) collective-permute-start(bf16[1,640,256]{2,1,0:T(8,128)(2,1)S(1)} %collective-permute-done.4.refs_4_), channel_id=1, source_target_pairs={{0,8},{1,9},{2,10},{3,11},{4,12},{5,13},{6,14},{7,15},{8,16},{9,17... | collective-permute-start | bytes 983048 | tf_op jit(solution)/shard_map/ppermute | solution.py:309
  28.0 9.1 %collective-permute-start.9 = (bf16[1,16,256]{2,1,0:T(8,128)(2,1)S(1)}, bf16[1,16,256]{2,1,0:T(8,128)(2,1)S(1)}, u32[]{:S(2)}, u32[]{:S(2)}) collective-permute-start(bf16[1,16,256]{2,1,0:T(8,128)(2,1)S(1)} %collective-permute-done.5.refs_5_), channel_id=1, source_target_pairs={{0,8},{1,9},{2,10},{3,11},{4,12},{5,13},{6,14},{7,15},{8,16},{9,17... | collective-permute-start | bytes 24584 | tf_op jit(solution)/shard_map/ppermute | solution.py:309
  37.2 16.2 %collective-permute-start.12 = (bf16[4,272,256]{2,1,0:T(8,128)(2,1)S(1)}, bf16[4,272,256]{2,1,0:T(8,128)(2,1)S(1)}, u32[]{:S(2)}, u32[]{:S(2)}) collective-permute-start(bf16[4,272,256]{2,1,0:T(8,128)(2,1)S(1)} %get-tuple-element.426.refs_0_), channel_id=1, source_target_pairs={{0,4},{1,5},{2,6},{3,7},{4,0},{5,1},{6,2},{7,3},{8,12},{9,13},{10,... | collective-permute-start | bytes 1671176 | tf_op jit(solution)/shard_map/ppermute | solution.py:309
  38.6 14.8 %collective-permute-start.13 = (bf16[4,272,256]{2,1,0:T(8,128)(2,1)S(1)}, bf16[4,272,256]{2,1,0:T(8,128)(2,1)S(1)}, u32[]{:S(2)}, u32[]{:S(2)}) collective-permute-start(bf16[4,272,256]{2,1,0:T(8,128)(2,1)S(1)} %get-tuple-element.393), channel_id=1, source_target_pairs={{0,2},{1,3},{2,0},{3,1},{4,6},{5,7},{6,4},{7,5},{8,10},{9,11},{10,... | collective-permute-start | bytes 1671176 | tf_op jit(solution)/shard_map/ppermute | solution.py:309
  39.9 13.5 %collective-permute-start.10 = (bf16[1,768,256]{2,1,0:T(8,128)(2,1)S(1)}, bf16[1,768,256]{2,1,0:T(8,128)(2,1)S(1)}, u32[]{:S(2)}, u32[]{:S(2)}) collective-permute-start(bf16[1,768,256]{2,1,0:T(8,128)(2,1)S(1)} %get-tuple-element.473.refs_2_), channel_id=1, source_target_pairs={{0,8},{1,9},{2,10},{3,11},{4,12},{5,13},{6,14},{7,15},{8,16},{9,17... | collective-permute-start | bytes 1179656 | tf_op jit(solution)/shard_map/ppermute | solution.py:309
  39.9 13.5 %collective-permute-start.11 = (bf16[1,384,256]{2,1,0:T(8,128)(2,1)S(1)}, bf16[1,384,256]{2,1,0:T(8,128)(2,1)S(1)}, u32[]{:S(2)}, u32[]{:S(2)}) collective-permute-start(bf16[1,384,256]{2,1,0:T(8,128)(2,1)S(1)} %get-tuple-element.421.refs_2_), channel_id=1, source_target_pairs={{0,8},{1,9},{2,10},{3,11},{4,12},{5,13},{6,14},{7,15},{8,16},{9,17... | collective-permute-start | bytes 589832 | tf_op jit(solution)/shard_map/ppermute | solution.py:309
  55.0 21.5 %collective-permute-start.18 = (bf16[4,528,256]{2,1,0:T(8,128)(2,1)}, bf16[4,528,256]{2,1,0:T(8,128)(2,1)S(1)}, u32[]{:S(2)}, u32[]{:S(2)}) collective-permute-start(bf16[4,528,256]{2,1,0:T(8,128)(2,1)} %get-tuple-element.411), channel_id=1, source_target_pairs={{0,2},{1,3},{2,0},{3,1},{4,6},{5,7},{6,4},{7,5},{8,10},{9,11},{10,... | collective-permute-start | bytes 3244040 | tf_op jit(solution)/shard_map/ppermute | solution.py:309
  55.6 20.4 %collective-permute-start.17 = (bf16[4,512,256]{2,1,0:T(8,128)(2,1)}, bf16[4,512,256]{2,1,0:T(8,128)(2,1)S(1)}, u32[]{:S(2)}, u32[]{:S(2)}) collective-permute-start(bf16[4,512,256]{2,1,0:T(8,128)(2,1)} %get-tuple-element.451.refs_0_), channel_id=1, source_target_pairs={{0,4},{1,5},{2,6},{3,7},{4,0},{5,1},{6,2},{7,3},{8,12},{9,13},{10,... | collective-permute-start | bytes 3145736 | tf_op jit(solution)/shard_map/ppermute | solution.py:309
  57.1 9.5 %collective-permute-start.15 = (bf16[1,384,256]{2,1,0:T(8,128)(2,1)S(1)}, bf16[1,384,256]{2,1,0:T(8,128)(2,1)}, u32[]{:S(2)}, u32[]{:S(2)}) collective-permute-start(bf16[1,384,256]{2,1,0:T(8,128)(2,1)S(1)} %collective-permute-done.11.refs_3_), channel_id=1, source_target_pairs={{0,8},{1,9},{2,10},{3,11},{4,12},{5,13},{6,14},{7,15},{8,16},{9,17... | collective-permute-start | bytes 589832 | tf_op jit(solution)/shard_map/ppermute | solution.py:309
  57.1 14.0 %collective-permute-start.14 = (bf16[1,768,256]{2,1,0:T(8,128)(2,1)S(1)}, bf16[1,768,256]{2,1,0:T(8,128)(2,1)S(1)}, u32[]{:S(2)}, u32[]{:S(2)}) collective-permute-start(bf16[1,768,256]{2,1,0:T(8,128)(2,1)S(1)} %collective-permute-done.10.refs_3_), channel_id=1, source_target_pairs={{0,8},{1,9},{2,10},{3,11},{4,12},{5,13},{6,14},{7,15},{8,16},{9,17... | collective-permute-start | bytes 1179656 | tf_op jit(solution)/shard_map/ppermute | solution.py:309
  66.6 7.8 %collective-permute-start.16 = (bf16[1,384,256]{2,1,0:T(8,128)(2,1)}, bf16[1,384,256]{2,1,0:T(8,128)(2,1)}, u32[]{:S(2)}, u32[]{:S(2)}) collective-permute-start(bf16[1,384,256]{2,1,0:T(8,128)(2,1)} %collective-permute-done.15.refs_4_), channel_id=1, source_target_pairs={{0,8},{1,9},{2,10},{3,11},{4,12},{5,13},{6,14},{7,15},{8,16},{9,17... | collective-permute-start | bytes 589832 | tf_op jit(solution)/shard_map/ppermute | solution.py:309
  84.5 28.6 %collective-permute-start.21 = (bf16[4,576,256]{2,1,0:T(8,128)(2,1)}, bf16[4,576,256]{2,1,0:T(8,128)(2,1)S(1)}, u32[]{:S(2)}, u32[]{:S(2)}) collective-permute-start(bf16[4,576,256]{2,1,0:T(8,128)(2,1)} %get-tuple-element.478.refs_0_), channel_id=1, source_target_pairs={{0,4},{1,5},{2,6},{3,7},{4,0},{5,1},{6,2},{7,3},{8,12},{9,13},{10,... | collective-permute-start | bytes 3538952 | tf_op jit(solution)/shard_map/ppermute | solution.py:309
  85.7 28.4 %collective-permute-start.22 = (bf16[4,576,256]{2,1,0:T(8,128)(2,1)}, bf16[4,576,256]{2,1,0:T(8,128)(2,1)}, u32[]{:S(2)}, u32[]{:S(2)}) collective-permute-start(bf16[4,576,256]{2,1,0:T(8,128)(2,1)} %get-tuple-element.437), channel_id=1, source_target_pairs={{0,2},{1,3},{2,0},{3,1},{4,6},{5,7},{6,4},{7,5},{8,10},{9,11},{10,... | collective-permute-start | bytes 3538952 | tf_op jit(solution)/shard_map/ppermute | solution.py:309
  86.5 22.4 %collective-permute-start.19 = (bf16[1,768,256]{2,1,0:T(8,128)(2,1)}, bf16[1,768,256]{2,1,0:T(8,128)(2,1)}, u32[]{:S(2)}, u32[]{:S(2)}) collective-permute-start(bf16[1,768,256]{2,1,0:T(8,128)(2,1)} %copy-done.51), channel_id=1, source_target_pairs={{0,8},{1,9},{2,10},{3,11},{4,12},{5,13},{6,14},{7,15},{8,16},{9,17... | collective-permute-start | bytes 1179656 | tf_op jit(solution)/shard_map/ppermute | solution.py:309
  121.5 34.3 %collective-permute-start.25 = (bf16[4,704,256]{2,1,0:T(8,128)(2,1)}, bf16[4,704,256]{2,1,0:T(8,128)(2,1)}, u32[]{:S(2)}, u32[]{:S(2)}) collective-permute-start(bf16[4,704,256]{2,1,0:T(8,128)(2,1)} %get-tuple-element.500.refs_0_), channel_id=1, source_target_pairs={{0,4},{1,5},{2,6},{3,7},{4,0},{5,1},{6,2},{7,3},{8,12},{9,13},{10,... | collective-permute-start | bytes 4325384 | tf_op jit(solution)/shard_map/ppermute | solution.py:309
  122.4 34.0 %collective-permute-start.26 = (bf16[4,704,256]{2,1,0:T(8,128)(2,1)}, bf16[4,704,256]{2,1,0:T(8,128)(2,1)}, u32[]{:S(2)}, u32[]{:S(2)}) collective-permute-start(bf16[4,704,256]{2,1,0:T(8,128)(2,1)} %get-tuple-element.464), channel_id=1, source_target_pairs={{0,2},{1,3},{2,0},{3,1},{4,6},{5,7},{6,4},{7,5},{8,10},{9,11},{10,... | collective-permute-start | bytes 4325384 | tf_op jit(solution)/shard_map/ppermute | solution.py:309
  123.6 15.8 %collective-permute-start.24 = (bf16[4,256,256]{2,1,0:T(8,128)(2,1)}, bf16[4,256,256]{2,1,0:T(8,128)(2,1)}, u32[]{:S(2)}, u32[]{:S(2)}) collective-permute-start(bf16[4,256,256]{2,1,0:T(8,128)(2,1)} %rearrange.16.refs_5_), channel_id=1, source_target_pairs={{0,8},{1,9},{2,10},{3,11},{4,12},{5,13},{6,14},{7,15},{8,16},{9,17... | collective-permute-start | bytes 1572872 | tf_op jit(solution)/shard_map/ppermute | solution.py:309
  162.5 13.2 %collective-permute-start.27 = (bf16[2,3072,256]{2,1,0:T(8,128)(2,1)S(1)}, bf16[2,3072,256]{2,1,0:T(8,128)(2,1)}, u32[]{:S(2)}, u32[]{:S(2)}) collective-permute-start(bf16[2,3072,256]{2,1,0:T(8,128)(2,1)S(1)} %half_weights.7.so_own.cq_own.own.co_own), channel_id=1, source_target_pairs={{0,1},{1,0},{2,3},{3,2},{4,5},{5,4},{6,7},{7,6},{8,9},{9,8},{10,11... | collective-permute-start | bytes 9437192 | tf_op jit(solution)/shard_map/ppermute | solution.py:309
  162.6 34.3 %collective-permute-start.29 = (bf16[4,512,256]{2,1,0:T(8,128)(2,1)}, bf16[4,512,256]{2,1,0:T(8,128)(2,1)}, u32[]{:S(2)}, u32[]{:S(2)}) collective-permute-start(bf16[4,512,256]{2,1,0:T(8,128)(2,1)} %get-tuple-element.530.refs_0_), channel_id=1, source_target_pairs={{0,4},{1,5},{2,6},{3,7},{4,0},{5,1},{6,2},{7,3},{8,12},{9,13},{10,... | collective-permute-start | bytes 3145736 | tf_op jit(solution)/shard_map/ppermute | solution.py:309
  163.9 33.0 %collective-permute-start.30 = (bf16[4,512,256]{2,1,0:T(8,128)(2,1)}, bf16[4,512,256]{2,1,0:T(8,128)(2,1)}, u32[]{:S(2)}, u32[]{:S(2)}) collective-permute-start(bf16[4,512,256]{2,1,0:T(8,128)(2,1)} %get-tuple-element.491), channel_id=1, source_target_pairs={{0,2},{1,3},{2,0},{3,1},{4,6},{5,7},{6,4},{7,5},{8,10},{9,11},{10,... | collective-permute-start | bytes 3145736 | tf_op jit(solution)/shard_map/ppermute | solution.py:309
  164.6 32.3 %collective-permute-start.28 = (bf16[4,256,256]{2,1,0:T(8,128)(2,1)}, bf16[4,256,256]{2,1,0:T(8,128)(2,1)}, u32[]{:S(2)}, u32[]{:S(2)}) collective-permute-start(bf16[4,256,256]{2,1,0:T(8,128)(2,1)} %collective-permute-done.24.refs_6_), channel_id=1, source_target_pairs={{0,8},{1,9},{2,10},{3,11},{4,12},{5,13},{6,14},{7,15},{8,16},{9,17... | collective-permute-start | bytes 1572872 | tf_op jit(solution)/shard_map/ppermute | solution.py:309
  200.1 8.6 %collective-permute-start.31 = (bf16[2,4096,256]{2,1,0:T(8,128)(2,1)S(1)}, bf16[2,4096,256]{2,1,0:T(8,128)(2,1)S(1)}, u32[]{:S(2)}, u32[]{:S(2)}) collective-permute-start(bf16[2,4096,256]{2,1,0:T(8,128)(2,1)S(1)} %half_weights.8.own), channel_id=1, source_target_pairs={{0,1},{1,0},{2,3},{3,2},{4,5},{5,4},{6,7},{7,6},{8,9},{9,8},{10,11... | collective-permute-start | bytes 12582920 | tf_op jit(solution)/shard_map/ppermute | solution.py:309
  200.2 16.6 %collective-permute-start.32 = (bf16[4,256,256]{2,1,0:T(8,128)(2,1)}, bf16[4,256,256]{2,1,0:T(8,128)(2,1)S(1)}, u32[]{:S(2)}, u32[]{:S(2)}) collective-permute-start(bf16[4,256,256]{2,1,0:T(8,128)(2,1)} %collective-permute-done.28.refs_7_), channel_id=1, source_target_pairs={{0,8},{1,9},{2,10},{3,11},{4,12},{5,13},{6,14},{7,15},{8,16},{9,17... | collective-permute-start | bytes 1572872 | tf_op jit(solution)/shard_map/ppermute | solution.py:309
  203.5 11.5 %collective-permute-start.34 = (bf16[4,128,256]{2,1,0:T(8,128)(2,1)S(1)}, bf16[4,128,256]{2,1,0:T(8,128)(2,1)S(1)}, u32[]{:S(2)}, u32[]{:S(2)}) collective-permute-start(bf16[4,128,256]{2,1,0:T(8,128)(2,1)S(1)} %get-tuple-element.514), channel_id=1, source_target_pairs={{0,2},{1,3},{2,0},{3,1},{4,6},{5,7},{6,4},{7,5},{8,10},{9,11},{10,... | collective-permute-start | bytes 786440 | tf_op jit(solution)/shard_map/ppermute | solution.py:309
  204.8 10.1 %collective-permute-start.33 = (bf16[4,128,256]{2,1,0:T(8,128)(2,1)S(1)}, bf16[4,128,256]{2,1,0:T(8,128)(2,1)S(1)}, u32[]{:S(2)}, u32[]{:S(2)}) collective-permute-start(bf16[4,128,256]{2,1,0:T(8,128)(2,1)S(1)} %get-tuple-element.512), channel_id=1, source_target_pairs={{0,4},{1,5},{2,6},{3,7},{4,0},{5,1},{6,2},{7,3},{8,12},{9,13},{10,... | collective-permute-start | bytes 786440 | tf_op jit(solution)/shard_map/ppermute | solution.py:309
  222.4 13.9 %collective-permute-start.36 = (bf16[2,4096,256]{2,1,0:T(8,128)(2,1)S(1)}, bf16[2,4096,256]{2,1,0:T(8,128)(2,1)S(1)}, u32[]{:S(2)}, u32[]{:S(2)}) collective-permute-start(bf16[2,4096,256]{2,1,0:T(8,128)(2,1)S(1)} %half_weights.9.own), channel_id=1, source_target_pairs={{0,1},{1,0},{2,3},{3,2},{4,5},{5,4},{6,7},{7,6},{8,9},{9,8},{10,11... | collective-permute-start | bytes 12582920 | tf_op jit(solution)/shard_map/ppermute | solution.py:309
  234.2 14.9 %collective-permute-start.37 = (bf16[4,1,256,256]{3,2,1,0:T(8,128)(2,1)S(1)}, bf16[4,1,256,256]{3,2,1,0:T(8,128)(2,1)S(1)}, u32[]{:S(2)}, u32[]{:S(2)}) collective-permute-start(bf16[4,1,256,256]{3,2,1,0:T(8,128)(2,1)S(1)} %get-tuple-element.542), channel_id=1, source_target_pairs={{0,4},{1,5},{2,6},{3,7},{4,0},{5,1},{6,2},{7,3},{8,12},{9,13},{10,... | collective-permute-start | bytes 1572872 | tf_op jit(solution)/shard_map/ppermute | solution.py:309
  235.5 13.7 %collective-permute-start.38 = (bf16[4,1,256,256]{3,2,1,0:T(8,128)(2,1)S(1)}, bf16[4,1,256,256]{3,2,1,0:T(8,128)(2,1)S(1)}, u32[]{:S(2)}, u32[]{:S(2)}) collective-permute-start(bf16[4,1,256,256]{3,2,1,0:T(8,128)(2,1)S(1)} %get-tuple-element.544), channel_id=1, source_target_pairs={{0,2},{1,3},{2,0},{3,1},{4,6},{5,7},{6,4},{7,5},{8,10},{9,11},{10,... | collective-permute-start | bytes 1572872 | tf_op jit(solution)/shard_map/ppermute | solution.py:309
  249.2 14.2 %collective-permute-start.39 = (bf16[1,2,1024,1024]{3,2,1,0:T(8,128)(2,1)}, bf16[1,2,1024,1024]{3,2,1,0:T(8,128)(2,1)}, u32[]{:S(2)}, u32[]{:S(2)}) collective-permute-start(bf16[1,2,1024,1024]{3,2,1,0:T(8,128)(2,1)} %get-tuple-element.547), channel_id=1, source_target_pairs={{0,1},{1,0},{2,3},{3,2},{4,5},{5,4},{6,7},{7,6},{8,9},{9,8},{10,11... | collective-permute-start | bytes 12582920 | tf_op jit(solution)/shard_map/ppermute | solution.py:309
  271.0 38.1 %collective-permute-start.40 = (bf16[4,1,512,256]{3,2,1,0:T(8,128)(2,1)}, bf16[4,1,512,256]{3,2,1,0:T(8,128)(2,1)S(1)}, u32[]{:S(2)}, u32[]{:S(2)}) collective-permute-start(bf16[4,1,512,256]{3,2,1,0:T(8,128)(2,1)} %get-tuple-element.559), channel_id=1, source_target_pairs={{0,4},{1,5},{2,6},{3,7},{4,0},{5,1},{6,2},{7,3},{8,12},{9,13},{10,... | collective-permute-start | bytes 3145736 | tf_op jit(solution)/shard_map/ppermute | solution.py:309
  272.2 36.8 %collective-permute-start.41 = (bf16[4,1,512,256]{3,2,1,0:T(8,128)(2,1)}, bf16[4,1,512,256]{3,2,1,0:T(8,128)(2,1)}, u32[]{:S(2)}, u32[]{:S(2)}) collective-permute-start(bf16[4,1,512,256]{3,2,1,0:T(8,128)(2,1)} %get-tuple-element.561), channel_id=1, source_target_pairs={{0,2},{1,3},{2,0},{3,1},{4,6},{5,7},{6,4},{7,5},{8,10},{9,11},{10,... | collective-permute-start | bytes 3145736 | tf_op jit(solution)/shard_map/ppermute | solution.py:309
  273.0 35.1 %collective-permute-start.42 = (bf16[4,1,64,1024]{3,2,1,0:T(8,128)(2,1)}, bf16[4,1,64,1024]{3,2,1,0:T(8,128)(2,1)S(1)}, u32[]{:S(2)}, u32[]{:S(2)}) collective-permute-start(bf16[4,1,64,1024]{3,2,1,0:T(8,128)(2,1)} %get-tuple-element.562), channel_id=1, source_target_pairs={{0,4},{1,5},{2,6},{3,7},{4,0},{5,1},{6,2},{7,3},{8,12},{9,13},{10,... | collective-permute-start | bytes 1572872 | tf_op jit(solution)/shard_map/ppermute | solution.py:309
  274.3 34.7 %collective-permute-start.43 = (bf16[4,1,64,1024]{3,2,1,0:T(8,128)(2,1)}, bf16[4,1,64,1024]{3,2,1,0:T(8,128)(2,1)}, u32[]{:S(2)}, u32[]{:S(2)}) collective-permute-start(bf16[4,1,64,1024]{3,2,1,0:T(8,128)(2,1)} %get-tuple-element.564), channel_id=1, source_target_pairs={{0,2},{1,3},{2,0},{3,1},{4,6},{5,7},{6,4},{7,5},{8,10},{9,11},{10,... | collective-permute-start | bytes 1572872 | tf_op jit(solution)/shard_map/ppermute | solution.py:309
  309.1 25.4 %collective-permute-start.44 = (bf16[2,2,1024,256]{3,2,1,0:T(8,128)(2,1)}, bf16[2,2,1024,256]{3,2,1,0:T(8,128)(2,1)}, u32[]{:S(2)}, u32[]{:S(2)}) collective-permute-start(bf16[2,2,1024,256]{3,2,1,0:T(8,128)(2,1)} %memory_terms.2), channel_id=1, source_target_pairs={{0,1},{1,0},{2,3},{3,2},{4,5},{5,4},{6,7},{7,6},{8,9},{9,8},{10,11... | collective-permute-start | bytes 6291464 | tf_op jit(solution)/shard_map/ppermute | solution.py:309
  313.4 34.6 %collective-permute-start.46 = (bf16[4,1,128,1024]{3,2,1,0:T(8,128)(2,1)}, bf16[4,1,128,1024]{3,2,1,0:T(8,128)(2,1)}, u32[]{:S(2)}, u32[]{:S(2)}) collective-permute-start(bf16[4,1,128,1024]{3,2,1,0:T(8,128)(2,1)} %get-tuple-element.588), channel_id=1, source_target_pairs={{0,4},{1,5},{2,6},{3,7},{4,0},{5,1},{6,2},{7,3},{8,12},{9,13},{10,... | collective-permute-start | bytes 3145736 | tf_op jit(solution)/shard_map/ppermute | solution.py:309
  314.3 33.8 %collective-permute-start.47 = (bf16[4,1,128,1024]{3,2,1,0:T(8,128)(2,1)}, bf16[4,1,128,1024]{3,2,1,0:T(8,128)(2,1)}, u32[]{:S(2)}, u32[]{:S(2)}) collective-permute-start(bf16[4,1,128,1024]{3,2,1,0:T(8,128)(2,1)} %get-tuple-element.590), channel_id=1, source_target_pairs={{0,2},{1,3},{2,0},{3,1},{4,6},{5,7},{6,4},{7,5},{8,10},{9,11},{10,... | collective-permute-start | bytes 3145736 | tf_op jit(solution)/shard_map/ppermute | solution.py:309
  316.5 31.5 %collective-permute-start.45 = (bf16[1,512,256]{2,1,0:T(8,128)(2,1)S(1)}, bf16[1,512,256]{2,1,0:T(8,128)(2,1)S(1)}, u32[]{:S(2)}, u32[]{:S(2)}) collective-permute-start(bf16[1,512,256]{2,1,0:T(8,128)(2,1)S(1)} %fusion.9), channel_id=1, source_target_pairs={{0,8},{1,9},{2,10},{3,11},{4,12},{5,13},{6,14},{7,15},{8,16},{9,17... | collective-permute-start | bytes 786440 | tf_op jit(solution)/shard_map/ppermute | solution.py:309
  348.0 15.8 %collective-permute-start.48 = (bf16[6,2,1024,256]{3,2,1,0:T(8,128)(2,1)}, bf16[6,2,1024,256]{3,2,1,0:T(8,128)(2,1)}, u32[]{:S(2)}, u32[]{:S(2)}) collective-permute-start(bf16[6,2,1024,256]{3,2,1,0:T(8,128)(2,1)} %weight_terms.8), channel_id=1, source_target_pairs={{0,1},{1,0},{2,3},{3,2},{4,5},{5,4},{6,7},{7,6},{8,9},{9,8},{10,11... | collective-permute-start | bytes 18874376 | tf_op jit(solution)/shard_map/ppermute | solution.py:309
  351.2 22.1 %collective-permute-start.50 = (bf16[1,128,1024]{2,1,0:T(8,128)(2,1)S(1)}, bf16[1,128,1024]{2,1,0:T(8,128)(2,1)S(1)}, u32[]{:S(2)}, u32[]{:S(2)}) collective-permute-start(bf16[1,128,1024]{2,1,0:T(8,128)(2,1)S(1)} %fusion.10), channel_id=1, source_target_pairs={{0,8},{1,9},{2,10},{3,11},{4,12},{5,13},{6,14},{7,15},{8,16},{9,17... | collective-permute-start | bytes 786440 | tf_op jit(solution)/shard_map/ppermute | solution.py:309
  352.5 21.5 %collective-permute-start.49 = (bf16[1,512,256]{2,1,0:T(8,128)(2,1)}, bf16[1,512,256]{2,1,0:T(8,128)(2,1)S(1)}, u32[]{:S(2)}, u32[]{:S(2)}) collective-permute-start(bf16[1,512,256]{2,1,0:T(8,128)(2,1)} %fusion.7), channel_id=1, source_target_pairs={{0,8},{1,9},{2,10},{3,11},{4,12},{5,13},{6,14},{7,15},{8,16},{9,17... | collective-permute-start | bytes 786440 | tf_op jit(solution)/shard_map/ppermute | solution.py:309
  354.2 19.8 %collective-permute-start.51 = (bf16[4,2,64,256]{3,2,1,0:T(8,128)(2,1)}, bf16[4,2,64,256]{3,2,1,0:T(8,128)(2,1)}, u32[]{:S(2)}, u32[]{:S(2)}) collective-permute-start(bf16[4,2,64,256]{3,2,1,0:T(8,128)(2,1)} %get-tuple-element.609), channel_id=1, source_target_pairs={{0,4},{1,5},{2,6},{3,7},{4,0},{5,1},{6,2},{7,3},{8,12},{9,13},{10,... | collective-permute-start | bytes 786440 | tf_op jit(solution)/shard_map/ppermute | solution.py:309
  355.1 18.9 %collective-permute-start.52 = (bf16[4,2,64,256]{3,2,1,0:T(8,128)(2,1)}, bf16[4,2,64,256]{3,2,1,0:T(8,128)(2,1)}, u32[]{:S(2)}, u32[]{:S(2)}) collective-permute-start(bf16[4,2,64,256]{3,2,1,0:T(8,128)(2,1)} %get-tuple-element.611), channel_id=1, source_target_pairs={{0,2},{1,3},{2,0},{3,1},{4,6},{5,7},{6,4},{7,5},{8,10},{9,11},{10,... | collective-permute-start | bytes 786440 | tf_op jit(solution)/shard_map/ppermute | solution.py:309
  374.0 35.1 %collective-permute-start.56 = (bf16[4,6,64,256]{3,2,1,0:T(8,128)(2,1)}, bf16[4,6,64,256]{3,2,1,0:T(8,128)(2,1)}, u32[]{:S(2)}, u32[]{:S(2)}) collective-permute-start(bf16[4,6,64,256]{3,2,1,0:T(8,128)(2,1)} %get-tuple-element.630), channel_id=1, source_target_pairs={{0,4},{1,5},{2,6},{3,7},{4,0},{5,1},{6,2},{7,3},{8,12},{9,13},{10,... | collective-permute-start | bytes 2359304 | tf_op jit(solution)/shard_map/ppermute | solution.py:309
  374.7 34.4 %collective-permute-start.57 = (bf16[4,6,64,256]{3,2,1,0:T(8,128)(2,1)}, bf16[4,6,64,256]{3,2,1,0:T(8,128)(2,1)}, u32[]{:S(2)}, u32[]{:S(2)}) collective-permute-start(bf16[4,6,64,256]{3,2,1,0:T(8,128)(2,1)} %get-tuple-element.632), channel_id=1, source_target_pairs={{0,2},{1,3},{2,0},{3,1},{4,6},{5,7},{6,4},{7,5},{8,10},{9,11},{10,... | collective-permute-start | bytes 2359304 | tf_op jit(solution)/shard_map/ppermute | solution.py:309
  379.4 29.6 %collective-permute-start.54 = (bf16[4,2,128,256]{3,2,1,0:T(8,128)(2,1)}, bf16[4,2,128,256]{3,2,1,0:T(8,128)(2,1)}, u32[]{:S(2)}, u32[]{:S(2)}) collective-permute-start(bf16[4,2,128,256]{3,2,1,0:T(8,128)(2,1)} %get-tuple-element.627), channel_id=1, source_target_pairs={{0,4},{1,5},{2,6},{3,7},{4,0},{5,1},{6,2},{7,3},{8,12},{9,13},{10,... | collective-permute-start | bytes 1572872 | tf_op jit(solution)/shard_map/ppermute | solution.py:309
  380.3 28.7 %collective-permute-start.55 = (bf16[4,2,128,256]{3,2,1,0:T(8,128)(2,1)}, bf16[4,2,128,256]{3,2,1,0:T(8,128)(2,1)}, u32[]{:S(2)}, u32[]{:S(2)}) collective-permute-start(bf16[4,2,128,256]{3,2,1,0:T(8,128)(2,1)} %get-tuple-element.629), channel_id=1, source_target_pairs={{0,2},{1,3},{2,0},{3,1},{4,6},{5,7},{6,4},{7,5},{8,10},{9,11},{10,... | collective-permute-start | bytes 1572872 | tf_op jit(solution)/shard_map/ppermute | solution.py:309
  383.3 25.8 %collective-permute-start.53 = (bf16[1,512,256]{2,1,0:T(8,128)(2,1)}, bf16[1,512,256]{2,1,0:T(8,128)(2,1)S(1)}, u32[]{:S(2)}, u32[]{:S(2)}) collective-permute-start(bf16[1,512,256]{2,1,0:T(8,128)(2,1)} %fusion.6), channel_id=1, source_target_pairs={{0,8},{1,9},{2,10},{3,11},{4,12},{5,13},{6,14},{7,15},{8,16},{9,17... | collective-permute-start | bytes 786440 | tf_op jit(solution)/shard_map/ppermute | solution.py:309
  413.9 37.0 %collective-permute-start.65 = (bf16[4,6,128,256]{3,2,1,0:T(8,128)(2,1)}, bf16[4,6,128,256]{3,2,1,0:T(8,128)(2,1)S(1)}, u32[]{:S(2)}, u32[]{:S(2)}) collective-permute-start(bf16[4,6,128,256]{3,2,1,0:T(8,128)(2,1)} %get-tuple-element.671), channel_id=1, source_target_pairs={{0,4},{1,5},{2,6},{3,7},{4,0},{5,1},{6,2},{7,3},{8,12},{9,13},{10,... | collective-permute-start | bytes 4718600 | tf_op jit(solution)/shard_map/ppermute | solution.py:309
  414.7 36.7 %collective-permute-start.66 = (bf16[4,6,128,256]{3,2,1,0:T(8,128)(2,1)}, bf16[4,6,128,256]{3,2,1,0:T(8,128)(2,1)S(1)}, u32[]{:S(2)}, u32[]{:S(2)}) collective-permute-start(bf16[4,6,128,256]{3,2,1,0:T(8,128)(2,1)} %get-tuple-element.673), channel_id=1, source_target_pairs={{0,2},{1,3},{2,0},{3,1},{4,6},{5,7},{6,4},{7,5},{8,10},{9,11},{10,... | collective-permute-start | bytes 4718600 | tf_op jit(solution)/shard_map/ppermute | solution.py:309
  417.5 14.8 %collective-permute-start.62 = (bf16[1,128,1024]{2,1,0:T(8,128)(2,1)S(1)}, bf16[1,128,1024]{2,1,0:T(8,128)(2,1)S(1)}, u32[]{:S(2)}, u32[]{:S(2)}) collective-permute-start(bf16[1,128,1024]{2,1,0:T(8,128)(2,1)S(1)} %fusion.4), channel_id=1, source_target_pairs={{0,8},{1,9},{2,10},{3,11},{4,12},{5,13},{6,14},{7,15},{8,16},{9,17... | collective-permute-start | bytes 786440 | tf_op jit(solution)/shard_map/ppermute | solution.py:309
  421.5 10.3 %collective-permute-start.60 = (f32[2,2,544]{2,1,0:T(2,128)S(1)}, f32[2,2,544]{2,1,0:T(2,128)S(1)}, u32[]{:S(2)}, u32[]{:S(2)}) collective-permute-start(f32[2,2,544]{2,1,0:T(2,128)S(1)} %fusion.24), channel_id=1, source_target_pairs={{0,8},{1,9},{2,10},{3,11},{4,12},{5,13},{6,14},{7,15},{8,16},{9,17... | collective-permute-start | bytes 26120 | tf_op jit(solution)/shard_map/ppermute | solution.py:309
  422.6 14.8 %collective-permute-start.64 = (bf16[2,128,256]{2,1,0:T(8,128)(2,1)S(1)}, bf16[2,128,256]{2,1,0:T(8,128)(2,1)S(1)}, u32[]{:S(2)}, u32[]{:S(2)}) collective-permute-start(bf16[2,128,256]{2,1,0:T(8,128)(2,1)S(1)} %fusion.13), channel_id=1, source_target_pairs={{0,8},{1,9},{2,10},{3,11},{4,12},{5,13},{6,14},{7,15},{8,16},{9,17... | collective-permute-start | bytes 393224 | tf_op jit(solution)/shard_map/ppermute | solution.py:309
  434.6 8.8 %collective-permute-start.63 = (bf16[1,128,1024]{2,1,0:T(8,128)(2,1)S(1)}, bf16[1,128,1024]{2,1,0:T(8,128)(2,1)S(1)}, u32[]{:S(2)}, u32[]{:S(2)}) collective-permute-start(bf16[1,128,1024]{2,1,0:T(8,128)(2,1)S(1)} %fusion.5), channel_id=1, source_target_pairs={{0,8},{1,9},{2,10},{3,11},{4,12},{5,13},{6,14},{7,15},{8,16},{9,17... | collective-permute-start | bytes 786440 | tf_op jit(solution)/shard_map/ppermute | solution.py:309
  452.8 14.7 %collective-permute-start.68 = (bf16[6,128,256]{2,1,0:T(8,128)(2,1)S(1)}, bf16[6,128,256]{2,1,0:T(8,128)(2,1)S(1)}, u32[]{:S(2)}, u32[]{:S(2)}) collective-permute-start(bf16[6,128,256]{2,1,0:T(8,128)(2,1)S(1)} %fusion.8), channel_id=1, source_target_pairs={{0,8},{1,9},{2,10},{3,11},{4,12},{5,13},{6,14},{7,15},{8,16},{9,17... | collective-permute-start | bytes 1179656 | tf_op jit(solution)/shard_map/ppermute | solution.py:309
  453.9 13.6 %collective-permute-start.69 = (bf16[2,128,256]{2,1,0:T(8,128)(2,1)S(1)}, bf16[2,128,256]{2,1,0:T(8,128)(2,1)S(1)}, u32[]{:S(2)}, u32[]{:S(2)}) collective-permute-start(bf16[2,128,256]{2,1,0:T(8,128)(2,1)S(1)} %fusion.12), channel_id=1, source_target_pairs={{0,8},{1,9},{2,10},{3,11},{4,12},{5,13},{6,14},{7,15},{8,16},{9,17... | collective-permute-start | bytes 393224 | tf_op jit(solution)/shard_map/ppermute | solution.py:309
  468.5 13.5 %collective-permute-start.71 = (bf16[6,128,256]{2,1,0:T(8,128)(2,1)S(1)}, bf16[6,128,256]{2,1,0:T(8,128)(2,1)S(1)}, u32[]{:S(2)}, u32[]{:S(2)}) collective-permute-start(bf16[6,128,256]{2,1,0:T(8,128)(2,1)S(1)} %fusion.1), channel_id=1, source_target_pairs={{0,8},{1,9},{2,10},{3,11},{4,12},{5,13},{6,14},{7,15},{8,16},{9,17... | collective-permute-start | bytes 1179656 | tf_op jit(solution)/shard_map/ppermute | solution.py:309
  469.6 12.4 %collective-permute-start.72 = (bf16[2,128,256]{2,1,0:T(8,128)(2,1)S(1)}, bf16[2,128,256]{2,1,0:T(8,128)(2,1)S(1)}, u32[]{:S(2)}, u32[]{:S(2)}) collective-permute-start(bf16[2,128,256]{2,1,0:T(8,128)(2,1)S(1)} %fusion.11), channel_id=1, source_target_pairs={{0,8},{1,9},{2,10},{3,11},{4,12},{5,13},{6,14},{7,15},{8,16},{9,17... | collective-permute-start | bytes 393224 | tf_op jit(solution)/shard_map/ppermute | solution.py:309
  482.3 9.8 %collective-permute-start.73 = (bf16[6,128,256]{2,1,0:T(8,128)(2,1)S(1)}, bf16[6,128,256]{2,1,0:T(8,128)(2,1)S(1)}, u32[]{:S(2)}, u32[]{:S(2)}) collective-permute-start(bf16[6,128,256]{2,1,0:T(8,128)(2,1)S(1)} %fusion), channel_id=1, source_target_pairs={{0,8},{1,9},{2,10},{3,11},{4,12},{5,13},{6,14},{7,15},{8,16},{9,17... | collective-permute-start | bytes 1179656 | tf_op jit(solution)/shard_map/ppermute | solution.py:309
  (115 other events, 1333.1 us)

commit v6 on v5

--- a/solution.py
+++ b/solution.py
@@ -24,6 +24,7 @@
 VMEM = 24 * 2**20
 CHEAP = pl.CostEstimate(flops=10**6, bytes_accessed=10**5, transcendentals=0)
 BIG_VMEM = pltpu.CompilerParams(vmem_limit_bytes=VMEM)
+SMALL_VMEM = pltpu.CompilerParams(vmem_limit_bytes=16 * 2**20)
 FULL_VMEM = pltpu.CompilerParams(vmem_limit_bytes=60 * 2**20)
 
 
@@ -371,7 +372,7 @@
             in_specs=[pl.BlockSpec(memory_space=pltpu.VMEM)] * len(self.ins),
             out_specs=[pl.BlockSpec(memory_space=pltpu.VMEM)] * len(self.shapes),
             out_shape=[jax.ShapeDtypeStruct(shape, BF16) for shape in self.shapes],
-            compiler_params=BIG_VMEM,
+            compiler_params=SMALL_VMEM,
             cost_estimate=CHEAP,
             name="rearrange",
         )(*clock.now(self.ins))
@@ -400,7 +401,7 @@
             in_specs=[PLACE] + [pl.BlockSpec(memory_space=pltpu.VMEM)] * len(arrays),
             out_specs=pl.BlockSpec(memory_space=pltpu.VMEM),
             out_shape=jax.ShapeDtypeStruct((2, grid.wide * self.height, self.cols), BF16),
-            compiler_params=BIG_VMEM,
+            compiler_params=SMALL_VMEM,
             cost_estimate=CHEAP,
             name="half_weights",
         )(self.place, *tie(grid.clock.now(arrays), *after))
@@ -1056,15 +1057,17 @@
         more.move(out, 0, k * rows, fc1[None], 0, 0, rows, k * cols)
     more.move(out, 0, 4 * rows, fc2[None], 0, part, part)
     ring_mix, ring_up = [[array] for array in more.run(clock)]
-    tick(ring_one[-1], ring_small[-1], ring_mix[0], ring_up[0], *exchange(grid, None, top))
+    came = exchange(grid, None, top)
+    tick(ring_one[-1], ring_small[-1], ring_mix[0], ring_up[0])
     ring_one.append(send("z", ring_one[-1]))
     ring_small.append(send("z", ring_small[-1]))
     memory = in_place(now(memory))
-    tick(ring_one[-1], ring_small[-1], memory, *exchange(grid, top, None))
+    tick(ring_one[-1], ring_small[-1], memory, *came)
+    came = exchange(grid, top, None)
     for _ in range(steps - 2):
         ring_one.append(send("z", ring_one[-1]))
         ring_small.append(send("z", ring_small[-1]))
-        tick(ring_one[-1], ring_small[-1])
+        tick(ring_one[-1], ring_small[-1], *came)
 
     def from_ring(arrays, first, count):
         return [[(array, 0, first, count, 0)] for array in arrays]
@@ -1097,6 +1100,7 @@
     came = exchange(grid, qkv, mix)
     for _ in range(steps - 2):
         ring_up.append(send("z", ring_up[-1]))
+    ring_top.append(send("z", ring_top[-1]))
     g_ckv.half(g_mix.parts[0][1])
     g_ckv.swap()
     small_all = g_ckv.small_rows()
@@ -1113,7 +1117,7 @@
         [by_memory(now(memory)), full(vectors)] + matrix(g_ckv, 0) + matrix(g_ckv, 1),
         [by_memory(mem_shape), by_memory(mem_shape)], grid=(mem_count,),
     )
-    tick(ring_up[-1], mem_keys, *came)
+    tick(ring_up[-1], ring_top[-1], mem_keys, *came)
 
     up = Square(g_fc1, from_ring(ring_up, 0, 4 * rows), 4 * rows)
     low = Square(g_fc2, from_ring(ring_up, 4 * rows, part), part, part)
@@ -1133,7 +1137,8 @@
     came = exchange(grid, up, low)
     g_mix.half(g_fc2.parts[0][1])
     g_mix.swap()
-    ring_top.append(send("z", ring_top[-1]))
+    for _ in range(steps - 2):
+        ring_top.append(send("z", ring_top[-1]))
     after_self, normed_two, cross_queries = dense_call(
         middle_kernel, "self_out_cross_q", place,
         [full(tokens), full(now(self_mixed)), full(vectors)] + matrix(g_mix, 0) + matrix(g_mix, 1),
@@ -1149,8 +1154,6 @@
     tick(cross_mixed, ring_top[-1], *came)
 
     came = exchange(grid, low, None)
-    for _ in range(steps - 2):
-        ring_top.append(send("z", ring_top[-1]))
     g_fc1.half()
     g_fc1.swap()
     after_cross, normed_three = dense_call(
@@ -1164,7 +1167,7 @@
         [full(normed_three), full(up_bias)] + by_y(g_fc1),
         [result((token_count, hidden), BF16)] * 2, grid=(2,),
     )
-    tick(activated, ring_top[-1], *came)
+    tick(activated, *came)
     spread = [(0, 0), (1, 0), (0, 1), (1, 1)]
     for step, array in enumerate(ring_top):
         g_fc2.put([(step, dx, dy) for dx, dy in spread], array, 0, part, 0)

time: 502 us -> 493 us (0.982)
  waiting for transfers between devices: 121 us -> 114 us
    ppermute x74, waiting for transfers between devices: 121 us -> 114 us  [send(): return lax.ppermute(self.clock.now(array), AXES, self.perms[name])]
    unnamed x212 -> x208, local copies, waits for them, and re-layouts: 36.2 us -> 32.9 us
  transfers between devices with their start and end apart: 74 -> 74, of which waited for: 28 -> 30; matrix products, arithmetic and copies ran while one was open for 8% -> 8% of each run, Pallas kernels for 40% -> 40%
where the time goes in v6:
time: 493 us; the launch traced here: 485 us
  Pallas kernels  225 us (46%)
  waiting for transfers between devices  114 us (23%)
  starting transfers between devices  68.5 us (14%)
  local copies, waits for them, and re-layouts  53.4 us (11%)
  other arithmetic  20.9 us (4%)
    ppermute x74, waiting for transfers between devices, send(): return lax.ppermute(self.clock.now(array), AXES, self.perms[name])  114 us
    pallas_call x11, Pallas kernels, dense_call(): pl.pallas_call(kernel, grid_spec=pltpu.PrefetchScalarGridSpec(num_scalar_...  88.1 us
    ppermute x74, starting transfers between devices, send(): return lax.ppermute(self.clock.now(array), AXES, self.perms[name])  68.5 us
    unnamed x208, local copies, waits for them, and re-layouts  32.9 us
    pallas_call x5, Pallas kernels, token_terms(): pl.pallas_call(kernel, grid_spec=pltpu.PrefetchScalarGridSpec(num_scalar_...  30.7 us
    pallas_call x2, Pallas kernels, memory_terms(): pl.pallas_call(functools.partial(memory_terms_kernel, near, len(pairs)),...  25.7 us
    pallas_call x1, Pallas kernels, cross_backward(): pl.pallas_call(cross_bwd_kernel, grid_spec=pltpu.PrefetchScalarGridSpec(n...  20 us
    pallas_call x4, Pallas kernels, add_corners(): pl.pallas_call(add_corners_kernel, grid=(ring,), in_specs=[full, full, ha...  16.5 us
  transfers between devices with their start and end apart: 74, of which 30 were waited for; matrix products, arithmetic and copies ran while one was open for 8% of the time, Pallas kernels for 40%

profile of v6, /device:TPU:0, one launch (start us, length us, event | category | flops | bytes accessed | tf_op | source)
XLA Modules:
  0.0 484.7 jit_solution(8590341746065867880)
XLA Ops:
  2.5 3.1 collective-permute-start
  13.2 2.3 collective-permute-done.1.refs_3_
  19.9 3.9 copy.44._
  23.9 2.1 copy-done.2
  30.9 5.5 %collective-permute-done.7.refs_7_ = bf16[1,16,256]{2,1,0:T(8,128)(2,1)S(1)} collective-permute-done((bf16[1,16,256]{2,1,0:T(8,128)(2,1)S(1)}, bf16[1,16,256]{2,1,0:T(8,128)(2,1)S(1)}, u32[]{:S(2)}, u32[]{:S(2)}) %collective-permute-start.7) | collective-permute-done | bytes 8224 | tf_op jit(solution)/shard_map/ppermute | solution.py:310
  39.8 13.7 %collective-permute-done.11.refs_3_ = bf16[1,384,256]{2,1,0:T(8,128)(2,1)S(1)} collective-permute-done((bf16[1,384,256]{2,1,0:T(8,128)(2,1)S(1)}, bf16[1,384,256]{2,1,0:T(8,128)(2,1)S(1)}, u32[]{:S(2)}, u32[]{:S(2)}) %collective-permute-start.11) | collective-permute-done | bytes 196640 | tf_op jit(solution)/shard_map/ppermute | solution.py:310
  56.9 9.7 %collective-permute-done.15.refs_4_ = bf16[1,384,256]{2,1,0:T(8,128)(2,1)} collective-permute-done((bf16[1,384,256]{2,1,0:T(8,128)(2,1)S(1)}, bf16[1,384,256]{2,1,0:T(8,128)(2,1)}, u32[]{:S(2)}, u32[]{:S(2)}) %collective-permute-start.15) | collective-permute-done | bytes 196640 | tf_op jit(solution)/shard_map/ppermute | solution.py:310
  68.6 2.9 collective-permute-done.14.refs_4_
  71.4 3.0 collective-permute-done.16.refs_5_
  74.4 1.9 collective-permute-done.17.refs_1_.refs_3_
  77.7 3.0 rearrange.18
  86.1 2.2 collective-permute-done.21.k_other.v_other
  92.0 2.4 copy-done.3
  94.4 13.8 %memory_keys_values.1 = (bf16[4,588,1024]{2,1,0:T(8,128)(2,1)S(1)}, bf16[4,588,1024]{2,1,0:T(8,128)(2,1)S(1)}) custom-call(s32[4]{0:T(128)S(1)} %pad_add_fusion.place, bf16[4,588,1024]{2,1,0:T(8,128)(2,1)S(1)} %copy-done.3, f32[13,1024]{1,0:T(8,128)S(1)} %reshape.468.vectors, bf16[2,2176,256]{2,1,0:T(8,128)(2,1)S(1)} %half_weights.5.k_own.v_own, ...), custom_call_target="tpu_custom_call" | custom-call | flops 1000000 | bytes 100000 | tf_op jit(solution)/shard_map/memory_keys_values/pallas_call | solution.py:958
  108.2 2.0 collective-permute-done.20.refs_6_
  110.2 2.2 collective-permute-done.22.refs_1_.refs_3_
  113.5 3.1 rearrange.19
  119.0 1.8 half_weights.6.refs_0_.refs_2_.refs_4_
  123.0 11.7 %collective-permute-start.25 = (bf16[4,256,256]{2,1,0:T(8,128)(2,1)}, bf16[4,256,256]{2,1,0:T(8,128)(2,1)}, u32[]{:S(2)}, u32[]{:S(2)}) collective-permute-start(bf16[4,256,256]{2,1,0:T(8,128)(2,1)} %collective-permute-done.20.refs_6_), channel_id=1, source_target_pairs={{0,8},{1,9},{2,10},{3,11},{4,12},{5,13},{6,14},{7,15},{8,16},{9,17... | collective-permute-start | bytes 1572872 | tf_op jit(solution)/shard_map/ppermute | solution.py:310
  136.0 4.7 self_qkv.1
  142.4 8.1 %collective-permute-done.25.refs_7_ = bf16[4,256,256]{2,1,0:T(8,128)(2,1)} collective-permute-done((bf16[4,256,256]{2,1,0:T(8,128)(2,1)}, bf16[4,256,256]{2,1,0:T(8,128)(2,1)}, u32[]{:S(2)}, u32[]{:S(2)}) %collective-permute-start.25) | collective-permute-done | bytes 524320 | tf_op jit(solution)/shard_map/ppermute | solution.py:310
  150.5 4.7 collective-permute-done.26.refs_1_.refs_3_
  155.7 3.4 rearrange.20
  159.2 2.7 half_weights.7.so_own.cq_own.own.co_own
  164.9 2.9 collective-permute-done.28.so_other.cq_other.other.co_other
  169.9 3.9 self_out_cross_q.1
  176.4 12.5 %cross_forward.1 = (bf16[256,1024]{1,0:T(8,128)(2,1)}, f32[2,8,256]{2,1,0:T(8,128)}) custom-call(s32[4]{0:T(128)} %copy-done.100, s32[4]{0:T(128)} %select_reduce_fusion.len_ref, s32[2,1,128]{2,1,0:T(1,128)} %bitcast.125, s32[2,128,1]{2,1,0:T(8,128)} %copy-done.32, bf16[256,1024]{1,0:T(8,128)(2,1)} %copy-done.38, bf16[4,588,1024]{2,1,0:T(8,128)(2,1)} %copy-done.7, ...), custom_call_target="tpu_custom_call" | custom-call | flops 1000000 | bytes 100000 | tf_op jit(solution)/shard_map/cross_forward/pallas_call | solution.py:229
  189.0 3.1 half_weights.8.own
  192.4 3.3 rearrange.21
  197.8 2.9 cross_out.1
  200.8 4.8 fc1_gelu.1
  207.0 2.9 weight_terms.5
  210.1 2.6 half_weights.9.own
  213.2 4.0 collective-permute-done.35.refs_2_
  217.2 3.9 weight_terms.6
  225.1 1.9 copy-done.71
  227.1 10.9 %fc2_gelu_back.1 = (bf16[256,4096]{1,0:T(8,128)(2,1)}, f32[1,4096]{1,0:T(1,128)}, bf16[1,2,1024,1024]{3,2,1,0:T(8,128)(2,1)}) custom-call(s32[4]{0:T(128)} %copy-done.59, bf16[256,1024]{1,0:T(8,128)(2,1)} %grad_out.1, bf16[256,4096]{1,0:T(8,128)(2,1)} %copy-done.44, bf16[256,1024]{1,0:T(8,128)(2,1)} %copy-done.23, bf16[2,4096,256]{2,1,0:T(8,128)(2,1)} %copy-done.5, ...), custom_call_target="tpu_custom_call" | custom-call | flops 1000000 | bytes 100000 | tf_op jit(solution)/shard_map/fc2_gelu_back/pallas_call | solution.py:958
  238.2 10.2 %fc1_norm_back.1 = (f32[256,1024]{1,0:T(8,128)}, bf16[256,1024]{1,0:T(8,128)(2,1)}, bf16[256,1024]{1,0:T(8,128)(2,1)}, f32[1,1024]{1,0:T(1,128)}, f32[1,1024]{1,...) custom-call(s32[4]{0:T(128)} %copy-done.59, bf16[256,4096]{1,0:T(8,128)(2,1)} %get-tuple-element.545.grad_pre.refs_1_, ...), custom_call_target="tpu_custom_call" | custom-call | flops 1000000 | bytes 100000 | tf_op jit(solution)/shard_map/fc1_norm_back/pallas_call | solution.py:958
  248.4 4.2 add_corners.4
  252.6 7.6 %weight_terms.7 = (bf16[4,1,64,1024]{3,2,1,0:T(8,128)(2,1)}, bf16[4,1,64,1024]{3,2,1,0:T(8,128)(2,1)}, bf16[4,1,128,1024]{3,2,1,0:T(8,128)(2,1)}, bf16[4,1,128,1024]{3,2,1,0:T(8,128)(2,1)}, f32[4,1,128,1024]{3,2,1,0:T(8,128)}) custom-call(s32[4]{0:T(128)} %copy-done.59, bf16[256,1024]{1,0:T(8,128)(2,1)} %copy-done.23, ...), custom_call_target="tpu_custom_call" | custom-call | flops 1000000 | bytes 100000 | tf_op jit(solution)/shard_map/weight_terms/pallas_call | solution.py:561
  264.3 20.0 %cross_backward.1 = (bf16[256,1024]{1,0:T(8,128)(2,1)}, bf16[4,588,1024]{2,1,0:T(8,128)(2,1)}, bf16[4,588,1024]{2,1,0:T(8,128)(2,1)}, f32[1,1024]{1,0:T(1,128)}) custom-call(s32[4]{0:T(128)} %copy-done.100, s32[4]{0:T(128)} %select_reduce_fusion.len_ref, s32[2,1,128]{2,1,0:T(1,128)} %bitcast.126, s32[2,128,1]{2,1,0:T(8,128)} %copy-done.32, ...), custom_call_target="tpu_custom_call" | custom-call | flops 1000000 | bytes 100000 | tf_op jit(solution)/shard_map/cross_backward/pallas_call | solution.py:251
  284.3 12.1 %memory_terms.2 = bf16[2,2,1024,256]{3,2,1,0:T(8,128)(2,1)} custom-call(s32[4]{0:T(128)} %copy-done.59, bf16[4,588,1024]{2,1,0:T(8,128)(2,1)} %copy-done.2, bf16[4,588,1024]{2,1,0:T(8,128)(2,1)} %get-tuple-element.620.dk.gk, bf16[4,588,1024]{2,1,0:T(8,128)(2,1)} %get-tuple-element.621.dv.gv), custom_call_target="tpu_custom_call" | custom-call | flops 1000000 | bytes 100000 | tf_op jit(solution)/shard_map/memory_terms/pallas_call | solution.py:622
  298.3 4.3 add_corners.5
  305.8 6.4 %cross_q_norm_back.1 = (f32[256,1024]{1,0:T(8,128)}, bf16[256,1024]{1,0:T(8,128)(2,1)}, bf16[256,1024]{1,0:T(8,128)(2,1)}, f32[1,1024]{1,0:T(1,128)}, f32[1,1024...) custom-call(s32[4]{0:T(128)} %copy-done.59, bf16[256,1024]{1,0:T(8,128)(2,1)} %get-tuple-element.570.grad_queries.refs_9_, ...), custom_call_target="tpu_custom_call" | custom-call | flops 1000000 | bytes 100000 | tf_op jit(solution)/shard_map/cross_q_norm_back/pallas_call | solution.py:958
  312.1 4.6 self_backward.1
  316.7 6.9 %weight_terms.8 = bf16[6,2,1024,256]{3,2,1,0:T(8,128)(2,1)} custom-call(s32[4]{0:T(128)} %copy-done.59, bf16[256,1024]{1,0:T(8,128)(2,1)} %copy-done.9, bf16[256,1024]{1,0:T(8,128)(2,1)} %get-tuple-element.595.refs_1_.gq, bf16[256,1024]{1,0:T(8,128)(2,1)} %copy-done.9, bf16[256,1024]{1,0:T(8,128)(2,1)} %get-tuple-element.596.refs_3_.gk, ...), custom_call_target="tpu_custom_call" | custom-call | flops 1000000 | bytes 100000 | tf_op jit(solution)/shard_map/weight_terms/pallas_call | solution.py:561
  323.7 13.5 %memory_terms.3 = (bf16[4,2,64,256]{3,2,1,0:T(8,128)(2,1)}, bf16[4,2,64,256]{3,2,1,0:T(8,128)(2,1)}, bf16[4,2,128,256]{3,2,1,0:T(8,128)(2,1)}, bf16[4,2,128,256]{3,2,1,0:T(8,128)(2,1)}, f32[4,2,128,256]{3,2,1,0:T(8,128)}) custom-call(s32[4]{0:T(128)} %copy-done.59, bf16[4,588,1024]{2,1,0:T(8,128)(2,1)} %copy-done.2, ...), custom_call_target="tpu_custom_call" | custom-call | flops 1000000 | bytes 100000 | tf_op jit(solution)/shard_map/memory_terms/pallas_call | solution.py:622
  344.3 7.5 %self_qkv_norm_back.1 = (bf16[256,1024]{1,0:T(8,128)(2,1)}, f32[1,1024]{1,0:T(1,128)}, f32[1,1024]{1,0:T(1,128)}, f32[1,1024]{1,0:T(1,128)}, f32[1,1024]{1,0:T(1,128)}) custom-call(s32[4]{0:T(128)} %copy-done.59, bf16[256,1024]{1,0:T(8,128)(2,1)} %tokens.4, f32[256,1024]{1,0:T(8,128)} %get-tuple-element.594.grad_after, ...), custom_call_target="tpu_custom_call" | custom-call | flops 1000000 | bytes 100000 | tf_op jit(solution)/shard_map/self_qkv_norm_back/pallas_call | solution.py:958
  351.8 9.3 %weight_terms.9 = (bf16[4,6,64,256]{3,2,1,0:T(8,128)(2,1)}, bf16[4,6,64,256]{3,2,1,0:T(8,128)(2,1)}, bf16[4,6,128,256]{3,2,1,0:T(8,128)(2,1)}, bf16[4,6,128,256]{3,2,1,0:T(8,128)(2,1)}, f32[4,6,128,256]{3,2,1,0:T(8,128)}) custom-call(s32[4]{0:T(128)} %copy-done.59, bf16[256,1024]{1,0:T(8,128)(2,1)} %copy-done.9, ...), custom_call_target="tpu_custom_call" | custom-call | flops 1000000 | bytes 100000 | tf_op jit(solution)/shard_map/weight_terms/pallas_call | solution.py:561
  364.1 3.5 add_corners.6
  371.3 3.1 collective-permute-start.53
  375.2 7.3 %fc2.1 = bf16[256,1024]{1,0:T(8,128)(2,1)} custom-call(s32[4]{0:T(128)} %copy-done.59, f32[256,1024]{1,0:T(8,128)} %copy-done.31, bf16[256,4096]{1,0:T(8,128)(2,1)} %copy-done.10, f32[13,1024]{1,0:T(8,128)} %copy-done.21, bf16[2,4096,256]{2,1,0:T(8,128)(2,1)} %copy-done.5, bf16[2,4096,256]{2,1,0:T(8,128)(2,1)} %copy-done.71), custom_call_target="tpu_custom_call" | custom-call | flops 1000000 | bytes 100000 | tf_op jit(solution)/shard_map/fc2/pallas_call | solution.py:958
  382.5 15.8 %memory_back.1 = bf16[4,588,1024]{2,1,0:T(8,128)(2,1)} custom-call(s32[4]{0:T(128)} %copy-done.59, bf16[4,588,1024]{2,1,0:T(8,128)(2,1)} %get-tuple-element.620.dk.gk, bf16[4,588,1024]{2,1,0:T(8,128)(2,1)} %get-tuple-element.621.dv.gv, bf16[2,2176,256]{2,1,0:T(8,128)(2,1)} %copy-done.4, bf16[2,2176,256]{2,1,0:T(8,128)(2,1)} %collective-permute-done.21.k_other.v_other, ...), custom_call_target="tpu_custom_call" | custom-call | flops 1000000 | bytes 100000 | tf_op jit(solution)/shard_map/memory_back/pallas_call | solution.py:958
  398.5 4.6 add_corners.7
  407.5 3.3 collective-permute-done.59
  412.7 8.3 %copy.63 = bf16[4,588,1024]{2,0,1:T(4,128)(2,1)} copy(bf16[4,588,1024]{2,1,0:T(8,128)(2,1)} %memory_back.1) | data formatting | bytes 9633792 | tf_op jit(solution)/shard_map/optimization_barrier | solution.py:275
  423.8 2.6 collective-permute-start.63
  426.7 6.0 %collective-permute-done.63 = bf16[1,128,1024]{2,1,0:T(8,128)(2,1)S(1)} collective-permute-done((bf16[1,128,1024]{2,1,0:T(8,128)(2,1)S(1)}, bf16[1,128,1024]{2,1,0:T(8,128)(2,1)S(1)}, u32[]{:S(2)}, u32[]{:S(2)}) %collective-permute-start.63) | collective-permute-done | bytes 262176 | tf_op jit(solution)/shard_map/ppermute | solution.py:310
  432.6 7.4 %collective-permute-done.65 = bf16[4,6,128,256]{3,2,1,0:T(8,128)(2,1)S(1)} collective-permute-done((bf16[4,6,128,256]{3,2,1,0:T(8,128)(2,1)}, bf16[4,6,128,256]{3,2,1,0:T(8,128)(2,1)S(1)}, u32[]{:S(2)}, u32[]{:S(2)}) %collective-permute-start.65) | collective-permute-done | bytes 1572896 | tf_op jit(solution)/shard_map/ppermute | solution.py:310
  444.3 12.4 %collective-permute-done.69 = bf16[2,128,256]{2,1,0:T(8,128)(2,1)S(1)} collective-permute-done((bf16[2,128,256]{2,1,0:T(8,128)(2,1)S(1)}, bf16[2,128,256]{2,1,0:T(8,128)(2,1)S(1)}, u32[]{:S(2)}, u32[]{:S(2)}) %collective-permute-start.69) | collective-permute-done | bytes 131104 | tf_op jit(solution)/shard_map/ppermute | solution.py:310
  459.0 1.9 fusion.2
  461.0 10.4 %collective-permute-done.72 = bf16[2,128,256]{2,1,0:T(8,128)(2,1)S(1)} collective-permute-done((bf16[2,128,256]{2,1,0:T(8,128)(2,1)S(1)}, bf16[2,128,256]{2,1,0:T(8,128)(2,1)S(1)}, u32[]{:S(2)}, u32[]{:S(2)}) %collective-permute-start.72) | collective-permute-done | bytes 131104 | tf_op jit(solution)/shard_map/ppermute | solution.py:310
  471.7 2.0 fusion.3
  477.4 4.1 collective-permute-done.73
  (393 shorter events, 109.4 us)
Async XLA Ops:
  2.5 13.0 %collective-permute-start = (bf16[1,640,256]{2,1,0:T(8,128)(2,1)S(1)}, bf16[1,640,256]{2,1,0:T(8,128)(2,1)S(1)}, u32[]{:S(2)}, u32[]{:S(2)}) collective-permute-start(bf16[1,640,256]{2,1,0:T(8,128)(2,1)S(1)} %rearrange.12.refs_0_.refs_2_), channel_id=1, source_target_pairs={{0,8},{1,9},{2,10},{3,11},{4,12},{5,13},{6,14},{7,15},{8,16},{9,17... | collective-permute-start | bytes 983048 | tf_op jit(solution)/shard_map/ppermute | solution.py:310
  7.1 8.4 %collective-permute-start.1 = (bf16[1,16,256]{2,1,0:T(8,128)(2,1)S(1)}, bf16[1,16,256]{2,1,0:T(8,128)(2,1)S(1)}, u32[]{:S(2)}, u32[]{:S(2)}) collective-permute-start(bf16[1,16,256]{2,1,0:T(8,128)(2,1)S(1)} %dynamic_update_slice.4.refs_1_), channel_id=1, source_target_pairs={{0,8},{1,9},{2,10},{3,11},{4,12},{5,13},{6,14},{7,15},{8,16},{9,17... | collective-permute-start | bytes 24584 | tf_op jit(solution)/shard_map/ppermute | solution.py:310
  15.5 10.9 %collective-permute-start.2 = (bf16[1,640,256]{2,1,0:T(8,128)(2,1)S(1)}, bf16[1,640,256]{2,1,0:T(8,128)(2,1)S(1)}, u32[]{:S(2)}, u32[]{:S(2)}) collective-permute-start(bf16[1,640,256]{2,1,0:T(8,128)(2,1)S(1)} %collective-permute-done.refs_2_.refs_3_), channel_id=1, source_target_pairs={{0,8},{1,9},{2,10},{3,11},{4,12},{5,13},{6,14},{7,15},{8,16},{9,17... | collective-permute-start | bytes 983048 | tf_op jit(solution)/shard_map/ppermute | solution.py:310
  15.5 10.5 %collective-permute-start.5 = (bf16[1,256,256]{2,1,0:T(8,128)(2,1)S(1)}, bf16[1,256,256]{2,1,0:T(8,128)(2,1)S(1)}, u32[]{:S(2)}, u32[]{:S(2)}) collective-permute-start(bf16[1,256,256]{2,1,0:T(8,128)(2,1)S(1)} %get-tuple-element.371), channel_id=1, source_target_pairs={{0,2},{1,3},{2,0},{3,1},{4,6},{5,7},{6,4},{7,5},{8,10},{9,11},{10,... | collective-permute-start | bytes 393224 | tf_op jit(solution)/shard_map/ppermute | solution.py:310
  17.1 8.9 %collective-permute-start.4 = (bf16[1,256,256]{2,1,0:T(8,128)(2,1)S(1)}, bf16[1,256,256]{2,1,0:T(8,128)(2,1)S(1)}, u32[]{:S(2)}, u32[]{:S(2)}) collective-permute-start(bf16[1,256,256]{2,1,0:T(8,128)(2,1)S(1)} %get-tuple-element.397.refs_0_), channel_id=1, source_target_pairs={{0,4},{1,5},{2,6},{3,7},{4,0},{5,1},{6,2},{7,3},{8,12},{9,13},{10,... | collective-permute-start | bytes 393224 | tf_op jit(solution)/shard_map/ppermute | solution.py:310
  26.4 10.0 %collective-permute-start.6 = (bf16[1,640,256]{2,1,0:T(8,128)(2,1)S(1)}, bf16[1,640,256]{2,1,0:T(8,128)(2,1)S(1)}, u32[]{:S(2)}, u32[]{:S(2)}) collective-permute-start(bf16[1,640,256]{2,1,0:T(8,128)(2,1)S(1)} %collective-permute-done.2.refs_4_), channel_id=1, source_target_pairs={{0,8},{1,9},{2,10},{3,11},{4,12},{5,13},{6,14},{7,15},{8,16},{9,17... | collective-permute-start | bytes 983048 | tf_op jit(solution)/shard_map/ppermute | solution.py:310
  27.7 8.7 %collective-permute-start.9 = (bf16[1,128,256]{2,1,0:T(8,128)(2,1)S(1)}, bf16[1,128,256]{2,1,0:T(8,128)(2,1)S(1)}, u32[]{:S(2)}, u32[]{:S(2)}) collective-permute-start(bf16[1,128,256]{2,1,0:T(8,128)(2,1)S(1)} %get-tuple-element.379), channel_id=1, source_target_pairs={{0,2},{1,3},{2,0},{3,1},{4,6},{5,7},{6,4},{7,5},{8,10},{9,11},{10,... | collective-permute-start | bytes 196616 | tf_op jit(solution)/shard_map/ppermute | solution.py:310
  28.2 8.1 %collective-permute-start.8 = (bf16[1,128,256]{2,1,0:T(8,128)(2,1)S(1)}, bf16[1,128,256]{2,1,0:T(8,128)(2,1)S(1)}, u32[]{:S(2)}, u32[]{:S(2)}) collective-permute-start(bf16[1,128,256]{2,1,0:T(8,128)(2,1)S(1)} %get-tuple-element.377), channel_id=1, source_target_pairs={{0,4},{1,5},{2,6},{3,7},{4,0},{5,1},{6,2},{7,3},{8,12},{9,13},{10,... | collective-permute-start | bytes 196616 | tf_op jit(solution)/shard_map/ppermute | solution.py:310
  36.4 17.1 %collective-permute-start.12 = (bf16[4,272,256]{2,1,0:T(8,128)(2,1)S(1)}, bf16[4,272,256]{2,1,0:T(8,128)(2,1)S(1)}, u32[]{:S(2)}, u32[]{:S(2)}) collective-permute-start(bf16[4,272,256]{2,1,0:T(8,128)(2,1)S(1)} %get-tuple-element.427.refs_0_), channel_id=1, source_target_pairs={{0,4},{1,5},{2,6},{3,7},{4,0},{5,1},{6,2},{7,3},{8,12},{9,13},{10,... | collective-permute-start | bytes 1671176 | tf_op jit(solution)/shard_map/ppermute | solution.py:310
  38.3 15.2 %collective-permute-start.13 = (bf16[4,272,256]{2,1,0:T(8,128)(2,1)S(1)}, bf16[4,272,256]{2,1,0:T(8,128)(2,1)S(1)}, u32[]{:S(2)}, u32[]{:S(2)}) collective-permute-start(bf16[4,272,256]{2,1,0:T(8,128)(2,1)S(1)} %get-tuple-element.393), channel_id=1, source_target_pairs={{0,2},{1,3},{2,0},{3,1},{4,6},{5,7},{6,4},{7,5},{8,10},{9,11},{10,... | collective-permute-start | bytes 1671176 | tf_op jit(solution)/shard_map/ppermute | solution.py:310
  39.8 13.7 %collective-permute-start.10 = (bf16[1,768,256]{2,1,0:T(8,128)(2,1)S(1)}, bf16[1,768,256]{2,1,0:T(8,128)(2,1)S(1)}, u32[]{:S(2)}, u32[]{:S(2)}) collective-permute-start(bf16[1,768,256]{2,1,0:T(8,128)(2,1)S(1)} %get-tuple-element.474.refs_2_), channel_id=1, source_target_pairs={{0,8},{1,9},{2,10},{3,11},{4,12},{5,13},{6,14},{7,15},{8,16},{9,17... | collective-permute-start | bytes 1179656 | tf_op jit(solution)/shard_map/ppermute | solution.py:310
  39.8 13.7 %collective-permute-start.11 = (bf16[1,384,256]{2,1,0:T(8,128)(2,1)S(1)}, bf16[1,384,256]{2,1,0:T(8,128)(2,1)S(1)}, u32[]{:S(2)}, u32[]{:S(2)}) collective-permute-start(bf16[1,384,256]{2,1,0:T(8,128)(2,1)S(1)} %get-tuple-element.422.refs_2_), channel_id=1, source_target_pairs={{0,8},{1,9},{2,10},{3,11},{4,12},{5,13},{6,14},{7,15},{8,16},{9,17... | collective-permute-start | bytes 589832 | tf_op jit(solution)/shard_map/ppermute | solution.py:310
  55.1 21.7 %collective-permute-start.18 = (bf16[4,528,256]{2,1,0:T(8,128)(2,1)}, bf16[4,528,256]{2,1,0:T(8,128)(2,1)S(1)}, u32[]{:S(2)}, u32[]{:S(2)}) collective-permute-start(bf16[4,528,256]{2,1,0:T(8,128)(2,1)} %get-tuple-element.411), channel_id=1, source_target_pairs={{0,2},{1,3},{2,0},{3,1},{4,6},{5,7},{6,4},{7,5},{8,10},{9,11},{10,... | collective-permute-start | bytes 3244040 | tf_op jit(solution)/shard_map/ppermute | solution.py:310
  55.6 20.7 %collective-permute-start.17 = (bf16[4,512,256]{2,1,0:T(8,128)(2,1)}, bf16[4,512,256]{2,1,0:T(8,128)(2,1)S(1)}, u32[]{:S(2)}, u32[]{:S(2)}) collective-permute-start(bf16[4,512,256]{2,1,0:T(8,128)(2,1)} %get-tuple-element.452.refs_0_), channel_id=1, source_target_pairs={{0,4},{1,5},{2,6},{3,7},{4,0},{5,1},{6,2},{7,3},{8,12},{9,13},{10,... | collective-permute-start | bytes 3145736 | tf_op jit(solution)/shard_map/ppermute | solution.py:310
  56.9 9.7 %collective-permute-start.15 = (bf16[1,384,256]{2,1,0:T(8,128)(2,1)S(1)}, bf16[1,384,256]{2,1,0:T(8,128)(2,1)}, u32[]{:S(2)}, u32[]{:S(2)}) collective-permute-start(bf16[1,384,256]{2,1,0:T(8,128)(2,1)S(1)} %collective-permute-done.11.refs_3_), channel_id=1, source_target_pairs={{0,8},{1,9},{2,10},{3,11},{4,12},{5,13},{6,14},{7,15},{8,16},{9,17... | collective-permute-start | bytes 589832 | tf_op jit(solution)/shard_map/ppermute | solution.py:310
  56.9 14.5 %collective-permute-start.14 = (bf16[1,768,256]{2,1,0:T(8,128)(2,1)S(1)}, bf16[1,768,256]{2,1,0:T(8,128)(2,1)S(1)}, u32[]{:S(2)}, u32[]{:S(2)}) collective-permute-start(bf16[1,768,256]{2,1,0:T(8,128)(2,1)S(1)} %collective-permute-done.10.refs_3_), channel_id=1, source_target_pairs={{0,8},{1,9},{2,10},{3,11},{4,12},{5,13},{6,14},{7,15},{8,16},{9,17... | collective-permute-start | bytes 1179656 | tf_op jit(solution)/shard_map/ppermute | solution.py:310
  66.6 7.8 %collective-permute-start.16 = (bf16[1,384,256]{2,1,0:T(8,128)(2,1)}, bf16[1,384,256]{2,1,0:T(8,128)(2,1)}, u32[]{:S(2)}, u32[]{:S(2)}) collective-permute-start(bf16[1,384,256]{2,1,0:T(8,128)(2,1)} %collective-permute-done.15.refs_4_), channel_id=1, source_target_pairs={{0,8},{1,9},{2,10},{3,11},{4,12},{5,13},{6,14},{7,15},{8,16},{9,17... | collective-permute-start | bytes 589832 | tf_op jit(solution)/shard_map/ppermute | solution.py:310
  83.8 28.6 %collective-permute-start.22 = (bf16[4,576,256]{2,1,0:T(8,128)(2,1)}, bf16[4,576,256]{2,1,0:T(8,128)(2,1)S(1)}, u32[]{:S(2)}, u32[]{:S(2)}) collective-permute-start(bf16[4,576,256]{2,1,0:T(8,128)(2,1)} %get-tuple-element.479.refs_0_), channel_id=1, source_target_pairs={{0,4},{1,5},{2,6},{3,7},{4,0},{5,1},{6,2},{7,3},{8,12},{9,13},{10,... | collective-permute-start | bytes 3538952 | tf_op jit(solution)/shard_map/ppermute | solution.py:310
  85.2 28.4 %collective-permute-start.23 = (bf16[4,576,256]{2,1,0:T(8,128)(2,1)}, bf16[4,576,256]{2,1,0:T(8,128)(2,1)}, u32[]{:S(2)}, u32[]{:S(2)}) collective-permute-start(bf16[4,576,256]{2,1,0:T(8,128)(2,1)} %get-tuple-element.438), channel_id=1, source_target_pairs={{0,2},{1,3},{2,0},{3,1},{4,6},{5,7},{6,4},{7,5},{8,10},{9,11},{10,... | collective-permute-start | bytes 3538952 | tf_op jit(solution)/shard_map/ppermute | solution.py:310
  85.9 22.3 %collective-permute-start.19 = (bf16[1,768,256]{2,1,0:T(8,128)(2,1)}, bf16[1,768,256]{2,1,0:T(8,128)(2,1)}, u32[]{:S(2)}, u32[]{:S(2)}) collective-permute-start(bf16[1,768,256]{2,1,0:T(8,128)(2,1)} %copy-done.51), channel_id=1, source_target_pairs={{0,8},{1,9},{2,10},{3,11},{4,12},{5,13},{6,14},{7,15},{8,16},{9,17... | collective-permute-start | bytes 1179656 | tf_op jit(solution)/shard_map/ppermute | solution.py:310
  86.0 24.2 %collective-permute-start.20 = (bf16[4,256,256]{2,1,0:T(8,128)(2,1)}, bf16[4,256,256]{2,1,0:T(8,128)(2,1)}, u32[]{:S(2)}, u32[]{:S(2)}) collective-permute-start(bf16[4,256,256]{2,1,0:T(8,128)(2,1)} %copy-done.39), channel_id=1, source_target_pairs={{0,8},{1,9},{2,10},{3,11},{4,12},{5,13},{6,14},{7,15},{8,16},{9,17... | collective-permute-start | bytes 1572872 | tf_op jit(solution)/shard_map/ppermute | solution.py:310
  120.8 14.0 %collective-permute-start.24 = (bf16[2,3072,256]{2,1,0:T(8,128)(2,1)S(1)}, bf16[2,3072,256]{2,1,0:T(8,128)(2,1)}, u32[]{:S(2)}, u32[]{:S(2)}) collective-permute-start(bf16[2,3072,256]{2,1,0:T(8,128)(2,1)S(1)} %half_weights.6.refs_0_.refs_2_.refs_4_), channel_id=1, source_target_pairs={{0,1},{1,0},{2,3},{3,2},{4,5},{5,4},{6,7},{7,6},{8,9},{9,8},{10,11... | collective-permute-start | bytes 9437192 | tf_op jit(solution)/shard_map/ppermute | solution.py:310
  120.9 34.3 %collective-permute-start.26 = (bf16[4,704,256]{2,1,0:T(8,128)(2,1)}, bf16[4,704,256]{2,1,0:T(8,128)(2,1)}, u32[]{:S(2)}, u32[]{:S(2)}) collective-permute-start(bf16[4,704,256]{2,1,0:T(8,128)(2,1)} %get-tuple-element.501.refs_0_), channel_id=1, source_target_pairs={{0,4},{1,5},{2,6},{3,7},{4,0},{5,1},{6,2},{7,3},{8,12},{9,13},{10,... | collective-permute-start | bytes 4325384 | tf_op jit(solution)/shard_map/ppermute | solution.py:310
  121.7 34.0 %collective-permute-start.27 = (bf16[4,704,256]{2,1,0:T(8,128)(2,1)}, bf16[4,704,256]{2,1,0:T(8,128)(2,1)}, u32[]{:S(2)}, u32[]{:S(2)}) collective-permute-start(bf16[4,704,256]{2,1,0:T(8,128)(2,1)} %get-tuple-element.465), channel_id=1, source_target_pairs={{0,2},{1,3},{2,0},{3,1},{4,6},{5,7},{6,4},{7,5},{8,10},{9,11},{10,... | collective-permute-start | bytes 4325384 | tf_op jit(solution)/shard_map/ppermute | solution.py:310
  123.0 27.5 %collective-permute-start.25 = (bf16[4,256,256]{2,1,0:T(8,128)(2,1)}, bf16[4,256,256]{2,1,0:T(8,128)(2,1)}, u32[]{:S(2)}, u32[]{:S(2)}) collective-permute-start(bf16[4,256,256]{2,1,0:T(8,128)(2,1)} %collective-permute-done.20.refs_6_), channel_id=1, source_target_pairs={{0,8},{1,9},{2,10},{3,11},{4,12},{5,13},{6,14},{7,15},{8,16},{9,17... | collective-permute-start | bytes 1572872 | tf_op jit(solution)/shard_map/ppermute | solution.py:310
  162.0 26.9 %collective-permute-start.30 = (bf16[4,512,256]{2,1,0:T(8,128)(2,1)}, bf16[4,512,256]{2,1,0:T(8,128)(2,1)}, u32[]{:S(2)}, u32[]{:S(2)}) collective-permute-start(bf16[4,512,256]{2,1,0:T(8,128)(2,1)} %get-tuple-element.530.refs_0_), channel_id=1, source_target_pairs={{0,4},{1,5},{2,6},{3,7},{4,0},{5,1},{6,2},{7,3},{8,12},{9,13},{10,... | collective-permute-start | bytes 3145736 | tf_op jit(solution)/shard_map/ppermute | solution.py:310
  163.4 25.6 %collective-permute-start.31 = (bf16[4,512,256]{2,1,0:T(8,128)(2,1)}, bf16[4,512,256]{2,1,0:T(8,128)(2,1)}, u32[]{:S(2)}, u32[]{:S(2)}) collective-permute-start(bf16[4,512,256]{2,1,0:T(8,128)(2,1)} %get-tuple-element.492), channel_id=1, source_target_pairs={{0,2},{1,3},{2,0},{3,1},{4,6},{5,7},{6,4},{7,5},{8,10},{9,11},{10,... | collective-permute-start | bytes 3145736 | tf_op jit(solution)/shard_map/ppermute | solution.py:310
  164.1 24.8 %collective-permute-start.29 = (bf16[4,256,256]{2,1,0:T(8,128)(2,1)}, bf16[4,256,256]{2,1,0:T(8,128)(2,1)}, u32[]{:S(2)}, u32[]{:S(2)}) collective-permute-start(bf16[4,256,256]{2,1,0:T(8,128)(2,1)} %collective-permute-done.25.refs_7_), channel_id=1, source_target_pairs={{0,8},{1,9},{2,10},{3,11},{4,12},{5,13},{6,14},{7,15},{8,16},{9,17... | collective-permute-start | bytes 1572872 | tf_op jit(solution)/shard_map/ppermute | solution.py:310
  192.2 8.6 %collective-permute-start.32 = (bf16[2,4096,256]{2,1,0:T(8,128)(2,1)S(1)}, bf16[2,4096,256]{2,1,0:T(8,128)(2,1)S(1)}, u32[]{:S(2)}, u32[]{:S(2)}) collective-permute-start(bf16[2,4096,256]{2,1,0:T(8,128)(2,1)S(1)} %half_weights.8.own), channel_id=1, source_target_pairs={{0,1},{1,0},{2,3},{3,2},{4,5},{5,4},{6,7},{7,6},{8,9},{9,8},{10,11... | collective-permute-start | bytes 12582920 | tf_op jit(solution)/shard_map/ppermute | solution.py:310
  195.7 11.4 %collective-permute-start.34 = (bf16[4,128,256]{2,1,0:T(8,128)(2,1)S(1)}, bf16[4,128,256]{2,1,0:T(8,128)(2,1)S(1)}, u32[]{:S(2)}, u32[]{:S(2)}) collective-permute-start(bf16[4,128,256]{2,1,0:T(8,128)(2,1)S(1)} %get-tuple-element.514), channel_id=1, source_target_pairs={{0,2},{1,3},{2,0},{3,1},{4,6},{5,7},{6,4},{7,5},{8,10},{9,11},{10,... | collective-permute-start | bytes 786440 | tf_op jit(solution)/shard_map/ppermute | solution.py:310
  197.0 10.0 %collective-permute-start.33 = (bf16[4,128,256]{2,1,0:T(8,128)(2,1)S(1)}, bf16[4,128,256]{2,1,0:T(8,128)(2,1)S(1)}, u32[]{:S(2)}, u32[]{:S(2)}) collective-permute-start(bf16[4,128,256]{2,1,0:T(8,128)(2,1)S(1)} %get-tuple-element.512), channel_id=1, source_target_pairs={{0,4},{1,5},{2,6},{3,7},{4,0},{5,1},{6,2},{7,3},{8,12},{9,13},{10,... | collective-permute-start | bytes 786440 | tf_op jit(solution)/shard_map/ppermute | solution.py:310
  212.7 12.4 %collective-permute-start.36 = (bf16[2,4096,256]{2,1,0:T(8,128)(2,1)S(1)}, bf16[2,4096,256]{2,1,0:T(8,128)(2,1)S(1)}, u32[]{:S(2)}, u32[]{:S(2)}) collective-permute-start(bf16[2,4096,256]{2,1,0:T(8,128)(2,1)S(1)} %half_weights.9.own), channel_id=1, source_target_pairs={{0,1},{1,0},{2,3},{3,2},{4,5},{5,4},{6,7},{7,6},{8,9},{9,8},{10,11... | collective-permute-start | bytes 12582920 | tf_op jit(solution)/shard_map/ppermute | solution.py:310
  223.1 14.8 %collective-permute-start.37 = (bf16[4,1,256,256]{3,2,1,0:T(8,128)(2,1)S(1)}, bf16[4,1,256,256]{3,2,1,0:T(8,128)(2,1)S(1)}, u32[]{:S(2)}, u32[]{:S(2)}) collective-permute-start(bf16[4,1,256,256]{3,2,1,0:T(8,128)(2,1)S(1)} %get-tuple-element.542), channel_id=1, source_target_pairs={{0,4},{1,5},{2,6},{3,7},{4,0},{5,1},{6,2},{7,3},{8,12},{9,13},{10,... | collective-permute-start | bytes 1572872 | tf_op jit(solution)/shard_map/ppermute | solution.py:310
  224.4 13.8 %collective-permute-start.38 = (bf16[4,1,256,256]{3,2,1,0:T(8,128)(2,1)S(1)}, bf16[4,1,256,256]{3,2,1,0:T(8,128)(2,1)}, u32[]{:S(2)}, u32[]{:S(2)}) collective-permute-start(bf16[4,1,256,256]{3,2,1,0:T(8,128)(2,1)S(1)} %get-tuple-element.544), channel_id=1, source_target_pairs={{0,2},{1,3},{2,0},{3,1},{4,6},{5,7},{6,4},{7,5},{8,10},{9,11},{10,... | collective-permute-start | bytes 1572872 | tf_op jit(solution)/shard_map/ppermute | solution.py:310
  238.2 14.4 %collective-permute-start.39 = (bf16[1,2,1024,1024]{3,2,1,0:T(8,128)(2,1)}, bf16[1,2,1024,1024]{3,2,1,0:T(8,128)(2,1)}, u32[]{:S(2)}, u32[]{:S(2)}) collective-permute-start(bf16[1,2,1024,1024]{3,2,1,0:T(8,128)(2,1)} %get-tuple-element.547), channel_id=1, source_target_pairs={{0,1},{1,0},{2,3},{3,2},{4,5},{5,4},{6,7},{7,6},{8,9},{9,8},{10,11... | collective-permute-start | bytes 12582920 | tf_op jit(solution)/shard_map/ppermute | solution.py:310
  260.2 38.0 %collective-permute-start.40 = (bf16[4,1,512,256]{3,2,1,0:T(8,128)(2,1)}, bf16[4,1,512,256]{3,2,1,0:T(8,128)(2,1)S(1)}, u32[]{:S(2)}, u32[]{:S(2)}) collective-permute-start(bf16[4,1,512,256]{3,2,1,0:T(8,128)(2,1)} %get-tuple-element.559), channel_id=1, source_target_pairs={{0,4},{1,5},{2,6},{3,7},{4,0},{5,1},{6,2},{7,3},{8,12},{9,13},{10,... | collective-permute-start | bytes 3145736 | tf_op jit(solution)/shard_map/ppermute | solution.py:310
  261.4 36.8 %collective-permute-start.41 = (bf16[4,1,512,256]{3,2,1,0:T(8,128)(2,1)}, bf16[4,1,512,256]{3,2,1,0:T(8,128)(2,1)}, u32[]{:S(2)}, u32[]{:S(2)}) collective-permute-start(bf16[4,1,512,256]{3,2,1,0:T(8,128)(2,1)} %get-tuple-element.561), channel_id=1, source_target_pairs={{0,2},{1,3},{2,0},{3,1},{4,6},{5,7},{6,4},{7,5},{8,10},{9,11},{10,... | collective-permute-start | bytes 3145736 | tf_op jit(solution)/shard_map/ppermute | solution.py:310
  262.3 35.0 %collective-permute-start.42 = (bf16[4,1,64,1024]{3,2,1,0:T(8,128)(2,1)}, bf16[4,1,64,1024]{3,2,1,0:T(8,128)(2,1)S(1)}, u32[]{:S(2)}, u32[]{:S(2)}) collective-permute-start(bf16[4,1,64,1024]{3,2,1,0:T(8,128)(2,1)} %get-tuple-element.562), channel_id=1, source_target_pairs={{0,4},{1,5},{2,6},{3,7},{4,0},{5,1},{6,2},{7,3},{8,12},{9,13},{10,... | collective-permute-start | bytes 1572872 | tf_op jit(solution)/shard_map/ppermute | solution.py:310
  263.5 34.8 %collective-permute-start.43 = (bf16[4,1,64,1024]{3,2,1,0:T(8,128)(2,1)}, bf16[4,1,64,1024]{3,2,1,0:T(8,128)(2,1)}, u32[]{:S(2)}, u32[]{:S(2)}) collective-permute-start(bf16[4,1,64,1024]{3,2,1,0:T(8,128)(2,1)} %get-tuple-element.564), channel_id=1, source_target_pairs={{0,2},{1,3},{2,0},{3,1},{4,6},{5,7},{6,4},{7,5},{8,10},{9,11},{10,... | collective-permute-start | bytes 1572872 | tf_op jit(solution)/shard_map/ppermute | solution.py:310
  298.2 25.4 %collective-permute-start.44 = (bf16[2,2,1024,256]{3,2,1,0:T(8,128)(2,1)}, bf16[2,2,1024,256]{3,2,1,0:T(8,128)(2,1)}, u32[]{:S(2)}, u32[]{:S(2)}) collective-permute-start(bf16[2,2,1024,256]{3,2,1,0:T(8,128)(2,1)} %memory_terms.2), channel_id=1, source_target_pairs={{0,1},{1,0},{2,3},{3,2},{4,5},{5,4},{6,7},{7,6},{8,9},{9,8},{10,11... | collective-permute-start | bytes 6291464 | tf_op jit(solution)/shard_map/ppermute | solution.py:310
  302.6 34.6 %collective-permute-start.46 = (bf16[4,1,128,1024]{3,2,1,0:T(8,128)(2,1)}, bf16[4,1,128,1024]{3,2,1,0:T(8,128)(2,1)}, u32[]{:S(2)}, u32[]{:S(2)}) collective-permute-start(bf16[4,1,128,1024]{3,2,1,0:T(8,128)(2,1)} %get-tuple-element.588), channel_id=1, source_target_pairs={{0,4},{1,5},{2,6},{3,7},{4,0},{5,1},{6,2},{7,3},{8,12},{9,13},{10,... | collective-permute-start | bytes 3145736 | tf_op jit(solution)/shard_map/ppermute | solution.py:310
  303.5 33.7 %collective-permute-start.47 = (bf16[4,1,128,1024]{3,2,1,0:T(8,128)(2,1)}, bf16[4,1,128,1024]{3,2,1,0:T(8,128)(2,1)}, u32[]{:S(2)}, u32[]{:S(2)}) collective-permute-start(bf16[4,1,128,1024]{3,2,1,0:T(8,128)(2,1)} %get-tuple-element.590), channel_id=1, source_target_pairs={{0,2},{1,3},{2,0},{3,1},{4,6},{5,7},{6,4},{7,5},{8,10},{9,11},{10,... | collective-permute-start | bytes 3145736 | tf_op jit(solution)/shard_map/ppermute | solution.py:310
  305.7 31.5 %collective-permute-start.45 = (bf16[1,512,256]{2,1,0:T(8,128)(2,1)S(1)}, bf16[1,512,256]{2,1,0:T(8,128)(2,1)S(1)}, u32[]{:S(2)}, u32[]{:S(2)}) collective-permute-start(bf16[1,512,256]{2,1,0:T(8,128)(2,1)S(1)} %fusion.9), channel_id=1, source_target_pairs={{0,8},{1,9},{2,10},{3,11},{4,12},{5,13},{6,14},{7,15},{8,16},{9,17... | collective-permute-start | bytes 786440 | tf_op jit(solution)/shard_map/ppermute | solution.py:310
  337.2 14.5 %collective-permute-start.48 = (bf16[6,2,1024,256]{3,2,1,0:T(8,128)(2,1)}, bf16[6,2,1024,256]{3,2,1,0:T(8,128)(2,1)}, u32[]{:S(2)}, u32[]{:S(2)}) collective-permute-start(bf16[6,2,1024,256]{3,2,1,0:T(8,128)(2,1)} %weight_terms.8), channel_id=1, source_target_pairs={{0,1},{1,0},{2,3},{3,2},{4,5},{5,4},{6,7},{7,6},{8,9},{9,8},{10,11... | collective-permute-start | bytes 18874376 | tf_op jit(solution)/shard_map/ppermute | solution.py:310
  340.4 20.9 %collective-permute-start.50 = (bf16[1,128,1024]{2,1,0:T(8,128)(2,1)S(1)}, bf16[1,128,1024]{2,1,0:T(8,128)(2,1)S(1)}, u32[]{:S(2)}, u32[]{:S(2)}) collective-permute-start(bf16[1,128,1024]{2,1,0:T(8,128)(2,1)S(1)} %fusion.10), channel_id=1, source_target_pairs={{0,8},{1,9},{2,10},{3,11},{4,12},{5,13},{6,14},{7,15},{8,16},{9,17... | collective-permute-start | bytes 786440 | tf_op jit(solution)/shard_map/ppermute | solution.py:310
  341.2 20.7 %collective-permute-start.49 = (bf16[1,512,256]{2,1,0:T(8,128)(2,1)}, bf16[1,512,256]{2,1,0:T(8,128)(2,1)S(1)}, u32[]{:S(2)}, u32[]{:S(2)}) collective-permute-start(bf16[1,512,256]{2,1,0:T(8,128)(2,1)} %fusion.7), channel_id=1, source_target_pairs={{0,8},{1,9},{2,10},{3,11},{4,12},{5,13},{6,14},{7,15},{8,16},{9,17... | collective-permute-start | bytes 786440 | tf_op jit(solution)/shard_map/ppermute | solution.py:310
  342.2 19.7 %collective-permute-start.51 = (bf16[4,2,64,256]{3,2,1,0:T(8,128)(2,1)}, bf16[4,2,64,256]{3,2,1,0:T(8,128)(2,1)}, u32[]{:S(2)}, u32[]{:S(2)}) collective-permute-start(bf16[4,2,64,256]{3,2,1,0:T(8,128)(2,1)} %get-tuple-element.609), channel_id=1, source_target_pairs={{0,4},{1,5},{2,6},{3,7},{4,0},{5,1},{6,2},{7,3},{8,12},{9,13},{10,... | collective-permute-start | bytes 786440 | tf_op jit(solution)/shard_map/ppermute | solution.py:310
  343.1 18.8 %collective-permute-start.52 = (bf16[4,2,64,256]{3,2,1,0:T(8,128)(2,1)}, bf16[4,2,64,256]{3,2,1,0:T(8,128)(2,1)}, u32[]{:S(2)}, u32[]{:S(2)}) collective-permute-start(bf16[4,2,64,256]{3,2,1,0:T(8,128)(2,1)} %get-tuple-element.611), channel_id=1, source_target_pairs={{0,2},{1,3},{2,0},{3,1},{4,6},{5,7},{6,4},{7,5},{8,10},{9,11},{10,... | collective-permute-start | bytes 786440 | tf_op jit(solution)/shard_map/ppermute | solution.py:310
  362.0 36.4 %collective-permute-start.56 = (bf16[4,6,64,256]{3,2,1,0:T(8,128)(2,1)}, bf16[4,6,64,256]{3,2,1,0:T(8,128)(2,1)}, u32[]{:S(2)}, u32[]{:S(2)}) collective-permute-start(bf16[4,6,64,256]{3,2,1,0:T(8,128)(2,1)} %get-tuple-element.630), channel_id=1, source_target_pairs={{0,4},{1,5},{2,6},{3,7},{4,0},{5,1},{6,2},{7,3},{8,12},{9,13},{10,... | collective-permute-start | bytes 2359304 | tf_op jit(solution)/shard_map/ppermute | solution.py:310
  362.9 35.4 %collective-permute-start.57 = (bf16[4,6,64,256]{3,2,1,0:T(8,128)(2,1)}, bf16[4,6,64,256]{3,2,1,0:T(8,128)(2,1)}, u32[]{:S(2)}, u32[]{:S(2)}) collective-permute-start(bf16[4,6,64,256]{3,2,1,0:T(8,128)(2,1)} %get-tuple-element.632), channel_id=1, source_target_pairs={{0,2},{1,3},{2,0},{3,1},{4,6},{5,7},{6,4},{7,5},{8,10},{9,11},{10,... | collective-permute-start | bytes 2359304 | tf_op jit(solution)/shard_map/ppermute | solution.py:310
  367.5 30.8 %collective-permute-start.54 = (bf16[4,2,128,256]{3,2,1,0:T(8,128)(2,1)}, bf16[4,2,128,256]{3,2,1,0:T(8,128)(2,1)}, u32[]{:S(2)}, u32[]{:S(2)}) collective-permute-start(bf16[4,2,128,256]{3,2,1,0:T(8,128)(2,1)} %get-tuple-element.627), channel_id=1, source_target_pairs={{0,4},{1,5},{2,6},{3,7},{4,0},{5,1},{6,2},{7,3},{8,12},{9,13},{10,... | collective-permute-start | bytes 1572872 | tf_op jit(solution)/shard_map/ppermute | solution.py:310
  368.4 29.9 %collective-permute-start.55 = (bf16[4,2,128,256]{3,2,1,0:T(8,128)(2,1)}, bf16[4,2,128,256]{3,2,1,0:T(8,128)(2,1)}, u32[]{:S(2)}, u32[]{:S(2)}) collective-permute-start(bf16[4,2,128,256]{3,2,1,0:T(8,128)(2,1)} %get-tuple-element.629), channel_id=1, source_target_pairs={{0,2},{1,3},{2,0},{3,1},{4,6},{5,7},{6,4},{7,5},{8,10},{9,11},{10,... | collective-permute-start | bytes 1572872 | tf_op jit(solution)/shard_map/ppermute | solution.py:310
  371.3 27.0 %collective-permute-start.53 = (bf16[1,512,256]{2,1,0:T(8,128)(2,1)}, bf16[1,512,256]{2,1,0:T(8,128)(2,1)S(1)}, u32[]{:S(2)}, u32[]{:S(2)}) collective-permute-start(bf16[1,512,256]{2,1,0:T(8,128)(2,1)} %fusion.6), channel_id=1, source_target_pairs={{0,8},{1,9},{2,10},{3,11},{4,12},{5,13},{6,14},{7,15},{8,16},{9,17... | collective-permute-start | bytes 786440 | tf_op jit(solution)/shard_map/ppermute | solution.py:310
  403.1 37.0 %collective-permute-start.65 = (bf16[4,6,128,256]{3,2,1,0:T(8,128)(2,1)}, bf16[4,6,128,256]{3,2,1,0:T(8,128)(2,1)S(1)}, u32[]{:S(2)}, u32[]{:S(2)}) collective-permute-start(bf16[4,6,128,256]{3,2,1,0:T(8,128)(2,1)} %get-tuple-element.671), channel_id=1, source_target_pairs={{0,4},{1,5},{2,6},{3,7},{4,0},{5,1},{6,2},{7,3},{8,12},{9,13},{10,... | collective-permute-start | bytes 4718600 | tf_op jit(solution)/shard_map/ppermute | solution.py:310
  404.0 36.7 %collective-permute-start.66 = (bf16[4,6,128,256]{3,2,1,0:T(8,128)(2,1)}, bf16[4,6,128,256]{3,2,1,0:T(8,128)(2,1)S(1)}, u32[]{:S(2)}, u32[]{:S(2)}) collective-permute-start(bf16[4,6,128,256]{3,2,1,0:T(8,128)(2,1)} %get-tuple-element.673), channel_id=1, source_target_pairs={{0,2},{1,3},{2,0},{3,1},{4,6},{5,7},{6,4},{7,5},{8,10},{9,11},{10,... | collective-permute-start | bytes 4718600 | tf_op jit(solution)/shard_map/ppermute | solution.py:310
  406.7 14.5 %collective-permute-start.62 = (bf16[1,128,1024]{2,1,0:T(8,128)(2,1)S(1)}, bf16[1,128,1024]{2,1,0:T(8,128)(2,1)S(1)}, u32[]{:S(2)}, u32[]{:S(2)}) collective-permute-start(bf16[1,128,1024]{2,1,0:T(8,128)(2,1)S(1)} %fusion.4), channel_id=1, source_target_pairs={{0,8},{1,9},{2,10},{3,11},{4,12},{5,13},{6,14},{7,15},{8,16},{9,17... | collective-permute-start | bytes 786440 | tf_op jit(solution)/shard_map/ppermute | solution.py:310
  410.7 10.3 %collective-permute-start.60 = (f32[2,2,544]{2,1,0:T(2,128)S(1)}, f32[2,2,544]{2,1,0:T(2,128)S(1)}, u32[]{:S(2)}, u32[]{:S(2)}) collective-permute-start(f32[2,2,544]{2,1,0:T(2,128)S(1)} %fusion.24), channel_id=1, source_target_pairs={{0,8},{1,9},{2,10},{3,11},{4,12},{5,13},{6,14},{7,15},{8,16},{9,17... | collective-permute-start | bytes 26120 | tf_op jit(solution)/shard_map/ppermute | solution.py:310
  411.8 14.8 %collective-permute-start.64 = (bf16[2,128,256]{2,1,0:T(8,128)(2,1)S(1)}, bf16[2,128,256]{2,1,0:T(8,128)(2,1)S(1)}, u32[]{:S(2)}, u32[]{:S(2)}) collective-permute-start(bf16[2,128,256]{2,1,0:T(8,128)(2,1)S(1)} %fusion.13), channel_id=1, source_target_pairs={{0,8},{1,9},{2,10},{3,11},{4,12},{5,13},{6,14},{7,15},{8,16},{9,17... | collective-permute-start | bytes 393224 | tf_op jit(solution)/shard_map/ppermute | solution.py:310
  423.8 8.8 %collective-permute-start.63 = (bf16[1,128,1024]{2,1,0:T(8,128)(2,1)S(1)}, bf16[1,128,1024]{2,1,0:T(8,128)(2,1)S(1)}, u32[]{:S(2)}, u32[]{:S(2)}) collective-permute-start(bf16[1,128,1024]{2,1,0:T(8,128)(2,1)S(1)} %fusion.5), channel_id=1, source_target_pairs={{0,8},{1,9},{2,10},{3,11},{4,12},{5,13},{6,14},{7,15},{8,16},{9,17... | collective-permute-start | bytes 786440 | tf_op jit(solution)/shard_map/ppermute | solution.py:310
  442.0 14.7 %collective-permute-start.68 = (bf16[6,128,256]{2,1,0:T(8,128)(2,1)S(1)}, bf16[6,128,256]{2,1,0:T(8,128)(2,1)S(1)}, u32[]{:S(2)}, u32[]{:S(2)}) collective-permute-start(bf16[6,128,256]{2,1,0:T(8,128)(2,1)S(1)} %fusion.8), channel_id=1, source_target_pairs={{0,8},{1,9},{2,10},{3,11},{4,12},{5,13},{6,14},{7,15},{8,16},{9,17... | collective-permute-start | bytes 1179656 | tf_op jit(solution)/shard_map/ppermute | solution.py:310
  443.2 13.6 %collective-permute-start.69 = (bf16[2,128,256]{2,1,0:T(8,128)(2,1)S(1)}, bf16[2,128,256]{2,1,0:T(8,128)(2,1)S(1)}, u32[]{:S(2)}, u32[]{:S(2)}) collective-permute-start(bf16[2,128,256]{2,1,0:T(8,128)(2,1)S(1)} %fusion.12), channel_id=1, source_target_pairs={{0,8},{1,9},{2,10},{3,11},{4,12},{5,13},{6,14},{7,15},{8,16},{9,17... | collective-permute-start | bytes 393224 | tf_op jit(solution)/shard_map/ppermute | solution.py:310
  457.9 13.5 %collective-permute-start.71 = (bf16[6,128,256]{2,1,0:T(8,128)(2,1)S(1)}, bf16[6,128,256]{2,1,0:T(8,128)(2,1)S(1)}, u32[]{:S(2)}, u32[]{:S(2)}) collective-permute-start(bf16[6,128,256]{2,1,0:T(8,128)(2,1)S(1)} %fusion.1), channel_id=1, source_target_pairs={{0,8},{1,9},{2,10},{3,11},{4,12},{5,13},{6,14},{7,15},{8,16},{9,17... | collective-permute-start | bytes 1179656 | tf_op jit(solution)/shard_map/ppermute | solution.py:310
  459.0 12.4 %collective-permute-start.72 = (bf16[2,128,256]{2,1,0:T(8,128)(2,1)S(1)}, bf16[2,128,256]{2,1,0:T(8,128)(2,1)S(1)}, u32[]{:S(2)}, u32[]{:S(2)}) collective-permute-start(bf16[2,128,256]{2,1,0:T(8,128)(2,1)S(1)} %fusion.11), channel_id=1, source_target_pairs={{0,8},{1,9},{2,10},{3,11},{4,12},{5,13},{6,14},{7,15},{8,16},{9,17... | collective-permute-start | bytes 393224 | tf_op jit(solution)/shard_map/ppermute | solution.py:310
  471.6 9.8 %collective-permute-start.73 = (bf16[6,128,256]{2,1,0:T(8,128)(2,1)S(1)}, bf16[6,128,256]{2,1,0:T(8,128)(2,1)S(1)}, u32[]{:S(2)}, u32[]{:S(2)}) collective-permute-start(bf16[6,128,256]{2,1,0:T(8,128)(2,1)S(1)} %fusion), channel_id=1, source_target_pairs={{0,8},{1,9},{2,10},{3,11},{4,12},{5,13},{6,14},{7,15},{8,16},{9,17... | collective-permute-start | bytes 1179656 | tf_op jit(solution)/shard_map/ppermute | solution.py:310
  (113 other events, 1297.0 us)

commit v7 on v6

--- a/solution.py
+++ b/solution.py
@@ -25,7 +25,7 @@
 CHEAP = pl.CostEstimate(flops=10**6, bytes_accessed=10**5, transcendentals=0)
 BIG_VMEM = pltpu.CompilerParams(vmem_limit_bytes=VMEM)
 SMALL_VMEM = pltpu.CompilerParams(vmem_limit_bytes=16 * 2**20)
-FULL_VMEM = pltpu.CompilerParams(vmem_limit_bytes=60 * 2**20)
+FULL_VMEM = pltpu.CompilerParams(vmem_limit_bytes=44 * 2**20)
 
 
 def dot_nt(a, b):
@@ -1203,20 +1203,21 @@
     r_fc1.out = far_fc1
     tick(far_fc1, *r_fc2.across())
     r_fc2.add()
+    came = list(r_fc2.pairs())
     r_fc1.swap()
     (
         grad_after_cross, grad_branch_two, grad_cross_mixed,
         grad_gain_three, grad_bias_eight, grad_bias_seven, grad_bias_nine,
     ) = dense_call(
         up_back_kernel, "fc1_norm_back", place,
-        [full(now(grad_pre)), full(cotangent), full(after_cross), full(vectors)]
+        [full(tie(now(grad_pre), r_fc2.sx)), full(cotangent), full(after_cross), full(vectors)]
         + by_y(g_fc1) + matrix(g_mix, 2),
         [result(wide_row, F32), result(wide_row, BF16), result(wide_row, BF16)] + [one_row] * 4,
         grid=(2,), scratch=[pltpu.VMEM(wide_row, F32)], params=FULL_VMEM,
     )
-    tick(r_fc1.near(), r_fc2.sx, grad_cross_mixed)
-
-    came = [*r_fc2.pairs(), *r_fc1.across()]
+    tick(r_fc1.near(), grad_cross_mixed)
+
+    came += r_fc1.across()
     grad_cq, grad_ck, grad_cv, grad_bias_six = cross_backward(
         local_map, row_lengths, segment_ids, cross_queries, mem_keys, mem_values,
         now(grad_cross_mixed), cross_lse,
@@ -1294,12 +1295,7 @@
         [by_memory(a) for a in tie(now((grad_ck, grad_cv)), r_mem.sx)] + matrix(g_ckv, 0) + matrix(g_ckv, 1),
         [by_memory(mem_shape)], grid=(mem_count,), params=FULL_VMEM,
     )
-    (layer_out,) = dense_call(
-        down_kernel, "fc2", place,
-        [full(after_cross), full(tie(now(activated), r_mem.sx)), full(vectors)] + by_y(g_fc2),
-        [result(wide_row, BF16)], grid=(2,), params=FULL_VMEM,
-    )
-    tick(grad_memory, layer_out, ring_fc2.came, *r_mem.pairs(), *r_rest.across())
+    tick(grad_memory, ring_fc2.came, *r_mem.pairs(), *r_rest.across())
     small_sum.step()
     ring_mem = RingSum(grid, [r_mem])
     r_rest.add()
@@ -1309,8 +1305,14 @@
     ring_mem.step()
     for _ in range(steps):
         small_sum.step()
+    (layer_out,) = dense_call(
+        down_kernel, "fc2", place,
+        [full(after_cross), full(tie(now(activated), turned_memory)), full(vectors)] + by_y(g_fc2),
+        [result(wide_row, BF16)], grid=(2,), params=FULL_VMEM,
+    )
     ring_fc1.step(turned_memory)
-    tick(turned_memory, small_sum.came, ring_fc1.came, ring_mem.came, *r_rest.pairs())
+    ring_mem.step(turned_memory)
+    tick(turned_memory, layer_out, small_sum.came, ring_fc1.came, ring_mem.came, *r_rest.pairs())
     ring_fc2.step()
     ring_rest = RingSum(grid, [r_rest])
     ring_rest.step()

time: 493 us -> 483 us (0.980)
  Pallas kernels: 225 us -> 198 us
  local copies, waits for them, and re-layouts: 53.4 us -> 72.1 us
  other arithmetic: 20.9 us -> 27.3 us
  starting transfers between devices: 68.5 us -> 63.3 us
    unnamed x208 -> x260, local copies, waits for them, and re-layouts: 32.9 us -> 52.8 us
    pallas_call x11, Pallas kernels: 88.1 us -> 77.5 us  [dense_call(): pl.pallas_call(kernel, grid_spec=pltpu.PrefetchScalarGridSpec(num_scalar_...]
    pallas_call x5, Pallas kernels: 30.7 us -> 24.4 us  [token_terms(): pl.pallas_call(kernel, grid_spec=pltpu.PrefetchScalarGridSpec(num_scalar_...]
    convert_element_type x12, other arithmetic: 12 us -> 17.7 us  [step(): self.came = self.grid.send('z', total.astype(BF16))]
    pallas_call x4, Pallas kernels: 16.5 us -> 10.9 us  [add_corners(): pl.pallas_call(add_corners_kernel, grid=(ring,), in_specs=[full, full, ha...]
    ppermute x74, starting transfers between devices: 68.5 us -> 63.3 us  [send(): return lax.ppermute(self.clock.now(array), AXES, self.perms[name])]
  transfers between devices with their start and end apart: 74 -> 74, of which waited for: 30 -> 32; matrix products, arithmetic and copies ran while one was open for 8% -> 8% of each run, Pallas kernels for 40% -> 36%
where the time goes in v7:
time: 483 us; the launch traced here: 475 us
  Pallas kernels  198 us (41%)
  waiting for transfers between devices  112 us (23%)
  local copies, waits for them, and re-layouts  72.1 us (15%)
  starting transfers between devices  63.3 us (13%)
  other arithmetic  27.3 us (6%)
    ppermute x74, waiting for transfers between devices, send(): return lax.ppermute(self.clock.now(array), AXES, self.perms[name])  112 us
    pallas_call x11, Pallas kernels, dense_call(): pl.pallas_call(kernel, grid_spec=pltpu.PrefetchScalarGridSpec(num_scalar_...  77.5 us
    ppermute x74, starting transfers between devices, send(): return lax.ppermute(self.clock.now(array), AXES, self.perms[name])  63.3 us
    unnamed x260, local copies, waits for them, and re-layouts  52.8 us
    pallas_call x5, Pallas kernels, token_terms(): pl.pallas_call(kernel, grid_spec=pltpu.PrefetchScalarGridSpec(num_scalar_...  24.4 us
    pallas_call x2, Pallas kernels, memory_terms(): pl.pallas_call(functools.partial(memory_terms_kernel, near, len(pairs)),...  22.4 us
    pallas_call x1, Pallas kernels, cross_backward(): pl.pallas_call(cross_bwd_kernel, grid_spec=pltpu.PrefetchScalarGridSpec(n...  19.2 us
    convert_element_type x12, other arithmetic, step(): self.came = self.grid.send('z', total.astype(BF16))  17.7 us
  transfers between devices with their start and end apart: 74, of which 32 were waited for; matrix products, arithmetic and copies ran while one was open for 8% of the time, Pallas kernels for 36%

profile of v7, /device:TPU:0, one launch (start us, length us, event | category | flops | bytes accessed | tf_op | source)
XLA Modules:
  0.0 474.9 jit_solution(17070451347441457464)
XLA Ops:
  2.5 3.1 collective-permute-start
  13.2 2.3 collective-permute-done.1.refs_3_
  19.9 3.9 copy.44._
  23.9 2.2 copy-done
  30.9 5.4 %collective-permute-done.7.refs_7_ = bf16[1,16,256]{2,1,0:T(8,128)(2,1)S(1)} collective-permute-done((bf16[1,16,256]{2,1,0:T(8,128)(2,1)S(1)}, bf16[1,16,256]{2,1,0:T(8,128)(2,1)S(1)}, u32[]{:S(2)}, u32[]{:S(2)}) %collective-permute-start.7) | collective-permute-done | bytes 8224 | tf_op jit(solution)/shard_map/ppermute | solution.py:310
  39.7 13.7 %collective-permute-done.11.refs_3_ = bf16[1,384,256]{2,1,0:T(8,128)(2,1)S(1)} collective-permute-done((bf16[1,384,256]{2,1,0:T(8,128)(2,1)S(1)}, bf16[1,384,256]{2,1,0:T(8,128)(2,1)S(1)}, u32[]{:S(2)}, u32[]{:S(2)}) %collective-permute-start.11) | collective-permute-done | bytes 196640 | tf_op jit(solution)/shard_map/ppermute | solution.py:310
  56.8 9.6 %collective-permute-done.15.refs_4_ = bf16[1,384,256]{2,1,0:T(8,128)(2,1)S(1)} collective-permute-done((bf16[1,384,256]{2,1,0:T(8,128)(2,1)S(1)}, bf16[1,384,256]{2,1,0:T(8,128)(2,1)S(1)}, u32[]{:S(2)}, u32[]{:S(2)}) %collective-permute-start.15) | collective-permute-done | bytes 196640 | tf_op jit(solution)/shard_map/ppermute | solution.py:310
  68.3 3.1 collective-permute-done.14.refs_4_
  71.4 2.6 collective-permute-done.16.refs_5_
  74.0 2.2 collective-permute-done.17.refs_1_.refs_3_
  76.6 2.7 rearrange.18
  83.5 2.3 collective-permute-done.21.k_other.v_other
  90.6 2.4 copy-done.1
  93.0 13.7 %memory_keys_values.1 = (bf16[4,588,1024]{2,1,0:T(8,128)(2,1)S(1)}, bf16[4,588,1024]{2,1,0:T(8,128)(2,1)S(1)}) custom-call(s32[4]{0:T(128)S(1)} %pad_add_fusion.place, bf16[4,588,1024]{2,1,0:T(8,128)(2,1)S(1)} %copy-done.1, f32[13,1024]{1,0:T(8,128)S(1)} %reshape.468.vectors, bf16[2,2176,256]{2,1,0:T(8,128)(2,1)S(1)} %half_weights.5.k_own.v_own, ...), custom_call_target="tpu_custom_call" | custom-call | flops 1000000 | bytes 100000 | tf_op jit(solution)/shard_map/memory_keys_values/pallas_call | solution.py:958
  107.7 2.2 collective-permute-done.22.refs_1_.refs_3_
  110.9 3.2 rearrange.19
  120.8 3.4 collective-permute-done.24.refs_1_.refs_3_.refs_5_
  125.2 4.7 self_qkv.1
  133.2 3.3 collective-permute-done.25.refs_7_
  136.4 16.2 %collective-permute-done.26.refs_1_.refs_3_ = bf16[4,704,256]{2,1,0:T(8,128)(2,1)} collective-permute-done((bf16[4,704,256]{2,1,0:T(8,128)(2,1)}, bf16[4,704,256]{2,1,0:T(8,128)(2,1)}, u32[]{:S(2)}, u32[]{:S(2)}) %collective-permute-start.26) | collective-permute-done | bytes 1441824 | tf_op jit(solution)/shard_map/ppermute | solution.py:310
  153.4 3.6 rearrange.20
  157.0 4.4 half_weights.7.so_own.cq_own.own.co_own
  163.8 3.7 collective-permute-done.28.so_other.cq_other.other.co_other
  169.5 4.5 self_out_cross_q.1
  174.8 2.8 copy-done.10
  177.6 11.2 %cross_forward.1 = (bf16[256,1024]{1,0:T(8,128)(2,1)S(1)}, f32[2,8,256]{2,1,0:T(8,128)S(1)}) custom-call(s32[4]{0:T(128)S(1)} %reshape.469.map_ref, s32[4]{0:T(128)S(1)} %select_reduce_fusion.len_ref, s32[2,1,128]{2,1,0:T(1,128)S(1)} %bitcast.129, s32[2,128,1]{2,1,0:T(8,128)S(1)} %copy.47.seg_col, bf16[256,1024]{1,0:T(8,128)(2,1)S(1)} %get-tuple-element.485.q_ref, ...), custom_call_target="tpu_custom_call" | custom-call | flops 1000000 | bytes 100000 | tf_op jit(solution)/shard_map/cross_forward/pallas_call | solution.py:229
  188.8 3.3 half_weights.8.own
  192.4 3.0 rearrange.21
  197.5 3.2 cross_out.1
  200.8 4.8 %fc1_gelu.1 = (bf16[256,4096]{1,0:T(8,128)(2,1)S(1)}, bf16[256,4096]{1,0:T(8,128)(2,1)S(1)}) custom-call(s32[4]{0:T(128)S(1)} %pad_add_fusion.place, bf16[256,1024]{1,0:T(8,128)(2,1)S(1)} %get-tuple-element.494.normed.refs_0_, f32[1,4096]{1,0:T(1,128)S(1)} %bitcast.123, bf16[2,4096,256]{2,1,0:T(8,128)(2,1)S(1)} %half_weights.8.own, ...), custom_call_target="tpu_custom_call" | custom-call | flops 1000000 | bytes 100000 | tf_op jit(solution)/shard_map/fc1_gelu/pallas_call | solution.py:958
  205.6 2.9 weight_terms.5
  208.6 2.8 half_weights.9.own
  212.0 3.8 collective-permute-done.35.refs_2_
  215.8 4.6 weight_terms.6
  229.4 7.8 %fc2_gelu_back.1 = (bf16[256,4096]{1,0:T(8,128)(2,1)S(1)}, f32[1,4096]{1,0:T(1,128)S(1)}, bf16[1,2,1024,1024]{3,2,1,0:T(8,128)(2,1)S(1)}) custom-call(s32[4]{0:T(128)S(1)} %pad_add_fusion.place, bf16[256,1024]{1,0:T(8,128)(2,1)S(1)} %copy-done.26, bf16[256,4096]{1,0:T(8,128)(2,1)S(1)} %copy-done.75, bf16[256,1024]{1,0:T(8,128)(2,1)S(1)} %get-tuple-element.494.normed.refs_0_, ...), custom_call_target="tpu_custom_call" | custom-call | flops 1000000 | bytes 100000 | tf_op jit(solution)/shard_map/fc2_gelu_back/pallas_call | solution.py:958
  238.8 3.5 add_corners.4
  244.4 8.1 %fc1_norm_back.1 = (f32[256,1024]{1,0:T(8,128)S(1)}, bf16[256,1024]{1,0:T(8,128)(2,1)S(1)}, bf16[256,1024]{1,0:T(8,128)(2,1)S(1)}, f32[1,1024]{1,0:T(1,128)S(1)}...) custom-call(s32[4]{0:T(128)S(1)} %pad_add_fusion.place, ...), custom_call_target="tpu_custom_call" | custom-call | flops 1000000 | bytes 100000 | tf_op jit(solution)/shard_map/fc1_norm_back/pallas_call | solution.py:958
  253.5 4.8 %weight_terms.7 = (bf16[4,1,64,1024]{3,2,1,0:T(8,128)(2,1)S(1)}, bf16[4,1,64,1024]{3,2,1,0:T(8,128)(2,1)S(1)}, bf16[4,1,128,1024]{3,2,1,0:T(8,128)(2,1)S(1)}, bf...) custom-call(s32[4]{0:T(128)S(1)} %pad_add_fusion.place, ...), custom_call_target="tpu_custom_call" | custom-call | flops 1000000 | bytes 100000 | tf_op jit(solution)/shard_map/weight_terms/pallas_call | solution.py:561
  261.6 19.2 %cross_backward.1 = (bf16[256,1024]{1,0:T(8,128)(2,1)S(1)}, bf16[4,588,1024]{2,1,0:T(8,128)(2,1)S(1)}, bf16[4,588,1024]{2,1,0:T(8,128)(2,1)}, f32[1,1024]{1,0:T(1,128)S(1)}) custom-call(s32[4]{0:T(128)S(1)} %reshape.469.map_ref, s32[4]{0:T(128)S(1)} %select_reduce_fusion.len_ref, s32[2,1,128]{2,1,0:T(1,128)S(1)} %bitcast.130, ...), custom_call_target="tpu_custom_call" | custom-call | flops 1000000 | bytes 100000 | tf_op jit(solution)/shard_map/cross_backward/pallas_call | solution.py:251
  280.8 2.2 copy-done.5
  282.9 11.5 %memory_terms.2 = bf16[2,2,1024,256]{3,2,1,0:T(8,128)(2,1)} custom-call(s32[4]{0:T(128)S(1)} %pad_add_fusion.place, bf16[4,588,1024]{2,1,0:T(8,128)(2,1)S(1)} %bitcast.116, bf16[4,588,1024]{2,1,0:T(8,128)(2,1)} %copy-done.5, bf16[4,588,1024]{2,1,0:T(8,128)(2,1)} %get-tuple-element.619.dv.gv), custom_call_target="tpu_custom_call" | custom-call | flops 1000000 | bytes 100000 | tf_op jit(solution)/shard_map/memory_terms/pallas_call | solution.py:622
  303.3 4.9 %cross_q_norm_back.1 = (f32[256,1024]{1,0:T(8,128)S(1)}, bf16[256,1024]{1,0:T(8,128)(2,1)S(1)}, bf16[256,1024]{1,0:T(8,128)(2,1)S(1)}, f32[1,1024]{1,0:T(1,128)S...) custom-call(s32[4]{0:T(128)S(1)} %pad_add_fusion.place, ...), custom_call_target="tpu_custom_call" | custom-call | flops 1000000 | bytes 100000 | tf_op jit(solution)/shard_map/cross_q_norm_back/pallas_call | solution.py:958
  308.3 2.3 self_backward.1
  310.7 4.6 weight_terms.8
  315.3 2.4 copy-done.2
  317.7 11.0 %memory_terms.3 = (bf16[4,2,64,256]{3,2,1,0:T(8,128)(2,1)S(1)}, bf16[4,2,64,256]{3,2,1,0:T(8,128)(2,1)S(1)}, bf16[4,2,128,256]{3,2,1,0:T(8,128)(2,1)S(1)}, bf16[...) custom-call(s32[4]{0:T(128)S(1)} %pad_add_fusion.place, bf16[4,588,1024]{2,1,0:T(8,128)(2,1)S(1)} %copy-done.2, ...), custom_call_target="tpu_custom_call" | custom-call | flops 1000000 | bytes 100000 | tf_op jit(solution)/shard_map/memory_terms/pallas_call | solution.py:622
  341.1 6.0 %self_qkv_norm_back.1 = (bf16[256,1024]{1,0:T(8,128)(2,1)}, f32[1,1024]{1,0:T(1,128)S(1)}, f32[1,1024]{1,0:T(1,128)S(1)}, f32[1,1024]{1,0:T(1,128)S(1)}, f32[1,1024]{1,0:T(1,128)S(1)}) custom-call(s32[4]{0:T(128)S(1)} %pad_add_fusion.place, bf16[256,1024]{1,0:T(8,128)(2,1)S(1)} %copy-done.42, f32[256,1024]{1,0:T(8,128)S(1)} %copy-done.89, ...), custom_call_target="tpu_custom_call" | custom-call | flops 1000000 | bytes 100000 | tf_op jit(solution)/shard_map/self_qkv_norm_back/pallas_call | solution.py:958
  347.2 7.5 %weight_terms.9 = (bf16[4,6,64,256]{3,2,1,0:T(8,128)(2,1)}, bf16[4,6,64,256]{3,2,1,0:T(8,128)(2,1)}, bf16[4,6,128,256]{3,2,1,0:T(8,128)(2,1)S(1)}, bf16[4,6,128,...) custom-call(s32[4]{0:T(128)S(1)} %pad_add_fusion.place, bf16[256,1024]{1,0:T(8,128)(2,1)S(1)} %copy-done.14, ...), custom_call_target="tpu_custom_call" | custom-call | flops 1000000 | bytes 100000 | tf_op jit(solution)/shard_map/weight_terms/pallas_call | solution.py:561
  364.9 2.8 collective-permute-start.53
  370.1 14.3 %memory_back.1 = bf16[4,588,1024]{2,1,0:T(8,128)(2,1)S(1)} custom-call(s32[4]{0:T(128)S(1)} %pad_add_fusion.place, bf16[4,588,1024]{2,1,0:T(8,128)(2,1)} %copy-done.5, bf16[4,588,1024]{2,1,0:T(8,128)(2,1)} %get-tuple-element.619.dv.gv, bf16[2,2176,256]{2,1,0:T(8,128)(2,1)S(1)} %copy-done.4, bf16[2,2176,256]{2,1,0:T(8,128)(2,1)} %collective-permute-done.21.k_other.v_other, ...), custom_call_target="tpu_custom_call" | custom-call | flops 1000000 | bytes 100000 | tf_op jit(solution)/shard_map/memory_back/pallas_call | solution.py:958
  384.4 3.2 collective-permute-done.54
  388.5 4.0 add_corners.7
  395.7 2.8 collective-permute-start.62
  400.4 5.9 %copy.63 = bf16[4,588,1024]{2,0,1:T(4,128)(2,1)} copy(bf16[4,588,1024]{2,1,0:T(8,128)(2,1)S(1)} %memory_back.1) | data formatting | bytes 9633792 | tf_op jit(solution)/shard_map/optimization_barrier | solution.py:275
  415.7 2.2 copy-done.7
  417.9 5.5 %fc2.1 = bf16[256,1024]{1,0:T(8,128)(2,1)} custom-call(s32[4]{0:T(128)S(1)} %pad_add_fusion.place, f32[256,1024]{1,0:T(8,128)S(1)} %copy-done.52, bf16[256,4096]{1,0:T(8,128)(2,1)S(1)} %copy-done.16, f32[13,1024]{1,0:T(8,128)S(1)} %reshape.468.vectors, bf16[2,4096,256]{2,1,0:T(8,128)(2,1)S(1)} %copy-done.7, bf16[2,4096,256]{2,1,0:T(8,128)(2,1)} %copy-done.116), custom_call_target="tpu_custom_call" | custom-call | flops 1000000 | bytes 100000 | tf_op jit(solution)/shard_map/fc2/pallas_call | solution.py:958
  423.4 6.2 %collective-permute-done.66 = bf16[4,6,128,256]{3,2,1,0:T(8,128)(2,1)} collective-permute-done((bf16[4,6,128,256]{3,2,1,0:T(8,128)(2,1)}, bf16[4,6,128,256]{3,2,1,0:T(8,128)(2,1)}, u32[]{:S(2)}, u32[]{:S(2)}) %collective-permute-start.66) | collective-permute-done | bytes 1572896 | tf_op jit(solution)/shard_map/ppermute | solution.py:310
  431.7 2.9 collective-permute-start.69
  437.2 2.6 collective-permute-done.68
  439.8 7.0 %collective-permute-done.70 = bf16[2,128,256]{2,1,0:T(8,128)(2,1)S(1)} collective-permute-done((bf16[2,128,256]{2,1,0:T(8,128)(2,1)S(1)}, bf16[2,128,256]{2,1,0:T(8,128)(2,1)S(1)}, u32[]{:S(2)}, u32[]{:S(2)}) %collective-permute-start.70) | collective-permute-done | bytes 131104 | tf_op jit(solution)/shard_map/ppermute | solution.py:310
  453.1 6.6 %collective-permute-done.72 = bf16[6,128,256]{2,1,0:T(8,128)(2,1)S(1)} collective-permute-done((bf16[6,128,256]{2,1,0:T(8,128)(2,1)S(1)}, bf16[6,128,256]{2,1,0:T(8,128)(2,1)S(1)}, u32[]{:S(2)}, u32[]{:S(2)}) %collective-permute-start.72) | collective-permute-done | bytes 393248 | tf_op jit(solution)/shard_map/ppermute | solution.py:310
  461.3 2.2 fusion.2
  463.5 2.1 fusion.3
  467.6 4.1 collective-permute-done.73
  (445 shorter events, 141.8 us)
Async XLA Ops:
  2.5 13.0 %collective-permute-start = (bf16[1,640,256]{2,1,0:T(8,128)(2,1)S(1)}, bf16[1,640,256]{2,1,0:T(8,128)(2,1)S(1)}, u32[]{:S(2)}, u32[]{:S(2)}) collective-permute-start(bf16[1,640,256]{2,1,0:T(8,128)(2,1)S(1)} %rearrange.12.refs_0_.refs_2_), channel_id=1, source_target_pairs={{0,8},{1,9},{2,10},{3,11},{4,12},{5,13},{6,14},{7,15},{8,16},{9,17... | collective-permute-start | bytes 983048 | tf_op jit(solution)/shard_map/ppermute | solution.py:310
  7.1 8.4 %collective-permute-start.1 = (bf16[1,16,256]{2,1,0:T(8,128)(2,1)S(1)}, bf16[1,16,256]{2,1,0:T(8,128)(2,1)S(1)}, u32[]{:S(2)}, u32[]{:S(2)}) collective-permute-start(bf16[1,16,256]{2,1,0:T(8,128)(2,1)S(1)} %dynamic_update_slice.4.refs_1_), channel_id=1, source_target_pairs={{0,8},{1,9},{2,10},{3,11},{4,12},{5,13},{6,14},{7,15},{8,16},{9,17... | collective-permute-start | bytes 24584 | tf_op jit(solution)/shard_map/ppermute | solution.py:310
  15.5 10.9 %collective-permute-start.2 = (bf16[1,640,256]{2,1,0:T(8,128)(2,1)S(1)}, bf16[1,640,256]{2,1,0:T(8,128)(2,1)S(1)}, u32[]{:S(2)}, u32[]{:S(2)}) collective-permute-start(bf16[1,640,256]{2,1,0:T(8,128)(2,1)S(1)} %collective-permute-done.refs_2_.refs_3_), channel_id=1, source_target_pairs={{0,8},{1,9},{2,10},{3,11},{4,12},{5,13},{6,14},{7,15},{8,16},{9,17... | collective-permute-start | bytes 983048 | tf_op jit(solution)/shard_map/ppermute | solution.py:310
  15.5 10.5 %collective-permute-start.5 = (bf16[1,256,256]{2,1,0:T(8,128)(2,1)S(1)}, bf16[1,256,256]{2,1,0:T(8,128)(2,1)S(1)}, u32[]{:S(2)}, u32[]{:S(2)}) collective-permute-start(bf16[1,256,256]{2,1,0:T(8,128)(2,1)S(1)} %get-tuple-element.370), channel_id=1, source_target_pairs={{0,2},{1,3},{2,0},{3,1},{4,6},{5,7},{6,4},{7,5},{8,10},{9,11},{10,... | collective-permute-start | bytes 393224 | tf_op jit(solution)/shard_map/ppermute | solution.py:310
  17.1 8.9 %collective-permute-start.4 = (bf16[1,256,256]{2,1,0:T(8,128)(2,1)S(1)}, bf16[1,256,256]{2,1,0:T(8,128)(2,1)S(1)}, u32[]{:S(2)}, u32[]{:S(2)}) collective-permute-start(bf16[1,256,256]{2,1,0:T(8,128)(2,1)S(1)} %get-tuple-element.396.refs_0_), channel_id=1, source_target_pairs={{0,4},{1,5},{2,6},{3,7},{4,0},{5,1},{6,2},{7,3},{8,12},{9,13},{10,... | collective-permute-start | bytes 393224 | tf_op jit(solution)/shard_map/ppermute | solution.py:310
  26.4 10.6 %collective-permute-start.6 = (bf16[1,640,256]{2,1,0:T(8,128)(2,1)S(1)}, bf16[1,640,256]{2,1,0:T(8,128)(2,1)S(1)}, u32[]{:S(2)}, u32[]{:S(2)}) collective-permute-start(bf16[1,640,256]{2,1,0:T(8,128)(2,1)S(1)} %collective-permute-done.2.refs_4_), channel_id=1, source_target_pairs={{0,8},{1,9},{2,10},{3,11},{4,12},{5,13},{6,14},{7,15},{8,16},{9,17... | collective-permute-start | bytes 983048 | tf_op jit(solution)/shard_map/ppermute | solution.py:310
  27.7 8.6 %collective-permute-start.9 = (bf16[1,128,256]{2,1,0:T(8,128)(2,1)S(1)}, bf16[1,128,256]{2,1,0:T(8,128)(2,1)S(1)}, u32[]{:S(2)}, u32[]{:S(2)}) collective-permute-start(bf16[1,128,256]{2,1,0:T(8,128)(2,1)S(1)} %get-tuple-element.378), channel_id=1, source_target_pairs={{0,2},{1,3},{2,0},{3,1},{4,6},{5,7},{6,4},{7,5},{8,10},{9,11},{10,... | collective-permute-start | bytes 196616 | tf_op jit(solution)/shard_map/ppermute | solution.py:310
  28.3 8.0 %collective-permute-start.8 = (bf16[1,128,256]{2,1,0:T(8,128)(2,1)S(1)}, bf16[1,128,256]{2,1,0:T(8,128)(2,1)S(1)}, u32[]{:S(2)}, u32[]{:S(2)}) collective-permute-start(bf16[1,128,256]{2,1,0:T(8,128)(2,1)S(1)} %get-tuple-element.376), channel_id=1, source_target_pairs={{0,4},{1,5},{2,6},{3,7},{4,0},{5,1},{6,2},{7,3},{8,12},{9,13},{10,... | collective-permute-start | bytes 196616 | tf_op jit(solution)/shard_map/ppermute | solution.py:310
  37.1 16.3 %collective-permute-start.12 = (bf16[4,272,256]{2,1,0:T(8,128)(2,1)S(1)}, bf16[4,272,256]{2,1,0:T(8,128)(2,1)S(1)}, u32[]{:S(2)}, u32[]{:S(2)}) collective-permute-start(bf16[4,272,256]{2,1,0:T(8,128)(2,1)S(1)} %get-tuple-element.426.refs_0_), channel_id=1, source_target_pairs={{0,4},{1,5},{2,6},{3,7},{4,0},{5,1},{6,2},{7,3},{8,12},{9,13},{10,... | collective-permute-start | bytes 1671176 | tf_op jit(solution)/shard_map/ppermute | solution.py:310
  38.1 15.2 %collective-permute-start.13 = (bf16[4,272,256]{2,1,0:T(8,128)(2,1)S(1)}, bf16[4,272,256]{2,1,0:T(8,128)(2,1)S(1)}, u32[]{:S(2)}, u32[]{:S(2)}) collective-permute-start(bf16[4,272,256]{2,1,0:T(8,128)(2,1)S(1)} %get-tuple-element.392), channel_id=1, source_target_pairs={{0,2},{1,3},{2,0},{3,1},{4,6},{5,7},{6,4},{7,5},{8,10},{9,11},{10,... | collective-permute-start | bytes 1671176 | tf_op jit(solution)/shard_map/ppermute | solution.py:310
  39.6 13.7 %collective-permute-start.10 = (bf16[1,768,256]{2,1,0:T(8,128)(2,1)S(1)}, bf16[1,768,256]{2,1,0:T(8,128)(2,1)S(1)}, u32[]{:S(2)}, u32[]{:S(2)}) collective-permute-start(bf16[1,768,256]{2,1,0:T(8,128)(2,1)S(1)} %get-tuple-element.473.refs_2_), channel_id=1, source_target_pairs={{0,8},{1,9},{2,10},{3,11},{4,12},{5,13},{6,14},{7,15},{8,16},{9,17... | collective-permute-start | bytes 1179656 | tf_op jit(solution)/shard_map/ppermute | solution.py:310
  39.6 13.7 %collective-permute-start.11 = (bf16[1,384,256]{2,1,0:T(8,128)(2,1)S(1)}, bf16[1,384,256]{2,1,0:T(8,128)(2,1)S(1)}, u32[]{:S(2)}, u32[]{:S(2)}) collective-permute-start(bf16[1,384,256]{2,1,0:T(8,128)(2,1)S(1)} %get-tuple-element.421.refs_2_), channel_id=1, source_target_pairs={{0,8},{1,9},{2,10},{3,11},{4,12},{5,13},{6,14},{7,15},{8,16},{9,17... | collective-permute-start | bytes 589832 | tf_op jit(solution)/shard_map/ppermute | solution.py:310
  55.0 21.7 %collective-permute-start.18 = (bf16[4,528,256]{2,1,0:T(8,128)(2,1)}, bf16[4,528,256]{2,1,0:T(8,128)(2,1)S(1)}, u32[]{:S(2)}, u32[]{:S(2)}) collective-permute-start(bf16[4,528,256]{2,1,0:T(8,128)(2,1)} %get-tuple-element.410), channel_id=1, source_target_pairs={{0,2},{1,3},{2,0},{3,1},{4,6},{5,7},{6,4},{7,5},{8,10},{9,11},{10,... | collective-permute-start | bytes 3244040 | tf_op jit(solution)/shard_map/ppermute | solution.py:310
  55.5 20.7 %collective-permute-start.17 = (bf16[4,512,256]{2,1,0:T(8,128)(2,1)}, bf16[4,512,256]{2,1,0:T(8,128)(2,1)S(1)}, u32[]{:S(2)}, u32[]{:S(2)}) collective-permute-start(bf16[4,512,256]{2,1,0:T(8,128)(2,1)} %get-tuple-element.451.refs_0_), channel_id=1, source_target_pairs={{0,4},{1,5},{2,6},{3,7},{4,0},{5,1},{6,2},{7,3},{8,12},{9,13},{10,... | collective-permute-start | bytes 3145736 | tf_op jit(solution)/shard_map/ppermute | solution.py:310
  56.7 9.6 %collective-permute-start.15 = (bf16[1,384,256]{2,1,0:T(8,128)(2,1)S(1)}, bf16[1,384,256]{2,1,0:T(8,128)(2,1)S(1)}, u32[]{:S(2)}, u32[]{:S(2)}) collective-permute-start(bf16[1,384,256]{2,1,0:T(8,128)(2,1)S(1)} %collective-permute-done.11.refs_3_), channel_id=1, source_target_pairs={{0,8},{1,9},{2,10},{3,11},{4,12},{5,13},{6,14},{7,15},{8,16},{9,17... | collective-permute-start | bytes 589832 | tf_op jit(solution)/shard_map/ppermute | solution.py:310
  56.7 14.6 %collective-permute-start.14 = (bf16[1,768,256]{2,1,0:T(8,128)(2,1)S(1)}, bf16[1,768,256]{2,1,0:T(8,128)(2,1)}, u32[]{:S(2)}, u32[]{:S(2)}) collective-permute-start(bf16[1,768,256]{2,1,0:T(8,128)(2,1)S(1)} %collective-permute-done.10.refs_3_), channel_id=1, source_target_pairs={{0,8},{1,9},{2,10},{3,11},{4,12},{5,13},{6,14},{7,15},{8,16},{9,17... | collective-permute-start | bytes 1179656 | tf_op jit(solution)/shard_map/ppermute | solution.py:310
  81.4 28.6 %collective-permute-start.22 = (bf16[4,576,256]{2,1,0:T(8,128)(2,1)}, bf16[4,576,256]{2,1,0:T(8,128)(2,1)S(1)}, u32[]{:S(2)}, u32[]{:S(2)}) collective-permute-start(bf16[4,576,256]{2,1,0:T(8,128)(2,1)} %get-tuple-element.478.refs_0_), channel_id=1, source_target_pairs={{0,4},{1,5},{2,6},{3,7},{4,0},{5,1},{6,2},{7,3},{8,12},{9,13},{10,... | collective-permute-start | bytes 3538952 | tf_op jit(solution)/shard_map/ppermute | solution.py:310
  82.5 28.4 %collective-permute-start.23 = (bf16[4,576,256]{2,1,0:T(8,128)(2,1)}, bf16[4,576,256]{2,1,0:T(8,128)(2,1)}, u32[]{:S(2)}, u32[]{:S(2)}) collective-permute-start(bf16[4,576,256]{2,1,0:T(8,128)(2,1)} %get-tuple-element.437), channel_id=1, source_target_pairs={{0,2},{1,3},{2,0},{3,1},{4,6},{5,7},{6,4},{7,5},{8,10},{9,11},{10,... | collective-permute-start | bytes 3538952 | tf_op jit(solution)/shard_map/ppermute | solution.py:310
  83.5 24.3 %collective-permute-start.20 = (bf16[4,256,256]{2,1,0:T(8,128)(2,1)}, bf16[4,256,256]{2,1,0:T(8,128)(2,1)}, u32[]{:S(2)}, u32[]{:S(2)}) collective-permute-start(bf16[4,256,256]{2,1,0:T(8,128)(2,1)} %rearrange.16.refs_5_), channel_id=1, source_target_pairs={{0,8},{1,9},{2,10},{3,11},{4,12},{5,13},{6,14},{7,15},{8,16},{9,17... | collective-permute-start | bytes 1572872 | tf_op jit(solution)/shard_map/ppermute | solution.py:310
  83.5 24.3 %collective-permute-start.19 = (bf16[1,768,256]{2,1,0:T(8,128)(2,1)}, bf16[1,768,256]{2,1,0:T(8,128)(2,1)}, u32[]{:S(2)}, u32[]{:S(2)}) collective-permute-start(bf16[1,768,256]{2,1,0:T(8,128)(2,1)} %collective-permute-done.14.refs_4_), channel_id=1, source_target_pairs={{0,8},{1,9},{2,10},{3,11},{4,12},{5,13},{6,14},{7,15},{8,16},{9,17... | collective-permute-start | bytes 1179656 | tf_op jit(solution)/shard_map/ppermute | solution.py:310
  118.4 34.3 %collective-permute-start.26 = (bf16[4,704,256]{2,1,0:T(8,128)(2,1)}, bf16[4,704,256]{2,1,0:T(8,128)(2,1)}, u32[]{:S(2)}, u32[]{:S(2)}) collective-permute-start(bf16[4,704,256]{2,1,0:T(8,128)(2,1)} %get-tuple-element.500.refs_0_), channel_id=1, source_target_pairs={{0,4},{1,5},{2,6},{3,7},{4,0},{5,1},{6,2},{7,3},{8,12},{9,13},{10,... | collective-permute-start | bytes 4325384 | tf_op jit(solution)/shard_map/ppermute | solution.py:310
  119.4 34.0 %collective-permute-start.27 = (bf16[4,704,256]{2,1,0:T(8,128)(2,1)}, bf16[4,704,256]{2,1,0:T(8,128)(2,1)}, u32[]{:S(2)}, u32[]{:S(2)}) collective-permute-start(bf16[4,704,256]{2,1,0:T(8,128)(2,1)} %get-tuple-element.464), channel_id=1, source_target_pairs={{0,2},{1,3},{2,0},{3,1},{4,6},{5,7},{6,4},{7,5},{8,10},{9,11},{10,... | collective-permute-start | bytes 4325384 | tf_op jit(solution)/shard_map/ppermute | solution.py:310
  120.5 16.0 %collective-permute-start.25 = (bf16[4,256,256]{2,1,0:T(8,128)(2,1)}, bf16[4,256,256]{2,1,0:T(8,128)(2,1)}, u32[]{:S(2)}, u32[]{:S(2)}) collective-permute-start(bf16[4,256,256]{2,1,0:T(8,128)(2,1)} %collective-permute-done.20.refs_6_), channel_id=1, source_target_pairs={{0,8},{1,9},{2,10},{3,11},{4,12},{5,13},{6,14},{7,15},{8,16},{9,17... | collective-permute-start | bytes 1572872 | tf_op jit(solution)/shard_map/ppermute | solution.py:310
  161.4 27.3 %collective-permute-start.30 = (bf16[4,512,256]{2,1,0:T(8,128)(2,1)}, bf16[4,512,256]{2,1,0:T(8,128)(2,1)}, u32[]{:S(2)}, u32[]{:S(2)}) collective-permute-start(bf16[4,512,256]{2,1,0:T(8,128)(2,1)} %get-tuple-element.528.refs_0_), channel_id=1, source_target_pairs={{0,4},{1,5},{2,6},{3,7},{4,0},{5,1},{6,2},{7,3},{8,12},{9,13},{10,... | collective-permute-start | bytes 3145736 | tf_op jit(solution)/shard_map/ppermute | solution.py:310
  162.5 26.3 %collective-permute-start.31 = (bf16[4,512,256]{2,1,0:T(8,128)(2,1)}, bf16[4,512,256]{2,1,0:T(8,128)(2,1)}, u32[]{:S(2)}, u32[]{:S(2)}) collective-permute-start(bf16[4,512,256]{2,1,0:T(8,128)(2,1)} %get-tuple-element.491), channel_id=1, source_target_pairs={{0,2},{1,3},{2,0},{3,1},{4,6},{5,7},{6,4},{7,5},{8,10},{9,11},{10,... | collective-permute-start | bytes 3145736 | tf_op jit(solution)/shard_map/ppermute | solution.py:310
  163.5 25.3 %collective-permute-start.29 = (bf16[4,256,256]{2,1,0:T(8,128)(2,1)}, bf16[4,256,256]{2,1,0:T(8,128)(2,1)}, u32[]{:S(2)}, u32[]{:S(2)}) collective-permute-start(bf16[4,256,256]{2,1,0:T(8,128)(2,1)} %collective-permute-done.25.refs_7_), channel_id=1, source_target_pairs={{0,8},{1,9},{2,10},{3,11},{4,12},{5,13},{6,14},{7,15},{8,16},{9,17... | collective-permute-start | bytes 1572872 | tf_op jit(solution)/shard_map/ppermute | solution.py:310
  192.1 8.6 %collective-permute-start.32 = (bf16[2,4096,256]{2,1,0:T(8,128)(2,1)S(1)}, bf16[2,4096,256]{2,1,0:T(8,128)(2,1)S(1)}, u32[]{:S(2)}, u32[]{:S(2)}) collective-permute-start(bf16[2,4096,256]{2,1,0:T(8,128)(2,1)S(1)} %half_weights.8.own), channel_id=1, source_target_pairs={{0,1},{1,0},{2,3},{3,2},{4,5},{5,4},{6,7},{7,6},{8,9},{9,8},{10,11... | collective-permute-start | bytes 12582920 | tf_op jit(solution)/shard_map/ppermute | solution.py:310
  195.4 10.2 %collective-permute-start.34 = (bf16[4,128,256]{2,1,0:T(8,128)(2,1)S(1)}, bf16[4,128,256]{2,1,0:T(8,128)(2,1)S(1)}, u32[]{:S(2)}, u32[]{:S(2)}) collective-permute-start(bf16[4,128,256]{2,1,0:T(8,128)(2,1)S(1)} %get-tuple-element.512), channel_id=1, source_target_pairs={{0,2},{1,3},{2,0},{3,1},{4,6},{5,7},{6,4},{7,5},{8,10},{9,11},{10,... | collective-permute-start | bytes 786440 | tf_op jit(solution)/shard_map/ppermute | solution.py:310
  196.5 9.1 %collective-permute-start.33 = (bf16[4,128,256]{2,1,0:T(8,128)(2,1)S(1)}, bf16[4,128,256]{2,1,0:T(8,128)(2,1)S(1)}, u32[]{:S(2)}, u32[]{:S(2)}) collective-permute-start(bf16[4,128,256]{2,1,0:T(8,128)(2,1)S(1)} %get-tuple-element.510), channel_id=1, source_target_pairs={{0,4},{1,5},{2,6},{3,7},{4,0},{5,1},{6,2},{7,3},{8,12},{9,13},{10,... | collective-permute-start | bytes 786440 | tf_op jit(solution)/shard_map/ppermute | solution.py:310
  211.4 14.3 %collective-permute-start.36 = (bf16[2,4096,256]{2,1,0:T(8,128)(2,1)S(1)}, bf16[2,4096,256]{2,1,0:T(8,128)(2,1)S(1)}, u32[]{:S(2)}, u32[]{:S(2)}) collective-permute-start(bf16[2,4096,256]{2,1,0:T(8,128)(2,1)S(1)} %half_weights.9.own), channel_id=1, source_target_pairs={{0,1},{1,0},{2,3},{3,2},{4,5},{5,4},{6,7},{7,6},{8,9},{9,8},{10,11... | collective-permute-start | bytes 12582920 | tf_op jit(solution)/shard_map/ppermute | solution.py:310
  223.7 14.2 %collective-permute-start.37 = (bf16[4,1,256,256]{3,2,1,0:T(8,128)(2,1)}, bf16[4,1,256,256]{3,2,1,0:T(8,128)(2,1)S(1)}, u32[]{:S(2)}, u32[]{:S(2)}) collective-permute-start(bf16[4,1,256,256]{3,2,1,0:T(8,128)(2,1)} %get-tuple-element.540), channel_id=1, source_target_pairs={{0,4},{1,5},{2,6},{3,7},{4,0},{5,1},{6,2},{7,3},{8,12},{9,13},{10,... | collective-permute-start | bytes 1572872 | tf_op jit(solution)/shard_map/ppermute | solution.py:310
  224.8 14.0 %collective-permute-start.38 = (bf16[4,1,256,256]{3,2,1,0:T(8,128)(2,1)}, bf16[4,1,256,256]{3,2,1,0:T(8,128)(2,1)}, u32[]{:S(2)}, u32[]{:S(2)}) collective-permute-start(bf16[4,1,256,256]{3,2,1,0:T(8,128)(2,1)} %get-tuple-element.542), channel_id=1, source_target_pairs={{0,2},{1,3},{2,0},{3,1},{4,6},{5,7},{6,4},{7,5},{8,10},{9,11},{10,... | collective-permute-start | bytes 1572872 | tf_op jit(solution)/shard_map/ppermute | solution.py:310
  238.8 14.7 %collective-permute-start.39 = (bf16[1,2,1024,1024]{3,2,1,0:T(8,128)(2,1)S(1)}, bf16[1,2,1024,1024]{3,2,1,0:T(8,128)(2,1)}, u32[]{:S(2)}, u32[]{:S(2)}) collective-permute-start(bf16[1,2,1024,1024]{3,2,1,0:T(8,128)(2,1)S(1)} %get-tuple-element.550), channel_id=1, source_target_pairs={{0,1},{1,0},{2,3},{3,2},{4,5},{5,4},{6,7},{7,6},{8,9},{9,8},{10,11... | collective-permute-start | bytes 12582920 | tf_op jit(solution)/shard_map/ppermute | solution.py:310
  242.3 52.1 %collective-permute-start.40 = (bf16[4,1,512,256]{3,2,1,0:T(8,128)(2,1)}, bf16[4,1,512,256]{3,2,1,0:T(8,128)(2,1)}, u32[]{:S(2)}, u32[]{:S(2)}) collective-permute-start(bf16[4,1,512,256]{3,2,1,0:T(8,128)(2,1)} %get-tuple-element.559), channel_id=1, source_target_pairs={{0,4},{1,5},{2,6},{3,7},{4,0},{5,1},{6,2},{7,3},{8,12},{9,13},{10,... | collective-permute-start | bytes 3145736 | tf_op jit(solution)/shard_map/ppermute | solution.py:310
  243.2 51.2 %collective-permute-start.41 = (bf16[4,1,512,256]{3,2,1,0:T(8,128)(2,1)}, bf16[4,1,512,256]{3,2,1,0:T(8,128)(2,1)}, u32[]{:S(2)}, u32[]{:S(2)}) collective-permute-start(bf16[4,1,512,256]{3,2,1,0:T(8,128)(2,1)} %get-tuple-element.561), channel_id=1, source_target_pairs={{0,2},{1,3},{2,0},{3,1},{4,6},{5,7},{6,4},{7,5},{8,10},{9,11},{10,... | collective-permute-start | bytes 3145736 | tf_op jit(solution)/shard_map/ppermute | solution.py:310
  259.6 34.8 %collective-permute-start.42 = (bf16[4,1,64,1024]{3,2,1,0:T(8,128)(2,1)S(1)}, bf16[4,1,64,1024]{3,2,1,0:T(8,128)(2,1)S(1)}, u32[]{:S(2)}, u32[]{:S(2)}) collective-permute-start(bf16[4,1,64,1024]{3,2,1,0:T(8,128)(2,1)S(1)} %get-tuple-element.562), channel_id=1, source_target_pairs={{0,4},{1,5},{2,6},{3,7},{4,0},{5,1},{6,2},{7,3},{8,12},{9,13},{10,... | collective-permute-start | bytes 1572872 | tf_op jit(solution)/shard_map/ppermute | solution.py:310
  260.5 33.9 %collective-permute-start.43 = (bf16[4,1,64,1024]{3,2,1,0:T(8,128)(2,1)S(1)}, bf16[4,1,64,1024]{3,2,1,0:T(8,128)(2,1)S(1)}, u32[]{:S(2)}, u32[]{:S(2)}) collective-permute-start(bf16[4,1,64,1024]{3,2,1,0:T(8,128)(2,1)S(1)} %get-tuple-element.564), channel_id=1, source_target_pairs={{0,2},{1,3},{2,0},{3,1},{4,6},{5,7},{6,4},{7,5},{8,10},{9,11},{10,... | collective-permute-start | bytes 1572872 | tf_op jit(solution)/shard_map/ppermute | solution.py:310
  294.4 20.9 %collective-permute-start.44 = (bf16[2,2,1024,256]{3,2,1,0:T(8,128)(2,1)}, bf16[2,2,1024,256]{3,2,1,0:T(8,128)(2,1)}, u32[]{:S(2)}, u32[]{:S(2)}) collective-permute-start(bf16[2,2,1024,256]{3,2,1,0:T(8,128)(2,1)} %memory_terms.2), channel_id=1, source_target_pairs={{0,1},{1,0},{2,3},{3,2},{4,5},{5,4},{6,7},{7,6},{8,9},{9,8},{10,11... | collective-permute-start | bytes 6291464 | tf_op jit(solution)/shard_map/ppermute | solution.py:310
  296.4 36.4 %collective-permute-start.46 = (bf16[4,1,128,1024]{3,2,1,0:T(8,128)(2,1)}, bf16[4,1,128,1024]{3,2,1,0:T(8,128)(2,1)}, u32[]{:S(2)}, u32[]{:S(2)}) collective-permute-start(bf16[4,1,128,1024]{3,2,1,0:T(8,128)(2,1)} %get-tuple-element.588), channel_id=1, source_target_pairs={{0,4},{1,5},{2,6},{3,7},{4,0},{5,1},{6,2},{7,3},{8,12},{9,13},{10,... | collective-permute-start | bytes 3145736 | tf_op jit(solution)/shard_map/ppermute | solution.py:310
  297.4 35.4 %collective-permute-start.47 = (bf16[4,1,128,1024]{3,2,1,0:T(8,128)(2,1)}, bf16[4,1,128,1024]{3,2,1,0:T(8,128)(2,1)}, u32[]{:S(2)}, u32[]{:S(2)}) collective-permute-start(bf16[4,1,128,1024]{3,2,1,0:T(8,128)(2,1)} %get-tuple-element.590), channel_id=1, source_target_pairs={{0,2},{1,3},{2,0},{3,1},{4,6},{5,7},{6,4},{7,5},{8,10},{9,11},{10,... | collective-permute-start | bytes 3145736 | tf_op jit(solution)/shard_map/ppermute | solution.py:310
  299.7 32.3 %collective-permute-start.45 = (bf16[1,512,256]{2,1,0:T(8,128)(2,1)S(1)}, bf16[1,512,256]{2,1,0:T(8,128)(2,1)S(1)}, u32[]{:S(2)}, u32[]{:S(2)}) collective-permute-start(bf16[1,512,256]{2,1,0:T(8,128)(2,1)S(1)} %fusion.9), channel_id=1, source_target_pairs={{0,8},{1,9},{2,10},{3,11},{4,12},{5,13},{6,14},{7,15},{8,16},{9,17... | collective-permute-start | bytes 786440 | tf_op jit(solution)/shard_map/ppermute | solution.py:310
  332.8 14.4 %collective-permute-start.48 = (bf16[6,2,1024,256]{3,2,1,0:T(8,128)(2,1)}, bf16[6,2,1024,256]{3,2,1,0:T(8,128)(2,1)}, u32[]{:S(2)}, u32[]{:S(2)}) collective-permute-start(bf16[6,2,1024,256]{3,2,1,0:T(8,128)(2,1)} %weight_terms.8), channel_id=1, source_target_pairs={{0,1},{1,0},{2,3},{3,2},{4,5},{5,4},{6,7},{7,6},{8,9},{9,8},{10,11... | collective-permute-start | bytes 18874376 | tf_op jit(solution)/shard_map/ppermute | solution.py:310
  335.7 21.4 %collective-permute-start.50 = (bf16[1,128,1024]{2,1,0:T(8,128)(2,1)S(1)}, bf16[1,128,1024]{2,1,0:T(8,128)(2,1)S(1)}, u32[]{:S(2)}, u32[]{:S(2)}) collective-permute-start(bf16[1,128,1024]{2,1,0:T(8,128)(2,1)S(1)} %fusion.10), channel_id=1, source_target_pairs={{0,8},{1,9},{2,10},{3,11},{4,12},{5,13},{6,14},{7,15},{8,16},{9,17... | collective-permute-start | bytes 786440 | tf_op jit(solution)/shard_map/ppermute | solution.py:310
  336.1 21.0 %collective-permute-start.49 = (bf16[1,512,256]{2,1,0:T(8,128)(2,1)S(1)}, bf16[1,512,256]{2,1,0:T(8,128)(2,1)S(1)}, u32[]{:S(2)}, u32[]{:S(2)}) collective-permute-start(bf16[1,512,256]{2,1,0:T(8,128)(2,1)S(1)} %fusion.7), channel_id=1, source_target_pairs={{0,8},{1,9},{2,10},{3,11},{4,12},{5,13},{6,14},{7,15},{8,16},{9,17... | collective-permute-start | bytes 786440 | tf_op jit(solution)/shard_map/ppermute | solution.py:310
  337.8 19.3 %collective-permute-start.51 = (bf16[4,2,64,256]{3,2,1,0:T(8,128)(2,1)S(1)}, bf16[4,2,64,256]{3,2,1,0:T(8,128)(2,1)S(1)}, u32[]{:S(2)}, u32[]{:S(2)}) collective-permute-start(bf16[4,2,64,256]{3,2,1,0:T(8,128)(2,1)S(1)} %copy-done.115), channel_id=1, source_target_pairs={{0,4},{1,5},{2,6},{3,7},{4,0},{5,1},{6,2},{7,3},{8,12},{9,13},{10,... | collective-permute-start | bytes 786440 | tf_op jit(solution)/shard_map/ppermute | solution.py:310
  338.9 18.2 %collective-permute-start.52 = (bf16[4,2,64,256]{3,2,1,0:T(8,128)(2,1)}, bf16[4,2,64,256]{3,2,1,0:T(8,128)(2,1)S(1)}, u32[]{:S(2)}, u32[]{:S(2)}) collective-permute-start(bf16[4,2,64,256]{3,2,1,0:T(8,128)(2,1)} %copy-done.113), channel_id=1, source_target_pairs={{0,2},{1,3},{2,0},{3,1},{4,6},{5,7},{6,4},{7,5},{8,10},{9,11},{10,... | collective-permute-start | bytes 786440 | tf_op jit(solution)/shard_map/ppermute | solution.py:310
  357.1 31.3 %collective-permute-start.56 = (bf16[4,6,64,256]{3,2,1,0:T(8,128)(2,1)}, bf16[4,6,64,256]{3,2,1,0:T(8,128)(2,1)S(1)}, u32[]{:S(2)}, u32[]{:S(2)}) collective-permute-start(bf16[4,6,64,256]{3,2,1,0:T(8,128)(2,1)} %get-tuple-element.628), channel_id=1, source_target_pairs={{0,4},{1,5},{2,6},{3,7},{4,0},{5,1},{6,2},{7,3},{8,12},{9,13},{10,... | collective-permute-start | bytes 2359304 | tf_op jit(solution)/shard_map/ppermute | solution.py:310
  358.3 30.1 %collective-permute-start.57 = (bf16[4,6,64,256]{3,2,1,0:T(8,128)(2,1)}, bf16[4,6,64,256]{3,2,1,0:T(8,128)(2,1)}, u32[]{:S(2)}, u32[]{:S(2)}) collective-permute-start(bf16[4,6,64,256]{3,2,1,0:T(8,128)(2,1)} %get-tuple-element.630), channel_id=1, source_target_pairs={{0,2},{1,3},{2,0},{3,1},{4,6},{5,7},{6,4},{7,5},{8,10},{9,11},{10,... | collective-permute-start | bytes 2359304 | tf_op jit(solution)/shard_map/ppermute | solution.py:310
  360.8 26.8 %collective-permute-start.54 = (bf16[4,2,128,256]{3,2,1,0:T(8,128)(2,1)}, bf16[4,2,128,256]{3,2,1,0:T(8,128)(2,1)}, u32[]{:S(2)}, u32[]{:S(2)}) collective-permute-start(bf16[4,2,128,256]{3,2,1,0:T(8,128)(2,1)} %get-tuple-element.625), channel_id=1, source_target_pairs={{0,4},{1,5},{2,6},{3,7},{4,0},{5,1},{6,2},{7,3},{8,12},{9,13},{10,... | collective-permute-start | bytes 1572872 | tf_op jit(solution)/shard_map/ppermute | solution.py:310
  361.9 26.5 %collective-permute-start.55 = (bf16[4,2,128,256]{3,2,1,0:T(8,128)(2,1)}, bf16[4,2,128,256]{3,2,1,0:T(8,128)(2,1)}, u32[]{:S(2)}, u32[]{:S(2)}) collective-permute-start(bf16[4,2,128,256]{3,2,1,0:T(8,128)(2,1)} %get-tuple-element.627), channel_id=1, source_target_pairs={{0,2},{1,3},{2,0},{3,1},{4,6},{5,7},{6,4},{7,5},{8,10},{9,11},{10,... | collective-permute-start | bytes 1572872 | tf_op jit(solution)/shard_map/ppermute | solution.py:310
  364.9 19.5 %collective-permute-start.53 = (bf16[1,512,256]{2,1,0:T(8,128)(2,1)}, bf16[1,512,256]{2,1,0:T(8,128)(2,1)}, u32[]{:S(2)}, u32[]{:S(2)}) collective-permute-start(bf16[1,512,256]{2,1,0:T(8,128)(2,1)} %fusion.6), channel_id=1, source_target_pairs={{0,8},{1,9},{2,10},{3,11},{4,12},{5,13},{6,14},{7,15},{8,16},{9,17... | collective-permute-start | bytes 786440 | tf_op jit(solution)/shard_map/ppermute | solution.py:310
  392.5 37.1 %collective-permute-start.66 = (bf16[4,6,128,256]{3,2,1,0:T(8,128)(2,1)}, bf16[4,6,128,256]{3,2,1,0:T(8,128)(2,1)}, u32[]{:S(2)}, u32[]{:S(2)}) collective-permute-start(bf16[4,6,128,256]{3,2,1,0:T(8,128)(2,1)} %get-tuple-element.674), channel_id=1, source_target_pairs={{0,4},{1,5},{2,6},{3,7},{4,0},{5,1},{6,2},{7,3},{8,12},{9,13},{10,... | collective-permute-start | bytes 4718600 | tf_op jit(solution)/shard_map/ppermute | solution.py:310
  393.4 36.8 %collective-permute-start.67 = (bf16[4,6,128,256]{3,2,1,0:T(8,128)(2,1)}, bf16[4,6,128,256]{3,2,1,0:T(8,128)(2,1)}, u32[]{:S(2)}, u32[]{:S(2)}) collective-permute-start(bf16[4,6,128,256]{3,2,1,0:T(8,128)(2,1)} %get-tuple-element.676), channel_id=1, source_target_pairs={{0,2},{1,3},{2,0},{3,1},{4,6},{5,7},{6,4},{7,5},{8,10},{9,11},{10,... | collective-permute-start | bytes 4718600 | tf_op jit(solution)/shard_map/ppermute | solution.py:310
  395.7 13.0 %collective-permute-start.62 = (bf16[1,128,1024]{2,1,0:T(8,128)(2,1)S(1)}, bf16[1,128,1024]{2,1,0:T(8,128)(2,1)S(1)}, u32[]{:S(2)}, u32[]{:S(2)}) collective-permute-start(bf16[1,128,1024]{2,1,0:T(8,128)(2,1)S(1)} %fusion.4), channel_id=1, source_target_pairs={{0,8},{1,9},{2,10},{3,11},{4,12},{5,13},{6,14},{7,15},{8,16},{9,17... | collective-permute-start | bytes 786440 | tf_op jit(solution)/shard_map/ppermute | solution.py:310
  398.6 8.4 %collective-permute-start.59 = (f32[2,2,544]{2,1,0:T(2,128)S(1)}, f32[2,2,544]{2,1,0:T(2,128)S(1)}, u32[]{:S(2)}, u32[]{:S(2)}) collective-permute-start(f32[2,2,544]{2,1,0:T(2,128)S(1)} %fusion.25), channel_id=1, source_target_pairs={{0,8},{1,9},{2,10},{3,11},{4,12},{5,13},{6,14},{7,15},{8,16},{9,17... | collective-permute-start | bytes 26120 | tf_op jit(solution)/shard_map/ppermute | solution.py:310
  400.0 8.7 %collective-permute-start.64 = (bf16[2,128,256]{2,1,0:T(8,128)(2,1)S(1)}, bf16[2,128,256]{2,1,0:T(8,128)(2,1)S(1)}, u32[]{:S(2)}, u32[]{:S(2)}) collective-permute-start(bf16[2,128,256]{2,1,0:T(8,128)(2,1)S(1)} %fusion.13), channel_id=1, source_target_pairs={{0,8},{1,9},{2,10},{3,11},{4,12},{5,13},{6,14},{7,15},{8,16},{9,17... | collective-permute-start | bytes 393224 | tf_op jit(solution)/shard_map/ppermute | solution.py:310
  407.0 7.9 %collective-permute-start.60 = (f32[2,2,544]{2,1,0:T(2,128)S(1)}, f32[2,2,544]{2,1,0:T(2,128)S(1)}, u32[]{:S(2)}, u32[]{:S(2)}) collective-permute-start(f32[2,2,544]{2,1,0:T(2,128)S(1)} %fusion.24), channel_id=1, source_target_pairs={{0,8},{1,9},{2,10},{3,11},{4,12},{5,13},{6,14},{7,15},{8,16},{9,17... | collective-permute-start | bytes 26120 | tf_op jit(solution)/shard_map/ppermute | solution.py:310
  410.6 12.7 %collective-permute-start.63 = (bf16[1,128,1024]{2,1,0:T(8,128)(2,1)}, bf16[1,128,1024]{2,1,0:T(8,128)(2,1)S(1)}, u32[]{:S(2)}, u32[]{:S(2)}) collective-permute-start(bf16[1,128,1024]{2,1,0:T(8,128)(2,1)} %fusion.5), channel_id=1, source_target_pairs={{0,8},{1,9},{2,10},{3,11},{4,12},{5,13},{6,14},{7,15},{8,16},{9,17... | collective-permute-start | bytes 786440 | tf_op jit(solution)/shard_map/ppermute | solution.py:310
  414.4 9.0 %collective-permute-start.65 = (bf16[2,128,256]{2,1,0:T(8,128)(2,1)}, bf16[2,128,256]{2,1,0:T(8,128)(2,1)}, u32[]{:S(2)}, u32[]{:S(2)}) collective-permute-start(bf16[2,128,256]{2,1,0:T(8,128)(2,1)} %fusion.12), channel_id=1, source_target_pairs={{0,8},{1,9},{2,10},{3,11},{4,12},{5,13},{6,14},{7,15},{8,16},{9,17... | collective-permute-start | bytes 393224 | tf_op jit(solution)/shard_map/ppermute | solution.py:310
  414.9 8.5 %collective-permute-start.61 = (f32[2,2,544]{2,1,0:T(2,128)S(1)}, f32[2,2,544]{2,1,0:T(2,128)S(1)}, u32[]{:S(2)}, u32[]{:S(2)}) collective-permute-start(f32[2,2,544]{2,1,0:T(2,128)S(1)} %fusion.22), channel_id=1, source_target_pairs={{0,8},{1,9},{2,10},{3,11},{4,12},{5,13},{6,14},{7,15},{8,16},{9,17... | collective-permute-start | bytes 26120 | tf_op jit(solution)/shard_map/ppermute | solution.py:310
  431.7 15.1 %collective-permute-start.69 = (bf16[6,128,256]{2,1,0:T(8,128)(2,1)S(1)}, bf16[6,128,256]{2,1,0:T(8,128)(2,1)S(1)}, u32[]{:S(2)}, u32[]{:S(2)}) collective-permute-start(bf16[6,128,256]{2,1,0:T(8,128)(2,1)S(1)} %fusion.8), channel_id=1, source_target_pairs={{0,8},{1,9},{2,10},{3,11},{4,12},{5,13},{6,14},{7,15},{8,16},{9,17... | collective-permute-start | bytes 1179656 | tf_op jit(solution)/shard_map/ppermute | solution.py:310
  435.7 11.1 %collective-permute-start.70 = (bf16[2,128,256]{2,1,0:T(8,128)(2,1)S(1)}, bf16[2,128,256]{2,1,0:T(8,128)(2,1)S(1)}, u32[]{:S(2)}, u32[]{:S(2)}) collective-permute-start(bf16[2,128,256]{2,1,0:T(8,128)(2,1)S(1)} %fusion.11), channel_id=1, source_target_pairs={{0,8},{1,9},{2,10},{3,11},{4,12},{5,13},{6,14},{7,15},{8,16},{9,17... | collective-permute-start | bytes 393224 | tf_op jit(solution)/shard_map/ppermute | solution.py:310
  448.3 11.4 %collective-permute-start.72 = (bf16[6,128,256]{2,1,0:T(8,128)(2,1)S(1)}, bf16[6,128,256]{2,1,0:T(8,128)(2,1)S(1)}, u32[]{:S(2)}, u32[]{:S(2)}) collective-permute-start(bf16[6,128,256]{2,1,0:T(8,128)(2,1)S(1)} %fusion.1), channel_id=1, source_target_pairs={{0,8},{1,9},{2,10},{3,11},{4,12},{5,13},{6,14},{7,15},{8,16},{9,17... | collective-permute-start | bytes 1179656 | tf_op jit(solution)/shard_map/ppermute | solution.py:310
  461.2 10.4 %collective-permute-start.73 = (bf16[6,128,256]{2,1,0:T(8,128)(2,1)S(1)}, bf16[6,128,256]{2,1,0:T(8,128)(2,1)S(1)}, u32[]{:S(2)}, u32[]{:S(2)}) collective-permute-start(bf16[6,128,256]{2,1,0:T(8,128)(2,1)S(1)} %fusion), channel_id=1, source_target_pairs={{0,8},{1,9},{2,10},{3,11},{4,12},{5,13},{6,14},{7,15},{8,16},{9,17... | collective-permute-start | bytes 1179656 | tf_op jit(solution)/shard_map/ppermute | solution.py:310
  (139 other events, 970.3 us)

commit v8 on v7

--- a/solution.py
+++ b/solution.py
@@ -25,7 +25,7 @@
 CHEAP = pl.CostEstimate(flops=10**6, bytes_accessed=10**5, transcendentals=0)
 BIG_VMEM = pltpu.CompilerParams(vmem_limit_bytes=VMEM)
 SMALL_VMEM = pltpu.CompilerParams(vmem_limit_bytes=16 * 2**20)
-FULL_VMEM = pltpu.CompilerParams(vmem_limit_bytes=44 * 2**20)
+FULL_VMEM = pltpu.CompilerParams(vmem_limit_bytes=39 * 2**20)
 
 
 def dot_nt(a, b):

time: 483 us -> 481 us (level)
  Pallas kernels: 198 us -> 190 us
  local copies, waits for them, and re-layouts: 72.1 us -> 77.3 us
    unnamed x260 -> x272, local copies, waits for them, and re-layouts: 52.8 us -> 58.1 us
  transfers between devices with their start and end apart: 74 -> 74, of which waited for: 32 -> 30; matrix products, arithmetic and copies ran while one was open for 8% -> 8% of each run, Pallas kernels for 36% -> 34%
where the time goes in v8:
time: 481 us; the launch traced here: 472 us
  Pallas kernels  190 us (40%)
  waiting for transfers between devices  109 us (23%)
  local copies, waits for them, and re-layouts  77.3 us (16%)
  starting transfers between devices  63.5 us (13%)
  other arithmetic  29.3 us (6%)
    ppermute x74, waiting for transfers between devices, send(): return lax.ppermute(self.clock.now(array), AXES, self.perms[name])  109 us
    pallas_call x11, Pallas kernels, dense_call(): pl.pallas_call(kernel, grid_spec=pltpu.PrefetchScalarGridSpec(num_scalar_...  77.1 us
    ppermute x74, starting transfers between devices, send(): return lax.ppermute(self.clock.now(array), AXES, self.perms[name])  63.5 us
    unnamed x272, local copies, waits for them, and re-layouts  58.1 us
    pallas_call x2, Pallas kernels, memory_terms(): pl.pallas_call(functools.partial(memory_terms_kernel, near, len(pairs)),...  22.6 us
    pallas_call x5, Pallas kernels, token_terms(): pl.pallas_call(kernel, grid_spec=pltpu.PrefetchScalarGridSpec(num_scalar_...  21.6 us
    convert_element_type x12, other arithmetic, step(): self.came = self.grid.send('z', total.astype(BF16))  19.7 us
    pallas_call x1, Pallas kernels, cross_backward(): pl.pallas_call(cross_bwd_kernel, grid_spec=pltpu.PrefetchScalarGridSpec(n...  18.2 us
  transfers between devices with their start and end apart: 74, of which 30 were waited for; matrix products, arithmetic and copies ran while one was open for 8% of the time, Pallas kernels for 34%

profile of v8, /device:TPU:0, one launch (start us, length us, event | category | flops | bytes accessed | tf_op | source)
XLA Modules:
  0.0 472.3 jit_solution(5752576811910389146)
XLA Ops:
  2.5 3.1 collective-permute-start
  13.2 2.3 collective-permute-done.1.refs_3_
  19.9 3.9 copy.44._
  23.9 2.3 copy-done
  31.0 5.3 %collective-permute-done.7.refs_7_ = bf16[1,16,256]{2,1,0:T(8,128)(2,1)S(1)} collective-permute-done((bf16[1,16,256]{2,1,0:T(8,128)(2,1)S(1)}, bf16[1,16,256]{2,1,0:T(8,128)(2,1)S(1)}, u32[]{:S(2)}, u32[]{:S(2)}) %collective-permute-start.7) | collective-permute-done | bytes 8224 | tf_op jit(solution)/shard_map/ppermute | solution.py:310
  39.7 13.6 %collective-permute-done.11.refs_3_ = bf16[1,384,256]{2,1,0:T(8,128)(2,1)S(1)} collective-permute-done((bf16[1,384,256]{2,1,0:T(8,128)(2,1)S(1)}, bf16[1,384,256]{2,1,0:T(8,128)(2,1)S(1)}, u32[]{:S(2)}, u32[]{:S(2)}) %collective-permute-start.11) | collective-permute-done | bytes 196640 | tf_op jit(solution)/shard_map/ppermute | solution.py:310
  56.8 9.6 %collective-permute-done.15.refs_4_ = bf16[1,384,256]{2,1,0:T(8,128)(2,1)S(1)} collective-permute-done((bf16[1,384,256]{2,1,0:T(8,128)(2,1)S(1)}, bf16[1,384,256]{2,1,0:T(8,128)(2,1)S(1)}, u32[]{:S(2)}, u32[]{:S(2)}) %collective-permute-start.15) | collective-permute-done | bytes 196640 | tf_op jit(solution)/shard_map/ppermute | solution.py:310
  68.4 3.1 collective-permute-done.14.refs_4_
  71.4 2.6 collective-permute-done.16.refs_5_
  74.0 2.2 collective-permute-done.17.refs_1_.refs_3_
  76.7 2.7 rearrange.18
  83.5 2.3 collective-permute-done.21.k_other.v_other
  90.7 2.4 copy-done.1
  93.0 13.7 %memory_keys_values.1 = (bf16[4,588,1024]{2,1,0:T(8,128)(2,1)S(1)}, bf16[4,588,1024]{2,1,0:T(8,128)(2,1)S(1)}) custom-call(s32[4]{0:T(128)S(1)} %pad_add_fusion.place, bf16[4,588,1024]{2,1,0:T(8,128)(2,1)S(1)} %copy-done.1, f32[13,1024]{1,0:T(8,128)S(1)} %reshape.468.vectors, bf16[2,2176,256]{2,1,0:T(8,128)(2,1)S(1)} %half_weights.5.k_own.v_own, ...), custom_call_target="tpu_custom_call" | custom-call | flops 1000000 | bytes 100000 | tf_op jit(solution)/shard_map/memory_keys_values/pallas_call | solution.py:958
  107.8 2.2 collective-permute-done.22.refs_1_.refs_3_
  110.9 3.2 rearrange.19
  120.8 3.4 collective-permute-done.24.refs_1_.refs_3_.refs_5_
  125.3 4.7 self_qkv.1
  131.7 4.8 %collective-permute-done.25.refs_7_ = bf16[4,256,256]{2,1,0:T(8,128)(2,1)} collective-permute-done((bf16[4,256,256]{2,1,0:T(8,128)(2,1)}, bf16[4,256,256]{2,1,0:T(8,128)(2,1)}, u32[]{:S(2)}, u32[]{:S(2)}) %collective-permute-start.25) | collective-permute-done | bytes 524320 | tf_op jit(solution)/shard_map/ppermute | solution.py:310
  136.5 16.2 %collective-permute-done.26.refs_1_.refs_3_ = bf16[4,704,256]{2,1,0:T(8,128)(2,1)} collective-permute-done((bf16[4,704,256]{2,1,0:T(8,128)(2,1)}, bf16[4,704,256]{2,1,0:T(8,128)(2,1)}, u32[]{:S(2)}, u32[]{:S(2)}) %collective-permute-start.26) | collective-permute-done | bytes 1441824 | tf_op jit(solution)/shard_map/ppermute | solution.py:310
  153.4 3.5 rearrange.20
  157.0 4.4 half_weights.7.so_own.cq_own.own.co_own
  163.7 3.7 collective-permute-done.28.so_other.cq_other.other.co_other
  169.5 4.5 self_out_cross_q.1
  174.8 2.9 copy-done.12
  177.7 2.4 copy-done.14
  180.1 9.8 %cross_forward.1 = (bf16[256,1024]{1,0:T(8,128)(2,1)S(1)}, f32[2,8,256]{2,1,0:T(8,128)S(1)}) custom-call(s32[4]{0:T(128)S(1)} %reshape.469.map_ref, s32[4]{0:T(128)S(1)} %select_reduce_fusion.len_ref, s32[2,1,128]{2,1,0:T(1,128)S(1)} %bitcast.131, s32[2,128,1]{2,1,0:T(8,128)S(1)} %copy.47.seg_col, bf16[256,1024]{1,0:T(8,128)(2,1)S(1)} %get-tuple-element.485.q_ref, ...), custom_call_target="tpu_custom_call" | custom-call | flops 1000000 | bytes 100000 | tf_op jit(solution)/shard_map/cross_forward/pallas_call | solution.py:229
  190.0 3.3 half_weights.8.own
  193.5 3.0 rearrange.21
  198.7 3.2 cross_out.1
  201.9 4.8 %fc1_gelu.1 = (bf16[256,4096]{1,0:T(8,128)(2,1)S(1)}, bf16[256,4096]{1,0:T(8,128)(2,1)S(1)}) custom-call(s32[4]{0:T(128)S(1)} %pad_add_fusion.place, bf16[256,1024]{1,0:T(8,128)(2,1)S(1)} %get-tuple-element.494.normed.refs_0_, f32[1,4096]{1,0:T(1,128)S(1)} %bitcast.125, bf16[2,4096,256]{2,1,0:T(8,128)(2,1)S(1)} %half_weights.8.own, ...), custom_call_target="tpu_custom_call" | custom-call | flops 1000000 | bytes 100000 | tf_op jit(solution)/shard_map/fc1_gelu/pallas_call | solution.py:958
  206.8 2.9 weight_terms.5
  209.8 2.8 half_weights.9.own
  213.1 3.8 collective-permute-done.35.refs_2_
  217.0 3.9 weight_terms.6
  227.9 9.4 %fc2_gelu_back.1 = (bf16[256,4096]{1,0:T(8,128)(2,1)S(1)}, f32[1,4096]{1,0:T(1,128)S(1)}, bf16[1,2,1024,1024]{3,2,1,0:T(8,128)(2,1)}) custom-call(s32[4]{0:T(128)S(1)} %pad_add_fusion.place, bf16[256,1024]{1,0:T(8,128)(2,1)S(1)} %copy-done.31, bf16[256,4096]{1,0:T(8,128)(2,1)S(1)} %copy-done.84, bf16[256,1024]{1,0:T(8,128)(2,1)S(1)} %get-tuple-element.494.normed.refs_0_, ...), custom_call_target="tpu_custom_call" | custom-call | flops 1000000 | bytes 100000 | tf_op jit(solution)/shard_map/fc2_gelu_back/pallas_call | solution.py:958
  241.0 8.1 %fc1_norm_back.1 = (f32[256,1024]{1,0:T(8,128)S(1)}, bf16[256,1024]{1,0:T(8,128)(2,1)S(1)}, bf16[256,1024]{1,0:T(8,128)(2,1)S(1)}, f32[1,1024]{1,0:T(1,128)S(1)}...) custom-call(s32[4]{0:T(128)S(1)} %pad_add_fusion.place, ...), custom_call_target="tpu_custom_call" | custom-call | flops 1000000 | bytes 100000 | tf_op jit(solution)/shard_map/fc1_norm_back/pallas_call | solution.py:958
  249.1 3.1 weight_terms.7
  255.6 18.2 %cross_backward.1 = (bf16[256,1024]{1,0:T(8,128)(2,1)S(1)}, bf16[4,588,1024]{2,1,0:T(8,128)(2,1)S(1)}, bf16[4,588,1024]{2,1,0:T(8,128)(2,1)S(1)}, f32[1,1024]{1,0:T(1,128)S(1)}) custom-call(s32[4]{0:T(128)S(1)} %reshape.469.map_ref, s32[4]{0:T(128)S(1)} %select_reduce_fusion.len_ref, s32[2,1,128]{2,1,0:T(1,128)S(1)} %bitcast.132, ...), custom_call_target="tpu_custom_call" | custom-call | flops 1000000 | bytes 100000 | tf_op jit(solution)/shard_map/cross_backward/pallas_call | solution.py:251
  276.0 12.0 %memory_terms.2 = bf16[2,2,1024,256]{3,2,1,0:T(8,128)(2,1)} custom-call(s32[4]{0:T(128)S(1)} %pad_add_fusion.place, bf16[4,588,1024]{2,1,0:T(8,128)(2,1)S(1)} %bitcast.116, bf16[4,588,1024]{2,1,0:T(8,128)(2,1)S(1)} %get-tuple-element.618.dk.gk, bf16[4,588,1024]{2,1,0:T(8,128)(2,1)} %copy-done.7), custom_call_target="tpu_custom_call" | custom-call | flops 1000000 | bytes 100000 | tf_op jit(solution)/shard_map/memory_terms/pallas_call | solution.py:622
  296.9 4.9 %cross_q_norm_back.1 = (f32[256,1024]{1,0:T(8,128)S(1)}, bf16[256,1024]{1,0:T(8,128)(2,1)S(1)}, bf16[256,1024]{1,0:T(8,128)(2,1)S(1)}, f32[1,1024]{1,0:T(1,128)S...) custom-call(s32[4]{0:T(128)S(1)} %pad_add_fusion.place, ...), custom_call_target="tpu_custom_call" | custom-call | flops 1000000 | bytes 100000 | tf_op jit(solution)/shard_map/cross_q_norm_back/pallas_call | solution.py:958
  302.9 2.3 self_backward.1
  305.2 4.6 weight_terms.8
  309.9 2.4 copy-done.2
  312.3 10.6 %memory_terms.3 = (bf16[4,2,64,256]{3,2,1,0:T(8,128)(2,1)S(1)}, bf16[4,2,64,256]{3,2,1,0:T(8,128)(2,1)S(1)}, bf16[4,2,128,256]{3,2,1,0:T(8,128)(2,1)S(1)}, bf16[...) custom-call(s32[4]{0:T(128)S(1)} %pad_add_fusion.place, bf16[4,588,1024]{2,1,0:T(8,128)(2,1)S(1)} %copy-done.2, ...), custom_call_target="tpu_custom_call" | custom-call | flops 1000000 | bytes 100000 | tf_op jit(solution)/shard_map/memory_terms/pallas_call | solution.py:622
  335.5 6.0 %self_qkv_norm_back.1 = (bf16[256,1024]{1,0:T(8,128)(2,1)}, f32[1,1024]{1,0:T(1,128)S(1)}, f32[1,1024]{1,0:T(1,128)S(1)}, f32[1,1024]{1,0:T(1,128)S(1)}, f32[1,1024]{1,0:T(1,128)S(1)}) custom-call(s32[4]{0:T(128)S(1)} %pad_add_fusion.place, bf16[256,1024]{1,0:T(8,128)(2,1)S(1)} %copy-done.47, f32[256,1024]{1,0:T(8,128)S(1)} %copy-done.98, ...), custom_call_target="tpu_custom_call" | custom-call | flops 1000000 | bytes 100000 | tf_op jit(solution)/shard_map/self_qkv_norm_back/pallas_call | solution.py:958
  341.6 7.0 %weight_terms.9 = (bf16[4,6,64,256]{3,2,1,0:T(8,128)(2,1)}, bf16[4,6,64,256]{3,2,1,0:T(8,128)(2,1)}, bf16[4,6,128,256]{3,2,1,0:T(8,128)(2,1)S(1)}, bf16[4,6,128,...) custom-call(s32[4]{0:T(128)S(1)} %pad_add_fusion.place, bf16[256,1024]{1,0:T(8,128)(2,1)S(1)} %copy-done.17, ...), custom_call_target="tpu_custom_call" | custom-call | flops 1000000 | bytes 100000 | tf_op jit(solution)/shard_map/weight_terms/pallas_call | solution.py:561
  360.5 2.6 collective-permute-start.53
  365.5 2.4 copy-done.6
  367.9 13.9 %memory_back.1 = bf16[4,588,1024]{2,1,0:T(8,128)(2,1)S(1)} custom-call(s32[4]{0:T(128)S(1)} %pad_add_fusion.place, bf16[4,588,1024]{2,1,0:T(8,128)(2,1)S(1)} %copy-done.6, bf16[4,588,1024]{2,1,0:T(8,128)(2,1)} %copy-done.7, bf16[2,2176,256]{2,1,0:T(8,128)(2,1)S(1)} %copy-done.4, bf16[2,2176,256]{2,1,0:T(8,128)(2,1)} %collective-permute-done.21.k_other.v_other, ...), custom_call_target="tpu_custom_call" | custom-call | flops 1000000 | bytes 100000 | tf_op jit(solution)/shard_map/memory_back/pallas_call | solution.py:958
  383.9 4.0 add_corners.7
  391.1 2.8 collective-permute-start.62
  395.8 5.9 %copy.63 = bf16[4,588,1024]{2,0,1:T(4,128)(2,1)} copy(bf16[4,588,1024]{2,1,0:T(8,128)(2,1)S(1)} %memory_back.1) | data formatting | bytes 9633792 | tf_op jit(solution)/shard_map/optimization_barrier | solution.py:275
  411.0 2.2 copy-done.9
  413.2 2.2 copy-done.21
  415.4 3.9 fc2.1
  419.3 5.7 %collective-permute-done.66 = bf16[4,6,128,256]{3,2,1,0:T(8,128)(2,1)} collective-permute-done((bf16[4,6,128,256]{3,2,1,0:T(8,128)(2,1)}, bf16[4,6,128,256]{3,2,1,0:T(8,128)(2,1)}, u32[]{:S(2)}, u32[]{:S(2)}) %collective-permute-start.66) | collective-permute-done | bytes 1572896 | tf_op jit(solution)/shard_map/ppermute | solution.py:310
  425.8 2.2 fusion.8
  428.0 2.6 collective-permute-start.69
  434.3 2.5 collective-permute-done.68
  436.8 6.6 %collective-permute-done.70 = bf16[2,128,256]{2,1,0:T(8,128)(2,1)} collective-permute-done((bf16[2,128,256]{2,1,0:T(8,128)(2,1)}, bf16[2,128,256]{2,1,0:T(8,128)(2,1)}, u32[]{:S(2)}, u32[]{:S(2)}) %collective-permute-start.70) | collective-permute-done | bytes 131104 | tf_op jit(solution)/shard_map/ppermute | solution.py:310
  449.7 6.7 %collective-permute-done.72 = bf16[6,128,256]{2,1,0:T(8,128)(2,1)S(1)} collective-permute-done((bf16[6,128,256]{2,1,0:T(8,128)(2,1)S(1)}, bf16[6,128,256]{2,1,0:T(8,128)(2,1)S(1)}, u32[]{:S(2)}, u32[]{:S(2)}) %collective-permute-start.72) | collective-permute-done | bytes 393248 | tf_op jit(solution)/shard_map/ppermute | solution.py:310
  458.5 2.2 fusion.2
  464.7 4.4 collective-permute-done.73
  (458 shorter events, 145.7 us)
Async XLA Ops:
  2.5 13.0 %collective-permute-start = (bf16[1,640,256]{2,1,0:T(8,128)(2,1)S(1)}, bf16[1,640,256]{2,1,0:T(8,128)(2,1)S(1)}, u32[]{:S(2)}, u32[]{:S(2)}) collective-permute-start(bf16[1,640,256]{2,1,0:T(8,128)(2,1)S(1)} %rearrange.12.refs_0_.refs_2_), channel_id=1, source_target_pairs={{0,8},{1,9},{2,10},{3,11},{4,12},{5,13},{6,14},{7,15},{8,16},{9,17... | collective-permute-start | bytes 983048 | tf_op jit(solution)/shard_map/ppermute | solution.py:310
  7.1 8.4 %collective-permute-start.1 = (bf16[1,16,256]{2,1,0:T(8,128)(2,1)S(1)}, bf16[1,16,256]{2,1,0:T(8,128)(2,1)S(1)}, u32[]{:S(2)}, u32[]{:S(2)}) collective-permute-start(bf16[1,16,256]{2,1,0:T(8,128)(2,1)S(1)} %dynamic_update_slice.4.refs_1_), channel_id=1, source_target_pairs={{0,8},{1,9},{2,10},{3,11},{4,12},{5,13},{6,14},{7,15},{8,16},{9,17... | collective-permute-start | bytes 24584 | tf_op jit(solution)/shard_map/ppermute | solution.py:310
  15.5 10.9 %collective-permute-start.2 = (bf16[1,640,256]{2,1,0:T(8,128)(2,1)S(1)}, bf16[1,640,256]{2,1,0:T(8,128)(2,1)S(1)}, u32[]{:S(2)}, u32[]{:S(2)}) collective-permute-start(bf16[1,640,256]{2,1,0:T(8,128)(2,1)S(1)} %collective-permute-done.refs_2_.refs_3_), channel_id=1, source_target_pairs={{0,8},{1,9},{2,10},{3,11},{4,12},{5,13},{6,14},{7,15},{8,16},{9,17... | collective-permute-start | bytes 983048 | tf_op jit(solution)/shard_map/ppermute | solution.py:310
  15.5 10.6 %collective-permute-start.5 = (bf16[1,256,256]{2,1,0:T(8,128)(2,1)S(1)}, bf16[1,256,256]{2,1,0:T(8,128)(2,1)S(1)}, u32[]{:S(2)}, u32[]{:S(2)}) collective-permute-start(bf16[1,256,256]{2,1,0:T(8,128)(2,1)S(1)} %get-tuple-element.370), channel_id=1, source_target_pairs={{0,2},{1,3},{2,0},{3,1},{4,6},{5,7},{6,4},{7,5},{8,10},{9,11},{10,... | collective-permute-start | bytes 393224 | tf_op jit(solution)/shard_map/ppermute | solution.py:310
  17.1 9.0 %collective-permute-start.4 = (bf16[1,256,256]{2,1,0:T(8,128)(2,1)S(1)}, bf16[1,256,256]{2,1,0:T(8,128)(2,1)S(1)}, u32[]{:S(2)}, u32[]{:S(2)}) collective-permute-start(bf16[1,256,256]{2,1,0:T(8,128)(2,1)S(1)} %get-tuple-element.396.refs_0_), channel_id=1, source_target_pairs={{0,4},{1,5},{2,6},{3,7},{4,0},{5,1},{6,2},{7,3},{8,12},{9,13},{10,... | collective-permute-start | bytes 393224 | tf_op jit(solution)/shard_map/ppermute | solution.py:310
  26.4 10.6 %collective-permute-start.6 = (bf16[1,640,256]{2,1,0:T(8,128)(2,1)S(1)}, bf16[1,640,256]{2,1,0:T(8,128)(2,1)S(1)}, u32[]{:S(2)}, u32[]{:S(2)}) collective-permute-start(bf16[1,640,256]{2,1,0:T(8,128)(2,1)S(1)} %collective-permute-done.2.refs_4_), channel_id=1, source_target_pairs={{0,8},{1,9},{2,10},{3,11},{4,12},{5,13},{6,14},{7,15},{8,16},{9,17... | collective-permute-start | bytes 983048 | tf_op jit(solution)/shard_map/ppermute | solution.py:310
  27.8 8.5 %collective-permute-start.9 = (bf16[1,128,256]{2,1,0:T(8,128)(2,1)S(1)}, bf16[1,128,256]{2,1,0:T(8,128)(2,1)S(1)}, u32[]{:S(2)}, u32[]{:S(2)}) collective-permute-start(bf16[1,128,256]{2,1,0:T(8,128)(2,1)S(1)} %get-tuple-element.378), channel_id=1, source_target_pairs={{0,2},{1,3},{2,0},{3,1},{4,6},{5,7},{6,4},{7,5},{8,10},{9,11},{10,... | collective-permute-start | bytes 196616 | tf_op jit(solution)/shard_map/ppermute | solution.py:310
  28.4 7.9 %collective-permute-start.8 = (bf16[1,128,256]{2,1,0:T(8,128)(2,1)S(1)}, bf16[1,128,256]{2,1,0:T(8,128)(2,1)S(1)}, u32[]{:S(2)}, u32[]{:S(2)}) collective-permute-start(bf16[1,128,256]{2,1,0:T(8,128)(2,1)S(1)} %get-tuple-element.376), channel_id=1, source_target_pairs={{0,4},{1,5},{2,6},{3,7},{4,0},{5,1},{6,2},{7,3},{8,12},{9,13},{10,... | collective-permute-start | bytes 196616 | tf_op jit(solution)/shard_map/ppermute | solution.py:310
  37.1 16.3 %collective-permute-start.12 = (bf16[4,272,256]{2,1,0:T(8,128)(2,1)S(1)}, bf16[4,272,256]{2,1,0:T(8,128)(2,1)S(1)}, u32[]{:S(2)}, u32[]{:S(2)}) collective-permute-start(bf16[4,272,256]{2,1,0:T(8,128)(2,1)S(1)} %get-tuple-element.426.refs_0_), channel_id=1, source_target_pairs={{0,4},{1,5},{2,6},{3,7},{4,0},{5,1},{6,2},{7,3},{8,12},{9,13},{10,... | collective-permute-start | bytes 1671176 | tf_op jit(solution)/shard_map/ppermute | solution.py:310
  38.1 15.2 %collective-permute-start.13 = (bf16[4,272,256]{2,1,0:T(8,128)(2,1)S(1)}, bf16[4,272,256]{2,1,0:T(8,128)(2,1)S(1)}, u32[]{:S(2)}, u32[]{:S(2)}) collective-permute-start(bf16[4,272,256]{2,1,0:T(8,128)(2,1)S(1)} %get-tuple-element.392), channel_id=1, source_target_pairs={{0,2},{1,3},{2,0},{3,1},{4,6},{5,7},{6,4},{7,5},{8,10},{9,11},{10,... | collective-permute-start | bytes 1671176 | tf_op jit(solution)/shard_map/ppermute | solution.py:310
  39.6 13.7 %collective-permute-start.10 = (bf16[1,768,256]{2,1,0:T(8,128)(2,1)S(1)}, bf16[1,768,256]{2,1,0:T(8,128)(2,1)S(1)}, u32[]{:S(2)}, u32[]{:S(2)}) collective-permute-start(bf16[1,768,256]{2,1,0:T(8,128)(2,1)S(1)} %get-tuple-element.473.refs_2_), channel_id=1, source_target_pairs={{0,8},{1,9},{2,10},{3,11},{4,12},{5,13},{6,14},{7,15},{8,16},{9,17... | collective-permute-start | bytes 1179656 | tf_op jit(solution)/shard_map/ppermute | solution.py:310
  39.6 13.7 %collective-permute-start.11 = (bf16[1,384,256]{2,1,0:T(8,128)(2,1)S(1)}, bf16[1,384,256]{2,1,0:T(8,128)(2,1)S(1)}, u32[]{:S(2)}, u32[]{:S(2)}) collective-permute-start(bf16[1,384,256]{2,1,0:T(8,128)(2,1)S(1)} %get-tuple-element.421.refs_2_), channel_id=1, source_target_pairs={{0,8},{1,9},{2,10},{3,11},{4,12},{5,13},{6,14},{7,15},{8,16},{9,17... | collective-permute-start | bytes 589832 | tf_op jit(solution)/shard_map/ppermute | solution.py:310
  55.0 21.7 %collective-permute-start.18 = (bf16[4,528,256]{2,1,0:T(8,128)(2,1)}, bf16[4,528,256]{2,1,0:T(8,128)(2,1)S(1)}, u32[]{:S(2)}, u32[]{:S(2)}) collective-permute-start(bf16[4,528,256]{2,1,0:T(8,128)(2,1)} %get-tuple-element.410), channel_id=1, source_target_pairs={{0,2},{1,3},{2,0},{3,1},{4,6},{5,7},{6,4},{7,5},{8,10},{9,11},{10,... | collective-permute-start | bytes 3244040 | tf_op jit(solution)/shard_map/ppermute | solution.py:310
  55.5 20.7 %collective-permute-start.17 = (bf16[4,512,256]{2,1,0:T(8,128)(2,1)}, bf16[4,512,256]{2,1,0:T(8,128)(2,1)S(1)}, u32[]{:S(2)}, u32[]{:S(2)}) collective-permute-start(bf16[4,512,256]{2,1,0:T(8,128)(2,1)} %get-tuple-element.451.refs_0_), channel_id=1, source_target_pairs={{0,4},{1,5},{2,6},{3,7},{4,0},{5,1},{6,2},{7,3},{8,12},{9,13},{10,... | collective-permute-start | bytes 3145736 | tf_op jit(solution)/shard_map/ppermute | solution.py:310
  56.8 9.6 %collective-permute-start.15 = (bf16[1,384,256]{2,1,0:T(8,128)(2,1)S(1)}, bf16[1,384,256]{2,1,0:T(8,128)(2,1)S(1)}, u32[]{:S(2)}, u32[]{:S(2)}) collective-permute-start(bf16[1,384,256]{2,1,0:T(8,128)(2,1)S(1)} %collective-permute-done.11.refs_3_), channel_id=1, source_target_pairs={{0,8},{1,9},{2,10},{3,11},{4,12},{5,13},{6,14},{7,15},{8,16},{9,17... | collective-permute-start | bytes 589832 | tf_op jit(solution)/shard_map/ppermute | solution.py:310
  56.8 14.6 %collective-permute-start.14 = (bf16[1,768,256]{2,1,0:T(8,128)(2,1)S(1)}, bf16[1,768,256]{2,1,0:T(8,128)(2,1)}, u32[]{:S(2)}, u32[]{:S(2)}) collective-permute-start(bf16[1,768,256]{2,1,0:T(8,128)(2,1)S(1)} %collective-permute-done.10.refs_3_), channel_id=1, source_target_pairs={{0,8},{1,9},{2,10},{3,11},{4,12},{5,13},{6,14},{7,15},{8,16},{9,17... | collective-permute-start | bytes 1179656 | tf_op jit(solution)/shard_map/ppermute | solution.py:310
  81.4 28.6 %collective-permute-start.22 = (bf16[4,576,256]{2,1,0:T(8,128)(2,1)}, bf16[4,576,256]{2,1,0:T(8,128)(2,1)S(1)}, u32[]{:S(2)}, u32[]{:S(2)}) collective-permute-start(bf16[4,576,256]{2,1,0:T(8,128)(2,1)} %get-tuple-element.478.refs_0_), channel_id=1, source_target_pairs={{0,4},{1,5},{2,6},{3,7},{4,0},{5,1},{6,2},{7,3},{8,12},{9,13},{10,... | collective-permute-start | bytes 3538952 | tf_op jit(solution)/shard_map/ppermute | solution.py:310
  82.6 28.4 %collective-permute-start.23 = (bf16[4,576,256]{2,1,0:T(8,128)(2,1)}, bf16[4,576,256]{2,1,0:T(8,128)(2,1)}, u32[]{:S(2)}, u32[]{:S(2)}) collective-permute-start(bf16[4,576,256]{2,1,0:T(8,128)(2,1)} %get-tuple-element.437), channel_id=1, source_target_pairs={{0,2},{1,3},{2,0},{3,1},{4,6},{5,7},{6,4},{7,5},{8,10},{9,11},{10,... | collective-permute-start | bytes 3538952 | tf_op jit(solution)/shard_map/ppermute | solution.py:310
  83.5 24.3 %collective-permute-start.20 = (bf16[4,256,256]{2,1,0:T(8,128)(2,1)}, bf16[4,256,256]{2,1,0:T(8,128)(2,1)}, u32[]{:S(2)}, u32[]{:S(2)}) collective-permute-start(bf16[4,256,256]{2,1,0:T(8,128)(2,1)} %rearrange.16.refs_5_), channel_id=1, source_target_pairs={{0,8},{1,9},{2,10},{3,11},{4,12},{5,13},{6,14},{7,15},{8,16},{9,17... | collective-permute-start | bytes 1572872 | tf_op jit(solution)/shard_map/ppermute | solution.py:310
  83.5 24.3 %collective-permute-start.19 = (bf16[1,768,256]{2,1,0:T(8,128)(2,1)}, bf16[1,768,256]{2,1,0:T(8,128)(2,1)}, u32[]{:S(2)}, u32[]{:S(2)}) collective-permute-start(bf16[1,768,256]{2,1,0:T(8,128)(2,1)} %collective-permute-done.14.refs_4_), channel_id=1, source_target_pairs={{0,8},{1,9},{2,10},{3,11},{4,12},{5,13},{6,14},{7,15},{8,16},{9,17... | collective-permute-start | bytes 1179656 | tf_op jit(solution)/shard_map/ppermute | solution.py:310
  118.4 34.3 %collective-permute-start.26 = (bf16[4,704,256]{2,1,0:T(8,128)(2,1)}, bf16[4,704,256]{2,1,0:T(8,128)(2,1)}, u32[]{:S(2)}, u32[]{:S(2)}) collective-permute-start(bf16[4,704,256]{2,1,0:T(8,128)(2,1)} %get-tuple-element.500.refs_0_), channel_id=1, source_target_pairs={{0,4},{1,5},{2,6},{3,7},{4,0},{5,1},{6,2},{7,3},{8,12},{9,13},{10,... | collective-permute-start | bytes 4325384 | tf_op jit(solution)/shard_map/ppermute | solution.py:310
  119.4 34.0 %collective-permute-start.27 = (bf16[4,704,256]{2,1,0:T(8,128)(2,1)}, bf16[4,704,256]{2,1,0:T(8,128)(2,1)}, u32[]{:S(2)}, u32[]{:S(2)}) collective-permute-start(bf16[4,704,256]{2,1,0:T(8,128)(2,1)} %get-tuple-element.464), channel_id=1, source_target_pairs={{0,2},{1,3},{2,0},{3,1},{4,6},{5,7},{6,4},{7,5},{8,10},{9,11},{10,... | collective-permute-start | bytes 4325384 | tf_op jit(solution)/shard_map/ppermute | solution.py:310
  120.5 16.0 %collective-permute-start.25 = (bf16[4,256,256]{2,1,0:T(8,128)(2,1)}, bf16[4,256,256]{2,1,0:T(8,128)(2,1)}, u32[]{:S(2)}, u32[]{:S(2)}) collective-permute-start(bf16[4,256,256]{2,1,0:T(8,128)(2,1)} %collective-permute-done.20.refs_6_), channel_id=1, source_target_pairs={{0,8},{1,9},{2,10},{3,11},{4,12},{5,13},{6,14},{7,15},{8,16},{9,17... | collective-permute-start | bytes 1572872 | tf_op jit(solution)/shard_map/ppermute | solution.py:310
  161.4 28.5 %collective-permute-start.30 = (bf16[4,512,256]{2,1,0:T(8,128)(2,1)}, bf16[4,512,256]{2,1,0:T(8,128)(2,1)}, u32[]{:S(2)}, u32[]{:S(2)}) collective-permute-start(bf16[4,512,256]{2,1,0:T(8,128)(2,1)} %get-tuple-element.528.refs_0_), channel_id=1, source_target_pairs={{0,4},{1,5},{2,6},{3,7},{4,0},{5,1},{6,2},{7,3},{8,12},{9,13},{10,... | collective-permute-start | bytes 3145736 | tf_op jit(solution)/shard_map/ppermute | solution.py:310
  162.5 27.5 %collective-permute-start.31 = (bf16[4,512,256]{2,1,0:T(8,128)(2,1)}, bf16[4,512,256]{2,1,0:T(8,128)(2,1)}, u32[]{:S(2)}, u32[]{:S(2)}) collective-permute-start(bf16[4,512,256]{2,1,0:T(8,128)(2,1)} %get-tuple-element.491), channel_id=1, source_target_pairs={{0,2},{1,3},{2,0},{3,1},{4,6},{5,7},{6,4},{7,5},{8,10},{9,11},{10,... | collective-permute-start | bytes 3145736 | tf_op jit(solution)/shard_map/ppermute | solution.py:310
  163.4 26.5 %collective-permute-start.29 = (bf16[4,256,256]{2,1,0:T(8,128)(2,1)}, bf16[4,256,256]{2,1,0:T(8,128)(2,1)}, u32[]{:S(2)}, u32[]{:S(2)}) collective-permute-start(bf16[4,256,256]{2,1,0:T(8,128)(2,1)} %collective-permute-done.25.refs_7_), channel_id=1, source_target_pairs={{0,8},{1,9},{2,10},{3,11},{4,12},{5,13},{6,14},{7,15},{8,16},{9,17... | collective-permute-start | bytes 1572872 | tf_op jit(solution)/shard_map/ppermute | solution.py:310
  193.3 8.6 %collective-permute-start.32 = (bf16[2,4096,256]{2,1,0:T(8,128)(2,1)S(1)}, bf16[2,4096,256]{2,1,0:T(8,128)(2,1)S(1)}, u32[]{:S(2)}, u32[]{:S(2)}) collective-permute-start(bf16[2,4096,256]{2,1,0:T(8,128)(2,1)S(1)} %half_weights.8.own), channel_id=1, source_target_pairs={{0,1},{1,0},{2,3},{3,2},{4,5},{5,4},{6,7},{7,6},{8,9},{9,8},{10,11... | collective-permute-start | bytes 12582920 | tf_op jit(solution)/shard_map/ppermute | solution.py:310
  196.5 10.2 %collective-permute-start.34 = (bf16[4,128,256]{2,1,0:T(8,128)(2,1)S(1)}, bf16[4,128,256]{2,1,0:T(8,128)(2,1)S(1)}, u32[]{:S(2)}, u32[]{:S(2)}) collective-permute-start(bf16[4,128,256]{2,1,0:T(8,128)(2,1)S(1)} %get-tuple-element.512), channel_id=1, source_target_pairs={{0,2},{1,3},{2,0},{3,1},{4,6},{5,7},{6,4},{7,5},{8,10},{9,11},{10,... | collective-permute-start | bytes 786440 | tf_op jit(solution)/shard_map/ppermute | solution.py:310
  197.7 9.1 %collective-permute-start.33 = (bf16[4,128,256]{2,1,0:T(8,128)(2,1)S(1)}, bf16[4,128,256]{2,1,0:T(8,128)(2,1)S(1)}, u32[]{:S(2)}, u32[]{:S(2)}) collective-permute-start(bf16[4,128,256]{2,1,0:T(8,128)(2,1)S(1)} %get-tuple-element.510), channel_id=1, source_target_pairs={{0,4},{1,5},{2,6},{3,7},{4,0},{5,1},{6,2},{7,3},{8,12},{9,13},{10,... | collective-permute-start | bytes 786440 | tf_op jit(solution)/shard_map/ppermute | solution.py:310
  212.6 11.7 %collective-permute-start.36 = (bf16[2,4096,256]{2,1,0:T(8,128)(2,1)S(1)}, bf16[2,4096,256]{2,1,0:T(8,128)(2,1)S(1)}, u32[]{:S(2)}, u32[]{:S(2)}) collective-permute-start(bf16[2,4096,256]{2,1,0:T(8,128)(2,1)S(1)} %half_weights.9.own), channel_id=1, source_target_pairs={{0,1},{1,0},{2,3},{3,2},{4,5},{5,4},{6,7},{7,6},{8,9},{9,8},{10,11... | collective-permute-start | bytes 12582920 | tf_op jit(solution)/shard_map/ppermute | solution.py:310
  222.3 14.9 %collective-permute-start.37 = (bf16[4,1,256,256]{3,2,1,0:T(8,128)(2,1)S(1)}, bf16[4,1,256,256]{3,2,1,0:T(8,128)(2,1)S(1)}, u32[]{:S(2)}, u32[]{:S(2)}) collective-permute-start(bf16[4,1,256,256]{3,2,1,0:T(8,128)(2,1)S(1)} %get-tuple-element.540), channel_id=1, source_target_pairs={{0,4},{1,5},{2,6},{3,7},{4,0},{5,1},{6,2},{7,3},{8,12},{9,13},{10,... | collective-permute-start | bytes 1572872 | tf_op jit(solution)/shard_map/ppermute | solution.py:310
  223.4 13.9 %collective-permute-start.38 = (bf16[4,1,256,256]{3,2,1,0:T(8,128)(2,1)S(1)}, bf16[4,1,256,256]{3,2,1,0:T(8,128)(2,1)S(1)}, u32[]{:S(2)}, u32[]{:S(2)}) collective-permute-start(bf16[4,1,256,256]{3,2,1,0:T(8,128)(2,1)S(1)} %get-tuple-element.542), channel_id=1, source_target_pairs={{0,2},{1,3},{2,0},{3,1},{4,6},{5,7},{6,4},{7,5},{8,10},{9,11},{10,... | collective-permute-start | bytes 1572872 | tf_op jit(solution)/shard_map/ppermute | solution.py:310
  237.2 11.9 %collective-permute-start.39 = (bf16[1,2,1024,1024]{3,2,1,0:T(8,128)(2,1)}, bf16[1,2,1024,1024]{3,2,1,0:T(8,128)(2,1)S(1)}, u32[]{:S(2)}, u32[]{:S(2)}) collective-permute-start(bf16[1,2,1024,1024]{3,2,1,0:T(8,128)(2,1)} %get-tuple-element.550), channel_id=1, source_target_pairs={{0,1},{1,0},{2,3},{3,2},{4,5},{5,4},{6,7},{7,6},{8,9},{9,8},{10,11... | collective-permute-start | bytes 12582920 | tf_op jit(solution)/shard_map/ppermute | solution.py:310
  238.9 49.1 %collective-permute-start.40 = (bf16[4,1,512,256]{3,2,1,0:T(8,128)(2,1)}, bf16[4,1,512,256]{3,2,1,0:T(8,128)(2,1)}, u32[]{:S(2)}, u32[]{:S(2)}) collective-permute-start(bf16[4,1,512,256]{3,2,1,0:T(8,128)(2,1)} %get-tuple-element.559), channel_id=1, source_target_pairs={{0,4},{1,5},{2,6},{3,7},{4,0},{5,1},{6,2},{7,3},{8,12},{9,13},{10,... | collective-permute-start | bytes 3145736 | tf_op jit(solution)/shard_map/ppermute | solution.py:310
  240.0 48.0 %collective-permute-start.41 = (bf16[4,1,512,256]{3,2,1,0:T(8,128)(2,1)S(1)}, bf16[4,1,512,256]{3,2,1,0:T(8,128)(2,1)}, u32[]{:S(2)}, u32[]{:S(2)}) collective-permute-start(bf16[4,1,512,256]{3,2,1,0:T(8,128)(2,1)S(1)} %get-tuple-element.561), channel_id=1, source_target_pairs={{0,2},{1,3},{2,0},{3,1},{4,6},{5,7},{6,4},{7,5},{8,10},{9,11},{10,... | collective-permute-start | bytes 3145736 | tf_op jit(solution)/shard_map/ppermute | solution.py:310
  253.6 34.5 %collective-permute-start.42 = (bf16[4,1,64,1024]{3,2,1,0:T(8,128)(2,1)S(1)}, bf16[4,1,64,1024]{3,2,1,0:T(8,128)(2,1)S(1)}, u32[]{:S(2)}, u32[]{:S(2)}) collective-permute-start(bf16[4,1,64,1024]{3,2,1,0:T(8,128)(2,1)S(1)} %get-tuple-element.562), channel_id=1, source_target_pairs={{0,4},{1,5},{2,6},{3,7},{4,0},{5,1},{6,2},{7,3},{8,12},{9,13},{10,... | collective-permute-start | bytes 1572872 | tf_op jit(solution)/shard_map/ppermute | solution.py:310
  254.6 33.4 %collective-permute-start.43 = (bf16[4,1,64,1024]{3,2,1,0:T(8,128)(2,1)S(1)}, bf16[4,1,64,1024]{3,2,1,0:T(8,128)(2,1)S(1)}, u32[]{:S(2)}, u32[]{:S(2)}) collective-permute-start(bf16[4,1,64,1024]{3,2,1,0:T(8,128)(2,1)S(1)} %get-tuple-element.564), channel_id=1, source_target_pairs={{0,2},{1,3},{2,0},{3,1},{4,6},{5,7},{6,4},{7,5},{8,10},{9,11},{10,... | collective-permute-start | bytes 1572872 | tf_op jit(solution)/shard_map/ppermute | solution.py:310
  288.0 21.8 %collective-permute-start.44 = (bf16[2,2,1024,256]{3,2,1,0:T(8,128)(2,1)}, bf16[2,2,1024,256]{3,2,1,0:T(8,128)(2,1)}, u32[]{:S(2)}, u32[]{:S(2)}) collective-permute-start(bf16[2,2,1024,256]{3,2,1,0:T(8,128)(2,1)} %memory_terms.2), channel_id=1, source_target_pairs={{0,1},{1,0},{2,3},{3,2},{4,5},{5,4},{6,7},{7,6},{8,9},{9,8},{10,11... | collective-permute-start | bytes 6291464 | tf_op jit(solution)/shard_map/ppermute | solution.py:310
  290.0 36.9 %collective-permute-start.46 = (bf16[4,1,128,1024]{3,2,1,0:T(8,128)(2,1)}, bf16[4,1,128,1024]{3,2,1,0:T(8,128)(2,1)}, u32[]{:S(2)}, u32[]{:S(2)}) collective-permute-start(bf16[4,1,128,1024]{3,2,1,0:T(8,128)(2,1)} %get-tuple-element.588), channel_id=1, source_target_pairs={{0,4},{1,5},{2,6},{3,7},{4,0},{5,1},{6,2},{7,3},{8,12},{9,13},{10,... | collective-permute-start | bytes 3145736 | tf_op jit(solution)/shard_map/ppermute | solution.py:310
  291.1 35.9 %collective-permute-start.47 = (bf16[4,1,128,1024]{3,2,1,0:T(8,128)(2,1)}, bf16[4,1,128,1024]{3,2,1,0:T(8,128)(2,1)}, u32[]{:S(2)}, u32[]{:S(2)}) collective-permute-start(bf16[4,1,128,1024]{3,2,1,0:T(8,128)(2,1)} %get-tuple-element.590), channel_id=1, source_target_pairs={{0,2},{1,3},{2,0},{3,1},{4,6},{5,7},{6,4},{7,5},{8,10},{9,11},{10,... | collective-permute-start | bytes 3145736 | tf_op jit(solution)/shard_map/ppermute | solution.py:310
  293.3 32.9 %collective-permute-start.45 = (bf16[1,512,256]{2,1,0:T(8,128)(2,1)S(1)}, bf16[1,512,256]{2,1,0:T(8,128)(2,1)S(1)}, u32[]{:S(2)}, u32[]{:S(2)}) collective-permute-start(bf16[1,512,256]{2,1,0:T(8,128)(2,1)S(1)} %fusion.9), channel_id=1, source_target_pairs={{0,8},{1,9},{2,10},{3,11},{4,12},{5,13},{6,14},{7,15},{8,16},{9,17... | collective-permute-start | bytes 786440 | tf_op jit(solution)/shard_map/ppermute | solution.py:310
  326.9 14.6 %collective-permute-start.48 = (bf16[6,2,1024,256]{3,2,1,0:T(8,128)(2,1)}, bf16[6,2,1024,256]{3,2,1,0:T(8,128)(2,1)}, u32[]{:S(2)}, u32[]{:S(2)}) collective-permute-start(bf16[6,2,1024,256]{3,2,1,0:T(8,128)(2,1)} %weight_terms.8), channel_id=1, source_target_pairs={{0,1},{1,0},{2,3},{3,2},{4,5},{5,4},{6,7},{7,6},{8,9},{9,8},{10,11... | collective-permute-start | bytes 18874376 | tf_op jit(solution)/shard_map/ppermute | solution.py:310
  329.9 22.8 %collective-permute-start.50 = (bf16[1,128,1024]{2,1,0:T(8,128)(2,1)S(1)}, bf16[1,128,1024]{2,1,0:T(8,128)(2,1)S(1)}, u32[]{:S(2)}, u32[]{:S(2)}) collective-permute-start(bf16[1,128,1024]{2,1,0:T(8,128)(2,1)S(1)} %fusion.10), channel_id=1, source_target_pairs={{0,8},{1,9},{2,10},{3,11},{4,12},{5,13},{6,14},{7,15},{8,16},{9,17... | collective-permute-start | bytes 786440 | tf_op jit(solution)/shard_map/ppermute | solution.py:310
  330.4 22.3 %collective-permute-start.49 = (bf16[1,512,256]{2,1,0:T(8,128)(2,1)S(1)}, bf16[1,512,256]{2,1,0:T(8,128)(2,1)S(1)}, u32[]{:S(2)}, u32[]{:S(2)}) collective-permute-start(bf16[1,512,256]{2,1,0:T(8,128)(2,1)S(1)} %fusion.7), channel_id=1, source_target_pairs={{0,8},{1,9},{2,10},{3,11},{4,12},{5,13},{6,14},{7,15},{8,16},{9,17... | collective-permute-start | bytes 786440 | tf_op jit(solution)/shard_map/ppermute | solution.py:310
  332.2 20.5 %collective-permute-start.51 = (bf16[4,2,64,256]{3,2,1,0:T(8,128)(2,1)S(1)}, bf16[4,2,64,256]{3,2,1,0:T(8,128)(2,1)S(1)}, u32[]{:S(2)}, u32[]{:S(2)}) collective-permute-start(bf16[4,2,64,256]{3,2,1,0:T(8,128)(2,1)S(1)} %copy-done.120), channel_id=1, source_target_pairs={{0,4},{1,5},{2,6},{3,7},{4,0},{5,1},{6,2},{7,3},{8,12},{9,13},{10,... | collective-permute-start | bytes 786440 | tf_op jit(solution)/shard_map/ppermute | solution.py:310
  333.2 19.5 %collective-permute-start.52 = (bf16[4,2,64,256]{3,2,1,0:T(8,128)(2,1)}, bf16[4,2,64,256]{3,2,1,0:T(8,128)(2,1)S(1)}, u32[]{:S(2)}, u32[]{:S(2)}) collective-permute-start(bf16[4,2,64,256]{3,2,1,0:T(8,128)(2,1)} %copy-done.118), channel_id=1, source_target_pairs={{0,2},{1,3},{2,0},{3,1},{4,6},{5,7},{6,4},{7,5},{8,10},{9,11},{10,... | collective-permute-start | bytes 786440 | tf_op jit(solution)/shard_map/ppermute | solution.py:310
  352.7 31.1 %collective-permute-start.56 = (bf16[4,6,64,256]{3,2,1,0:T(8,128)(2,1)}, bf16[4,6,64,256]{3,2,1,0:T(8,128)(2,1)S(1)}, u32[]{:S(2)}, u32[]{:S(2)}) collective-permute-start(bf16[4,6,64,256]{3,2,1,0:T(8,128)(2,1)} %get-tuple-element.628), channel_id=1, source_target_pairs={{0,4},{1,5},{2,6},{3,7},{4,0},{5,1},{6,2},{7,3},{8,12},{9,13},{10,... | collective-permute-start | bytes 2359304 | tf_op jit(solution)/shard_map/ppermute | solution.py:310
  353.7 30.2 %collective-permute-start.57 = (bf16[4,6,64,256]{3,2,1,0:T(8,128)(2,1)}, bf16[4,6,64,256]{3,2,1,0:T(8,128)(2,1)}, u32[]{:S(2)}, u32[]{:S(2)}) collective-permute-start(bf16[4,6,64,256]{3,2,1,0:T(8,128)(2,1)} %get-tuple-element.630), channel_id=1, source_target_pairs={{0,2},{1,3},{2,0},{3,1},{4,6},{5,7},{6,4},{7,5},{8,10},{9,11},{10,... | collective-permute-start | bytes 2359304 | tf_op jit(solution)/shard_map/ppermute | solution.py:310
  356.4 26.8 %collective-permute-start.54 = (bf16[4,2,128,256]{3,2,1,0:T(8,128)(2,1)}, bf16[4,2,128,256]{3,2,1,0:T(8,128)(2,1)}, u32[]{:S(2)}, u32[]{:S(2)}) collective-permute-start(bf16[4,2,128,256]{3,2,1,0:T(8,128)(2,1)} %get-tuple-element.625), channel_id=1, source_target_pairs={{0,4},{1,5},{2,6},{3,7},{4,0},{5,1},{6,2},{7,3},{8,12},{9,13},{10,... | collective-permute-start | bytes 1572872 | tf_op jit(solution)/shard_map/ppermute | solution.py:310
  357.4 26.5 %collective-permute-start.55 = (bf16[4,2,128,256]{3,2,1,0:T(8,128)(2,1)}, bf16[4,2,128,256]{3,2,1,0:T(8,128)(2,1)}, u32[]{:S(2)}, u32[]{:S(2)}) collective-permute-start(bf16[4,2,128,256]{3,2,1,0:T(8,128)(2,1)} %get-tuple-element.627), channel_id=1, source_target_pairs={{0,2},{1,3},{2,0},{3,1},{4,6},{5,7},{6,4},{7,5},{8,10},{9,11},{10,... | collective-permute-start | bytes 1572872 | tf_op jit(solution)/shard_map/ppermute | solution.py:310
  360.5 21.3 %collective-permute-start.53 = (bf16[1,512,256]{2,1,0:T(8,128)(2,1)}, bf16[1,512,256]{2,1,0:T(8,128)(2,1)}, u32[]{:S(2)}, u32[]{:S(2)}) collective-permute-start(bf16[1,512,256]{2,1,0:T(8,128)(2,1)} %fusion.6), channel_id=1, source_target_pairs={{0,8},{1,9},{2,10},{3,11},{4,12},{5,13},{6,14},{7,15},{8,16},{9,17... | collective-permute-start | bytes 786440 | tf_op jit(solution)/shard_map/ppermute | solution.py:310
  387.9 37.1 %collective-permute-start.66 = (bf16[4,6,128,256]{3,2,1,0:T(8,128)(2,1)}, bf16[4,6,128,256]{3,2,1,0:T(8,128)(2,1)}, u32[]{:S(2)}, u32[]{:S(2)}) collective-permute-start(bf16[4,6,128,256]{3,2,1,0:T(8,128)(2,1)} %get-tuple-element.674), channel_id=1, source_target_pairs={{0,4},{1,5},{2,6},{3,7},{4,0},{5,1},{6,2},{7,3},{8,12},{9,13},{10,... | collective-permute-start | bytes 4718600 | tf_op jit(solution)/shard_map/ppermute | solution.py:310
  389.0 36.8 %collective-permute-start.67 = (bf16[4,6,128,256]{3,2,1,0:T(8,128)(2,1)}, bf16[4,6,128,256]{3,2,1,0:T(8,128)(2,1)}, u32[]{:S(2)}, u32[]{:S(2)}) collective-permute-start(bf16[4,6,128,256]{3,2,1,0:T(8,128)(2,1)} %get-tuple-element.676), channel_id=1, source_target_pairs={{0,2},{1,3},{2,0},{3,1},{4,6},{5,7},{6,4},{7,5},{8,10},{9,11},{10,... | collective-permute-start | bytes 4718600 | tf_op jit(solution)/shard_map/ppermute | solution.py:310
  391.1 13.0 %collective-permute-start.62 = (bf16[1,128,1024]{2,1,0:T(8,128)(2,1)S(1)}, bf16[1,128,1024]{2,1,0:T(8,128)(2,1)S(1)}, u32[]{:S(2)}, u32[]{:S(2)}) collective-permute-start(bf16[1,128,1024]{2,1,0:T(8,128)(2,1)S(1)} %fusion.4), channel_id=1, source_target_pairs={{0,8},{1,9},{2,10},{3,11},{4,12},{5,13},{6,14},{7,15},{8,16},{9,17... | collective-permute-start | bytes 786440 | tf_op jit(solution)/shard_map/ppermute | solution.py:310
  394.0 8.4 %collective-permute-start.59 = (f32[2,2,544]{2,1,0:T(2,128)S(1)}, f32[2,2,544]{2,1,0:T(2,128)S(1)}, u32[]{:S(2)}, u32[]{:S(2)}) collective-permute-start(f32[2,2,544]{2,1,0:T(2,128)S(1)} %fusion.25), channel_id=1, source_target_pairs={{0,8},{1,9},{2,10},{3,11},{4,12},{5,13},{6,14},{7,15},{8,16},{9,17... | collective-permute-start | bytes 26120 | tf_op jit(solution)/shard_map/ppermute | solution.py:310
  395.5 8.7 %collective-permute-start.64 = (bf16[2,128,256]{2,1,0:T(8,128)(2,1)S(1)}, bf16[2,128,256]{2,1,0:T(8,128)(2,1)S(1)}, u32[]{:S(2)}, u32[]{:S(2)}) collective-permute-start(bf16[2,128,256]{2,1,0:T(8,128)(2,1)S(1)} %fusion.13), channel_id=1, source_target_pairs={{0,8},{1,9},{2,10},{3,11},{4,12},{5,13},{6,14},{7,15},{8,16},{9,17... | collective-permute-start | bytes 393224 | tf_op jit(solution)/shard_map/ppermute | solution.py:310
  402.4 8.0 %collective-permute-start.60 = (f32[2,2,544]{2,1,0:T(2,128)S(1)}, f32[2,2,544]{2,1,0:T(2,128)S(1)}, u32[]{:S(2)}, u32[]{:S(2)}) collective-permute-start(f32[2,2,544]{2,1,0:T(2,128)S(1)} %fusion.24), channel_id=1, source_target_pairs={{0,8},{1,9},{2,10},{3,11},{4,12},{5,13},{6,14},{7,15},{8,16},{9,17... | collective-permute-start | bytes 26120 | tf_op jit(solution)/shard_map/ppermute | solution.py:310
  406.0 13.3 %collective-permute-start.63 = (bf16[1,128,1024]{2,1,0:T(8,128)(2,1)}, bf16[1,128,1024]{2,1,0:T(8,128)(2,1)S(1)}, u32[]{:S(2)}, u32[]{:S(2)}) collective-permute-start(bf16[1,128,1024]{2,1,0:T(8,128)(2,1)} %fusion.5), channel_id=1, source_target_pairs={{0,8},{1,9},{2,10},{3,11},{4,12},{5,13},{6,14},{7,15},{8,16},{9,17... | collective-permute-start | bytes 786440 | tf_op jit(solution)/shard_map/ppermute | solution.py:310
  409.7 9.6 %collective-permute-start.65 = (bf16[2,128,256]{2,1,0:T(8,128)(2,1)}, bf16[2,128,256]{2,1,0:T(8,128)(2,1)}, u32[]{:S(2)}, u32[]{:S(2)}) collective-permute-start(bf16[2,128,256]{2,1,0:T(8,128)(2,1)} %fusion.12), channel_id=1, source_target_pairs={{0,8},{1,9},{2,10},{3,11},{4,12},{5,13},{6,14},{7,15},{8,16},{9,17... | collective-permute-start | bytes 393224 | tf_op jit(solution)/shard_map/ppermute | solution.py:310
  410.4 8.9 %collective-permute-start.61 = (f32[2,2,544]{2,1,0:T(2,128)S(1)}, f32[2,2,544]{2,1,0:T(2,128)S(1)}, u32[]{:S(2)}, u32[]{:S(2)}) collective-permute-start(f32[2,2,544]{2,1,0:T(2,128)S(1)} %fusion.22), channel_id=1, source_target_pairs={{0,8},{1,9},{2,10},{3,11},{4,12},{5,13},{6,14},{7,15},{8,16},{9,17... | collective-permute-start | bytes 26120 | tf_op jit(solution)/shard_map/ppermute | solution.py:310
  428.0 15.4 %collective-permute-start.69 = (bf16[6,128,256]{2,1,0:T(8,128)(2,1)}, bf16[6,128,256]{2,1,0:T(8,128)(2,1)}, u32[]{:S(2)}, u32[]{:S(2)}) collective-permute-start(bf16[6,128,256]{2,1,0:T(8,128)(2,1)} %fusion.8), channel_id=1, source_target_pairs={{0,8},{1,9},{2,10},{3,11},{4,12},{5,13},{6,14},{7,15},{8,16},{9,17... | collective-permute-start | bytes 1179656 | tf_op jit(solution)/shard_map/ppermute | solution.py:310
  432.5 10.9 %collective-permute-start.70 = (bf16[2,128,256]{2,1,0:T(8,128)(2,1)}, bf16[2,128,256]{2,1,0:T(8,128)(2,1)}, u32[]{:S(2)}, u32[]{:S(2)}) collective-permute-start(bf16[2,128,256]{2,1,0:T(8,128)(2,1)} %fusion.11), channel_id=1, source_target_pairs={{0,8},{1,9},{2,10},{3,11},{4,12},{5,13},{6,14},{7,15},{8,16},{9,17... | collective-permute-start | bytes 393224 | tf_op jit(solution)/shard_map/ppermute | solution.py:310
  445.1 11.4 %collective-permute-start.72 = (bf16[6,128,256]{2,1,0:T(8,128)(2,1)S(1)}, bf16[6,128,256]{2,1,0:T(8,128)(2,1)S(1)}, u32[]{:S(2)}, u32[]{:S(2)}) collective-permute-start(bf16[6,128,256]{2,1,0:T(8,128)(2,1)S(1)} %fusion.1), channel_id=1, source_target_pairs={{0,8},{1,9},{2,10},{3,11},{4,12},{5,13},{6,14},{7,15},{8,16},{9,17... | collective-permute-start | bytes 1179656 | tf_op jit(solution)/shard_map/ppermute | solution.py:310
  458.5 10.7 %collective-permute-start.73 = (bf16[6,128,256]{2,1,0:T(8,128)(2,1)}, bf16[6,128,256]{2,1,0:T(8,128)(2,1)}, u32[]{:S(2)}, u32[]{:S(2)}) collective-permute-start(bf16[6,128,256]{2,1,0:T(8,128)(2,1)} %fusion), channel_id=1, source_target_pairs={{0,8},{1,9},{2,10},{3,11},{4,12},{5,13},{6,14},{7,15},{8,16},{9,17... | collective-permute-start | bytes 1179656 | tf_op jit(solution)/shard_map/ppermute | solution.py:310
  (145 other events, 1079.0 us)
